TPU v7x, 32 devices: a whole 2x2x4 slice. The times are simulated.
32 devices in a mesh: grp: 4 (over z), slab: 8 (over y, x, core).
Axes of the slice: x: 2, y: 2, z: 4, core: 2. Of those that a mesh axis runs over, the one named last changes fastest.
Arguments:
- spectra: bfloat16 [16384, 2048], P(('grp', 'slab')), may hold values from -6 to 6
- ctf_sq: bfloat16 [16384, 1024], P(('grp', 'slab')), may hold values from 0.049804688 to 1
- dest: int32 [16384, 1], P(('grp', 'slab')), may hold values from 0 to 7; in each aligned block of 512 rows (0 to 511, 512 to 1023, ...) at most 128 rows name the same one
- block: int32 [16384], P(('grp', 'slab')), may hold values from 0 to 63
- pattern: int32 [16384], P(('grp', 'slab')), may hold values from 0 to 63
- pattern_table: bfloat16 [64, 8], replicated, may hold values from 0.049804688 to 1
- tau: float32 [1024], replicated, may hold values from 0.5 to 4
Outputs:
- image: float32 [2, 16, 256, 1024], P(None, 'grp', None, 'slab')
Inputs may be any that keep to these rules, and one draw needn't show every extreme that they name: `dest`: among the rows of one device at most 128 name the same slab; in some device's rows one slab is named by exactly 128.
All inputs are finite; a program needn't handle non-finite values.
Results may differ from a plain program's by a relative error of at most 0.0003.
Values may be sent and summed in bfloat16 or wider, within the bound.
No kernel may reach another device: no remote copies, remote signals or barrier semaphores. Data moves between devices by JAX's collectives and lax.ppermute only.
A program may use at most 192 MiB of HBM per device.

v0:
```python
import math

import jax
import jax.numpy as jnp
from jax import lax
from jax.sharding import PartitionSpec as P

KZ_DEV = 32
YWIN = 16
NBLK = 64


def dft_tables(length):
    indices = jnp.arange(length, dtype=jnp.int32)
    product = indices[:, None] * indices[None, :] % length
    angles = product.astype(jnp.float32) * (2.0 * math.pi / length)
    return (jnp.cos(angles), jnp.sin(angles))


def inverse_kz(filtered, cosine, sine):
    real_part = filtered[:, :, 0, :]
    imag_part = filtered[:, :, 1, :]
    scaling = 1.0 / math.sqrt(cosine.shape[0])
    highest = lax.Precision.HIGHEST
    out_real = jnp.einsum("zk,ykx->yzx", cosine, real_part, precision=highest) - jnp.einsum(
        "zk,ykx->yzx", sine, imag_part, precision=highest
    )
    out_imag = jnp.einsum("zk,ykx->yzx", sine, real_part, precision=highest) + jnp.einsum(
        "zk,ykx->yzx", cosine, imag_part, precision=highest
    )
    return jnp.stack([out_real * scaling, out_imag * scaling])


def on_device(spectra, ctf_sq, dest, block, pattern, pattern_table, tau):
    slab_count = lax.axis_size("slab")
    rows_here = spectra.shape[0]
    kx_width = ctf_sq.shape[1]
    spread = pattern_table.shape[1]
    capacity = max(2, 2 * rows_here // slab_count)
    slot_total = slab_count * capacity
    slab_ids = jnp.arange(slab_count, dtype=jnp.int32)
    matches = (dest == slab_ids[None, :]).astype(jnp.int32)
    earlier = jnp.cumsum(matches, axis=0) - matches
    position = jnp.sum(earlier * matches, axis=1)
    target = dest[:, 0] * capacity + position
    pattern_ids = jnp.arange(pattern_table.shape[0], dtype=jnp.int32)
    pattern_onehot = (pattern[:, None] == pattern_ids[None, :]).astype(jnp.bfloat16)
    row_weights = jnp.dot(pattern_onehot, pattern_table, preferred_element_type=jnp.float32).astype(
        jnp.bfloat16
    )
    block_label = (block + 1).astype(jnp.float32).astype(jnp.bfloat16)[:, None]
    send_spec = jnp.zeros((slot_total, 2 * kx_width), jnp.bfloat16).at[target].set(spectra)
    send_ctf = jnp.zeros((slot_total, kx_width), jnp.bfloat16).at[target].set(ctf_sq)
    send_weights = jnp.zeros((slot_total, spread), jnp.bfloat16).at[target].set(row_weights)
    send_label = jnp.zeros((slot_total, 1), jnp.bfloat16).at[target].set(block_label)
    got_spec, got_ctf, got_weights, got_label = (
        lax.all_to_all(send_spec, "slab", split_axis=0, concat_axis=0, tiled=True),
        lax.all_to_all(send_ctf, "slab", split_axis=0, concat_axis=0, tiled=True),
        lax.all_to_all(send_weights, "slab", split_axis=0, concat_axis=0, tiled=True),
        lax.all_to_all(send_label, "slab", split_axis=0, concat_axis=0, tiled=True),
    )
    block_ids = jnp.arange(1, NBLK + 1, dtype=jnp.int32).astype(jnp.float32)
    block_match = (got_label.astype(jnp.float32) == block_ids[None, :]).astype(jnp.bfloat16)
    spreader = (block_match[:, :, None] * got_weights[:, None, :]).reshape(
        slot_total, NBLK * spread
    )
    contract = (((0,), (0,)), ((), ()))
    cosine, sine = dft_tables(KZ_DEV * slab_count)
    column_width = kx_width // slab_count
    data_sum = lax.dot_general(spreader, got_spec, contract, preferred_element_type=jnp.float32)
    weight_sum = lax.dot_general(spreader, got_ctf, contract, preferred_element_type=jnp.float32)
    data_sum = data_sum.reshape(YWIN, KZ_DEV, 2, kx_width)
    weight_sum = weight_sum.reshape(YWIN, KZ_DEV, 1, kx_width)
    volume = jnp.concatenate([data_sum, weight_sum], axis=2)
    columns_all = lax.all_to_all(volume, "slab", split_axis=3, concat_axis=1, tiled=True)
    summed = lax.psum_scatter(columns_all, "grp", scatter_dimension=0, tiled=True)
    tau_part = lax.dynamic_slice_in_dim(tau, lax.axis_index("slab") * column_width, column_width, 0)
    filtered = summed[:, :, 0:2, :] / (summed[:, :, 2:3, :] + tau_part[None, None, None, :])
    image = inverse_kz(filtered, cosine, sine)
    return image


def solution(mesh):
    in_specs = (
        P(("grp", "slab"), None),
        P(("grp", "slab"), None),
        P(("grp", "slab"), None),
        P(("grp", "slab")),
        P(("grp", "slab")),
        P(),
        P(),
    )
    out_specs = P(None, "grp", None, "slab")
    return jax.shard_map(
        on_device, mesh=mesh, in_specs=in_specs, out_specs=out_specs, check_vma=False
    )
```

profile of v0, /device:TPU:0, one launch (start us, length us, event | category | flops | bytes accessed | tf_op | source)
XLA Modules:
  0.0 547.0 jit_solution(4065495544797125418)
XLA Ops:
  6.5 0.7 fusion.32
  7.2 1.1 reduce-window.6
  8.4 0.2 slice_reduce_fusion
  8.6 0.8 fusion.31
  9.4 0.7 compare_select_fusion
  10.1 0.7 convert_convert_fusion
  10.8 3.8 scatter_custom_fusion
  14.5 0.6 copy.34
  15.1 5.2 all-to-all-start
  20.3 0.9 convolution_convert_fusion
  21.3 0.2 copy.36
  21.4 1.8 scatter_custom_fusion.1
  23.3 0.7 copy.37
  24.0 1.0 all-to-all-done
  25.0 3.3 all-to-all-start.1
  28.3 4.8 scatter_custom_fusion.3
  33.1 4.3 all-to-all-start.3
  37.5 7.3 %scatter_custom_fusion.2 = bf16[1024,2048]{1,0:T(8,128)(2,1)} fusion(s32[512]{0:T(512)S(1)} %bitcast.105, bf16[512,2048]{1,0:T(8,128)(2,1)} %param.7, bf16[]{:T(256)} %constant.12.clone.1), kind=kCustom, calls=%fused_computation.5 | custom fusion | bytes 4194816 | tf_op jit(solution)/shard_map/scatter | solution.py:52
  44.7 19.4 %all-to-all-done.3 = bf16[8,128,1024]{2,1,0:T(8,128)(2,1)S(1)} async-done(((bf16[8,128,1024]{2,1,0:T(8,128)(2,1)}), bf16[8,128,1024]{2,1,0:T(8,128)(2,1)S(1)}, u32[]{:S(2)}, u32[]{:S(2)}) %all-to-all-start.3) | async-done | bytes 2097184 | tf_op jit(solution)/shard_map/all_to_all | solution.py:58
  64.1 4.5 all-to-all-start.2
  68.6 0.0 all-reduce.3.cloned.1.call-start
  68.7 0.1 compare_convert_fusion
  68.8 0.1 broadcast_multiply_fusion
  69.0 2.7 convolution_bitcast_fusion
  71.6 46.1 %all-to-all-done.2 = bf16[8,128,2048]{2,1,0:T(8,128)(2,1)} async-done(((bf16[8,128,2048]{2,1,0:T(8,128)(2,1)}), bf16[8,128,2048]{2,1,0:T(8,128)(2,1)}, u32[]{:S(2)}, u32[]{:S(2)}) %all-to-all-start.2) | async-done | bytes 4194336 | tf_op jit(solution)/shard_map/all_to_all | solution.py:57
  117.8 6.4 %copy.45 = bf16[1024,2048]{0,1:T(8,128)(2,1)} copy(bf16[1024,2048]{1,0:T(8,128)(2,1)} %bitcast.16) | data formatting | bytes 8388608 | tf_op jit(solution)/shard_map/all_to_all | solution.py:57
  124.2 4.7 fusion.51
  128.9 3.3 pad_maximum_fusion
  132.2 18.1 %copy.39 = f32[16,32,3,1024]{1,0,2,3:T(8,128)} copy(f32[16,32,3,1024]{3,1,2,0:T(8,128)} %pad_maximum_fusion) | data formatting | bytes 12582912 | tf_op jit(solution)/shard_map/concatenate | solution.py:74
  150.3 16.7 %reshape.141 = f32[8,1,196608]{2,1,0:T(1,128)} reshape(f32[1024,3,16,32]{3,2,1,0:T(8,128)} %bitcast.89) | data formatting | bytes 12582912
  167.0 77.1 %all_to_all.60 = f32[8,1,196608]{2,1,0:T(1,128)} all-to-all(f32[8,1,196608]{2,1,0:T(1,128)} %reshape.141), channel_id=1, replica_groups=mesh['grp'=4,'slab'=8] {'slab'}, dimensions={0} | all-to-all | bytes 12582912 | tf_op jit(solution)/shard_map/all_to_all | solution.py:75
  244.1 0.5 broadcast.96
  244.6 19.9 %reduce.2 = f32[8,196608]{1,0:T(8,128)} reduce(f32[8,1,196608]{2,1,0:T(1,128)} %all_to_all.60, f32[]{:T(128)} %broadcast.96), dimensions={1}, to_apply=%all_to_all.51.reduce_sub_computation | reduce | bytes 12582916 | tf_op jit(solution)/shard_map/all_to_all | solution.py:75
  264.5 19.2 %reshape.142 = f32[1024,3,16,32]{3,2,1,0:T(8,128)} reshape(f32[8,196608]{1,0:T(8,128)} %reduce.2) | data formatting | bytes 12582912
  283.7 16.6 %copy.41 = f32[16,8,32,3,128]{4,2,1,3,0:T(8,128)} copy(f32[16,8,32,3,128]{2,0,3,4,1:T(8,128)} %bitcast.90) | data formatting | bytes 12582912 | tf_op jit(solution)/shard_map/all_to_all | solution.py:75
  300.3 6.8 %copy.42 = f32[16,256,3,128]{1,3,0,2:T(8,128)} copy(f32[16,256,3,128]{3,1,2,0:T(8,128)} %bitcast.91) | data formatting | bytes 12582912 | tf_op jit(solution)/shard_map/all_to_all | solution.py:75
  307.1 0.0 all-reduce.3.cloned.1.call-update
  307.1 0.8 dynamic_slice.3
  307.9 0.6 dynamic-slice
  309.1 220.4 %all-reduce.3.cloned.1.call-done = f32[16,256,3,128]{1,3,0,2:T(8,128)} async-done(((f32[16,256,3,128]{1,3,0,2:T(8,128)}), f32[16,256,3,128]{1,3,0,2:T(8,128)}) %all-reduce.3.cloned.1.call-update) | async-done | bytes 6291472
  529.4 1.1 fusion.8
  530.6 1.4 dynamic-slice_divide_fusion
  532.0 1.6 fusion.10
  533.6 1.6 fusion.9
  535.1 1.6 fusion.5
  536.7 1.6 fusion.3
  538.3 0.1 pad_maximum_fusion.1
  538.4 1.3 copy.43
  (13 shorter events, 0.1 us)
Async XLA Ops:
  6.5 13.8 %copy-start = (bf16[64,8]{0,1:T(8,128)(2,1)S(1)}, bf16[64,8]{0,1:T(8,128)(2,1)}, u32[]{:S(2)}) copy-start(bf16[64,8]{0,1:T(8,128)(2,1)} %param.12) | copy-start | bytes 3076
  15.1 9.8 %all-to-all-start = ((bf16[8,128,1]{1,2,0:T(2,128)(2,1)}), bf16[8,128,1]{1,2,0:T(2,128)(2,1)S(1)}, u32[]{:S(2)}, u32[]{:S(2)}) async-start(bf16[8,128,1]{1,2,0:T(2,128)(2,1)} %copy.34), calls=%async_computation | async-start | bytes 8192 | tf_op jit(solution)/shard_map/all_to_all | solution.py:60
  25.0 8.2 %all-to-all-start.1 = ((bf16[8,128,8]{1,2,0:T(8,128)(2,1)}), bf16[8,128,8]{1,2,0:T(8,128)(2,1)S(1)}, u32[]{:S(2)}, u32[]{:S(2)}) async-start(bf16[8,128,8]{1,2,0:T(8,128)(2,1)} %bitcast.8), calls=%async_computation.1 | async-start | bytes 32768 | tf_op jit(solution)/shard_map/all_to_all | solution.py:59
  33.1 30.9 %all-to-all-start.3 = ((bf16[8,128,1024]{2,1,0:T(8,128)(2,1)}), bf16[8,128,1024]{2,1,0:T(8,128)(2,1)S(1)}, u32[]{:S(2)}, u32[]{:S(2)}) async-start(bf16[8,128,1024]{2,1,0:T(8,128)(2,1)} %bitcast.22), calls=%async_computation.3 | async-start | bytes 4194304 | tf_op jit(solution)/shard_map/all_to_all | solution.py:58
  64.1 53.7 %all-to-all-start.2 = ((bf16[8,128,2048]{2,1,0:T(8,128)(2,1)}), bf16[8,128,2048]{2,1,0:T(8,128)(2,1)}, u32[]{:S(2)}, u32[]{:S(2)}) async-start(bf16[8,128,2048]{2,1,0:T(8,128)(2,1)} %bitcast.92), calls=%async_computation.2 | async-start | bytes 8388608 | tf_op jit(solution)/shard_map/all_to_all | solution.py:57
  68.6 460.8 %all-reduce.3.cloned.1.call-start = ((), (), s32[]{:S(2)}) async-start(), calls=%async_computation.5 | async-start | bytes 12582912
  124.2 4.7 copy-start.2
  307.0 0.8 copy-start.3
  532.0 7.7 %copy-start.1 = (bf16[64,8]{0,1:T(8,128)(2,1)S(1)}, bf16[64,8]{0,1:T(8,128)(2,1)}, u32[]{:S(2)}) copy-start(bf16[64,8]{0,1:T(8,128)(2,1)} %param.12) | copy-start | bytes 3076
Sparse Core Ops, SparseCore 0:
  307.2 222.1 all-reduce.2
where the time goes:
time: 555 us; the launch traced here: 547 us
  waiting for transfers between devices  287 us (52%)
  local copies, waits for them, and re-layouts  106 us (19%)
  blocking collectives  77.1 us (14%)
  other arithmetic  30 us (5%)
  starting transfers between devices  17.4 us (3%)
  between operations  14.7 us (3%)
  matrix products  14.6 us (3%)
    unnamed x2, waiting for transfers between devices  220 us
    all_to_all x1, blocking collectives, on_device(): lax.all_to_all(volume, 'slab', split_axis=3, concat_axis=1, tiled=True)  77.1 us
    all_to_all x1, waiting for transfers between devices, on_device(): lax.all_to_all(send_spec, 'slab', split_axis=0, concat_axis=0, tiled=True)  46.1 us
    unnamed x11, local copies, waits for them, and re-layouts  36.5 us
    all_to_all x3, local copies, waits for them, and re-layouts, on_device(): lax.all_to_all(volume, 'slab', split_axis=3, concat_axis=1, tiled=True)  23.9 us
    all_to_all x1, other arithmetic, on_device(): lax.all_to_all(volume, 'slab', split_axis=3, concat_axis=1, tiled=True)  19.9 us
    all_to_all x1, waiting for transfers between devices, on_device(): lax.all_to_all(send_ctf, 'slab', split_axis=0, concat_axis=0, tiled=True)  19.4 us
    concatenate x1, local copies, waits for them, and re-layouts, on_device(): volume = jnp.concatenate([data_sum, weight_sum], axis=2)  18.1 us
  transfers between devices with their start and end apart: 5, of which 4 were waited for; matrix products, arithmetic and copies ran while one was open for 4% of the time, Pallas kernels for 0%

commit v1 on v0

v1 whole, which is shorter than its diff:
```python
import functools
import math

import jax
import jax.numpy as jnp
import numpy as np
from jax import lax
from jax.experimental import pallas as pl
from jax.experimental.pallas import tpu as pltpu
from jax.sharding import PartitionSpec as P

KZ_DEV = 32
YWIN = 16
NBLK = 64
LANES = 128
ALIGN = 16
TOP = 32767.0
STEPS = 256.0
VMEM = 60 * 1024 * 1024

WHOLE = pl.BlockSpec(memory_space=pltpu.VMEM)
SCALARS = pl.BlockSpec(memory_space=pltpu.SMEM)


def params():
    return pltpu.CompilerParams(vmem_limit_bytes=VMEM)


def iota(shape, axis):
    return lax.broadcasted_iota(jnp.int32, shape, axis)


def plan_kernel(slabs, window, dest_ref, block_ref, pattern_ref, table_ref, order_ref, meta_ref):
    rows = dest_ref.shape[1]
    dest = dest_ref[...]
    mine = (dest == iota((slabs, rows), 0)).astype(jnp.float32)
    before = (iota((rows, rows), 0) < iota((rows, rows), 1)).astype(jnp.bfloat16)
    rank = jnp.dot(mine.astype(jnp.bfloat16), before, preferred_element_type=jnp.float32)
    counts = jnp.sum(mine, axis=1, keepdims=True)
    slab_of = iota((slabs, rows), 0)
    first = jnp.sum(jnp.where(slab_of < dest, counts, 0.0), axis=0, keepdims=True)
    target = (first + jnp.sum(mine * rank, axis=0, keepdims=True)).astype(jnp.int32)
    order = (target == iota((rows, rows), 0)).astype(jnp.bfloat16)
    order_ref[...] = order
    ids = (pattern_ref[...] == iota((table_ref.shape[1], rows), 0)).astype(jnp.bfloat16)
    weights = jnp.dot(table_ref[...], ids, preferred_element_type=jnp.float32)
    line = iota((8, rows), 0)
    named = jnp.where(line == 0, dest, jnp.where(line == 1, block_ref[...], 0)).astype(jnp.float32)
    given = jnp.concatenate([weights, named], axis=0).astype(jnp.bfloat16)
    ordered = lax.dot_general(given, order, (((1,), (1,)), ((), ())), preferred_element_type=jnp.float32)
    start = jnp.sum(jnp.where(slab_of < iota((slabs, rows), 1), counts, 0.0), axis=0, keepdims=True)
    start = jnp.minimum(start.astype(jnp.int32) // ALIGN, (rows - window) // ALIGN).astype(jnp.float32)
    ordered = jnp.where(iota((16, rows), 0) == 10, start, ordered)
    meta_ref[...] = ordered.astype(jnp.bfloat16)


def plan_rows(slabs, window, dest, block, pattern, table):
    rows = dest.shape[0]
    return pl.pallas_call(
        functools.partial(plan_kernel, slabs, window),
        out_shape=(
            jax.ShapeDtypeStruct((rows, rows), jnp.bfloat16),
            jax.ShapeDtypeStruct((16, rows), jnp.bfloat16),
        ),
        in_specs=[WHOLE] * 4,
        out_specs=(WHOLE, WHOLE),
        compiler_params=params(),
        name="plan_rows",
    )(dest.reshape(1, rows), block.reshape(1, rows), pattern.reshape(1, rows), table.T)


def sort_kernel(slabs, width, me_ref, order_ref, x_ref, *out_refs):
    order = order_ref[...]
    for offset in range(slabs):
        column = jnp.bitwise_xor(me_ref[0], offset)
        if len(x_ref.shape) == 3:
            piece = x_ref[column]
        else:
            piece = x_ref[:, pl.ds(pl.multiple_of(column * width, width), width)]
        out_refs[offset][...] = jnp.dot(order, piece, preferred_element_type=jnp.float32).astype(jnp.bfloat16)


def sort_columns(slabs, me, order, x, part, kx):
    rows, width = order.shape[0], kx // slabs
    if width % LANES:
        x = lax.slice_in_dim(x, part * kx, (part + 1) * kx, axis=1)
        x = x.reshape(rows, slabs, width).transpose(1, 0, 2)
        x_spec = pl.BlockSpec((slabs, rows, width), lambda i, s: (0, 0, 0))
    else:
        x_spec = pl.BlockSpec((rows, kx), lambda i, s: (0, part))
    return pl.pallas_call(
        functools.partial(sort_kernel, slabs, width),
        out_shape=[jax.ShapeDtypeStruct((rows, width), jnp.bfloat16)] * slabs,
        grid_spec=pltpu.PrefetchScalarGridSpec(
            num_scalar_prefetch=1,
            grid=(1,),
            in_specs=[pl.BlockSpec((rows, rows), lambda i, s: (0, 0)), x_spec],
            out_specs=[pl.BlockSpec((rows, width), lambda i, s: (0, 0))] * slabs,
        ),
        compiler_params=params(),
        name="sort_columns",
    )(me, order, x)


def exchange(pieces):
    slabs = len(pieces)
    return [pieces[0]] + [
        lax.ppermute(pieces[o], "slab", [(i, i ^ o) for i in range(slabs)]) for o in range(1, slabs)
    ]


def spread_kernel(slabs, window, me_ref, meta_ref, weight_ref, start_ref, all_ref, here_ref, line_ref, scalar_ref, sem):
    slab = pl.program_id(0)
    rows = meta_ref.shape[2]

    @pl.when(slab == 0)
    def _():
        pick = (iota((16, LANES), 0) == iota((16, LANES), 1)).astype(jnp.bfloat16)
        for offset in range(slabs):
            meta = meta_ref[jnp.bitwise_xor(me_ref[0], offset)]
            all_ref[offset] = lax.dot_general(
                meta, pick, (((0,), (0,)), ((), ())), preferred_element_type=jnp.float32
            ).astype(jnp.bfloat16)
            line_ref[offset : offset + 1, :] = meta.astype(jnp.float32)[10:11, 0:LANES].astype(jnp.int32) * ALIGN
        copy = pltpu.make_async_copy(line_ref, scalar_ref, sem)
        copy.start()
        copy.wait()
        start_ref[...] = line_ref[...]

    for offset in range(slabs):
        start = pl.multiple_of(scalar_ref[offset, slab], ALIGN)
        here_ref[offset * window : (offset + 1) * window, :] = all_ref[offset, pl.ds(start, window), :]
    pick = (iota((16, LANES), 0) == iota((16, LANES), 1)).astype(jnp.bfloat16)
    meta = lax.dot_general(pick, here_ref[...], (((1,), (1,)), ((), ())), preferred_element_type=jnp.float32)
    weights = meta[0:8]
    total = weights.shape[1]
    block = jnp.where(meta[8:9] == slab.astype(jnp.float32), meta[9:10], -1.0)
    block = jnp.broadcast_to(block, (8, total))
    for b in range(0, NBLK, 2):
        pair = [jnp.where(block == float(b + i), weights, 0.0) for i in range(2)]
        weight_ref[0, b * 8 : b * 8 + 16, :] = jnp.concatenate(pair, axis=0).astype(jnp.bfloat16)


def spread_weights(window, me, meta):
    slabs, _, rows = meta.shape
    total = slabs * window
    return pl.pallas_call(
        functools.partial(spread_kernel, slabs, window),
        out_shape=(
            jax.ShapeDtypeStruct((slabs, NBLK * 8, total), jnp.bfloat16),
            jax.ShapeDtypeStruct((slabs, LANES), jnp.int32),
        ),
        grid_spec=pltpu.PrefetchScalarGridSpec(
            num_scalar_prefetch=1,
            grid=(slabs,),
            in_specs=[pl.BlockSpec((slabs, 16, rows), lambda d, s: (0, 0, 0))],
            out_specs=(
                pl.BlockSpec((1, NBLK * 8, total), lambda d, s: (d, 0, 0)),
                pl.BlockSpec((slabs, LANES), lambda d, s: (0, 0)),
            ),
            scratch_shapes=[
                pltpu.VMEM((slabs, rows, LANES), jnp.bfloat16),
                pltpu.VMEM((total, LANES), jnp.bfloat16),
                pltpu.VMEM((slabs, LANES), jnp.int32),
                pltpu.SMEM((slabs, LANES), jnp.int32),
                pltpu.SemaphoreType.DMA,
            ],
        ),
        compiler_params=params(),
        name="spread_weights",
    )(me, meta)


def volume_kernel(slabs, window, start_ref, weight_ref, *refs):
    piece_refs, out_ref, here_ref = refs[:slabs], refs[slabs], refs[slabs + 1]
    slab = pl.program_id(0)
    for offset in range(slabs):
        start = pl.multiple_of(start_ref[offset, slab], ALIGN)
        here_ref[offset * window : (offset + 1) * window, :] = piece_refs[offset][pl.ds(start, window), :]
    sums = jnp.dot(weight_ref[0], here_ref[...], preferred_element_type=jnp.float32)
    out_ref[:, 0] = sums.reshape(YWIN, KZ_DEV, sums.shape[1])


def volume_sums(window, starts, weights, pieces):
    slabs = len(pieces)
    rows, width = pieces[0].shape
    total = slabs * window
    return pl.pallas_call(
        functools.partial(volume_kernel, slabs, window),
        out_shape=jax.ShapeDtypeStruct((YWIN, slabs, KZ_DEV, width), jnp.float32),
        grid_spec=pltpu.PrefetchScalarGridSpec(
            num_scalar_prefetch=1,
            grid=(slabs,),
            in_specs=[pl.BlockSpec((1, NBLK * 8, total), lambda d, s: (d, 0, 0))]
            + [pl.BlockSpec((rows, width), lambda d, s: (0, 0))] * slabs,
            out_specs=pl.BlockSpec((YWIN, 1, KZ_DEV, width), lambda d, s: (0, d, 0, 0)),
            scratch_shapes=[pltpu.VMEM((total, width), jnp.bfloat16)],
        ),
        compiler_params=params(),
        name="volume_sums",
    )(starts, weights, *pieces)


def encode(x):
    rows, width = x.shape
    groups = rows // 8
    tiles = x.reshape(groups, 8, width)
    size = jnp.abs(tiles)
    most = jnp.max(jnp.max(size, axis=1), axis=1, keepdims=True)
    level = jnp.ceil(jnp.log2(jnp.maximum(most, 1e-30)) * STEPS) + 1.0
    inverse = jnp.broadcast_to(jnp.exp2(level * (-1.0 / STEPS)), (groups, width)).reshape(groups, 1, width)
    share = jnp.maximum(size * inverse, 1e-12)
    root = jnp.minimum(share * lax.rsqrt(share) * TOP + 0.5, TOP)
    code = jnp.where(tiles < 0, -root, root).reshape(rows, width).astype(jnp.int32).astype(jnp.int16)
    eye = iota((width, width), 0) == iota((width, width), 1)
    lines = [
        jnp.sum(jnp.where(eye, level[i * width : (i + 1) * width], 0.0), axis=0, keepdims=True)
        for i in range(groups // width)
    ]
    lines.append(jnp.zeros((ALIGN - len(lines), width), jnp.float32))
    return code, jnp.concatenate(lines, axis=0).astype(jnp.int32).astype(jnp.int16)


def decode(code, lines):
    rows, width = code.shape
    groups = rows // 8
    x = code.astype(jnp.int32).astype(jnp.float32)
    lines = lines.astype(jnp.int32).astype(jnp.float32)
    eye = iota((width, width), 0) == iota((width, width), 1)
    level = jnp.concatenate(
        [jnp.sum(jnp.where(eye, lines[i : i + 1], 0.0), axis=1, keepdims=True) for i in range(groups // width)],
        axis=0,
    )
    scale = jnp.exp2(level * (1.0 / STEPS)) * (1.0 / (TOP * TOP))
    scale = jnp.broadcast_to(scale, (groups, width)).reshape(groups, 1, width)
    return ((x * jnp.abs(x)).reshape(groups, 8, width) * scale).reshape(rows, width)


def hop_kernel(has_prev, idx_ref, sums_ref, *refs):
    out_ref = refs[-1]
    rows = sums_ref.shape[1]
    x = sums_ref[0]
    if has_prev:
        x = x + decode(refs[0][0, :rows, :], refs[0][0, rows:, :])
    code, lines = encode(x)
    out_ref[0, :rows, :] = code
    out_ref[0, rows:, :] = lines


def hop(index, sums, count, prev, place):
    _, rows, width = sums.shape
    shape = (1, rows + ALIGN, width)
    in_specs = [pl.BlockSpec((1, rows, width), lambda i, s: (s[i], 0, 0))]
    operands = [sums]
    if prev is not None:
        in_specs.append(pl.BlockSpec(shape, lambda i, s: (place(i), 0, 0)))
        operands.append(prev)
    return pl.pallas_call(
        functools.partial(hop_kernel, prev is not None),
        out_shape=jax.ShapeDtypeStruct((count, rows + ALIGN, width), jnp.int16),
        grid_spec=pltpu.PrefetchScalarGridSpec(
            num_scalar_prefetch=1,
            grid=(count,),
            in_specs=in_specs,
            out_specs=pl.BlockSpec(shape, lambda i, s: (i, 0, 0)),
        ),
        compiler_params=params(),
        name="hop",
    )(index, *operands)


def along_z(sums, z, groups):
    half = groups // 2
    far = z >= half

    def portions(first, count):
        r = jnp.arange(first, first + count, dtype=jnp.int32)
        return jnp.where(far, groups - 1 - r, r)

    def both(pairs):
        return pairs + [(groups - 1 - a, groups - 1 - b) for a, b in pairs]

    ends = []
    prev = None
    for k in range(1, half):
        payload = hop(portions(k, groups - k), sums, groups - k, prev, lambda i: i + 1)
        prev = lax.ppermute(payload, "grp", both([(k - 1, k)]))
        ends.append((prev, 0))
    payload = hop(portions(half, half), sums, half, prev, lambda i: i + 1)
    prev = lax.ppermute(payload, "grp", both([(half - 1, half)]))
    ends.append((prev, 0))
    place = lambda i: half - 1 - i
    for j in range(half - 1, 0, -1):
        payload = hop(portions(0, j), sums, j, prev, place)
        prev = lax.ppermute(payload, "grp", both([(j, j - 1)]))
        ends.append((prev, j - 1))
        place = lambda i: i
    return ends


def image_kernel(parts, zs, own_ref, *refs):
    tau_ref, high_ref, low_ref, out_ref = refs[-4:]
    each = len(refs[:-4]) // 3
    volume = []
    for c in range(3):
        sums_ref, coded = refs[c * each], refs[c * each + 1 : (c + 1) * each]
        rows = sums_ref.shape[1]
        x = sums_ref[0]
        for ref in coded:
            x = x + decode(ref[0, :rows, :], ref[0, rows:, :])
        volume.append(x)
    below = volume[2] + tau_ref[...]
    columns = []
    for c in range(2):
        x = volume[c] / below
        columns += [x[k * zs : (k + 1) * zs] for k in range(parts)]
    x = jnp.concatenate(columns, axis=1)
    x_high = x.astype(jnp.bfloat16)
    x_low = (x - x_high.astype(jnp.float32)).astype(jnp.bfloat16)
    dot = functools.partial(jnp.dot, preferred_element_type=jnp.float32)
    y = dot(high_ref[...], x_high) + (dot(high_ref[...], x_low) + dot(low_ref[...], x_high))
    span = x.shape[1] // 2
    width = span // parts
    real = y[:zs, :span] - y[zs:, span:]
    imag = y[zs:, :span] + y[:zs, span:]
    for k in range(parts):
        out_ref[0, k] = real[:, k * width : (k + 1) * width]
        out_ref[1, k] = imag[:, k * width : (k + 1) * width]


def image_of(own, fields, tau, zs):
    rows, width = fields[0][0].shape[1:]
    parts = rows // zs
    operands, specs = [], []
    for sums, ends in fields:
        operands.append(sums)
        specs.append(pl.BlockSpec((1, rows, width), lambda i, s: (s[0], 0, 0)))
        for payload, place in ends:
            operands.append(payload)
            specs.append(pl.BlockSpec((1, rows + ALIGN, width), functools.partial(lambda place, i, s: (place, 0, 0), place)))
    steps = np.arange(zs)
    angles = (steps[:, None] * steps[None, :] % zs) * (2.0 * math.pi / zs)
    table = (np.concatenate([np.cos(angles), np.sin(angles)], axis=0) / math.sqrt(zs)).astype(np.float32)
    high = table.astype(jnp.bfloat16)
    low = (table - high.astype(np.float32)).astype(jnp.bfloat16)
    for x in (tau.reshape(1, width), jnp.asarray(high), jnp.asarray(low)):
        operands.append(x)
        specs.append(pl.BlockSpec(x.shape, lambda i, s: (0, 0)))
    return pl.pallas_call(
        functools.partial(image_kernel, parts, zs),
        out_shape=jax.ShapeDtypeStruct((2, parts, zs, width), jnp.float32),
        grid_spec=pltpu.PrefetchScalarGridSpec(
            num_scalar_prefetch=1,
            grid=(1,),
            in_specs=specs,
            out_specs=pl.BlockSpec((2, parts, zs, width), lambda i, s: (0, 0, 0, 0)),
        ),
        compiler_params=params(),
        name="image_of",
    )(own, *operands)


def on_device(spectra, ctf_sq, dest, block, pattern, pattern_table, tau):
    slabs, groups = lax.axis_size("slab"), lax.axis_size("grp")
    rows, kx = ctf_sq.shape
    capacity = max(2, 2 * rows // slabs)
    window = min(rows, -(-capacity // ALIGN) * ALIGN + ALIGN)
    width = kx // slabs
    slab, z = lax.axis_index("slab"), lax.axis_index("grp")
    me = slab.astype(jnp.int32).reshape(1)
    order, meta = plan_rows(slabs, window, dest, block, pattern, pattern_table)
    meta = lax.all_gather(meta, "slab")
    sources = ((ctf_sq, 0), (spectra, 0), (spectra, 1))
    pieces = [exchange(sort_columns(slabs, me, order, x, part, kx)) for x, part in sources]
    weights, starts = spread_weights(window, me, meta)
    fields = []
    for piece in pieces:
        sums = volume_sums(window, starts, weights, piece)
        sums = sums.reshape(groups, YWIN // groups * slabs * KZ_DEV, width)
        fields.append((sums, along_z(sums, z, groups)))
    tau_here = lax.dynamic_slice_in_dim(tau, slab * width, width, 0)
    own = z.astype(jnp.int32).reshape(1)
    return image_of(own, [fields[1], fields[2], fields[0]], tau_here, KZ_DEV * slabs)


def solution(mesh):
    in_specs = (
        P(("grp", "slab"), None),
        P(("grp", "slab"), None),
        P(("grp", "slab"), None),
        P(("grp", "slab")),
        P(("grp", "slab")),
        P(),
        P(),
    )
    out_specs = P(None, "grp", None, "slab")
    return jax.shard_map(
        on_device, mesh=mesh, in_specs=in_specs, out_specs=out_specs, check_vma=False
    )
```

time: 555 us -> 191 us (0.34); the launches traced: 547 us -> 190 us
  waiting for transfers between devices: 287 us -> 41.7 us
  local copies, waits for them, and re-layouts: 106 us -> 7.22 us
  Pallas kernels: 0 us -> 89.7 us
  blocking collectives: 77.1 us -> 12.9 us
  other arithmetic: 30 us -> 1.03 us
  starting transfers between devices: 17.4 us -> 36.9 us
  matrix products: 14.6 us -> 0 us
  between operations: 14.7 us -> 0.48 us
    unnamed x2 -> x0, waiting for transfers between devices: 220 us -> none
    pallas_call x0 -> x18, Pallas kernels: none -> 89.7 us  [the longest x9 34.2 us: hop(): pl.pallas_call(functools.partial(hop_kernel, prev is not None), out_shape...]
    all_to_all x1 -> x0, blocking collectives: 77.1 us -> none  [on_device(): lax.all_to_all(volume, 'slab', split_axis=3, concat_axis=1, tiled=True)]
    all_to_all x4 -> x0, waiting for transfers between devices: 66.5 us -> none  [the longest x1 46.1 us: on_device(): lax.all_to_all(send_spec, 'slab', split_axis=0, concat_axis=0, tiled=True)]
    ppermute x0 -> x30, waiting for transfers between devices: none -> 41.7 us  [the longest x3 21.6 us: along_z(): prev = lax.ppermute(payload, 'grp', both([(k - 1, k)]))]
    ppermute x0 -> x30, starting transfers between devices: none -> 36.9 us  [the longest x21 24.6 us: exchange(): lax.ppermute(pieces[o], 'slab', [(i, i ^ o) for i in range(slabs)])]
    all_to_all x5 -> x0, local copies, waits for them, and re-layouts: 30.9 us -> none  [the longest x3 23.9 us: on_device(): lax.all_to_all(volume, 'slab', split_axis=3, concat_axis=1, tiled=True)]
    unnamed x11 -> x82, local copies, waits for them, and re-layouts: 36.5 us -> 6.61 us
  transfers between devices with their start and end apart: 5 -> 30, of which waited for: 4 -> 9; matrix products, arithmetic and copies ran while one was open for 4% -> 1% of each run, Pallas kernels for 0% -> 42%
where the time goes in v1:
time: 191 us; the launch traced here: 190 us
  Pallas kernels  89.7 us (47%)
  waiting for transfers between devices  41.7 us (22%)
  starting transfers between devices  36.9 us (19%)
  blocking collectives  12.9 us (7%)
  local copies, waits for them, and re-layouts  7.22 us (4%)
    pallas_call x9, Pallas kernels, hop(): pl.pallas_call(functools.partial(hop_kernel, prev is not None), out_shape...  34.2 us
    pallas_call x3, Pallas kernels, volume_sums(): pl.pallas_call(functools.partial(volume_kernel, slabs, window), out_shape...  30 us
    ppermute x21, starting transfers between devices, exchange(): lax.ppermute(pieces[o], 'slab', [(i, i ^ o) for i in range(slabs)])  24.6 us
    ppermute x3, waiting for transfers between devices, along_z(): prev = lax.ppermute(payload, 'grp', both([(k - 1, k)]))  21.6 us
    all_gather x1, blocking collectives, on_device(): meta = lax.all_gather(meta, 'slab')  12.9 us
    ppermute x3, waiting for transfers between devices, along_z(): prev = lax.ppermute(payload, 'grp', both([(j, j - 1)]))  12.7 us
    pallas_call x3, Pallas kernels, sort_columns(): pl.pallas_call(functools.partial(sort_kernel, slabs, width), out_shape=[j...  10.2 us
    pallas_call x1, Pallas kernels, spread_weights(): pl.pallas_call(functools.partial(spread_kernel, slabs, window), out_shape...  7.91 us
  transfers between devices with their start and end apart: 30, of which 9 were waited for; matrix products, arithmetic and copies ran while one was open for 1% of the time, Pallas kernels for 42%

profile of v1, /device:TPU:0, one launch (start us, length us, event | category | flops | bytes accessed | tf_op | source)
XLA Modules:
  0.0 189.8 jit_solution(3607001546615616416)
XLA Ops:
  0.0 1.9 plan_rows.1
  1.9 3.4 %sort_columns.5 = (bf16[512,128]{1,0:T(8,128)(2,1)}, bf16[512,128]{1,0:T(8,128)(2,1)}, bf16[512,128]{1,0:T(8,128)(2,1)}, bf16[512,128]{1,0:T(8,128)(2,1)}, bf16[...) custom-call(s32[1]{0:T(128)} %bitcast.1.me_ref, ...), custom_call_target="tpu_custom_call" | custom-call | tf_op jit(solution)/shard_map/sort_columns/pallas_call | solution.py:91
  5.7 2.5 %collective-permute-start.21 = (bf16[512,128]{1,0:T(8,128)(2,1)}, bf16[512,128]{1,0:T(8,128)(2,1)S(1)}, u32[]{:S(2)}, u32[]{:S(2)}) collective-permute-start(bf16[512,128]{1,0:T(8,128)(2,1)} %get-tuple-element.55), channel_id=1, source_target_pairs={{0,2},{1,3},{2,0},{3,1},{4,6},{5,7},{6,4},{7,5},{8,10},{9,11},{10,... | collective-permute-start | bytes 393224 | tf_op jit(solution)/shard_map/ppermute | solution.py:108
  8.3 1.7 collective-permute-start.23
  10.1 2.6 %collective-permute-start.25 = (bf16[512,128]{1,0:T(8,128)(2,1)}, bf16[512,128]{1,0:T(8,128)(2,1)S(1)}, u32[]{:S(2)}, u32[]{:S(2)}) collective-permute-start(bf16[512,128]{1,0:T(8,128)(2,1)} %get-tuple-element.59), channel_id=1, source_target_pairs={{0,6},{1,7},{2,4},{3,5},{4,2},{5,3},{6,0},{7,1},{8,14},{9,15},{10,... | collective-permute-start | bytes 393224 | tf_op jit(solution)/shard_map/ppermute | solution.py:108
  12.7 3.4 %sort_columns.4 = (bf16[512,128]{1,0:T(8,128)(2,1)}, bf16[512,128]{1,0:T(8,128)(2,1)}, bf16[512,128]{1,0:T(8,128)(2,1)}, bf16[512,128]{1,0:T(8,128)(2,1)}, bf16[...) custom-call(s32[1]{0:T(128)} %bitcast.1.me_ref, ...), custom_call_target="tpu_custom_call" | custom-call | tf_op jit(solution)/shard_map/sort_columns/pallas_call | solution.py:91
  16.1 3.5 %sort_columns.3 = (bf16[512,128]{1,0:T(8,128)(2,1)}, bf16[512,128]{1,0:T(8,128)(2,1)}, bf16[512,128]{1,0:T(8,128)(2,1)}, bf16[512,128]{1,0:T(8,128)(2,1)}, bf16[...) custom-call(s32[1]{0:T(128)} %bitcast.1.me_ref, ...), custom_call_target="tpu_custom_call" | custom-call | tf_op jit(solution)/shard_map/sort_columns/pallas_call | solution.py:91
  20.3 1.6 collective-permute-start.11
  22.5 3.6 %collective-permute-done.26.refs_7_ = bf16[512,128]{1,0:T(8,128)(2,1)S(1)} collective-permute-done((bf16[512,128]{1,0:T(8,128)(2,1)S(1)}, bf16[512,128]{1,0:T(8,128)(2,1)S(1)}, u32[]{:S(2)}, u32[]{:S(2)}) %collective-permute-start.26) | collective-permute-done | bytes 131104 | tf_op jit(solution)/shard_map/ppermute | solution.py:108
  27.1 1.5 collective-permute-done.11.refs_2_
  29.1 1.0 collective-permute-start.5
  30.1 1.2 collective-permute-done.1.refs_2_
  31.4 1.1 collective-permute-start.6
  32.5 1.0 collective-permute-done.2.refs_3_
  33.5 0.9 collective-permute-start.12
  34.4 1.7 collective-permute-start.13
  36.0 4.5 %collective-permute-start.14 = (bf16[512,128]{1,0:T(8,128)(2,1)S(1)}, bf16[512,128]{1,0:T(8,128)(2,1)S(1)}, u32[]{:S(2)}, u32[]{:S(2)}) collective-permute-start(bf16[512,128]{1,0:T(8,128)(2,1)S(1)} %copy-done.35), channel_id=1, source_target_pairs={{0,5},{1,4},{2,7},{3,6},{4,1},{5,0},{6,3},{7,2},{8,13},{9,12},{10,... | collective-permute-start | bytes 393224 | tf_op jit(solution)/shard_map/ppermute | solution.py:108
  40.5 3.6 %collective-permute-start.15 = (bf16[512,128]{1,0:T(8,128)(2,1)S(1)}, bf16[512,128]{1,0:T(8,128)(2,1)S(1)}, u32[]{:S(2)}, u32[]{:S(2)}) collective-permute-start(bf16[512,128]{1,0:T(8,128)(2,1)S(1)} %copy-done.34), channel_id=1, source_target_pairs={{0,6},{1,7},{2,4},{3,5},{4,2},{5,3},{6,0},{7,1},{8,14},{9,15},{10,... | collective-permute-start | bytes 393224 | tf_op jit(solution)/shard_map/ppermute | solution.py:108
  44.3 12.9 %all-gather = bf16[128,512]{1,0:T(8,128)(2,1)} all-gather(bf16[16,512]{1,0:T(8,128)(2,1)S(1)} %copy-done.32), channel_id=2, replica_groups=mesh['grp'=4,'slab'=8] {'slab'}, dimensions={0}, use_global_device_ids=true | all-gather | bytes 147456 | tf_op jit(solution)/shard_map/all_gather | solution.py:372
  57.1 7.9 %spread_weights.1 = (bf16[8,512,1152]{2,1,0:T(8,128)(2,1)}, s32[8,128]{1,0:T(8,128)}) custom-call(s32[1]{0:T(128)} %bitcast.1.me_ref, bf16[8,16,512]{2,1,0:T(8,128)(2,1)} %bitcast.25), custom_call_target="tpu_custom_call" | custom-call | tf_op jit(solution)/shard_map/spread_weights/pallas_call | solution.py:147
  65.6 10.0 %volume_sums.5 = f32[16,8,32,128]{3,2,1,0:T(8,128)} custom-call(s32[8,128]{1,0:T(8,128)} %get-tuple-element.34.start_ref, bf16[8,512,1152]{2,1,0:T(8,128)(2,1)} %get-tuple-element.35.weight_ref, bf16[512,128]{1,0:T(8,128)(2,1)} %get-tuple-element.53.refs_0_, bf16[512,128]{1,0:T(8,128)(2,1)} %copy-done.11, bf16[512,128]{1,0:T(8,128)(2,1)} %copy-done.12, ...), custom_call_target="tpu_custom_call" | custom-call | tf_op jit(solution)/shard_map/volume_sums/pallas_call | solution.py:188
  75.7 4.7 %hop.15 = s16[3,1040,128]{2,1,0:T(8,128)(2,1)} custom-call(s32[3]{0:T(128)} %broadcast_select_fusion.1.idx_ref, f32[4,1024,128]{2,1,0:T(8,128)} %bitcast.13), custom_call_target="tpu_custom_call" | custom-call | tf_op jit(solution)/shard_map/hop/pallas_call | solution.py:258
  80.4 10.0 %volume_sums.3 = f32[16,8,32,128]{3,2,1,0:T(8,128)} custom-call(s32[8,128]{1,0:T(8,128)} %get-tuple-element.34.start_ref, bf16[8,512,1152]{2,1,0:T(8,128)(2,1)} %get-tuple-element.35.weight_ref, bf16[512,128]{1,0:T(8,128)(2,1)} %get-tuple-element.37.refs_0_, bf16[512,128]{1,0:T(8,128)(2,1)} %copy-done.20, bf16[512,128]{1,0:T(8,128)(2,1)} %copy-done.21, ...), custom_call_target="tpu_custom_call" | custom-call | tf_op jit(solution)/shard_map/volume_sums/pallas_call | solution.py:188
  90.4 4.8 %hop.9 = s16[3,1040,128]{2,1,0:T(8,128)(2,1)} custom-call(s32[3]{0:T(128)} %broadcast_select_fusion.1.idx_ref, f32[4,1024,128]{2,1,0:T(8,128)} %bitcast.17), custom_call_target="tpu_custom_call" | custom-call | tf_op jit(solution)/shard_map/hop/pallas_call | solution.py:258
  95.3 3.5 %collective-permute-start.27 = (s16[3,1040,128]{2,1,0:T(8,128)(2,1)S(1)}, s16[3,1040,128]{2,1,0:T(8,128)(2,1)S(1)}, u32[]{:S(2)}, u32[]{:S(2)}) collective-permute-start(s16[3,1040,128]{2,1,0:T(8,128)(2,1)S(1)} %copy-done.7), channel_id=1, source_target_pairs={{0,8},{24,16},{1,9},{25,17},{2,10},{26,18},{3,11},{27,19},{4,12},{... | collective-permute-start | bytes 2396168 | tf_op jit(solution)/shard_map/ppermute | solution.py:287
  98.8 1.3 collective-permute-start.7
  100.9 10.0 %volume_sums.4 = f32[16,8,32,128]{3,2,1,0:T(8,128)} custom-call(s32[8,128]{1,0:T(8,128)} %get-tuple-element.34.start_ref, bf16[8,512,1152]{2,1,0:T(8,128)(2,1)} %get-tuple-element.35.weight_ref, bf16[512,128]{1,0:T(8,128)(2,1)} %get-tuple-element.45.refs_0_, bf16[512,128]{1,0:T(8,128)(2,1)} %copy-done.15, bf16[512,128]{1,0:T(8,128)(2,1)} %copy-done.17, ...), custom_call_target="tpu_custom_call" | custom-call | tf_op jit(solution)/shard_map/volume_sums/pallas_call | solution.py:188
  110.9 4.7 %hop.12 = s16[3,1040,128]{2,1,0:T(8,128)(2,1)} custom-call(s32[3]{0:T(128)} %broadcast_select_fusion.1.idx_ref, f32[4,1024,128]{2,1,0:T(8,128)} %bitcast.21), custom_call_target="tpu_custom_call" | custom-call | tf_op jit(solution)/shard_map/hop/pallas_call | solution.py:258
  115.6 1.3 collective-permute-start.17
  117.5 0.9 copy-done.1
  118.4 4.1 %hop.16 = s16[2,1040,128]{2,1,0:T(8,128)(2,1)} custom-call(s32[2]{0:T(128)} %broadcast_select_fusion.idx_ref, f32[4,1024,128]{2,1,0:T(8,128)} %bitcast.14, s16[3,1040,128]{2,1,0:T(8,128)(2,1)} %copy-done.1), custom_call_target="tpu_custom_call" | custom-call | tf_op jit(solution)/shard_map/hop/pallas_call | solution.py:258
  122.5 0.9 collective-permute-start.28
  123.4 10.7 %collective-permute-done.7.refs_0_.refs_1_ = s16[3,1040,128]{2,1,0:T(8,128)(2,1)S(1)} collective-permute-done((s16[3,1040,128]{2,1,0:T(8,128)(2,1)}, s16[3,1040,128]{2,1,0:T(8,128)(2,1)S(1)}, u32[]{:S(2)}, u32[]{:S(2)}) %collective-permute-start.7) | collective-permute-done | bytes 798752 | tf_op jit(solution)/shard_map/ppermute | solution.py:287
  134.1 0.9 copy-done.2
  135.0 4.1 %hop.10 = s16[2,1040,128]{2,1,0:T(8,128)(2,1)} custom-call(s32[2]{0:T(128)} %broadcast_select_fusion.idx_ref, f32[4,1024,128]{2,1,0:T(8,128)} %bitcast.18, s16[3,1040,128]{2,1,0:T(8,128)(2,1)} %copy-done.2), custom_call_target="tpu_custom_call" | custom-call | tf_op jit(solution)/shard_map/hop/pallas_call | solution.py:258
  139.8 10.9 %collective-permute-done.17.refs_0_.refs_5_ = s16[3,1040,128]{2,1,0:T(8,128)(2,1)S(1)} collective-permute-done((s16[3,1040,128]{2,1,0:T(8,128)(2,1)}, s16[3,1040,128]{2,1,0:T(8,128)(2,1)S(1)}, u32[]{:S(2)}, u32[]{:S(2)}) %collective-permute-start.17) | collective-permute-done | bytes 798752 | tf_op jit(solution)/shard_map/ppermute | solution.py:287
  150.7 0.9 copy-done.3
  151.5 4.1 %hop.13 = s16[2,1040,128]{2,1,0:T(8,128)(2,1)} custom-call(s32[2]{0:T(128)} %broadcast_select_fusion.idx_ref, f32[4,1024,128]{2,1,0:T(8,128)} %bitcast.22, s16[3,1040,128]{2,1,0:T(8,128)(2,1)} %copy-done.3), custom_call_target="tpu_custom_call" | custom-call | tf_op jit(solution)/shard_map/hop/pallas_call | solution.py:258
  157.1 2.6 %hop.17 = s16[1,1040,128]{2,1,0:T(8,128)(2,1)} custom-call(s32[1]{0:T(128)} %bitcast.8.idx_ref, f32[4,1024,128]{2,1,0:T(8,128)} %bitcast.15, s16[2,1040,128]{2,1,0:T(8,128)(2,1)} %copy-done.4), custom_call_target="tpu_custom_call" | custom-call | tf_op jit(solution)/shard_map/hop/pallas_call | solution.py:258
  159.7 1.3 collective-permute-start.29
  161.8 2.6 %hop.11 = s16[1,1040,128]{2,1,0:T(8,128)(2,1)} custom-call(s32[1]{0:T(128)} %bitcast.8.idx_ref, f32[4,1024,128]{2,1,0:T(8,128)} %bitcast.19, s16[2,1040,128]{2,1,0:T(8,128)(2,1)} %copy-done.5), custom_call_target="tpu_custom_call" | custom-call | tf_op jit(solution)/shard_map/hop/pallas_call | solution.py:258
  164.4 1.3 collective-permute-start.9
  166.5 2.6 %hop.14 = s16[1,1040,128]{2,1,0:T(8,128)(2,1)} custom-call(s32[1]{0:T(128)} %bitcast.8.idx_ref, f32[4,1024,128]{2,1,0:T(8,128)} %bitcast.23, s16[2,1040,128]{2,1,0:T(8,128)(2,1)} %copy-done.6), custom_call_target="tpu_custom_call" | custom-call | tf_op jit(solution)/shard_map/hop/pallas_call | solution.py:258
  169.1 1.3 collective-permute-start.19
  171.0 2.1 %collective-permute-done.29.refs_11_ = s16[1,1040,128]{2,1,0:T(8,128)(2,1)S(1)} collective-permute-done((s16[1,1040,128]{2,1,0:T(8,128)(2,1)}, s16[1,1040,128]{2,1,0:T(8,128)(2,1)S(1)}, u32[]{:S(2)}, u32[]{:S(2)}) %collective-permute-start.29) | collective-permute-done | bytes 266272 | tf_op jit(solution)/shard_map/ppermute | solution.py:295
  173.1 4.8 %collective-permute-done.9.refs_3_ = s16[1,1040,128]{2,1,0:T(8,128)(2,1)S(1)} collective-permute-done((s16[1,1040,128]{2,1,0:T(8,128)(2,1)}, s16[1,1040,128]{2,1,0:T(8,128)(2,1)S(1)}, u32[]{:S(2)}, u32[]{:S(2)}) %collective-permute-start.9) | collective-permute-done | bytes 266272 | tf_op jit(solution)/shard_map/ppermute | solution.py:295
  177.9 5.8 %collective-permute-done.19.refs_7_ = s16[1,1040,128]{2,1,0:T(8,128)(2,1)S(1)} collective-permute-done((s16[1,1040,128]{2,1,0:T(8,128)(2,1)}, s16[1,1040,128]{2,1,0:T(8,128)(2,1)S(1)}, u32[]{:S(2)}, u32[]{:S(2)}) %collective-permute-start.19) | collective-permute-done | bytes 266272 | tf_op jit(solution)/shard_map/ppermute | solution.py:295
  184.4 5.4 %image_of.1 = f32[2,4,256,128]{3,2,1,0:T(8,128)} custom-call(s32[1]{0:T(128)} %bitcast.own_ref, f32[4,1024,128]{2,1,0:T(8,128)} %bitcast.20, s16[3,1040,128]{2,1,0:T(8,128)(2,1)} %copy-done.2, s16[2,1040,128]{2,1,0:T(8,128)(2,1)} %copy-done.5, s16[1,1040,128]{2,1,0:T(8,128)(2,1)} %copy-done.9, f32[4,1024,128]{2,1,0:T(8,128)} %bitcast.24, ...), custom_call_target="tpu_custom_call" | custom-call | tf_op jit(solution)/shard_map/image_of/pallas_call | solution.py:349
  (116 shorter events, 10.4 us)
Async XLA Ops:
  0.0 170.4 %copy-start = (f32[1024]{0:T(1024)S(1)}, f32[1024]{0:T(1024)}, u32[]{:S(2)}) copy-start(f32[1024]{0:T(1024)} %param.15) | copy-start | bytes 12292
  5.3 4.8 %collective-permute-start.20 = (bf16[512,128]{1,0:T(8,128)(2,1)}, bf16[512,128]{1,0:T(8,128)(2,1)S(1)}, u32[]{:S(2)}, u32[]{:S(2)}) collective-permute-start(bf16[512,128]{1,0:T(8,128)(2,1)} %get-tuple-element.54), channel_id=1, source_target_pairs={{0,1},{1,0},{2,3},{3,2},{4,5},{5,4},{6,7},{7,6},{8,9},{9,8},{10,11... | collective-permute-start | bytes 393224 | tf_op jit(solution)/shard_map/ppermute | solution.py:108
  5.7 13.9 %collective-permute-start.21 = (bf16[512,128]{1,0:T(8,128)(2,1)}, bf16[512,128]{1,0:T(8,128)(2,1)S(1)}, u32[]{:S(2)}, u32[]{:S(2)}) collective-permute-start(bf16[512,128]{1,0:T(8,128)(2,1)} %get-tuple-element.55), channel_id=1, source_target_pairs={{0,2},{1,3},{2,0},{3,1},{4,6},{5,7},{6,4},{7,5},{8,10},{9,11},{10,... | collective-permute-start | bytes 393224 | tf_op jit(solution)/shard_map/ppermute | solution.py:108
  8.2 11.6 %collective-permute-start.22 = (bf16[512,128]{1,0:T(8,128)(2,1)}, bf16[512,128]{1,0:T(8,128)(2,1)S(1)}, u32[]{:S(2)}, u32[]{:S(2)}) collective-permute-start(bf16[512,128]{1,0:T(8,128)(2,1)} %get-tuple-element.56), channel_id=1, source_target_pairs={{0,3},{1,2},{2,1},{3,0},{4,7},{5,6},{6,5},{7,4},{8,11},{9,10},{10,... | collective-permute-start | bytes 393224 | tf_op jit(solution)/shard_map/ppermute | solution.py:108
  8.3 11.9 %collective-permute-start.23 = (bf16[512,128]{1,0:T(8,128)(2,1)}, bf16[512,128]{1,0:T(8,128)(2,1)S(1)}, u32[]{:S(2)}, u32[]{:S(2)}) collective-permute-start(bf16[512,128]{1,0:T(8,128)(2,1)} %get-tuple-element.57), channel_id=1, source_target_pairs={{0,4},{1,5},{2,6},{3,7},{4,0},{5,1},{6,2},{7,3},{8,12},{9,13},{10,... | collective-permute-start | bytes 393224 | tf_op jit(solution)/shard_map/ppermute | solution.py:108
  10.1 11.8 %collective-permute-start.24 = (bf16[512,128]{1,0:T(8,128)(2,1)}, bf16[512,128]{1,0:T(8,128)(2,1)S(1)}, u32[]{:S(2)}, u32[]{:S(2)}) collective-permute-start(bf16[512,128]{1,0:T(8,128)(2,1)} %get-tuple-element.58), channel_id=1, source_target_pairs={{0,5},{1,4},{2,7},{3,6},{4,1},{5,0},{6,3},{7,2},{8,13},{9,12},{10,... | collective-permute-start | bytes 393224 | tf_op jit(solution)/shard_map/ppermute | solution.py:108
  10.1 34.1 %copy-start.32 = (bf16[16,512]{1,0:T(8,128)(2,1)S(1)}, bf16[16,512]{1,0:T(8,128)(2,1)}, u32[]{:S(2)}) copy-start(bf16[16,512]{1,0:T(8,128)(2,1)} %get-tuple-element.33) | copy-start | bytes 49156
  10.1 11.8 %collective-permute-start.25 = (bf16[512,128]{1,0:T(8,128)(2,1)}, bf16[512,128]{1,0:T(8,128)(2,1)S(1)}, u32[]{:S(2)}, u32[]{:S(2)}) collective-permute-start(bf16[512,128]{1,0:T(8,128)(2,1)} %get-tuple-element.59), channel_id=1, source_target_pairs={{0,6},{1,7},{2,4},{3,5},{4,2},{5,3},{6,0},{7,1},{8,14},{9,15},{10,... | collective-permute-start | bytes 393224 | tf_op jit(solution)/shard_map/ppermute | solution.py:108
  16.1 28.0 %copy-start.33 = (bf16[512,128]{1,0:T(8,128)(2,1)S(1)}, bf16[512,128]{1,0:T(8,128)(2,1)}, u32[]{:S(2)}) copy-start(bf16[512,128]{1,0:T(8,128)(2,1)} %get-tuple-element.52) | copy-start | bytes 393220
  19.6 46.0 %copy-start.12 = (bf16[512,128]{1,0:T(8,128)(2,1)}, bf16[512,128]{1,0:T(8,128)(2,1)S(1)}, u32[]{:S(2)}) copy-start(bf16[512,128]{1,0:T(8,128)(2,1)S(1)} %collective-permute-done.21.refs_2_) | copy-start | bytes 393220
  19.6 6.4 %collective-permute-start.26 = (bf16[512,128]{1,0:T(8,128)(2,1)S(1)}, bf16[512,128]{1,0:T(8,128)(2,1)S(1)}, u32[]{:S(2)}, u32[]{:S(2)}) collective-permute-start(bf16[512,128]{1,0:T(8,128)(2,1)S(1)} %copy-done.38), channel_id=1, source_target_pairs={{0,7},{1,6},{2,5},{3,4},{4,3},{5,2},{6,1},{7,0},{8,15},{9,14},{10,... | collective-permute-start | bytes 393224 | tf_op jit(solution)/shard_map/ppermute | solution.py:108
  19.8 45.7 %copy-start.13 = (bf16[512,128]{1,0:T(8,128)(2,1)}, bf16[512,128]{1,0:T(8,128)(2,1)S(1)}, u32[]{:S(2)}) copy-start(bf16[512,128]{1,0:T(8,128)(2,1)S(1)} %collective-permute-done.22.refs_3_) | copy-start | bytes 393220
  19.8 6.8 %collective-permute-start.10 = (bf16[512,128]{1,0:T(8,128)(2,1)S(1)}, bf16[512,128]{1,0:T(8,128)(2,1)S(1)}, u32[]{:S(2)}, u32[]{:S(2)}) collective-permute-start(bf16[512,128]{1,0:T(8,128)(2,1)S(1)} %copy-done.40), channel_id=1, source_target_pairs={{0,1},{1,0},{2,3},{3,2},{4,5},{5,4},{6,7},{7,6},{8,9},{9,8},{10,11... | collective-permute-start | bytes 393224 | tf_op jit(solution)/shard_map/ppermute | solution.py:108
  20.3 45.3 %copy-start.14 = (bf16[512,128]{1,0:T(8,128)(2,1)}, bf16[512,128]{1,0:T(8,128)(2,1)S(1)}, u32[]{:S(2)}) copy-start(bf16[512,128]{1,0:T(8,128)(2,1)S(1)} %collective-permute-done.23.refs_4_) | copy-start | bytes 393220
  20.3 8.3 %collective-permute-start.11 = (bf16[512,128]{1,0:T(8,128)(2,1)S(1)}, bf16[512,128]{1,0:T(8,128)(2,1)S(1)}, u32[]{:S(2)}, u32[]{:S(2)}) collective-permute-start(bf16[512,128]{1,0:T(8,128)(2,1)S(1)} %copy-done.39), channel_id=1, source_target_pairs={{0,2},{1,3},{2,0},{3,1},{4,6},{5,7},{6,4},{7,5},{8,10},{9,11},{10,... | collective-permute-start | bytes 393224 | tf_op jit(solution)/shard_map/ppermute | solution.py:108
  21.9 43.7 %copy-start.16 = (bf16[512,128]{1,0:T(8,128)(2,1)}, bf16[512,128]{1,0:T(8,128)(2,1)S(1)}, u32[]{:S(2)}) copy-start(bf16[512,128]{1,0:T(8,128)(2,1)S(1)} %collective-permute-done.24.refs_5_) | copy-start | bytes 393220
  21.9 7.2 %collective-permute-start = (bf16[512,128]{1,0:T(8,128)(2,1)}, bf16[512,128]{1,0:T(8,128)(2,1)S(1)}, u32[]{:S(2)}, u32[]{:S(2)}) collective-permute-start(bf16[512,128]{1,0:T(8,128)(2,1)} %get-tuple-element.38), channel_id=1, source_target_pairs={{0,1},{1,0},{2,3},{3,2},{4,5},{5,4},{6,7},{7,6},{8,9},{9,8},{10,11... | collective-permute-start | bytes 393224 | tf_op jit(solution)/shard_map/ppermute | solution.py:108
  21.9 43.7 %copy-start.18 = (bf16[512,128]{1,0:T(8,128)(2,1)}, bf16[512,128]{1,0:T(8,128)(2,1)S(1)}, u32[]{:S(2)}) copy-start(bf16[512,128]{1,0:T(8,128)(2,1)S(1)} %collective-permute-done.25.refs_6_) | copy-start | bytes 393220
  21.9 9.4 %collective-permute-start.1 = (bf16[512,128]{1,0:T(8,128)(2,1)}, bf16[512,128]{1,0:T(8,128)(2,1)S(1)}, u32[]{:S(2)}, u32[]{:S(2)}) collective-permute-start(bf16[512,128]{1,0:T(8,128)(2,1)} %get-tuple-element.39), channel_id=1, source_target_pairs={{0,2},{1,3},{2,0},{3,1},{4,6},{5,7},{6,4},{7,5},{8,10},{9,11},{10,... | collective-permute-start | bytes 393224 | tf_op jit(solution)/shard_map/ppermute | solution.py:108
  26.0 39.5 %copy-start.19 = (bf16[512,128]{1,0:T(8,128)(2,1)}, bf16[512,128]{1,0:T(8,128)(2,1)S(1)}, u32[]{:S(2)}) copy-start(bf16[512,128]{1,0:T(8,128)(2,1)S(1)} %collective-permute-done.26.refs_7_) | copy-start | bytes 393220
  26.1 7.4 %collective-permute-start.2 = (bf16[512,128]{1,0:T(8,128)(2,1)}, bf16[512,128]{1,0:T(8,128)(2,1)S(1)}, u32[]{:S(2)}, u32[]{:S(2)}) collective-permute-start(bf16[512,128]{1,0:T(8,128)(2,1)} %get-tuple-element.40), channel_id=1, source_target_pairs={{0,3},{1,2},{2,1},{3,0},{4,7},{5,6},{6,5},{7,4},{8,11},{9,10},{10,... | collective-permute-start | bytes 393224 | tf_op jit(solution)/shard_map/ppermute | solution.py:108
  26.7 48.9 %copy-start.15 = (bf16[512,128]{1,0:T(8,128)(2,1)}, bf16[512,128]{1,0:T(8,128)(2,1)S(1)}, u32[]{:S(2)}) copy-start(bf16[512,128]{1,0:T(8,128)(2,1)S(1)} %collective-permute-done.10.refs_1_) | copy-start | bytes 393220
  26.7 7.7 %collective-permute-start.3 = (bf16[512,128]{1,0:T(8,128)(2,1)}, bf16[512,128]{1,0:T(8,128)(2,1)S(1)}, u32[]{:S(2)}, u32[]{:S(2)}) collective-permute-start(bf16[512,128]{1,0:T(8,128)(2,1)} %get-tuple-element.41), channel_id=1, source_target_pairs={{0,4},{1,5},{2,6},{3,7},{4,0},{5,1},{6,2},{7,3},{8,12},{9,13},{10,... | collective-permute-start | bytes 393224 | tf_op jit(solution)/shard_map/ppermute | solution.py:108
  28.6 47.1 %copy-start.17 = (bf16[512,128]{1,0:T(8,128)(2,1)}, bf16[512,128]{1,0:T(8,128)(2,1)S(1)}, u32[]{:S(2)}) copy-start(bf16[512,128]{1,0:T(8,128)(2,1)S(1)} %collective-permute-done.11.refs_2_) | copy-start | bytes 393220
  28.6 7.5 %collective-permute-start.4 = (bf16[512,128]{1,0:T(8,128)(2,1)}, bf16[512,128]{1,0:T(8,128)(2,1)S(1)}, u32[]{:S(2)}, u32[]{:S(2)}) collective-permute-start(bf16[512,128]{1,0:T(8,128)(2,1)} %get-tuple-element.42), channel_id=1, source_target_pairs={{0,5},{1,4},{2,7},{3,6},{4,1},{5,0},{6,3},{7,2},{8,13},{9,12},{10,... | collective-permute-start | bytes 393224 | tf_op jit(solution)/shard_map/ppermute | solution.py:108
  29.1 46.5 %copy-start.20 = (bf16[512,128]{1,0:T(8,128)(2,1)}, bf16[512,128]{1,0:T(8,128)(2,1)S(1)}, u32[]{:S(2)}) copy-start(bf16[512,128]{1,0:T(8,128)(2,1)S(1)} %collective-permute-done.refs_1_) | copy-start | bytes 393220
  29.1 11.4 %collective-permute-start.5 = (bf16[512,128]{1,0:T(8,128)(2,1)}, bf16[512,128]{1,0:T(8,128)(2,1)S(1)}, u32[]{:S(2)}, u32[]{:S(2)}) collective-permute-start(bf16[512,128]{1,0:T(8,128)(2,1)} %get-tuple-element.43), channel_id=1, source_target_pairs={{0,6},{1,7},{2,4},{3,5},{4,2},{5,3},{6,0},{7,1},{8,14},{9,15},{10,... | collective-permute-start | bytes 393224 | tf_op jit(solution)/shard_map/ppermute | solution.py:108
  31.4 44.3 %copy-start.21 = (bf16[512,128]{1,0:T(8,128)(2,1)}, bf16[512,128]{1,0:T(8,128)(2,1)S(1)}, u32[]{:S(2)}) copy-start(bf16[512,128]{1,0:T(8,128)(2,1)S(1)} %collective-permute-done.1.refs_2_) | copy-start | bytes 393220
  31.4 12.8 %collective-permute-start.6 = (bf16[512,128]{1,0:T(8,128)(2,1)}, bf16[512,128]{1,0:T(8,128)(2,1)S(1)}, u32[]{:S(2)}, u32[]{:S(2)}) collective-permute-start(bf16[512,128]{1,0:T(8,128)(2,1)} %get-tuple-element.44), channel_id=1, source_target_pairs={{0,7},{1,6},{2,5},{3,4},{4,3},{5,2},{6,1},{7,0},{8,15},{9,14},{10,... | collective-permute-start | bytes 393224 | tf_op jit(solution)/shard_map/ppermute | solution.py:108
  33.5 42.2 %copy-start.22 = (bf16[512,128]{1,0:T(8,128)(2,1)}, bf16[512,128]{1,0:T(8,128)(2,1)S(1)}, u32[]{:S(2)}) copy-start(bf16[512,128]{1,0:T(8,128)(2,1)S(1)} %collective-permute-done.2.refs_3_) | copy-start | bytes 393220
  33.5 61.8 %collective-permute-start.12 = (bf16[512,128]{1,0:T(8,128)(2,1)S(1)}, bf16[512,128]{1,0:T(8,128)(2,1)S(1)}, u32[]{:S(2)}, u32[]{:S(2)}) collective-permute-start(bf16[512,128]{1,0:T(8,128)(2,1)S(1)} %copy-done.37), channel_id=1, source_target_pairs={{0,3},{1,2},{2,1},{3,0},{4,7},{5,6},{6,5},{7,4},{8,11},{9,10},{10,... | collective-permute-start | bytes 393224 | tf_op jit(solution)/shard_map/ppermute | solution.py:108
  34.4 41.3 %copy-start.23 = (bf16[512,128]{1,0:T(8,128)(2,1)}, bf16[512,128]{1,0:T(8,128)(2,1)S(1)}, u32[]{:S(2)}) copy-start(bf16[512,128]{1,0:T(8,128)(2,1)S(1)} %collective-permute-done.3.refs_4_) | copy-start | bytes 393220
  34.4 64.4 %collective-permute-start.13 = (bf16[512,128]{1,0:T(8,128)(2,1)S(1)}, bf16[512,128]{1,0:T(8,128)(2,1)S(1)}, u32[]{:S(2)}, u32[]{:S(2)}) collective-permute-start(bf16[512,128]{1,0:T(8,128)(2,1)S(1)} %copy-done.36), channel_id=1, source_target_pairs={{0,4},{1,5},{2,6},{3,7},{4,0},{5,1},{6,2},{7,3},{8,12},{9,13},{10,... | collective-permute-start | bytes 393224 | tf_op jit(solution)/shard_map/ppermute | solution.py:108
  36.0 39.6 %copy-start.25 = (bf16[512,128]{1,0:T(8,128)(2,1)}, bf16[512,128]{1,0:T(8,128)(2,1)S(1)}, u32[]{:S(2)}) copy-start(bf16[512,128]{1,0:T(8,128)(2,1)S(1)} %collective-permute-done.4.refs_5_) | copy-start | bytes 393220
  36.0 64.1 %collective-permute-start.14 = (bf16[512,128]{1,0:T(8,128)(2,1)S(1)}, bf16[512,128]{1,0:T(8,128)(2,1)S(1)}, u32[]{:S(2)}, u32[]{:S(2)}) collective-permute-start(bf16[512,128]{1,0:T(8,128)(2,1)S(1)} %copy-done.35), channel_id=1, source_target_pairs={{0,5},{1,4},{2,7},{3,6},{4,1},{5,0},{6,3},{7,2},{8,13},{9,12},{10,... | collective-permute-start | bytes 393224 | tf_op jit(solution)/shard_map/ppermute | solution.py:108
  40.5 35.2 %copy-start.27 = (bf16[512,128]{1,0:T(8,128)(2,1)}, bf16[512,128]{1,0:T(8,128)(2,1)S(1)}, u32[]{:S(2)}) copy-start(bf16[512,128]{1,0:T(8,128)(2,1)S(1)} %collective-permute-done.5.refs_6_) | copy-start | bytes 393220
  40.5 59.7 %collective-permute-start.15 = (bf16[512,128]{1,0:T(8,128)(2,1)S(1)}, bf16[512,128]{1,0:T(8,128)(2,1)S(1)}, u32[]{:S(2)}, u32[]{:S(2)}) collective-permute-start(bf16[512,128]{1,0:T(8,128)(2,1)S(1)} %copy-done.34), channel_id=1, source_target_pairs={{0,6},{1,7},{2,4},{3,5},{4,2},{5,3},{6,0},{7,1},{8,14},{9,15},{10,... | collective-permute-start | bytes 393224 | tf_op jit(solution)/shard_map/ppermute | solution.py:108
  44.2 31.5 %copy-start.29 = (bf16[512,128]{1,0:T(8,128)(2,1)}, bf16[512,128]{1,0:T(8,128)(2,1)S(1)}, u32[]{:S(2)}) copy-start(bf16[512,128]{1,0:T(8,128)(2,1)S(1)} %collective-permute-done.6.refs_7_) | copy-start | bytes 393220
  44.2 56.1 %collective-permute-start.16 = (bf16[512,128]{1,0:T(8,128)(2,1)S(1)}, bf16[512,128]{1,0:T(8,128)(2,1)S(1)}, u32[]{:S(2)}, u32[]{:S(2)}) collective-permute-start(bf16[512,128]{1,0:T(8,128)(2,1)S(1)} %copy-done.33), channel_id=1, source_target_pairs={{0,7},{1,6},{2,5},{3,4},{4,3},{5,2},{6,1},{7,0},{8,15},{9,14},{10,... | collective-permute-start | bytes 393224 | tf_op jit(solution)/shard_map/ppermute | solution.py:108
  95.3 22.2 %collective-permute-start.27 = (s16[3,1040,128]{2,1,0:T(8,128)(2,1)S(1)}, s16[3,1040,128]{2,1,0:T(8,128)(2,1)S(1)}, u32[]{:S(2)}, u32[]{:S(2)}) collective-permute-start(s16[3,1040,128]{2,1,0:T(8,128)(2,1)S(1)} %copy-done.7), channel_id=1, source_target_pairs={{0,8},{24,16},{1,9},{25,17},{2,10},{26,18},{3,11},{27,19},{4,12},{... | collective-permute-start | bytes 2396168 | tf_op jit(solution)/shard_map/ppermute | solution.py:287
  98.8 35.3 %collective-permute-start.7 = (s16[3,1040,128]{2,1,0:T(8,128)(2,1)}, s16[3,1040,128]{2,1,0:T(8,128)(2,1)S(1)}, u32[]{:S(2)}, u32[]{:S(2)}) collective-permute-start(s16[3,1040,128]{2,1,0:T(8,128)(2,1)} %hop.9), channel_id=1, source_target_pairs={{0,8},{24,16},{1,9},{25,17},{2,10},{26,18},{3,11},{27,19},{4,12},{... | collective-permute-start | bytes 2396168 | tf_op jit(solution)/shard_map/ppermute | solution.py:287
  115.6 35.0 %collective-permute-start.17 = (s16[3,1040,128]{2,1,0:T(8,128)(2,1)}, s16[3,1040,128]{2,1,0:T(8,128)(2,1)S(1)}, u32[]{:S(2)}, u32[]{:S(2)}) collective-permute-start(s16[3,1040,128]{2,1,0:T(8,128)(2,1)} %hop.12), channel_id=1, source_target_pairs={{0,8},{24,16},{1,9},{25,17},{2,10},{26,18},{3,11},{27,19},{4,12},{... | collective-permute-start | bytes 2396168 | tf_op jit(solution)/shard_map/ppermute | solution.py:287
  122.5 33.8 %collective-permute-start.28 = (s16[2,1040,128]{2,1,0:T(8,128)(2,1)}, s16[2,1040,128]{2,1,0:T(8,128)(2,1)S(1)}, u32[]{:S(2)}, u32[]{:S(2)}) collective-permute-start(s16[2,1040,128]{2,1,0:T(8,128)(2,1)} %hop.16), channel_id=1, source_target_pairs={{8,16},{16,8},{9,17},{17,9},{10,18},{18,10},{11,19},{19,11},{12,20... | collective-permute-start | bytes 1597448 | tf_op jit(solution)/shard_map/ppermute | solution.py:290
  139.1 21.9 %collective-permute-start.8 = (s16[2,1040,128]{2,1,0:T(8,128)(2,1)}, s16[2,1040,128]{2,1,0:T(8,128)(2,1)S(1)}, u32[]{:S(2)}, u32[]{:S(2)}) collective-permute-start(s16[2,1040,128]{2,1,0:T(8,128)(2,1)} %hop.10), channel_id=1, source_target_pairs={{8,16},{16,8},{9,17},{17,9},{10,18},{18,10},{11,19},{19,11},{12,20... | collective-permute-start | bytes 1597448 | tf_op jit(solution)/shard_map/ppermute | solution.py:290
  155.6 10.1 %collective-permute-start.18 = (s16[2,1040,128]{2,1,0:T(8,128)(2,1)}, s16[2,1040,128]{2,1,0:T(8,128)(2,1)S(1)}, u32[]{:S(2)}, u32[]{:S(2)}) collective-permute-start(s16[2,1040,128]{2,1,0:T(8,128)(2,1)} %hop.13), channel_id=1, source_target_pairs={{8,16},{16,8},{9,17},{17,9},{10,18},{18,10},{11,19},{19,11},{12,20... | collective-permute-start | bytes 1597448 | tf_op jit(solution)/shard_map/ppermute | solution.py:290
  159.7 13.4 %collective-permute-start.29 = (s16[1,1040,128]{2,1,0:T(8,128)(2,1)}, s16[1,1040,128]{2,1,0:T(8,128)(2,1)S(1)}, u32[]{:S(2)}, u32[]{:S(2)}) collective-permute-start(s16[1,1040,128]{2,1,0:T(8,128)(2,1)} %hop.17), channel_id=1, source_target_pairs={{8,0},{16,24},{9,1},{17,25},{10,2},{18,26},{11,3},{19,27},{12,4},{... | collective-permute-start | bytes 798728 | tf_op jit(solution)/shard_map/ppermute | solution.py:295
  164.4 13.5 %collective-permute-start.9 = (s16[1,1040,128]{2,1,0:T(8,128)(2,1)}, s16[1,1040,128]{2,1,0:T(8,128)(2,1)S(1)}, u32[]{:S(2)}, u32[]{:S(2)}) collective-permute-start(s16[1,1040,128]{2,1,0:T(8,128)(2,1)} %hop.11), channel_id=1, source_target_pairs={{8,0},{16,24},{9,1},{17,25},{10,2},{18,26},{11,3},{19,27},{12,4},{... | collective-permute-start | bytes 798728 | tf_op jit(solution)/shard_map/ppermute | solution.py:295
  169.1 14.6 %collective-permute-start.19 = (s16[1,1040,128]{2,1,0:T(8,128)(2,1)}, s16[1,1040,128]{2,1,0:T(8,128)(2,1)S(1)}, u32[]{:S(2)}, u32[]{:S(2)}) collective-permute-start(s16[1,1040,128]{2,1,0:T(8,128)(2,1)} %hop.14), channel_id=1, source_target_pairs={{8,0},{16,24},{9,1},{17,25},{10,2},{18,26},{11,3},{19,27},{12,4},{... | collective-permute-start | bytes 798728 | tf_op jit(solution)/shard_map/ppermute | solution.py:295
  (23 other events, 142.5 us)

commit v2 on v0

v2 whole, which is shorter than its diff:
```python
import functools
import math

import jax
import jax.numpy as jnp
import numpy as np
from jax import lax
from jax.experimental import pallas as pl
from jax.experimental.pallas import tpu as pltpu
from jax.sharding import PartitionSpec as P

KZ_DEV = 32
YWIN = 16
NBLK = 64
LANES = 128
ALIGN = 16
TIE = 1
TOP = 32767.0
STEPS = 256.0
VMEM = 60 * 1024 * 1024

WHOLE = pl.BlockSpec(memory_space=pltpu.VMEM)
SCALARS = pl.BlockSpec(memory_space=pltpu.SMEM)


def params(width):
    return pltpu.CompilerParams(vmem_limit_bytes=VMEM if width < LANES else VMEM // 2)


def near(x):
    return pltpu.with_memory_space_constraint(x, pltpu.VMEM)


def far(x):
    return pltpu.with_memory_space_constraint(x, pltpu.HBM)


def cost(micros):
    return pl.CostEstimate(flops=0, bytes_accessed=int(micros * 3.0e6), transcendentals=0)


def iota(shape, axis):
    return lax.broadcasted_iota(jnp.int32, shape, axis)


def plan(slabs, window, dest, block, pattern, table):
    rows = dest.shape[1]
    mine = (dest == iota((slabs, rows), 0)).astype(jnp.float32)
    before = (iota((rows, rows), 0) < iota((rows, rows), 1)).astype(jnp.bfloat16)
    rank = jnp.dot(mine.astype(jnp.bfloat16), before, preferred_element_type=jnp.float32)
    counts = jnp.sum(mine, axis=1, keepdims=True)
    slab_of = iota((slabs, rows), 0)
    first = jnp.sum(jnp.where(slab_of < dest, counts, 0.0), axis=0, keepdims=True)
    target = (first + jnp.sum(mine * rank, axis=0, keepdims=True)).astype(jnp.int32)
    order = (target == iota((rows, rows), 0)).astype(jnp.bfloat16)
    ids = (pattern == iota((table.shape[1], rows), 0)).astype(jnp.bfloat16)
    weights = jnp.dot(table, ids, preferred_element_type=jnp.float32)
    line = iota((8, rows), 0)
    named = jnp.where(line == 0, dest, jnp.where(line == 1, block, 0)).astype(jnp.float32)
    given = jnp.concatenate([weights, named], axis=0).astype(jnp.bfloat16)
    ordered = lax.dot_general(given, order, (((1,), (1,)), ((), ())), preferred_element_type=jnp.float32)
    start = jnp.sum(jnp.where(slab_of < iota((slabs, rows), 1), counts, 0.0), axis=0, keepdims=True)
    start = jnp.minimum(start.astype(jnp.int32) // ALIGN, (rows - window) // ALIGN).astype(jnp.float32)
    meta = jnp.where(iota((16, rows), 0) == 10, start, ordered).astype(jnp.bfloat16)
    return order, meta


def piece_of(x_ref, column, width):
    if len(x_ref.shape) == 3:
        return x_ref[column]
    return x_ref[:, pl.ds(pl.multiple_of(column * width, width), width)]


def by_slab(x, slabs, width):
    if width % LANES == 0:
        return x
    return x.reshape(x.shape[0], -1, width).transpose(1, 0, 2)


def sorted_piece(order, x_ref, column, width):
    piece = piece_of(x_ref, column, width)
    return jnp.dot(order, piece, preferred_element_type=jnp.float32).astype(jnp.bfloat16)


def plan_kernel(slabs, window, width, me_ref, *refs):
    ids_refs, table_ref, x_refs, order_ref, out_refs = refs[0:2], refs[2], refs[3:5], refs[5], refs[6:]
    rows = order_ref.shape[1]
    lines = 16 * (rows // width)
    for half in range(2):
        ids = ids_refs[half][...]
        order, meta = plan(slabs, window, ids[0:1], ids[1:2], ids[2:3], table_ref[...])
        order_ref[half] = order
        for i, out in enumerate(out_refs):
            column = jnp.bitwise_xor(me_ref[0], 2 * i)
            out[half * rows : (half + 1) * rows, :] = sorted_piece(order, x_refs[half], column, width)
            for j in range(rows // width):
                at = 2 * rows + half * lines + 16 * j
                out[at : at + 16, :] = meta[:, j * width : (j + 1) * width]


def plan_rows(slabs, window, me, ids, table, xs):
    rows, kx = xs[0].shape
    width = kx // slabs
    out = jax.ShapeDtypeStruct((2 * rows + 32 * (rows // width), width), jnp.bfloat16)
    done = pl.pallas_call(
        functools.partial(plan_kernel, slabs, window, width),
        out_shape=[jax.ShapeDtypeStruct((2, rows, rows), jnp.bfloat16)] + [out] * (slabs // 2),
        in_specs=[SCALARS] + [WHOLE] * 5,
        out_specs=[WHOLE] * (1 + slabs // 2),
        compiler_params=params(width),
        cost_estimate=cost(6.0),
        name="plan_rows",
    )(me, *[far(x) for x in ids], far(table.T), *[far(by_slab(x, slabs, width)) for x in xs])
    return done[0], done[1:]


def sort_kernel(slabs, width, me_ref, order_ref, *refs):
    x_refs, out_refs = refs[0:2], refs[2:]
    rows = order_ref.shape[1]
    for part in range(2):
        for half in range(2):
            order = order_ref[half]
            for i in range(slabs // 2):
                column = jnp.bitwise_xor(me_ref[0], 2 * i) + part * slabs
                out = out_refs[part * (slabs // 2) + i]
                out[half * rows : (half + 1) * rows, :] = sorted_piece(order, x_refs[half], column, width)


def sort_columns(slabs, me, order, xs):
    rows, width = order.shape[1], xs[0].shape[1] // (2 * slabs)
    done = pl.pallas_call(
        functools.partial(sort_kernel, slabs, width),
        out_shape=[jax.ShapeDtypeStruct((2 * rows, width), jnp.bfloat16)] * slabs,
        in_specs=[SCALARS] + [WHOLE] * 3,
        out_specs=[WHOLE] * slabs,
        compiler_params=params(width),
        cost_estimate=cost(5.0),
        name="sort_columns",
    )(me, order, *[by_slab(x, slabs, width) for x in xs])
    return done[: slabs // 2], done[slabs // 2 :]


def swap(x, slabs, offset):
    return lax.ppermute(x, "slab", [(i, i ^ offset) for i in range(slabs)])


def exchange(pieces, after=None):
    got = [pieces[0]]
    for i in range(1, len(pieces)):
        piece = pieces[i]
        if after is not None:
            piece, after[i] = lax.optimization_barrier((piece, after[i]))
        got.append(swap(piece, 2 * len(pieces), 2 * i))
    return got


def volume_kernel(slabs, window, count, first, idx_ref, *refs):
    piece_refs, refs = refs[: slabs // 2], refs[slabs // 2 :]
    if first:
        sums_ref, code_ref, meta_ref, all_ref, line_ref, scalar_ref, sem = refs
    else:
        meta_ref, sums_ref, code_ref, all_ref, line_ref, scalar_ref, sem = refs
    width = sums_ref.shape[3]
    rows = all_ref.shape[1]
    pick = (iota((16, LANES), 0) == iota((16, LANES), 1)).astype(jnp.bfloat16)
    for offset in range(slabs):
        if first:
            for i in range(rows // width):
                at = 2 * rows + 16 * (offset % 2 * (rows // width) + i)
                meta_ref[offset, :, i * width : (i + 1) * width] = piece_refs[offset // 2][at : at + 16, :]
        meta = meta_ref[offset]
        all_ref[offset] = lax.dot_general(
            meta, pick, (((0,), (0,)), ((), ())), preferred_element_type=jnp.float32
        ).astype(jnp.bfloat16)
        line_ref[offset : offset + 1, :] = meta.astype(jnp.float32)[10:11, 0:LANES].astype(jnp.int32) * ALIGN
    copy = pltpu.make_async_copy(line_ref, scalar_ref, sem)
    copy.start()
    copy.wait()

    def slab_sums(slab):
        about, here = [], []
        for offset in range(slabs):
            start = pl.multiple_of(scalar_ref[offset, slab], ALIGN)
            about.append(all_ref[offset, pl.ds(start, window), :])
            start = pl.multiple_of(offset % 2 * rows + start, ALIGN)
            here.append(piece_refs[offset // 2][pl.ds(start, window), :])
        about, here = jnp.concatenate(about, axis=0), jnp.concatenate(here, axis=0)
        meta = lax.dot_general(pick, about, (((1,), (1,)), ((), ())), preferred_element_type=jnp.float32)
        weights = meta[0:8]
        own = meta[8:9] == jnp.asarray(slab, jnp.float32)
        block = jnp.broadcast_to(jnp.where(own, meta[9:10], -1.0), weights.shape)
        spread = jnp.concatenate([jnp.where(block == float(b), weights, 0.0) for b in range(NBLK)], axis=0)
        sums = jnp.dot(spread.astype(jnp.bfloat16), here, preferred_element_type=jnp.float32)
        sums_ref[:, slab] = sums.reshape(YWIN, KZ_DEV, width)

    if slabs <= 8:
        for slab in range(slabs):
            slab_sums(slab)
    else:
        lax.fori_loop(0, slabs, lambda slab, carry: (slab_sums(slab), carry)[1], 0)
    portion = code_ref.shape[1] - ALIGN
    lines = portion // (slabs * KZ_DEV)
    for i in range(count):
        x = sums_ref[pl.ds(idx_ref[i] * lines, lines)].reshape(portion, width)
        code_ref[i, :portion, :], code_ref[i, portion:, :] = encode(x)


def volume_sums(window, index, count, groups, pieces, meta=None):
    slabs = 2 * len(pieces)
    width = pieces[0].shape[1]
    first = meta is None
    rows = pieces[0].shape[0] // 2
    if first:
        rows = rows * width // (width + 16)
    portion = YWIN // groups * slabs * KZ_DEV
    out_shape = [
        jax.ShapeDtypeStruct((YWIN, slabs, KZ_DEV, width), jnp.float32),
        jax.ShapeDtypeStruct((count, portion + ALIGN, width), jnp.int16),
    ]
    if first:
        out_shape.append(jax.ShapeDtypeStruct((slabs, 16, rows), jnp.bfloat16))
    done = pl.pallas_call(
        functools.partial(volume_kernel, slabs, window, count, first),
        out_shape=out_shape,
        in_specs=[SCALARS] + [WHOLE] * (slabs // 2 + (0 if first else 1)),
        out_specs=[WHOLE] * len(out_shape),
        scratch_shapes=[
            pltpu.VMEM((slabs, rows, LANES), jnp.bfloat16),
            pltpu.VMEM((slabs, LANES), jnp.int32),
            pltpu.SMEM((slabs, LANES), jnp.int32),
            pltpu.SemaphoreType.DMA,
        ],
        compiler_params=params(width),
        cost_estimate=cost(7.0),
        name="volume_sums",
    )(index, *[far(x) for x in pieces], *([] if first else [far(meta)]))
    return done[0].reshape(groups, portion, width), done[1], done[2] if first else meta


def encode(x):
    rows, width = x.shape
    groups = rows // 8
    tiles = x.reshape(groups, 8, width)
    size = jnp.abs(tiles)
    most = jnp.max(jnp.max(size, axis=1), axis=1, keepdims=True)
    level = jnp.ceil(jnp.log2(jnp.maximum(most, 1e-30)) * STEPS) + 1.0
    inverse = jnp.broadcast_to(jnp.exp2(level * (-1.0 / STEPS)), (groups, width)).reshape(groups, 1, width)
    share = jnp.maximum(size * inverse, 1e-12)
    root = jnp.minimum(share * lax.rsqrt(share) * TOP + 0.5, TOP)
    code = jnp.where(tiles < 0, -root, root).reshape(rows, width).astype(jnp.int32).astype(jnp.int16)
    eye = iota((width, width), 0) == iota((width, width), 1)
    lines = [
        jnp.sum(jnp.where(eye, level[i * width : (i + 1) * width], 0.0), axis=0, keepdims=True)
        for i in range(groups // width)
    ]
    lines.append(jnp.zeros((ALIGN - len(lines), width), jnp.float32))
    return code, jnp.concatenate(lines, axis=0).astype(jnp.int32).astype(jnp.int16)


def decode(code, lines):
    rows, width = code.shape
    groups = rows // 8
    x = code.astype(jnp.int32).astype(jnp.float32)
    lines = lines.astype(jnp.int32).astype(jnp.float32)
    eye = iota((width, width), 0) == iota((width, width), 1)
    level = jnp.concatenate(
        [jnp.sum(jnp.where(eye, lines[i : i + 1], 0.0), axis=1, keepdims=True) for i in range(groups // width)],
        axis=0,
    )
    scale = jnp.exp2(level * (1.0 / STEPS)) * (1.0 / (TOP * TOP))
    scale = jnp.broadcast_to(scale, (groups, width)).reshape(groups, 1, width)
    return ((x * jnp.abs(x)).reshape(groups, 8, width) * scale).reshape(rows, width)


def hop_kernel(places, idx_ref, sums_ref, prev_ref, out_ref):
    rows = sums_ref.shape[1]
    for i, place in enumerate(places):
        x = sums_ref[idx_ref[i]] + decode(prev_ref[place, :rows, :], prev_ref[place, rows:, :])
        out_ref[i, :rows, :], out_ref[i, rows:, :] = encode(x)


def hop(index, sums, prev, places):
    _, rows, width = sums.shape
    count = len(places)
    return pl.pallas_call(
        functools.partial(hop_kernel, places),
        out_shape=jax.ShapeDtypeStruct((count, rows + ALIGN, width), jnp.int16),
        in_specs=[SCALARS, WHOLE, WHOLE],
        out_specs=WHOLE,
        compiler_params=params(width),
        cost_estimate=cost(2.0 + count),
        name="hop",
    )(index, far(sums), far(prev))


def portions(z, groups, r):
    return jnp.where(z >= groups // 2, groups - 1 - r, r).astype(jnp.int32)


def along_z(sums, payload, z, groups):
    half = groups // 2
    depth = jnp.minimum(z, groups - 1 - z)
    steps = np.arange(groups)

    def send(payload, pairs):
        return lax.ppermute(payload, "grp", pairs + [(groups - 1 - a, groups - 1 - b) for a, b in pairs])

    def add(r, prev, places):
        return hop(portions(z, groups, r), sums, prev, list(places))

    prev = send(payload, [(0, 1)])
    inward = [None, prev]
    for k in range(2, half):
        prev = send(add(steps[k + 1 :], prev, range(1, groups - k)), [(k - 1, k)])
        inward.append(prev)
    prev = send(add(steps[half:], prev, range(half)), [(half - 1, half)])
    ends = [(prev, 0)]
    places = list(range(half - 1, -1, -1))
    for j in range(half - 1, 1, -1):
        ends.append((send(add(steps[j : j + 1], inward[j - 1], [0]), [(j - 1, j)]), 0))
        prev = send(add(steps[:j], prev, places[:j]), [(j, j - 1)])
        ends.append((prev, j - 1))
        places = list(range(half))
    prev = send(add(jnp.where(depth == 0, 1, steps[:1]), prev, places[:1]), [(1, 0), (0, 1)])
    ends.append((prev, 0))
    return ends


def image_kernel(parts, zs, own_ref, *refs):
    tau_ref, high_ref, low_ref, out_ref = refs[-4:]
    each = len(refs[:-4]) // 3
    volume = []
    for c in range(3):
        sums_ref, coded = refs[c * each], refs[c * each + 1 : (c + 1) * each]
        rows = sums_ref.shape[1]
        x = sums_ref[0]
        for ref in coded:
            x = x + decode(ref[0, :rows, :], ref[0, rows:, :])
        volume.append(x)
    below = volume[2] + tau_ref[...]
    columns = []
    for c in range(2):
        x = volume[c] / below
        columns += [x[k * zs : (k + 1) * zs] for k in range(parts)]
    x = jnp.concatenate(columns, axis=1)
    x_high = x.astype(jnp.bfloat16)
    x_low = (x - x_high.astype(jnp.float32)).astype(jnp.bfloat16)
    dot = functools.partial(jnp.dot, preferred_element_type=jnp.float32)
    y = dot(high_ref[...], x_high) + (dot(high_ref[...], x_low) + dot(low_ref[...], x_high))
    span = x.shape[1] // 2
    width = span // parts
    real = y[:zs, :span] - y[zs:, span:]
    imag = y[zs:, :span] + y[:zs, span:]
    for k in range(parts):
        out_ref[0, k] = real[:, k * width : (k + 1) * width]
        out_ref[1, k] = imag[:, k * width : (k + 1) * width]


def image_of(own, fields, tau, zs):
    rows, width = fields[0][0].shape[1:]
    parts = rows // zs
    operands, specs = [], []
    for sums, ends in fields:
        operands.append(sums)
        specs.append(pl.BlockSpec((1, rows, width), lambda i, s: (s[0], 0, 0)))
        for payload, place in ends:
            operands.append(payload)
            specs.append(pl.BlockSpec((1, rows + ALIGN, width), functools.partial(lambda place, i, s: (place, 0, 0), place)))
    steps = np.arange(zs)
    angles = (steps[:, None] * steps[None, :] % zs) * (2.0 * math.pi / zs)
    table = (np.concatenate([np.cos(angles), np.sin(angles)], axis=0) / math.sqrt(zs)).astype(np.float32)
    high = table.astype(jnp.bfloat16)
    low = (table - high.astype(np.float32)).astype(jnp.bfloat16)
    for x in (tau.reshape(1, width), jnp.asarray(high), jnp.asarray(low)):
        operands.append(x)
        specs.append(pl.BlockSpec(x.shape, lambda i, s: (0, 0)))
    return pl.pallas_call(
        functools.partial(image_kernel, parts, zs),
        out_shape=jax.ShapeDtypeStruct((2, parts, zs, width), jnp.float32),
        grid_spec=pltpu.PrefetchScalarGridSpec(
            num_scalar_prefetch=1,
            grid=(1,),
            in_specs=specs,
            out_specs=pl.BlockSpec((2, parts, zs, width), lambda i, s: (0, 0, 0, 0)),
        ),
        compiler_params=params(width),
        cost_estimate=cost(6.0),
        name="image_of",
    )(own, *[far(x) for x in operands])


def on_device(spectra, ctf_sq, dest, block, pattern, pattern_table, tau):
    slabs, groups = lax.axis_size("slab"), lax.axis_size("grp")
    rows, kx = ctf_sq.shape
    capacity = max(2, 2 * rows // slabs)
    window = min(rows, -(-capacity // ALIGN) * ALIGN + ALIGN)
    width = kx // slabs
    slab, z = lax.axis_index("slab"), lax.axis_index("grp")
    me = slab.astype(jnp.int32).reshape(1)
    ids = jnp.stack([dest[:, 0], block, pattern])
    ids, ctf_sq, spectra = [(x, swap(x, slabs, 1)) for x in (ids, ctf_sq, spectra)]
    order, ctf = plan_rows(slabs, window, me, ids, pattern_table, ctf_sq)
    real, imag = sort_columns(slabs, me, order, spectra)
    pieces = [exchange(ctf)]
    pieces.append(exchange(real, pieces[0]))
    index = portions(z, groups, np.arange(2, groups))
    fields, meta = [], None
    for piece in range(3):
        if piece == 2:
            pieces.append(exchange(imag, [lax.optimization_barrier((x, fields[0][1][0][0]))[0] for x in pieces[1]] if TIE == 1 else [payload0] * len(imag)))
        piece = pieces[piece]
        sums, payload, meta = volume_sums(window, index, groups - 2, groups, piece, meta)
        if not fields:
            payload0 = payload
        fields.append((sums, along_z(sums, payload, z, groups)))
    tau_here = lax.dynamic_slice_in_dim(tau, slab * width, width, 0)
    own = z.astype(jnp.int32).reshape(1)
    return image_of(own, [fields[1], fields[2], fields[0]], tau_here, KZ_DEV * slabs)


def solution(mesh):
    in_specs = (
        P(("grp", "slab"), None),
        P(("grp", "slab"), None),
        P(("grp", "slab"), None),
        P(("grp", "slab")),
        P(("grp", "slab")),
        P(),
        P(),
    )
    out_specs = P(None, "grp", None, "slab")
    return jax.shard_map(
        on_device, mesh=mesh, in_specs=in_specs, out_specs=out_specs, check_vma=False
    )
```

time: 555 us -> 124 us (0.22); the launches traced: 547 us -> 123 us
  waiting for transfers between devices: 287 us -> 18.7 us
  local copies, waits for them, and re-layouts: 106 us -> 14.8 us
  blocking collectives: 77.1 us -> 0 us
  Pallas kernels: 0 us -> 48.7 us
  other arithmetic: 30 us -> 0.84 us
  starting transfers between devices: 17.4 us -> 39.1 us
  matrix products: 14.6 us -> 0 us
  between operations: 14.7 us -> 0.41 us
    unnamed x2 -> x0, waiting for transfers between devices: 220 us -> none
    all_to_all x1 -> x0, blocking collectives: 77.1 us -> none  [on_device(): lax.all_to_all(volume, 'slab', split_axis=3, concat_axis=1, tiled=True)]
    all_to_all x4 -> x0, waiting for transfers between devices: 66.5 us -> none  [the longest x1 46.1 us: on_device(): lax.all_to_all(send_spec, 'slab', split_axis=0, concat_axis=0, tiled=True)]
    pallas_call x0 -> x12, Pallas kernels: none -> 48.7 us  [the longest x3 19.4 us: volume_sums(): pl.pallas_call(functools.partial(volume_kernel, slabs, window, count, fir...]
    ppermute x0 -> x21, starting transfers between devices: none -> 39.1 us  [the longest x9 25 us: send(): lax.ppermute(payload, 'grp', pairs + [(groups - 1 - a, groups - 1 - b) fo...]
    all_to_all x5 -> x0, local copies, waits for them, and re-layouts: 30.9 us -> none  [the longest x3 23.9 us: on_device(): lax.all_to_all(volume, 'slab', split_axis=3, concat_axis=1, tiled=True)]
    unnamed x11 -> x62, local copies, waits for them, and re-layouts: 36.5 us -> 14.1 us
    all_to_all x1 -> x0, other arithmetic: 19.9 us -> none  [on_device(): lax.all_to_all(volume, 'slab', split_axis=3, concat_axis=1, tiled=True)]
  transfers between devices with their start and end apart: 5 -> 21, of which waited for: 4 -> 5; matrix products, arithmetic and copies ran while one was open for 4% -> 1% of each run, Pallas kernels for 0% -> 36%
where the time goes in v2:
time: 124 us; the launch traced here: 123 us
  Pallas kernels  48.7 us (39%)
  starting transfers between devices  39.1 us (32%)
  waiting for transfers between devices  18.7 us (15%)
  local copies, waits for them, and re-layouts  14.8 us (12%)
    ppermute x9, starting transfers between devices, send(): lax.ppermute(payload, 'grp', pairs + [(groups - 1 - a, groups - 1 - b) fo...  25 us
    pallas_call x3, Pallas kernels, volume_sums(): pl.pallas_call(functools.partial(volume_kernel, slabs, window, count, fir...  19.4 us
    pallas_call x6, Pallas kernels, hop(): pl.pallas_call(functools.partial(hop_kernel, places), out_shape=jax.Shape...  16.9 us
    ppermute x12, waiting for transfers between devices, swap(): return lax.ppermute(x, 'slab', [(i, i ^ offset) for i in range(slabs)])  15 us
    unnamed x62, local copies, waits for them, and re-layouts  14.1 us
    ppermute x12, starting transfers between devices, swap(): return lax.ppermute(x, 'slab', [(i, i ^ offset) for i in range(slabs)])  14.1 us
    pallas_call x1, Pallas kernels, image_of(): pl.pallas_call(functools.partial(image_kernel, parts, zs), out_shape=jax....  4.77 us
    pallas_call x1, Pallas kernels, sort_columns(): pl.pallas_call(functools.partial(sort_kernel, slabs, width), out_shape=[j...  3.98 us
  transfers between devices with their start and end apart: 21, of which 5 were waited for; matrix products, arithmetic and copies ran while one was open for 1% of the time, Pallas kernels for 36%

profile of v2, /device:TPU:0, one launch (start us, length us, event | category | flops | bytes accessed | tf_op | source)
XLA Modules:
  0.0 122.6 jit_solution(14436298440501475621)
XLA Ops:
  0.5 0.8 pad_add_fusion.refs_0_
  1.9 3.1 %collective-permute-done.refs_1_ = s32[3,512]{1,0:T(4,128)S(1)} collective-permute-done((s32[3,512]{1,0:T(4,128)S(1)}, s32[3,512]{1,0:T(4,128)S(1)}, u32[]{:S(2)}, u32[]{:S(2)}) %collective-permute-start) | collective-permute-done | bytes 6176 | tf_op jit(solution)/shard_map/ppermute | solution.py:144
  5.0 0.9 collective-permute-done.1.refs_4_
  5.9 1.0 copy-done.12
  6.9 3.7 %plan_rows.1 = (bf16[2,512,512]{2,1,0:T(8,128)(2,1)S(1)}, bf16[1152,128]{1,0:T(8,128)(2,1)S(1)}, bf16[1152,128]{1,0:T(8,128)(2,1)S(1)}, bf16[1152,128]{1,0:T(8,128)(2,1)S(1)}, bf16[1152,128]{1,0:T(8,128)(2,1)S(1)}) custom-call(s32[1]{0:T(128)} %bitcast.1.me_ref, s32[3,512]{1,0:T(4,128)} %copy-done.27, s32[3,512]{1,0:T(4,128)} %copy-done.28, ...), custom_call_target="tpu_custom_call" | custom-call | bytes 18000000 | tf_op jit(solution)/shard_map/plan_rows/pallas_call | solution.py:105
  10.6 2.6 %collective-permute-start.3 = (bf16[1152,128]{1,0:T(8,128)(2,1)S(1)}, bf16[1152,128]{1,0:T(8,128)(2,1)S(1)}, u32[]{:S(2)}, u32[]{:S(2)}) collective-permute-start(bf16[1152,128]{1,0:T(8,128)(2,1)S(1)} %get-tuple-element.34), channel_id=1, source_target_pairs={{0,2},{1,3},{2,0},{3,1},{4,6},{5,7},{6,4},{7,5},{8,10},{9,11},{10,... | collective-permute-start | bytes 884744 | tf_op jit(solution)/shard_map/ppermute | solution.py:144
  13.2 1.5 %collective-permute-start.5 = (bf16[1152,128]{1,0:T(8,128)(2,1)S(1)}, bf16[1152,128]{1,0:T(8,128)(2,1)S(1)}, u32[]{:S(2)}, u32[]{:S(2)}) collective-permute-start(bf16[1152,128]{1,0:T(8,128)(2,1)S(1)} %get-tuple-element.37), channel_id=1, source_target_pairs={{0,4},{1,5},{2,6},{3,7},{4,0},{5,1},{6,2},{7,3},{8,12},{9,13},{10,... | collective-permute-start | bytes 884744 | tf_op jit(solution)/shard_map/ppermute | solution.py:144
  14.8 4.0 %sort_columns.1 = (bf16[1024,128]{1,0:T(8,128)(2,1)S(1)}, bf16[1024,128]{1,0:T(8,128)(2,1)S(1)}, bf16[1024,128]{1,0:T(8,128)(2,1)S(1)}, bf16[1024,128]{1,0:T(8,1...) custom-call(s32[1]{0:T(128)} %bitcast.1.me_ref, ...), custom_call_target="tpu_custom_call" | custom-call | bytes 15000000 | tf_op jit(solution)/shard_map/sort_columns/pallas_call | solution.py:131
  18.8 0.7 copy-done.7
  19.5 0.7 copy-done.8
  20.2 1.9 %collective-permute-start.12 = (bf16[1024,128]{1,0:T(8,128)(2,1)S(1)}, bf16[1024,128]{1,0:T(8,128)(2,1)S(1)}, u32[]{:S(2)}, u32[]{:S(2)}) collective-permute-start(bf16[1024,128]{1,0:T(8,128)(2,1)S(1)} %get-tuple-element.50), channel_id=1, source_target_pairs={{0,2},{1,3},{2,0},{3,1},{4,6},{5,7},{6,4},{7,5},{8,10},{9,11},{10,... | collective-permute-start | bytes 786440 | tf_op jit(solution)/shard_map/ppermute | solution.py:144
  22.1 6.0 %collective-permute-done.5.refs_2_ = bf16[1152,128]{1,0:T(8,128)(2,1)S(1)} collective-permute-done((bf16[1152,128]{1,0:T(8,128)(2,1)S(1)}, bf16[1152,128]{1,0:T(8,128)(2,1)S(1)}, u32[]{:S(2)}, u32[]{:S(2)}) %collective-permute-start.5) | collective-permute-done | bytes 294944 | tf_op jit(solution)/shard_map/ppermute | solution.py:144
  28.2 1.9 %collective-permute-start.13 = (bf16[1024,128]{1,0:T(8,128)(2,1)S(1)}, bf16[1024,128]{1,0:T(8,128)(2,1)S(1)}, u32[]{:S(2)}, u32[]{:S(2)}) collective-permute-start(bf16[1024,128]{1,0:T(8,128)(2,1)S(1)} %get-tuple-element.51), channel_id=1, source_target_pairs={{0,4},{1,5},{2,6},{3,7},{4,0},{5,1},{6,2},{7,3},{8,12},{9,13},{10,... | collective-permute-start | bytes 786440 | tf_op jit(solution)/shard_map/ppermute | solution.py:144
  30.1 2.9 %collective-permute-start.8 = (bf16[1024,128]{1,0:T(8,128)(2,1)S(1)}, bf16[1024,128]{1,0:T(8,128)(2,1)S(1)}, u32[]{:S(2)}, u32[]{:S(2)}) collective-permute-start(bf16[1024,128]{1,0:T(8,128)(2,1)S(1)} %get-tuple-element.41), channel_id=1, source_target_pairs={{0,6},{1,7},{2,4},{3,5},{4,2},{5,3},{6,0},{7,1},{8,14},{9,15},{10,... | collective-permute-start | bytes 786440 | tf_op jit(solution)/shard_map/ppermute | solution.py:144
  33.2 1.9 %collective-permute-start.4 = (bf16[1024,128]{1,0:T(8,128)(2,1)S(1)}, bf16[1024,128]{1,0:T(8,128)(2,1)}, u32[]{:S(2)}, u32[]{:S(2)}) collective-permute-start(bf16[1024,128]{1,0:T(8,128)(2,1)S(1)} %get-tuple-element.35), channel_id=1, source_target_pairs={{0,2},{1,3},{2,0},{3,1},{4,6},{5,7},{6,4},{7,5},{8,10},{9,11},{10,... | collective-permute-start | bytes 786440 | tf_op jit(solution)/shard_map/ppermute | solution.py:144
  35.1 6.6 %volume_sums.3 = (f32[16,8,32,128]{3,2,1,0:T(8,128)S(1)}, s16[2,1040,128]{2,1,0:T(8,128)(2,1)S(1)}, bf16[8,16,512]{2,1,0:T(8,128)(2,1)S(1)}) custom-call(s32[2]{0:T(128)S(1)} %broadcast_select_fusion.idx_ref, bf16[1152,128]{1,0:T(8,128)(2,1)} %copy-done.6, bf16[1152,128]{1,0:T(8,128)(2,1)} %copy-done.16, bf16[1152,128]{1,0:T(8,128)(2,1)} %copy-done.17, ...), custom_call_target="tpu_custom_call" | custom-call | bytes 21000000 | tf_op jit(solution)/shard_map/volume_sums/pallas_call | solution.py:222
  41.7 1.3 %copy-done.1 = f32[16,8,32,128]{3,2,1,0:T(8,128)} copy-done((f32[16,8,32,128]{3,2,1,0:T(8,128)}, f32[16,8,32,128]{3,2,1,0:T(8,128)S(1)}, u32[]{:S(2)}) %copy-start.1) | copy-done | bytes 2097176
  43.7 5.0 %collective-permute-done.13.refs_2_ = bf16[1024,128]{1,0:T(8,128)(2,1)S(1)} collective-permute-done((bf16[1024,128]{1,0:T(8,128)(2,1)S(1)}, bf16[1024,128]{1,0:T(8,128)(2,1)S(1)}, u32[]{:S(2)}, u32[]{:S(2)}) %collective-permute-start.13) | collective-permute-done | bytes 262176 | tf_op jit(solution)/shard_map/ppermute | solution.py:144
  48.7 3.7 %collective-permute-start.18 = (s16[2,1040,128]{2,1,0:T(8,128)(2,1)S(1)}, s16[2,1040,128]{2,1,0:T(8,128)(2,1)S(1)}, u32[]{:S(2)}, u32[]{:S(2)}) collective-permute-start(s16[2,1040,128]{2,1,0:T(8,128)(2,1)S(1)} %get-tuple-element.56), channel_id=1, source_target_pairs={{0,8},{24,16},{1,9},{25,17},{2,10},{26,18},{3,11},{27,19},{4,12},{... | collective-permute-start | bytes 1597448 | tf_op jit(solution)/shard_map/ppermute | solution.py:306
  52.4 0.7 copy-done.26
  53.1 6.4 %volume_sums.5 = (f32[16,8,32,128]{3,2,1,0:T(8,128)S(1)}, s16[2,1040,128]{2,1,0:T(8,128)(2,1)S(1)}) custom-call(s32[2]{0:T(128)S(1)} %broadcast_select_fusion.idx_ref, bf16[1024,128]{1,0:T(8,128)(2,1)} %copy-done.8, bf16[1024,128]{1,0:T(8,128)(2,1)} %copy-done.22, bf16[1024,128]{1,0:T(8,128)(2,1)} %copy-done.25, bf16[1024,128]{1,0:T(8,128)(2,1)} %copy-done.26, ...), custom_call_target="tpu_custom_call" | custom-call | bytes 21000000 | tf_op jit(solution)/shard_map/volume_sums/pallas_call | solution.py:222
  59.5 1.3 %copy-done.2 = f32[16,8,32,128]{3,2,1,0:T(8,128)} copy-done((f32[16,8,32,128]{3,2,1,0:T(8,128)}, f32[16,8,32,128]{3,2,1,0:T(8,128)S(1)}, u32[]{:S(2)}) %copy-start.2) | copy-done | bytes 2097176
  60.9 1.3 %collective-permute-start.15 = (s16[2,1040,128]{2,1,0:T(8,128)(2,1)S(1)}, s16[2,1040,128]{2,1,0:T(8,128)(2,1)S(1)}, u32[]{:S(2)}, u32[]{:S(2)}) collective-permute-start(s16[2,1040,128]{2,1,0:T(8,128)(2,1)S(1)} %get-tuple-element.54), channel_id=1, source_target_pairs={{0,8},{24,16},{1,9},{25,17},{2,10},{26,18},{3,11},{27,19},{4,12},{... | collective-permute-start | bytes 1597448 | tf_op jit(solution)/shard_map/ppermute | solution.py:306
  62.2 0.7 copy-done.23
  63.0 6.4 %volume_sums.4 = (f32[16,8,32,128]{3,2,1,0:T(8,128)S(1)}, s16[2,1040,128]{2,1,0:T(8,128)(2,1)S(1)}) custom-call(s32[2]{0:T(128)S(1)} %broadcast_select_fusion.idx_ref, bf16[1024,128]{1,0:T(8,128)(2,1)} %copy-done.7, bf16[1024,128]{1,0:T(8,128)(2,1)} %collective-permute-done.4.refs_1_, bf16[1024,128]{1,0:T(8,128)(2,1)} %copy-done.24, ...), custom_call_target="tpu_custom_call" | custom-call | bytes 21000000 | tf_op jit(solution)/shard_map/volume_sums/pallas_call | solution.py:222
  69.4 1.4 %copy-done.3 = f32[16,8,32,128]{3,2,1,0:T(8,128)} copy-done((f32[16,8,32,128]{3,2,1,0:T(8,128)}, f32[16,8,32,128]{3,2,1,0:T(8,128)S(1)}, u32[]{:S(2)}) %copy-start.3) | copy-done | bytes 2097176
  70.8 1.3 %collective-permute-start.9 = (s16[2,1040,128]{2,1,0:T(8,128)(2,1)S(1)}, s16[2,1040,128]{2,1,0:T(8,128)(2,1)S(1)}, u32[]{:S(2)}, u32[]{:S(2)}) collective-permute-start(s16[2,1040,128]{2,1,0:T(8,128)(2,1)S(1)} %get-tuple-element.48), channel_id=1, source_target_pairs={{0,8},{24,16},{1,9},{25,17},{2,10},{26,18},{3,11},{27,19},{4,12},{... | collective-permute-start | bytes 1597448 | tf_op jit(solution)/shard_map/ppermute | solution.py:306
  72.1 0.8 copy-done.13
  72.9 3.2 %hop.10 = s16[2,1040,128]{2,1,0:T(8,128)(2,1)S(1)} custom-call(s32[2]{0:T(128)S(1)} %broadcast_select_fusion.idx_ref, f32[4,1024,128]{2,1,0:T(8,128)} %bitcast.13, s16[2,1040,128]{2,1,0:T(8,128)(2,1)} %copy-done.13), custom_call_target="tpu_custom_call" | custom-call | bytes 12000000 | tf_op jit(solution)/shard_map/hop/pallas_call | solution.py:285
  76.1 0.9 collective-permute-start.19
  77.1 0.8 copy-done.14
  77.8 3.2 %hop.8 = s16[2,1040,128]{2,1,0:T(8,128)(2,1)S(1)} custom-call(s32[2]{0:T(128)S(1)} %broadcast_select_fusion.idx_ref, f32[4,1024,128]{2,1,0:T(8,128)} %bitcast.16, s16[2,1040,128]{2,1,0:T(8,128)(2,1)} %copy-done.14), custom_call_target="tpu_custom_call" | custom-call | bytes 12000000 | tf_op jit(solution)/shard_map/hop/pallas_call | solution.py:285
  81.0 0.7 collective-permute-start.16
  81.7 0.8 copy-done.15
  82.5 3.2 %hop.6 = s16[2,1040,128]{2,1,0:T(8,128)(2,1)S(1)} custom-call(s32[2]{0:T(128)S(1)} %broadcast_select_fusion.idx_ref, f32[4,1024,128]{2,1,0:T(8,128)} %bitcast.19, s16[2,1040,128]{2,1,0:T(8,128)(2,1)} %copy-done.15), custom_call_target="tpu_custom_call" | custom-call | bytes 12000000 | tf_op jit(solution)/shard_map/hop/pallas_call | solution.py:285
  85.7 0.7 collective-permute-start.10
  86.5 0.9 copy-done.9
  87.3 2.4 %hop.11 = s16[1,1040,128]{2,1,0:T(8,128)(2,1)S(1)} custom-call(s32[1]{0:T(128)S(6)} %select_n.61.idx_ref, f32[4,1024,128]{2,1,0:T(8,128)} %bitcast.14, s16[2,1040,128]{2,1,0:T(8,128)(2,1)} %copy-done.9), custom_call_target="tpu_custom_call" | custom-call | bytes 9000000 | tf_op jit(solution)/shard_map/hop/pallas_call | solution.py:285
  89.8 6.6 %collective-permute-start.20 = (s16[1,1040,128]{2,1,0:T(8,128)(2,1)S(1)}, s16[1,1040,128]{2,1,0:T(8,128)(2,1)S(1)}, u32[]{:S(2)}, u32[]{:S(2)}) collective-permute-start(s16[1,1040,128]{2,1,0:T(8,128)(2,1)S(1)} %hop.11), channel_id=1, source_target_pairs={{8,0},{0,8},{16,24},{24,16},{9,1},{1,9},{17,25},{25,17},{10,2},{2,... | collective-permute-start | bytes 798728 | tf_op jit(solution)/shard_map/ppermute | solution.py:306
  96.4 0.8 copy-done.10
  97.2 2.4 %hop.9 = s16[1,1040,128]{2,1,0:T(8,128)(2,1)S(1)} custom-call(s32[1]{0:T(128)S(6)} %select_n.61.idx_ref, f32[4,1024,128]{2,1,0:T(8,128)} %bitcast.17, s16[2,1040,128]{2,1,0:T(8,128)(2,1)} %copy-done.10), custom_call_target="tpu_custom_call" | custom-call | bytes 9000000 | tf_op jit(solution)/shard_map/hop/pallas_call | solution.py:285
  99.6 6.1 %collective-permute-start.17 = (s16[1,1040,128]{2,1,0:T(8,128)(2,1)S(1)}, s16[1,1040,128]{2,1,0:T(8,128)(2,1)S(1)}, u32[]{:S(2)}, u32[]{:S(2)}) collective-permute-start(s16[1,1040,128]{2,1,0:T(8,128)(2,1)S(1)} %hop.9), channel_id=1, source_target_pairs={{8,0},{0,8},{16,24},{24,16},{9,1},{1,9},{17,25},{25,17},{10,2},{2,... | collective-permute-start | bytes 798728 | tf_op jit(solution)/shard_map/ppermute | solution.py:306
  105.7 0.8 copy-done.11
  106.5 2.4 %hop.7 = s16[1,1040,128]{2,1,0:T(8,128)(2,1)S(1)} custom-call(s32[1]{0:T(128)S(6)} %select_n.61.idx_ref, f32[4,1024,128]{2,1,0:T(8,128)} %bitcast.20, s16[2,1040,128]{2,1,0:T(8,128)(2,1)} %copy-done.11), custom_call_target="tpu_custom_call" | custom-call | bytes 9000000 | tf_op jit(solution)/shard_map/hop/pallas_call | solution.py:285
  109.0 3.7 %collective-permute-start.11 = (s16[1,1040,128]{2,1,0:T(8,128)(2,1)S(1)}, s16[1,1040,128]{2,1,0:T(8,128)(2,1)S(1)}, u32[]{:S(2)}, u32[]{:S(2)}) collective-permute-start(s16[1,1040,128]{2,1,0:T(8,128)(2,1)S(1)} %hop.7), channel_id=1, source_target_pairs={{8,0},{0,8},{16,24},{24,16},{9,1},{1,9},{17,25},{25,17},{10,2},{2,... | collective-permute-start | bytes 798728 | tf_op jit(solution)/shard_map/ppermute | solution.py:306
  113.4 3.7 %collective-permute-done.11.refs_2_ = s16[1,1040,128]{2,1,0:T(8,128)(2,1)S(1)} collective-permute-done((s16[1,1040,128]{2,1,0:T(8,128)(2,1)S(1)}, s16[1,1040,128]{2,1,0:T(8,128)(2,1)S(1)}, u32[]{:S(2)}, u32[]{:S(2)}) %collective-permute-start.11) | collective-permute-done | bytes 266272 | tf_op jit(solution)/shard_map/ppermute | solution.py:306
  117.1 0.7 copy-done.21
  117.8 4.8 %image_of.1 = f32[2,4,256,128]{3,2,1,0:T(8,128)} custom-call(s32[1]{0:T(128)} %bitcast.own_ref, f32[4,1024,128]{2,1,0:T(8,128)} %bitcast.21, s16[2,1040,128]{2,1,0:T(8,128)(2,1)} %copy-done.11, s16[1,1040,128]{2,1,0:T(8,128)(2,1)} %copy-done.21, f32[4,1024,128]{2,1,0:T(8,128)} %bitcast.18, s16[2,1040,128]{2,1,0:T(8,128)(2,1)} %copy-done.10, ...), custom_call_target="tpu_custom_call" | custom-call | bytes 18000000 | tf_op jit(solution)/shard_map/image_of/pallas_call | solution.py:377
  (71 shorter events, 2.8 us)
Async XLA Ops:
  0.0 112.7 %copy-start = (f32[1024]{0:T(1024)S(1)}, f32[1024]{0:T(1024)}, u32[]{:S(2)}) copy-start(f32[1024]{0:T(1024)} %param.26) | copy-start | bytes 12292
  0.0 14.8 %copy-start.4 = (bf16[512,2048]{1,0:T(8,128)(2,1)S(1)}, bf16[512,2048]{1,0:T(8,128)(2,1)}, u32[]{:S(2)}) copy-start(bf16[512,2048]{1,0:T(8,128)(2,1)} %refs_0_.1) | copy-start | bytes 6291460
  0.0 14.8 %collective-permute-start.2 = (bf16[512,2048]{1,0:T(8,128)(2,1)}, bf16[512,2048]{1,0:T(8,128)(2,1)}, u32[]{:S(2)}, u32[]{:S(2)}) collective-permute-start(bf16[512,2048]{1,0:T(8,128)(2,1)} %refs_0_.1), channel_id=1, source_target_pairs={{0,1},{1,0},{2,3},{3,2},{4,5},{5,4},{6,7},{7,6},{8,9},{9,8},{10,11... | collective-permute-start | bytes 6291464 | tf_op jit(solution)/shard_map/ppermute | solution.py:144
  0.5 5.4 %collective-permute-start.1 = (bf16[512,1024]{1,0:T(8,128)(2,1)}, bf16[512,1024]{1,0:T(8,128)(2,1)S(1)}, u32[]{:S(2)}, u32[]{:S(2)}) collective-permute-start(bf16[512,1024]{1,0:T(8,128)(2,1)} %refs_3_.1), channel_id=1, source_target_pairs={{0,1},{1,0},{2,3},{3,2},{4,5},{5,4},{6,7},{7,6},{8,9},{9,8},{10,11... | collective-permute-start | bytes 3145736 | tf_op jit(solution)/shard_map/ppermute | solution.py:144
  1.4 4.5 %copy-start.27 = (s32[3,512]{1,0:T(4,128)}, s32[3,512]{1,0:T(4,128)S(1)}, u32[]{:S(2)}) copy-start(s32[3,512]{1,0:T(4,128)S(1)} %pad_add_fusion.refs_0_) | copy-start | bytes 18436
  1.4 3.6 %collective-permute-start = (s32[3,512]{1,0:T(4,128)S(1)}, s32[3,512]{1,0:T(4,128)S(1)}, u32[]{:S(2)}, u32[]{:S(2)}) collective-permute-start(s32[3,512]{1,0:T(4,128)S(1)} %pad_add_fusion.refs_0_), channel_id=1, source_target_pairs={{0,1},{1,0},{2,3},{3,2},{4,5},{5,4},{6,7},{7,6},{8,9},{9,8},{10,11... | collective-permute-start | bytes 18440 | tf_op jit(solution)/shard_map/ppermute | solution.py:144
  5.0 0.9 copy-start.28
  5.9 1.0 copy-start.12
  10.6 8.2 %copy-start.6 = (bf16[1152,128]{1,0:T(8,128)(2,1)}, bf16[1152,128]{1,0:T(8,128)(2,1)S(1)}, u32[]{:S(2)}) copy-start(bf16[1152,128]{1,0:T(8,128)(2,1)S(1)} %get-tuple-element.42.refs_0_) | copy-start | bytes 884740
  10.6 11.6 %collective-permute-start.3 = (bf16[1152,128]{1,0:T(8,128)(2,1)S(1)}, bf16[1152,128]{1,0:T(8,128)(2,1)S(1)}, u32[]{:S(2)}, u32[]{:S(2)}) collective-permute-start(bf16[1152,128]{1,0:T(8,128)(2,1)S(1)} %get-tuple-element.34), channel_id=1, source_target_pairs={{0,2},{1,3},{2,0},{3,1},{4,6},{5,7},{6,4},{7,5},{8,10},{9,11},{10,... | collective-permute-start | bytes 884744 | tf_op jit(solution)/shard_map/ppermute | solution.py:144
  13.2 15.0 %collective-permute-start.5 = (bf16[1152,128]{1,0:T(8,128)(2,1)S(1)}, bf16[1152,128]{1,0:T(8,128)(2,1)S(1)}, u32[]{:S(2)}, u32[]{:S(2)}) collective-permute-start(bf16[1152,128]{1,0:T(8,128)(2,1)S(1)} %get-tuple-element.37), channel_id=1, source_target_pairs={{0,4},{1,5},{2,6},{3,7},{4,0},{5,1},{6,2},{7,3},{8,12},{9,13},{10,... | collective-permute-start | bytes 884744 | tf_op jit(solution)/shard_map/ppermute | solution.py:144
  14.7 15.3 %collective-permute-start.7 = (bf16[1152,128]{1,0:T(8,128)(2,1)S(1)}, bf16[1152,128]{1,0:T(8,128)(2,1)S(1)}, u32[]{:S(2)}, u32[]{:S(2)}) collective-permute-start(bf16[1152,128]{1,0:T(8,128)(2,1)S(1)} %get-tuple-element.40), channel_id=1, source_target_pairs={{0,6},{1,7},{2,4},{3,5},{4,2},{5,3},{6,0},{7,1},{8,14},{9,15},{10,... | collective-permute-start | bytes 884744 | tf_op jit(solution)/shard_map/ppermute | solution.py:144
  14.8 20.3 %copy-start.29 = (s32[2]{0:T(128)S(1)}, s32[2]{0:T(128)}, u32[]{:S(2)}) copy-start(s32[2]{0:T(128)} %constant.34.clone) | copy-start | bytes 28
  14.8 20.3 %copy-start.30 = (s32[2]{0:T(128)S(1)}, s32[2]{0:T(128)}, u32[]{:S(2)}) copy-start(s32[2]{0:T(128)} %constant.33.clone) | copy-start | bytes 28
  19.5 0.7 copy-start.8
  20.2 13.0 %collective-permute-start.12 = (bf16[1024,128]{1,0:T(8,128)(2,1)S(1)}, bf16[1024,128]{1,0:T(8,128)(2,1)S(1)}, u32[]{:S(2)}, u32[]{:S(2)}) collective-permute-start(bf16[1024,128]{1,0:T(8,128)(2,1)S(1)} %get-tuple-element.50), channel_id=1, source_target_pairs={{0,2},{1,3},{2,0},{3,1},{4,6},{5,7},{6,4},{7,5},{8,10},{9,11},{10,... | collective-permute-start | bytes 786440 | tf_op jit(solution)/shard_map/ppermute | solution.py:144
  22.1 11.0 %copy-start.16 = (bf16[1152,128]{1,0:T(8,128)(2,1)}, bf16[1152,128]{1,0:T(8,128)(2,1)S(1)}, u32[]{:S(2)}) copy-start(bf16[1152,128]{1,0:T(8,128)(2,1)S(1)} %collective-permute-done.3.refs_1_) | copy-start | bytes 884740
  28.2 5.0 %copy-start.17 = (bf16[1152,128]{1,0:T(8,128)(2,1)}, bf16[1152,128]{1,0:T(8,128)(2,1)S(1)}, u32[]{:S(2)}) copy-start(bf16[1152,128]{1,0:T(8,128)(2,1)S(1)} %collective-permute-done.5.refs_2_) | copy-start | bytes 884740
  28.2 20.5 %collective-permute-start.13 = (bf16[1024,128]{1,0:T(8,128)(2,1)S(1)}, bf16[1024,128]{1,0:T(8,128)(2,1)S(1)}, u32[]{:S(2)}, u32[]{:S(2)}) collective-permute-start(bf16[1024,128]{1,0:T(8,128)(2,1)S(1)} %get-tuple-element.51), channel_id=1, source_target_pairs={{0,4},{1,5},{2,6},{3,7},{4,0},{5,1},{6,2},{7,3},{8,12},{9,13},{10,... | collective-permute-start | bytes 786440 | tf_op jit(solution)/shard_map/ppermute | solution.py:144
  30.0 22.3 %collective-permute-start.14 = (bf16[1024,128]{1,0:T(8,128)(2,1)S(1)}, bf16[1024,128]{1,0:T(8,128)(2,1)S(1)}, u32[]{:S(2)}, u32[]{:S(2)}) collective-permute-start(bf16[1024,128]{1,0:T(8,128)(2,1)S(1)} %get-tuple-element.52), channel_id=1, source_target_pairs={{0,6},{1,7},{2,4},{3,5},{4,2},{5,3},{6,0},{7,1},{8,14},{9,15},{10,... | collective-permute-start | bytes 786440 | tf_op jit(solution)/shard_map/ppermute | solution.py:144
  30.1 3.1 %copy-start.18 = (bf16[1152,128]{1,0:T(8,128)(2,1)}, bf16[1152,128]{1,0:T(8,128)(2,1)S(1)}, u32[]{:S(2)}) copy-start(bf16[1152,128]{1,0:T(8,128)(2,1)S(1)} %collective-permute-done.7.refs_3_) | copy-start | bytes 884740
  30.1 32.1 %collective-permute-start.8 = (bf16[1024,128]{1,0:T(8,128)(2,1)S(1)}, bf16[1024,128]{1,0:T(8,128)(2,1)S(1)}, u32[]{:S(2)}, u32[]{:S(2)}) collective-permute-start(bf16[1024,128]{1,0:T(8,128)(2,1)S(1)} %get-tuple-element.41), channel_id=1, source_target_pairs={{0,6},{1,7},{2,4},{3,5},{4,2},{5,3},{6,0},{7,1},{8,14},{9,15},{10,... | collective-permute-start | bytes 786440 | tf_op jit(solution)/shard_map/ppermute | solution.py:144
  33.0 29.2 %collective-permute-start.6 = (bf16[1024,128]{1,0:T(8,128)(2,1)S(1)}, bf16[1024,128]{1,0:T(8,128)(2,1)S(1)}, u32[]{:S(2)}, u32[]{:S(2)}) collective-permute-start(bf16[1024,128]{1,0:T(8,128)(2,1)S(1)} %get-tuple-element.38), channel_id=1, source_target_pairs={{0,4},{1,5},{2,6},{3,7},{4,0},{5,1},{6,2},{7,3},{8,12},{9,13},{10,... | collective-permute-start | bytes 786440 | tf_op jit(solution)/shard_map/ppermute | solution.py:144
  33.2 19.2 %copy-start.22 = (bf16[1024,128]{1,0:T(8,128)(2,1)}, bf16[1024,128]{1,0:T(8,128)(2,1)S(1)}, u32[]{:S(2)}) copy-start(bf16[1024,128]{1,0:T(8,128)(2,1)S(1)} %collective-permute-done.12.refs_1_) | copy-start | bytes 786436
  33.2 29.1 %collective-permute-start.4 = (bf16[1024,128]{1,0:T(8,128)(2,1)S(1)}, bf16[1024,128]{1,0:T(8,128)(2,1)}, u32[]{:S(2)}, u32[]{:S(2)}) collective-permute-start(bf16[1024,128]{1,0:T(8,128)(2,1)S(1)} %get-tuple-element.35), channel_id=1, source_target_pairs={{0,2},{1,3},{2,0},{3,1},{4,6},{5,7},{6,4},{7,5},{8,10},{9,11},{10,... | collective-permute-start | bytes 786440 | tf_op jit(solution)/shard_map/ppermute | solution.py:144
  41.7 1.4 %copy-start.1 = (f32[16,8,32,128]{3,2,1,0:T(8,128)}, f32[16,8,32,128]{3,2,1,0:T(8,128)S(1)}, u32[]{:S(2)}) copy-start(f32[16,8,32,128]{3,2,1,0:T(8,128)S(1)} %get-tuple-element.55) | copy-start | bytes 6291460
  48.7 3.7 %copy-start.25 = (bf16[1024,128]{1,0:T(8,128)(2,1)}, bf16[1024,128]{1,0:T(8,128)(2,1)S(1)}, u32[]{:S(2)}) copy-start(bf16[1024,128]{1,0:T(8,128)(2,1)S(1)} %collective-permute-done.13.refs_2_) | copy-start | bytes 786436
  48.7 23.5 %collective-permute-start.18 = (s16[2,1040,128]{2,1,0:T(8,128)(2,1)S(1)}, s16[2,1040,128]{2,1,0:T(8,128)(2,1)S(1)}, u32[]{:S(2)}, u32[]{:S(2)}) collective-permute-start(s16[2,1040,128]{2,1,0:T(8,128)(2,1)S(1)} %get-tuple-element.56), channel_id=1, source_target_pairs={{0,8},{24,16},{1,9},{25,17},{2,10},{26,18},{3,11},{27,19},{4,12},{... | collective-permute-start | bytes 1597448 | tf_op jit(solution)/shard_map/ppermute | solution.py:306
  59.5 1.4 %copy-start.2 = (f32[16,8,32,128]{3,2,1,0:T(8,128)}, f32[16,8,32,128]{3,2,1,0:T(8,128)S(1)}, u32[]{:S(2)}) copy-start(f32[16,8,32,128]{3,2,1,0:T(8,128)S(1)} %get-tuple-element.53) | copy-start | bytes 6291460
  60.9 16.2 %collective-permute-start.15 = (s16[2,1040,128]{2,1,0:T(8,128)(2,1)S(1)}, s16[2,1040,128]{2,1,0:T(8,128)(2,1)S(1)}, u32[]{:S(2)}, u32[]{:S(2)}) collective-permute-start(s16[2,1040,128]{2,1,0:T(8,128)(2,1)S(1)} %get-tuple-element.54), channel_id=1, source_target_pairs={{0,8},{24,16},{1,9},{25,17},{2,10},{26,18},{3,11},{27,19},{4,12},{... | collective-permute-start | bytes 1597448 | tf_op jit(solution)/shard_map/ppermute | solution.py:306
  62.2 0.8 copy-start.24
  69.4 1.4 %copy-start.3 = (f32[16,8,32,128]{3,2,1,0:T(8,128)}, f32[16,8,32,128]{3,2,1,0:T(8,128)S(1)}, u32[]{:S(2)}) copy-start(f32[16,8,32,128]{3,2,1,0:T(8,128)S(1)} %get-tuple-element.47) | copy-start | bytes 6291460
  70.8 10.9 %collective-permute-start.9 = (s16[2,1040,128]{2,1,0:T(8,128)(2,1)S(1)}, s16[2,1040,128]{2,1,0:T(8,128)(2,1)S(1)}, u32[]{:S(2)}, u32[]{:S(2)}) collective-permute-start(s16[2,1040,128]{2,1,0:T(8,128)(2,1)S(1)} %get-tuple-element.48), channel_id=1, source_target_pairs={{0,8},{24,16},{1,9},{25,17},{2,10},{26,18},{3,11},{27,19},{4,12},{... | collective-permute-start | bytes 1597448 | tf_op jit(solution)/shard_map/ppermute | solution.py:306
  72.1 0.8 copy-start.13
  76.1 10.3 %collective-permute-start.19 = (s16[2,1040,128]{2,1,0:T(8,128)(2,1)S(1)}, s16[2,1040,128]{2,1,0:T(8,128)(2,1)S(1)}, u32[]{:S(2)}, u32[]{:S(2)}) collective-permute-start(s16[2,1040,128]{2,1,0:T(8,128)(2,1)S(1)} %hop.10), channel_id=1, source_target_pairs={{8,16},{16,8},{9,17},{17,9},{10,18},{18,10},{11,19},{19,11},{12,20... | collective-permute-start | bytes 1597448 | tf_op jit(solution)/shard_map/ppermute | solution.py:306
  77.0 0.8 copy-start.14
  81.0 15.3 %collective-permute-start.16 = (s16[2,1040,128]{2,1,0:T(8,128)(2,1)S(1)}, s16[2,1040,128]{2,1,0:T(8,128)(2,1)S(1)}, u32[]{:S(2)}, u32[]{:S(2)}) collective-permute-start(s16[2,1040,128]{2,1,0:T(8,128)(2,1)S(1)} %hop.8), channel_id=1, source_target_pairs={{8,16},{16,8},{9,17},{17,9},{10,18},{18,10},{11,19},{19,11},{12,20... | collective-permute-start | bytes 1597448 | tf_op jit(solution)/shard_map/ppermute | solution.py:306
  81.7 0.8 copy-start.15
  85.7 20.0 %collective-permute-start.10 = (s16[2,1040,128]{2,1,0:T(8,128)(2,1)S(1)}, s16[2,1040,128]{2,1,0:T(8,128)(2,1)S(1)}, u32[]{:S(2)}, u32[]{:S(2)}) collective-permute-start(s16[2,1040,128]{2,1,0:T(8,128)(2,1)S(1)} %hop.6), channel_id=1, source_target_pairs={{8,16},{16,8},{9,17},{17,9},{10,18},{18,10},{11,19},{19,11},{12,20... | collective-permute-start | bytes 1597448 | tf_op jit(solution)/shard_map/ppermute | solution.py:306
  86.4 0.9 copy-start.9
  89.8 23.6 %collective-permute-start.20 = (s16[1,1040,128]{2,1,0:T(8,128)(2,1)S(1)}, s16[1,1040,128]{2,1,0:T(8,128)(2,1)S(1)}, u32[]{:S(2)}, u32[]{:S(2)}) collective-permute-start(s16[1,1040,128]{2,1,0:T(8,128)(2,1)S(1)} %hop.11), channel_id=1, source_target_pairs={{8,0},{0,8},{16,24},{24,16},{9,1},{1,9},{17,25},{25,17},{10,2},{2,... | collective-permute-start | bytes 798728 | tf_op jit(solution)/shard_map/ppermute | solution.py:306
  96.4 0.8 copy-start.10
  99.6 13.8 %collective-permute-start.17 = (s16[1,1040,128]{2,1,0:T(8,128)(2,1)S(1)}, s16[1,1040,128]{2,1,0:T(8,128)(2,1)S(1)}, u32[]{:S(2)}, u32[]{:S(2)}) collective-permute-start(s16[1,1040,128]{2,1,0:T(8,128)(2,1)S(1)} %hop.9), channel_id=1, source_target_pairs={{8,0},{0,8},{16,24},{24,16},{9,1},{1,9},{17,25},{25,17},{10,2},{2,... | collective-permute-start | bytes 798728 | tf_op jit(solution)/shard_map/ppermute | solution.py:306
  105.7 0.8 copy-start.11
  109.0 8.1 %collective-permute-start.11 = (s16[1,1040,128]{2,1,0:T(8,128)(2,1)S(1)}, s16[1,1040,128]{2,1,0:T(8,128)(2,1)S(1)}, u32[]{:S(2)}, u32[]{:S(2)}) collective-permute-start(s16[1,1040,128]{2,1,0:T(8,128)(2,1)S(1)} %hop.7), channel_id=1, source_target_pairs={{8,0},{0,8},{16,24},{24,16},{9,1},{1,9},{17,25},{25,17},{10,2},{2,... | collective-permute-start | bytes 798728 | tf_op jit(solution)/shard_map/ppermute | solution.py:306
  113.4 3.7 %copy-start.19 = (s16[1,1040,128]{2,1,0:T(8,128)(2,1)}, s16[1,1040,128]{2,1,0:T(8,128)(2,1)S(1)}, u32[]{:S(2)}) copy-start(s16[1,1040,128]{2,1,0:T(8,128)(2,1)S(1)} %collective-permute-done.20.refs_8_) | copy-start | bytes 798724
  113.4 3.7 %copy-start.20 = (s16[1,1040,128]{2,1,0:T(8,128)(2,1)}, s16[1,1040,128]{2,1,0:T(8,128)(2,1)S(1)}, u32[]{:S(2)}) copy-start(s16[1,1040,128]{2,1,0:T(8,128)(2,1)S(1)} %collective-permute-done.17.refs_5_) | copy-start | bytes 798724
  117.1 0.7 copy-start.21
  (4 other events, 2.8 us)

commit v3 on v2

--- a/solution.py
+++ b/solution.py
@@ -14,21 +14,17 @@
 NBLK = 64
 LANES = 128
 ALIGN = 16
-TIE = 1
 TOP = 32767.0
 STEPS = 256.0
 VMEM = 60 * 1024 * 1024
 
 WHOLE = pl.BlockSpec(memory_space=pltpu.VMEM)
 SCALARS = pl.BlockSpec(memory_space=pltpu.SMEM)
+UNREAD = pl.BlockSpec(memory_space=pl.ANY)
 
 
 def params(width):
     return pltpu.CompilerParams(vmem_limit_bytes=VMEM if width < LANES else VMEM // 2)
-
-
-def near(x):
-    return pltpu.with_memory_space_constraint(x, pltpu.VMEM)
 
 
 def far(x):
@@ -114,52 +110,55 @@
     return done[0], done[1:]
 
 
-def sort_kernel(slabs, width, me_ref, order_ref, *refs):
-    x_refs, out_refs = refs[0:2], refs[2:]
+def sort_kernel(slabs, width, part, ties, me_ref, order_ref, *refs):
+    x_refs, out_refs = refs[0:2], refs[2 + ties :]
     rows = order_ref.shape[1]
-    for part in range(2):
+    for i, out in enumerate(out_refs):
+        column = jnp.bitwise_xor(me_ref[0], 2 * i) + part * slabs
         for half in range(2):
-            order = order_ref[half]
-            for i in range(slabs // 2):
-                column = jnp.bitwise_xor(me_ref[0], 2 * i) + part * slabs
-                out = out_refs[part * (slabs // 2) + i]
-                out[half * rows : (half + 1) * rows, :] = sorted_piece(order, x_refs[half], column, width)
-
-
-def sort_columns(slabs, me, order, xs):
-    rows, width = order.shape[1], xs[0].shape[1] // (2 * slabs)
-    done = pl.pallas_call(
-        functools.partial(sort_kernel, slabs, width),
-        out_shape=[jax.ShapeDtypeStruct((2 * rows, width), jnp.bfloat16)] * slabs,
-        in_specs=[SCALARS] + [WHOLE] * 3,
-        out_specs=[WHOLE] * slabs,
+            out[half * rows : (half + 1) * rows, :] = sorted_piece(order_ref[half], x_refs[half], column, width)
+
+
+def sort_columns(slabs, me, order, xs, part, ties):
+    rows, kx = order.shape[1], xs[0].shape[1] // 2
+    width = kx // slabs
+    if width % LANES == 0:
+        x_spec = pl.BlockSpec((rows, kx), functools.partial(lambda part, i, s: (0, part), part))
+        part = 0
+    else:
+        x_spec = pl.BlockSpec((2 * slabs, rows, width), lambda i, s: (0, 0, 0))
+    out = pl.BlockSpec((2 * rows, width), lambda i, s: (0, 0))
+    return pl.pallas_call(
+        functools.partial(sort_kernel, slabs, width, part, len(ties)),
+        out_shape=[jax.ShapeDtypeStruct((2 * rows, width), jnp.bfloat16)] * (slabs // 2),
+        grid_spec=pltpu.PrefetchScalarGridSpec(
+            num_scalar_prefetch=1,
+            grid=(1,),
+            in_specs=[pl.BlockSpec(order.shape, lambda i, s: (0, 0, 0)), x_spec, x_spec] + [UNREAD] * len(ties),
+            out_specs=[out] * (slabs // 2),
+        ),
         compiler_params=params(width),
-        cost_estimate=cost(5.0),
+        cost_estimate=cost(3.0),
         name="sort_columns",
-    )(me, order, *[by_slab(x, slabs, width) for x in xs])
-    return done[: slabs // 2], done[slabs // 2 :]
+    )(me, order, *[far(by_slab(x, slabs, width)) for x in xs], *ties)
 
 
 def swap(x, slabs, offset):
     return lax.ppermute(x, "slab", [(i, i ^ offset) for i in range(slabs)])
 
 
-def exchange(pieces, after=None):
-    got = [pieces[0]]
-    for i in range(1, len(pieces)):
-        piece = pieces[i]
-        if after is not None:
-            piece, after[i] = lax.optimization_barrier((piece, after[i]))
-        got.append(swap(piece, 2 * len(pieces), 2 * i))
-    return got
-
-
-def volume_kernel(slabs, window, count, first, idx_ref, *refs):
+def exchange(pieces):
+    return [pieces[0]] + [swap(pieces[i], 2 * len(pieces), 2 * i) for i in range(1, len(pieces))]
+
+
+def volume_kernel(slabs, window, messages, first, ties, idx_ref, *refs):
+    refs = refs[ties:]
     piece_refs, refs = refs[: slabs // 2], refs[slabs // 2 :]
     if first:
-        sums_ref, code_ref, meta_ref, all_ref, line_ref, scalar_ref, sem = refs
+        sums_ref, meta_ref, code_refs = refs[0], refs[1], refs[2:-4]
     else:
-        meta_ref, sums_ref, code_ref, all_ref, line_ref, scalar_ref, sem = refs
+        meta_ref, sums_ref, code_refs = refs[0], refs[1], refs[2:-4]
+    all_ref, line_ref, scalar_ref, sem = refs[-4:]
     width = sums_ref.shape[3]
     rows = all_ref.shape[1]
     pick = (iota((16, LANES), 0) == iota((16, LANES), 1)).astype(jnp.bfloat16)
@@ -198,14 +197,17 @@
             slab_sums(slab)
     else:
         lax.fori_loop(0, slabs, lambda slab, carry: (slab_sums(slab), carry)[1], 0)
-    portion = code_ref.shape[1] - ALIGN
+    portion = code_refs[0].shape[1] - ALIGN
     lines = portion // (slabs * KZ_DEV)
-    for i in range(count):
-        x = sums_ref[pl.ds(idx_ref[i] * lines, lines)].reshape(portion, width)
-        code_ref[i, :portion, :], code_ref[i, portion:, :] = encode(x)
-
-
-def volume_sums(window, index, count, groups, pieces, meta=None):
+    at = 0
+    for code_ref, count in zip(code_refs, messages):
+        for i in range(count):
+            x = sums_ref[pl.ds(idx_ref[at] * lines, lines)].reshape(portion, width)
+            code_ref[i, :portion, :], code_ref[i, portion:, :] = encode(x)
+            at += 1
+
+
+def volume_sums(window, index, messages, groups, pieces, meta, ties):
     slabs = 2 * len(pieces)
     width = pieces[0].shape[1]
     first = meta is None
@@ -215,14 +217,14 @@
     portion = YWIN // groups * slabs * KZ_DEV
     out_shape = [
         jax.ShapeDtypeStruct((YWIN, slabs, KZ_DEV, width), jnp.float32),
-        jax.ShapeDtypeStruct((count, portion + ALIGN, width), jnp.int16),
     ]
     if first:
         out_shape.append(jax.ShapeDtypeStruct((slabs, 16, rows), jnp.bfloat16))
+    out_shape += [jax.ShapeDtypeStruct((count, portion + ALIGN, width), jnp.int16) for count in messages]
     done = pl.pallas_call(
-        functools.partial(volume_kernel, slabs, window, count, first),
+        functools.partial(volume_kernel, slabs, window, messages, first, len(ties)),
         out_shape=out_shape,
-        in_specs=[SCALARS] + [WHOLE] * (slabs // 2 + (0 if first else 1)),
+        in_specs=[SCALARS] + [UNREAD] * len(ties) + [WHOLE] * (len(pieces) + (0 if first else 1)),
         out_specs=[WHOLE] * len(out_shape),
         scratch_shapes=[
             pltpu.VMEM((slabs, rows, LANES), jnp.bfloat16),
@@ -233,8 +235,9 @@
         compiler_params=params(width),
         cost_estimate=cost(7.0),
         name="volume_sums",
-    )(index, *[far(x) for x in pieces], *([] if first else [far(meta)]))
-    return done[0].reshape(groups, portion, width), done[1], done[2] if first else meta
+    )(index, *ties, *[far(x) for x in pieces], *([] if first else [meta]))
+    sums = done[0].reshape(groups, portion, width)
+    return (sums, done[2:], done[1]) if first else (sums, done[1:], meta)
 
 
 def encode(x):
@@ -290,39 +293,51 @@
         compiler_params=params(width),
         cost_estimate=cost(2.0 + count),
         name="hop",
-    )(index, far(sums), far(prev))
+    )(index, sums, prev)
 
 
 def portions(z, groups, r):
     return jnp.where(z >= groups // 2, groups - 1 - r, r).astype(jnp.int32)
 
 
-def along_z(sums, payload, z, groups):
+def along_z(sums, messages, payloads, z, groups, split):
     half = groups // 2
     depth = jnp.minimum(z, groups - 1 - z)
-    steps = np.arange(groups)
 
     def send(payload, pairs):
         return lax.ppermute(payload, "grp", pairs + [(groups - 1 - a, groups - 1 - b) for a, b in pairs])
 
-    def add(r, prev, places):
-        return hop(portions(z, groups, r), sums, prev, list(places))
-
-    prev = send(payload, [(0, 1)])
-    inward = [None, prev]
+    def cut(rs):
+        return [[r] for r in rs] if split else [list(rs)]
+
+    def add(rs, got):
+        return hop(portions(z, groups, np.array(rs)), sums, got[rs[0]][0], [got[r][1] for r in rs])
+
+    def step(rs, got, pairs):
+        new = {}
+        for part in cut(rs):
+            payload = send(add(part, got), pairs)
+            new.update({r: (payload, i) for i, r in enumerate(part)})
+        return new
+
+    got = {}
+    for part, payload in zip(messages, payloads):
+        payload = send(payload, [(0, 1)])
+        got.update({r: (payload, i) for i, r in enumerate(part)})
+    inward = [None, got]
     for k in range(2, half):
-        prev = send(add(steps[k + 1 :], prev, range(1, groups - k)), [(k - 1, k)])
-        inward.append(prev)
-    prev = send(add(steps[half:], prev, range(half)), [(half - 1, half)])
-    ends = [(prev, 0)]
-    places = list(range(half - 1, -1, -1))
+        got = step(range(groups - 1, k, -1), got, [(k - 1, k)])
+        inward.append(got)
+    got = step(range(groups - 1, half - 1, -1), got, [(half - 1, half)])
+    got = {groups - 1 - r: x for r, x in got.items()}
+    ends = [got[half - 1]]
     for j in range(half - 1, 1, -1):
-        ends.append((send(add(steps[j : j + 1], inward[j - 1], [0]), [(j - 1, j)]), 0))
-        prev = send(add(steps[:j], prev, places[:j]), [(j, j - 1)])
-        ends.append((prev, j - 1))
-        places = list(range(half))
-    prev = send(add(jnp.where(depth == 0, 1, steps[:1]), prev, places[:1]), [(1, 0), (0, 1)])
-    ends.append((prev, 0))
+        ends.append((send(add([j], inward[j - 1]), [(j - 1, j)]), 0))
+        got = step(range(j), got, [(j, j - 1)])
+        ends.append(got[j - 1])
+    last = jnp.where(depth == 0, 1, 0).reshape(1)
+    payload = hop(portions(z, groups, last), sums, got[0][0], [got[0][1]])
+    ends.append((send(payload, [(1, 0), (0, 1)]), 0))
     return ends
 
 
@@ -400,19 +415,22 @@
     ids = jnp.stack([dest[:, 0], block, pattern])
     ids, ctf_sq, spectra = [(x, swap(x, slabs, 1)) for x in (ids, ctf_sq, spectra)]
     order, ctf = plan_rows(slabs, window, me, ids, pattern_table, ctf_sq)
-    real, imag = sort_columns(slabs, me, order, spectra)
-    pieces = [exchange(ctf)]
-    pieces.append(exchange(real, pieces[0]))
-    index = portions(z, groups, np.arange(2, groups))
-    fields, meta = [], None
-    for piece in range(3):
-        if piece == 2:
-            pieces.append(exchange(imag, [lax.optimization_barrier((x, fields[0][1][0][0]))[0] for x in pieces[1]] if TIE == 1 else [payload0] * len(imag)))
-        piece = pieces[piece]
-        sums, payload, meta = volume_sums(window, index, groups - 2, groups, piece, meta)
-        if not fields:
-            payload0 = payload
-        fields.append((sums, along_z(sums, payload, z, groups)))
+    first = list(range(groups - 1, 1, -1))
+    index = portions(z, groups, np.array(first))
+
+    def volume(piece, meta, ties, split):
+        messages = [[r] for r in first] if split else [first]
+        sums, payloads, meta = volume_sums(window, index, [len(x) for x in messages], groups, piece, meta, ties)
+        return (sums, messages, payloads, z, groups, split), payloads[0], meta
+
+    real = sort_columns(slabs, me, order, spectra, 0, ())
+    ctf, real_there = exchange(ctf), exchange(real)
+    ctf_part, ctf_code, meta = volume(ctf, None, (real[0],), True)
+    imag = sort_columns(slabs, me, order, spectra, 1, (ctf_code, real_there[1]))
+    imag_there = exchange(imag)
+    real_part, real_code, _ = volume(real_there, meta, (imag[0],), True)
+    imag_part, imag_code, _ = volume(imag_there, meta, (real_code,), True)
+    fields = [(part[0], along_z(*part)) for part in (ctf_part, real_part, imag_part)]
     tau_here = lax.dynamic_slice_in_dim(tau, slab * width, width, 0)
     own = z.astype(jnp.int32).reshape(1)
     return image_of(own, [fields[1], fields[2], fields[0]], tau_here, KZ_DEV * slabs)

time: 124 us -> 117 us (0.944)
  local copies, waits for them, and re-layouts: 14.8 us -> 6.85 us
  starting transfers between devices: 39.1 us -> 42.7 us
  Pallas kernels: 48.7 us -> 46.6 us
    unnamed x62 -> x52, local copies, waits for them, and re-layouts: 14.1 us -> 6.21 us
    ppermute x12, waiting for transfers between devices: 15 us -> 9 us  [swap(): return lax.ppermute(x, 'slab', [(i, i ^ offset) for i in range(slabs)])]
    ppermute x9 -> x15, waiting for transfers between devices: 3.73 us -> 9.64 us  [send(): lax.ppermute(payload, 'grp', pairs + [(groups - 1 - a, groups - 1 - b) fo...]
    pallas_call x6 -> x9, Pallas kernels: 16.9 us -> 11 us  [hop(): pl.pallas_call(functools.partial(hop_kernel, places), out_shape=jax.Shape...]
    pallas_call x4 -> x5, Pallas kernels: 23.4 us -> 27.2 us  [the longest x3 20 us: volume_sums(): pl.pallas_call(functools.partial(volume_kernel, slabs, window, messages,...]
    ppermute x9 -> x15, starting transfers between devices: 25 us -> 28.1 us  [send(): lax.ppermute(payload, 'grp', pairs + [(groups - 1 - a, groups - 1 - b) fo...]
  transfers between devices with their start and end apart: 21 -> 27, of which waited for: 5 -> 8; matrix products, arithmetic and copies ran while one was open for 1% -> 1% of each run, Pallas kernels for 36% -> 36%
where the time goes in v3:
time: 117 us; the launch traced here: 116 us
  Pallas kernels  46.6 us (40%)
  starting transfers between devices  42.7 us (36%)
  waiting for transfers between devices  18.6 us (16%)
  local copies, waits for them, and re-layouts  6.85 us (6%)
    ppermute x15, starting transfers between devices, send(): lax.ppermute(payload, 'grp', pairs + [(groups - 1 - a, groups - 1 - b) fo...  28.1 us
    pallas_call x3, Pallas kernels, volume_sums(): pl.pallas_call(functools.partial(volume_kernel, slabs, window, messages,...  20 us
    ppermute x12, starting transfers between devices, swap(): return lax.ppermute(x, 'slab', [(i, i ^ offset) for i in range(slabs)])  14.6 us
    pallas_call x9, Pallas kernels, hop(): pl.pallas_call(functools.partial(hop_kernel, places), out_shape=jax.Shape...  11 us
    ppermute x15, waiting for transfers between devices, send(): lax.ppermute(payload, 'grp', pairs + [(groups - 1 - a, groups - 1 - b) fo...  9.64 us
    ppermute x12, waiting for transfers between devices, swap(): return lax.ppermute(x, 'slab', [(i, i ^ offset) for i in range(slabs)])  9 us
    pallas_call x2, Pallas kernels, sort_columns(): pl.pallas_call(functools.partial(sort_kernel, slabs, width, part, len(tie...  7.12 us
    unnamed x52, local copies, waits for them, and re-layouts  6.21 us
  transfers between devices with their start and end apart: 27, of which 8 were waited for; matrix products, arithmetic and copies ran while one was open for 1% of the time, Pallas kernels for 36%

profile of v3, /device:TPU:0, one launch (start us, length us, event | category | flops | bytes accessed | tf_op | source)
XLA Modules:
  0.0 116.0 jit_solution(9094432127277073814)
XLA Ops:
  0.5 0.7 pad_add_fusion.refs_0_
  1.8 3.2 %collective-permute-done.refs_1_ = s32[3,512]{1,0:T(4,128)S(1)} collective-permute-done((s32[3,512]{1,0:T(4,128)S(1)}, s32[3,512]{1,0:T(4,128)S(1)}, u32[]{:S(2)}, u32[]{:S(2)}) %collective-permute-start) | collective-permute-done | bytes 6176 | tf_op jit(solution)/shard_map/ppermute | solution.py:147
  5.0 0.9 collective-permute-done.1.refs_4_
  5.9 1.0 copy-done.10
  6.9 3.7 %plan_rows.1 = (bf16[2,512,512]{2,1,0:T(8,128)(2,1)S(1)}, bf16[1152,128]{1,0:T(8,128)(2,1)S(1)}, bf16[1152,128]{1,0:T(8,128)(2,1)S(1)}, bf16[1152,128]{1,0:T(8,128)(2,1)S(1)}, bf16[1152,128]{1,0:T(8,128)(2,1)S(1)}) custom-call(s32[1]{0:T(128)} %bitcast.1.me_ref, s32[3,512]{1,0:T(4,128)} %copy-done.23, s32[3,512]{1,0:T(4,128)} %copy-done.24, ...), custom_call_target="tpu_custom_call" | custom-call | bytes 18000000 | tf_op jit(solution)/shard_map/plan_rows/pallas_call | solution.py:101
  10.6 2.6 %collective-permute-start.3 = (bf16[1152,128]{1,0:T(8,128)(2,1)S(1)}, bf16[1152,128]{1,0:T(8,128)(2,1)S(1)}, u32[]{:S(2)}, u32[]{:S(2)}) collective-permute-start(bf16[1152,128]{1,0:T(8,128)(2,1)S(1)} %get-tuple-element.31), channel_id=1, source_target_pairs={{0,2},{1,3},{2,0},{3,1},{4,6},{5,7},{6,4},{7,5},{8,10},{9,11},{10,... | collective-permute-start | bytes 884744 | tf_op jit(solution)/shard_map/ppermute | solution.py:147
  13.2 1.5 %collective-permute-start.4 = (bf16[1152,128]{1,0:T(8,128)(2,1)S(1)}, bf16[1152,128]{1,0:T(8,128)(2,1)S(1)}, u32[]{:S(2)}, u32[]{:S(2)}) collective-permute-start(bf16[1152,128]{1,0:T(8,128)(2,1)S(1)} %get-tuple-element.32), channel_id=1, source_target_pairs={{0,4},{1,5},{2,6},{3,7},{4,0},{5,1},{6,2},{7,3},{8,12},{9,13},{10,... | collective-permute-start | bytes 884744 | tf_op jit(solution)/shard_map/ppermute | solution.py:147
  14.8 3.5 %sort_columns.2 = (bf16[1024,128]{1,0:T(8,128)(2,1)S(1)}, bf16[1024,128]{1,0:T(8,128)(2,1)}, bf16[1024,128]{1,0:T(8,128)(2,1)}, bf16[1024,128]{1,0:T(8,128)(2,1)}) custom-call(s32[1]{0:T(128)} %bitcast.1.me_ref, bf16[2,512,512]{2,1,0:T(8,128)(2,1)S(1)} %get-tuple-element.28.order_ref, bf16[512,2048]{1,0:T(8,128)(2,1)} %refs_0_.3, ...), custom_call_target="tpu_custom_call" | custom-call | bytes 9000000 | tf_op jit(solution)/shard_map/sort_columns/pallas_call | solution.py:131
  18.3 2.0 %collective-permute-start.6 = (bf16[1024,128]{1,0:T(8,128)(2,1)}, bf16[1024,128]{1,0:T(8,128)(2,1)}, u32[]{:S(2)}, u32[]{:S(2)}) collective-permute-start(bf16[1024,128]{1,0:T(8,128)(2,1)} %get-tuple-element.35), channel_id=1, source_target_pairs={{0,2},{1,3},{2,0},{3,1},{4,6},{5,7},{6,4},{7,5},{8,10},{9,11},{10,... | collective-permute-start | bytes 786440 | tf_op jit(solution)/shard_map/ppermute | solution.py:147
  20.3 1.5 %collective-permute-start.7 = (bf16[1024,128]{1,0:T(8,128)(2,1)}, bf16[1024,128]{1,0:T(8,128)(2,1)S(1)}, u32[]{:S(2)}, u32[]{:S(2)}) collective-permute-start(bf16[1024,128]{1,0:T(8,128)(2,1)} %get-tuple-element.37), channel_id=1, source_target_pairs={{0,4},{1,5},{2,6},{3,7},{4,0},{5,1},{6,2},{7,3},{8,12},{9,13},{10,... | collective-permute-start | bytes 786440 | tf_op jit(solution)/shard_map/ppermute | solution.py:147
  21.8 2.2 %collective-permute-start.8 = (bf16[1024,128]{1,0:T(8,128)(2,1)}, bf16[1024,128]{1,0:T(8,128)(2,1)S(1)}, u32[]{:S(2)}, u32[]{:S(2)}) collective-permute-start(bf16[1024,128]{1,0:T(8,128)(2,1)} %get-tuple-element.38), channel_id=1, source_target_pairs={{0,6},{1,7},{2,4},{3,5},{4,2},{5,3},{6,0},{7,1},{8,14},{9,15},{10,... | collective-permute-start | bytes 786440 | tf_op jit(solution)/shard_map/ppermute | solution.py:147
  24.0 4.7 %collective-permute-done.4.refs_3_ = bf16[1152,128]{1,0:T(8,128)(2,1)S(1)} collective-permute-done((bf16[1152,128]{1,0:T(8,128)(2,1)S(1)}, bf16[1152,128]{1,0:T(8,128)(2,1)S(1)}, u32[]{:S(2)}, u32[]{:S(2)}) %collective-permute-start.4) | collective-permute-done | bytes 294944 | tf_op jit(solution)/shard_map/ppermute | solution.py:147
  29.6 6.6 %volume_sums.3 = (f32[16,8,32,128]{3,2,1,0:T(8,128)S(1)}, bf16[8,16,512]{2,1,0:T(8,128)(2,1)S(1)}, s16[1,1040,128]{2,1,0:T(8,128)(2,1)S(1)}, s16[1,1040,128]{2,1,0:T(8,128)(2,1)S(1)}) custom-call(s32[2]{0:T(128)S(1)} %broadcast_select_fusion.idx_ref, bf16[1024,128]{1,0:T(8,128)(2,1)S(1)} %get-tuple-element.29.refs_0_.refs_1_, bf16[1152,128]{1,0:T(8,128)(2,1)} %copy-done.9, ...), custom_call_target="tpu_custom_call" | custom-call | bytes 21000000 | tf_op jit(solution)/shard_map/volume_sums/pallas_call | solution.py:224
  36.2 3.6 %sort_columns.3 = (bf16[1024,128]{1,0:T(8,128)(2,1)S(1)}, bf16[1024,128]{1,0:T(8,128)(2,1)S(1)}, bf16[1024,128]{1,0:T(8,128)(2,1)S(1)}, bf16[1024,128]{1,0:T(8,128)(2,1)S(1)}) custom-call(s32[1]{0:T(128)} %bitcast.1.me_ref, bf16[2,512,512]{2,1,0:T(8,128)(2,1)S(1)} %get-tuple-element.28.order_ref, bf16[512,2048]{1,0:T(8,128)(2,1)} %refs_0_.3, ...), custom_call_target="tpu_custom_call" | custom-call | bytes 9000000 | tf_op jit(solution)/shard_map/sort_columns/pallas_call | solution.py:131
  39.8 1.6 %collective-permute-start.14 = (bf16[1024,128]{1,0:T(8,128)(2,1)S(1)}, bf16[1024,128]{1,0:T(8,128)(2,1)S(1)}, u32[]{:S(2)}, u32[]{:S(2)}) collective-permute-start(bf16[1024,128]{1,0:T(8,128)(2,1)S(1)} %get-tuple-element.43), channel_id=1, source_target_pairs={{0,2},{1,3},{2,0},{3,1},{4,6},{5,7},{6,4},{7,5},{8,10},{9,11},{10,... | collective-permute-start | bytes 786440 | tf_op jit(solution)/shard_map/ppermute | solution.py:147
  41.3 0.8 collective-permute-start.15
  42.1 1.4 %collective-permute-start.16 = (bf16[1024,128]{1,0:T(8,128)(2,1)S(1)}, bf16[1024,128]{1,0:T(8,128)(2,1)S(1)}, u32[]{:S(2)}, u32[]{:S(2)}) collective-permute-start(bf16[1024,128]{1,0:T(8,128)(2,1)S(1)} %get-tuple-element.45), channel_id=1, source_target_pairs={{0,6},{1,7},{2,4},{3,5},{4,2},{5,3},{6,0},{7,1},{8,14},{9,15},{10,... | collective-permute-start | bytes 786440 | tf_op jit(solution)/shard_map/ppermute | solution.py:147
  43.5 3.7 %collective-permute-start.24 = (s16[1,1040,128]{2,1,0:T(8,128)(2,1)S(1)}, s16[1,1040,128]{2,1,0:T(8,128)(2,1)S(1)}, u32[]{:S(2)}, u32[]{:S(2)}) collective-permute-start(s16[1,1040,128]{2,1,0:T(8,128)(2,1)S(1)} %get-tuple-element.34.refs_2_), channel_id=1, source_target_pairs={{0,8},{24,16},{1,9},{25,17},{2,10},{26,18},{3,11},{27,19},{4,12},{... | collective-permute-start | bytes 798728 | tf_op jit(solution)/shard_map/ppermute | solution.py:308
  47.9 6.5 %volume_sums.4 = (f32[16,8,32,128]{3,2,1,0:T(8,128)S(1)}, s16[1,1040,128]{2,1,0:T(8,128)(2,1)S(1)}, s16[1,1040,128]{2,1,0:T(8,128)(2,1)S(1)}) custom-call(s32[2]{0:T(128)S(1)} %broadcast_select_fusion.idx_ref, bf16[1024,128]{1,0:T(8,128)(2,1)S(1)} %get-tuple-element.36.refs_0_.refs_1_, bf16[1024,128]{1,0:T(8,128)(2,1)} %copy-done.7, ...), custom_call_target="tpu_custom_call" | custom-call | bytes 21000000 | tf_op jit(solution)/shard_map/volume_sums/pallas_call | solution.py:224
  54.4 1.3 %collective-permute-start.11 = (s16[1,1040,128]{2,1,0:T(8,128)(2,1)S(1)}, s16[1,1040,128]{2,1,0:T(8,128)(2,1)S(1)}, u32[]{:S(2)}, u32[]{:S(2)}) collective-permute-start(s16[1,1040,128]{2,1,0:T(8,128)(2,1)S(1)} %get-tuple-element.42.refs_0_), channel_id=1, source_target_pairs={{0,8},{24,16},{1,9},{25,17},{2,10},{26,18},{3,11},{27,19},{4,12},{... | collective-permute-start | bytes 798728 | tf_op jit(solution)/shard_map/ppermute | solution.py:308
  56.5 0.7 copy-done.22
  57.3 7.0 %volume_sums.5 = (f32[16,8,32,128]{3,2,1,0:T(8,128)S(1)}, s16[1,1040,128]{2,1,0:T(8,128)(2,1)S(1)}, s16[1,1040,128]{2,1,0:T(8,128)(2,1)}) custom-call(s32[2]{0:T(128)S(1)} %broadcast_select_fusion.idx_ref, s16[1,1040,128]{2,1,0:T(8,128)(2,1)S(1)} %get-tuple-element.42.refs_0_, bf16[1024,128]{1,0:T(8,128)(2,1)} %copy-done.8, bf16[1024,128]{1,0:T(8,128)(2,1)} %copy-done.20, ...), custom_call_target="tpu_custom_call" | custom-call | bytes 21000000 | tf_op jit(solution)/shard_map/volume_sums/pallas_call | solution.py:224
  64.3 1.6 %collective-permute-start.19 = (s16[1,1040,128]{2,1,0:T(8,128)(2,1)S(1)}, s16[1,1040,128]{2,1,0:T(8,128)(2,1)S(1)}, u32[]{:S(2)}, u32[]{:S(2)}) collective-permute-start(s16[1,1040,128]{2,1,0:T(8,128)(2,1)S(1)} %get-tuple-element.48), channel_id=1, source_target_pairs={{0,8},{24,16},{1,9},{25,17},{2,10},{26,18},{3,11},{27,19},{4,12},{... | collective-permute-start | bytes 798728 | tf_op jit(solution)/shard_map/ppermute | solution.py:308
  65.8 1.3 %collective-permute-start.22 = (s16[1,1040,128]{2,1,0:T(8,128)(2,1)S(1)}, s16[1,1040,128]{2,1,0:T(8,128)(2,1)S(1)}, u32[]{:S(2)}, u32[]{:S(2)}) collective-permute-start(s16[1,1040,128]{2,1,0:T(8,128)(2,1)S(1)} %get-tuple-element.50), channel_id=1, source_target_pairs={{0,8},{24,16},{1,9},{25,17},{2,10},{26,18},{3,11},{27,19},{4,12},{... | collective-permute-start | bytes 798728 | tf_op jit(solution)/shard_map/ppermute | solution.py:308
  67.1 1.3 %collective-permute-start.9 = (s16[1,1040,128]{2,1,0:T(8,128)(2,1)S(1)}, s16[1,1040,128]{2,1,0:T(8,128)(2,1)S(1)}, u32[]{:S(2)}, u32[]{:S(2)}) collective-permute-start(s16[1,1040,128]{2,1,0:T(8,128)(2,1)S(1)} %get-tuple-element.41), channel_id=1, source_target_pairs={{0,8},{24,16},{1,9},{25,17},{2,10},{26,18},{3,11},{27,19},{4,12},{... | collective-permute-start | bytes 798728 | tf_op jit(solution)/shard_map/ppermute | solution.py:308
  68.5 1.5 %hop.16 = s16[1,1040,128]{2,1,0:T(8,128)(2,1)} custom-call(s32[1]{0:T(128)S(6)} %select_n.61.idx_ref, f32[4,1024,128]{2,1,0:T(8,128)S(1)} %bitcast.13, s16[1,1040,128]{2,1,0:T(8,128)(2,1)S(1)} %collective-permute-done.24.prev_ref), custom_call_target="tpu_custom_call" | custom-call | bytes 9000000 | tf_op jit(solution)/shard_map/hop/pallas_call | solution.py:288
  69.9 1.4 %collective-permute-start.25 = (s16[1,1040,128]{2,1,0:T(8,128)(2,1)}, s16[1,1040,128]{2,1,0:T(8,128)(2,1)}, u32[]{:S(2)}, u32[]{:S(2)}) collective-permute-start(s16[1,1040,128]{2,1,0:T(8,128)(2,1)} %hop.16), channel_id=1, source_target_pairs={{8,16},{16,8},{9,17},{17,9},{10,18},{18,10},{11,19},{19,11},{12,20... | collective-permute-start | bytes 798728 | tf_op jit(solution)/shard_map/ppermute | solution.py:308
  71.3 3.4 %collective-permute-start.17 = (s16[1,1040,128]{2,1,0:T(8,128)(2,1)}, s16[1,1040,128]{2,1,0:T(8,128)(2,1)S(1)}, u32[]{:S(2)}, u32[]{:S(2)}) collective-permute-start(s16[1,1040,128]{2,1,0:T(8,128)(2,1)} %get-tuple-element.47), channel_id=1, source_target_pairs={{0,8},{24,16},{1,9},{25,17},{2,10},{26,18},{3,11},{27,19},{4,12},{... | collective-permute-start | bytes 798728 | tf_op jit(solution)/shard_map/ppermute | solution.py:308
  74.7 0.8 hop.10
  76.2 0.8 hop.13
  77.0 1.4 %collective-permute-done.22.prev_ref = s16[1,1040,128]{2,1,0:T(8,128)(2,1)S(1)} collective-permute-done((s16[1,1040,128]{2,1,0:T(8,128)(2,1)S(1)}, s16[1,1040,128]{2,1,0:T(8,128)(2,1)S(1)}, u32[]{:S(2)}, u32[]{:S(2)}) %collective-permute-start.22) | collective-permute-done | bytes 266272 | tf_op jit(solution)/shard_map/ppermute | solution.py:308
  78.3 1.4 %collective-permute-start.20 = (s16[1,1040,128]{2,1,0:T(8,128)(2,1)S(1)}, s16[1,1040,128]{2,1,0:T(8,128)(2,1)}, u32[]{:S(2)}, u32[]{:S(2)}) collective-permute-start(s16[1,1040,128]{2,1,0:T(8,128)(2,1)S(1)} %hop.13), channel_id=1, source_target_pairs={{8,16},{16,8},{9,17},{17,9},{10,18},{18,10},{11,19},{19,11},{12,20... | collective-permute-start | bytes 798728 | tf_op jit(solution)/shard_map/ppermute | solution.py:308
  79.7 1.5 %hop.15 = s16[1,1040,128]{2,1,0:T(8,128)(2,1)} custom-call(s32[1]{0:T(128)S(6)} %select_n.58.idx_ref, f32[4,1024,128]{2,1,0:T(8,128)S(1)} %bitcast.14, s16[1,1040,128]{2,1,0:T(8,128)(2,1)S(1)} %collective-permute-done.22.prev_ref), custom_call_target="tpu_custom_call" | custom-call | bytes 9000000 | tf_op jit(solution)/shard_map/hop/pallas_call | solution.py:288
  81.2 2.4 %collective-permute-done.9.prev_ref = s16[1,1040,128]{2,1,0:T(8,128)(2,1)S(1)} collective-permute-done((s16[1,1040,128]{2,1,0:T(8,128)(2,1)S(1)}, s16[1,1040,128]{2,1,0:T(8,128)(2,1)S(1)}, u32[]{:S(2)}, u32[]{:S(2)}) %collective-permute-start.9) | collective-permute-done | bytes 266272 | tf_op jit(solution)/shard_map/ppermute | solution.py:308
  83.6 1.4 %collective-permute-start.23 = (s16[1,1040,128]{2,1,0:T(8,128)(2,1)}, s16[1,1040,128]{2,1,0:T(8,128)(2,1)}, u32[]{:S(2)}, u32[]{:S(2)}) collective-permute-start(s16[1,1040,128]{2,1,0:T(8,128)(2,1)} %hop.15), channel_id=1, source_target_pairs={{8,16},{16,8},{9,17},{17,9},{10,18},{18,10},{11,19},{19,11},{12,20... | collective-permute-start | bytes 798728 | tf_op jit(solution)/shard_map/ppermute | solution.py:308
  85.0 1.6 %copy-done.3 = f32[16,8,32,128]{3,2,1,0:T(8,128)S(1)} copy-done((f32[16,8,32,128]{3,2,1,0:T(8,128)S(1)}, f32[16,8,32,128]{3,2,1,0:T(8,128)}, u32[]{:S(2)}) %copy-start.3) | copy-done | bytes 2097176
  86.6 1.5 %hop.9 = s16[1,1040,128]{2,1,0:T(8,128)(2,1)} custom-call(s32[1]{0:T(128)S(6)} %select_n.58.idx_ref, f32[4,1024,128]{2,1,0:T(8,128)S(1)} %bitcast.19, s16[1,1040,128]{2,1,0:T(8,128)(2,1)S(1)} %collective-permute-done.9.prev_ref), custom_call_target="tpu_custom_call" | custom-call | bytes 9000000 | tf_op jit(solution)/shard_map/hop/pallas_call | solution.py:288
  88.1 1.5 %collective-permute-start.10 = (s16[1,1040,128]{2,1,0:T(8,128)(2,1)}, s16[1,1040,128]{2,1,0:T(8,128)(2,1)}, u32[]{:S(2)}, u32[]{:S(2)}) collective-permute-start(s16[1,1040,128]{2,1,0:T(8,128)(2,1)} %hop.9), channel_id=1, source_target_pairs={{8,16},{16,8},{9,17},{17,9},{10,18},{18,10},{11,19},{19,11},{12,20... | collective-permute-start | bytes 798728 | tf_op jit(solution)/shard_map/ppermute | solution.py:308
  89.5 1.7 %hop.17 = s16[1,1040,128]{2,1,0:T(8,128)(2,1)S(1)} custom-call(s32[1]{0:T(128)S(6)} %select_n.60.idx_ref, f32[4,1024,128]{2,1,0:T(8,128)S(1)} %bitcast.15, s16[1,1040,128]{2,1,0:T(8,128)(2,1)} %collective-permute-done.25.prev_ref), custom_call_target="tpu_custom_call" | custom-call | bytes 9000000 | tf_op jit(solution)/shard_map/hop/pallas_call | solution.py:288
  91.3 5.7 %collective-permute-start.26 = (s16[1,1040,128]{2,1,0:T(8,128)(2,1)S(1)}, s16[1,1040,128]{2,1,0:T(8,128)(2,1)S(1)}, u32[]{:S(2)}, u32[]{:S(2)}) collective-permute-start(s16[1,1040,128]{2,1,0:T(8,128)(2,1)S(1)} %hop.17), channel_id=1, source_target_pairs={{8,0},{0,8},{16,24},{24,16},{9,1},{1,9},{17,25},{25,17},{10,2},{2,... | collective-permute-start | bytes 798728 | tf_op jit(solution)/shard_map/ppermute | solution.py:308
  97.0 0.8 hop.12
  98.5 0.8 hop.11
  99.3 2.9 %collective-permute-start.13 = (s16[1,1040,128]{2,1,0:T(8,128)(2,1)S(1)}, s16[1,1040,128]{2,1,0:T(8,128)(2,1)S(1)}, u32[]{:S(2)}, u32[]{:S(2)}) collective-permute-start(s16[1,1040,128]{2,1,0:T(8,128)(2,1)S(1)} %hop.11), channel_id=1, source_target_pairs={{8,0},{0,8},{16,24},{24,16},{9,1},{1,9},{17,25},{25,17},{10,2},{2,... | collective-permute-start | bytes 798728 | tf_op jit(solution)/shard_map/ppermute | solution.py:308
  102.2 1.7 %hop.14 = s16[1,1040,128]{2,1,0:T(8,128)(2,1)S(1)} custom-call(s32[1]{0:T(128)S(6)} %select_n.60.idx_ref, f32[4,1024,128]{2,1,0:T(8,128)S(1)} %bitcast.24, s16[1,1040,128]{2,1,0:T(8,128)(2,1)} %collective-permute-done.20.prev_ref), custom_call_target="tpu_custom_call" | custom-call | bytes 9000000 | tf_op jit(solution)/shard_map/hop/pallas_call | solution.py:288
  104.7 3.0 %collective-permute-done.13.refs_2_ = s16[1,1040,128]{2,1,0:T(8,128)(2,1)S(1)} collective-permute-done((s16[1,1040,128]{2,1,0:T(8,128)(2,1)S(1)}, s16[1,1040,128]{2,1,0:T(8,128)(2,1)S(1)}, u32[]{:S(2)}, u32[]{:S(2)}) %collective-permute-start.13) | collective-permute-done | bytes 266272 | tf_op jit(solution)/shard_map/ppermute | solution.py:308
  107.6 2.9 %collective-permute-done.21.refs_5_ = s16[1,1040,128]{2,1,0:T(8,128)(2,1)S(1)} collective-permute-done((s16[1,1040,128]{2,1,0:T(8,128)(2,1)S(1)}, s16[1,1040,128]{2,1,0:T(8,128)(2,1)S(1)}, u32[]{:S(2)}, u32[]{:S(2)}) %collective-permute-start.21) | collective-permute-done | bytes 266272 | tf_op jit(solution)/shard_map/ppermute | solution.py:308
  110.5 0.7 copy-done.17
  111.2 4.8 %image_of.1 = f32[2,4,256,128]{3,2,1,0:T(8,128)} custom-call(s32[1]{0:T(128)} %bitcast.own_ref, f32[4,1024,128]{2,1,0:T(8,128)} %bitcast.18, s16[1,1040,128]{2,1,0:T(8,128)(2,1)} %collective-permute-done.10.refs_1_, s16[1,1040,128]{2,1,0:T(8,128)(2,1)} %copy-done.16, f32[4,1024,128]{2,1,0:T(8,128)} %bitcast.22, s16[1,1040,128]{2,1,0:T(8,128)(2,1)} %copy-done.15, ...), custom_call_target="tpu_custom_call" | custom-call | bytes 18000000 | tf_op jit(solution)/shard_map/image_of/pallas_call | solution.py:392
  (77 shorter events, 5.5 us)
Async XLA Ops:
  0.0 104.0 %copy-start = (f32[1024]{0:T(1024)S(1)}, f32[1024]{0:T(1024)}, u32[]{:S(2)}) copy-start(f32[1024]{0:T(1024)} %param.29) | copy-start | bytes 12292
  0.0 14.7 %collective-permute-start.2 = (bf16[512,2048]{1,0:T(8,128)(2,1)}, bf16[512,2048]{1,0:T(8,128)(2,1)}, u32[]{:S(2)}, u32[]{:S(2)}) collective-permute-start(bf16[512,2048]{1,0:T(8,128)(2,1)} %refs_0_.3), channel_id=1, source_target_pairs={{0,1},{1,0},{2,3},{3,2},{4,5},{5,4},{6,7},{7,6},{8,9},{9,8},{10,11... | collective-permute-start | bytes 6291464 | tf_op jit(solution)/shard_map/ppermute | solution.py:147
  0.5 5.4 %collective-permute-start.1 = (bf16[512,1024]{1,0:T(8,128)(2,1)}, bf16[512,1024]{1,0:T(8,128)(2,1)S(1)}, u32[]{:S(2)}, u32[]{:S(2)}) collective-permute-start(bf16[512,1024]{1,0:T(8,128)(2,1)} %refs_3_.1), channel_id=1, source_target_pairs={{0,1},{1,0},{2,3},{3,2},{4,5},{5,4},{6,7},{7,6},{8,9},{9,8},{10,11... | collective-permute-start | bytes 3145736 | tf_op jit(solution)/shard_map/ppermute | solution.py:147
  1.3 4.6 %copy-start.23 = (s32[3,512]{1,0:T(4,128)}, s32[3,512]{1,0:T(4,128)S(1)}, u32[]{:S(2)}) copy-start(s32[3,512]{1,0:T(4,128)S(1)} %pad_add_fusion.refs_0_) | copy-start | bytes 18436
  1.3 3.7 %collective-permute-start = (s32[3,512]{1,0:T(4,128)S(1)}, s32[3,512]{1,0:T(4,128)S(1)}, u32[]{:S(2)}, u32[]{:S(2)}) collective-permute-start(s32[3,512]{1,0:T(4,128)S(1)} %pad_add_fusion.refs_0_), channel_id=1, source_target_pairs={{0,1},{1,0},{2,3},{3,2},{4,5},{5,4},{6,7},{7,6},{8,9},{9,8},{10,11... | collective-permute-start | bytes 18440 | tf_op jit(solution)/shard_map/ppermute | solution.py:147
  5.0 0.9 copy-start.24
  5.9 1.0 copy-start.10
  10.6 7.8 %copy-start.9 = (bf16[1152,128]{1,0:T(8,128)(2,1)}, bf16[1152,128]{1,0:T(8,128)(2,1)S(1)}, u32[]{:S(2)}) copy-start(bf16[1152,128]{1,0:T(8,128)(2,1)S(1)} %get-tuple-element.30.refs_1_) | copy-start | bytes 884740
  10.6 11.2 %collective-permute-start.3 = (bf16[1152,128]{1,0:T(8,128)(2,1)S(1)}, bf16[1152,128]{1,0:T(8,128)(2,1)S(1)}, u32[]{:S(2)}, u32[]{:S(2)}) collective-permute-start(bf16[1152,128]{1,0:T(8,128)(2,1)S(1)} %get-tuple-element.31), channel_id=1, source_target_pairs={{0,2},{1,3},{2,0},{3,1},{4,6},{5,7},{6,4},{7,5},{8,10},{9,11},{10,... | collective-permute-start | bytes 884744 | tf_op jit(solution)/shard_map/ppermute | solution.py:147
  13.2 15.5 %collective-permute-start.4 = (bf16[1152,128]{1,0:T(8,128)(2,1)S(1)}, bf16[1152,128]{1,0:T(8,128)(2,1)S(1)}, u32[]{:S(2)}, u32[]{:S(2)}) collective-permute-start(bf16[1152,128]{1,0:T(8,128)(2,1)S(1)} %get-tuple-element.32), channel_id=1, source_target_pairs={{0,4},{1,5},{2,6},{3,7},{4,0},{5,1},{6,2},{7,3},{8,12},{9,13},{10,... | collective-permute-start | bytes 884744 | tf_op jit(solution)/shard_map/ppermute | solution.py:147
  14.7 14.1 %collective-permute-start.5 = (bf16[1152,128]{1,0:T(8,128)(2,1)S(1)}, bf16[1152,128]{1,0:T(8,128)(2,1)S(1)}, u32[]{:S(2)}, u32[]{:S(2)}) collective-permute-start(bf16[1152,128]{1,0:T(8,128)(2,1)S(1)} %get-tuple-element.33), channel_id=1, source_target_pairs={{0,6},{1,7},{2,4},{3,5},{4,2},{5,3},{6,0},{7,1},{8,14},{9,15},{10,... | collective-permute-start | bytes 884744 | tf_op jit(solution)/shard_map/ppermute | solution.py:147
  14.8 5.5 %copy-start.25 = (s32[2]{0:T(128)S(1)}, s32[2]{0:T(128)}, u32[]{:S(2)}) copy-start(s32[2]{0:T(128)} %constant.38.clone) | copy-start | bytes 28
  18.3 21.4 %copy-start.7 = (bf16[1024,128]{1,0:T(8,128)(2,1)}, bf16[1024,128]{1,0:T(8,128)(2,1)S(1)}, u32[]{:S(2)}) copy-start(bf16[1024,128]{1,0:T(8,128)(2,1)S(1)} %get-tuple-element.29.refs_0_.refs_1_) | copy-start | bytes 786436
  18.3 17.8 %collective-permute-start.6 = (bf16[1024,128]{1,0:T(8,128)(2,1)}, bf16[1024,128]{1,0:T(8,128)(2,1)}, u32[]{:S(2)}, u32[]{:S(2)}) collective-permute-start(bf16[1024,128]{1,0:T(8,128)(2,1)} %get-tuple-element.35), channel_id=1, source_target_pairs={{0,2},{1,3},{2,0},{3,1},{4,6},{5,7},{6,4},{7,5},{8,10},{9,11},{10,... | collective-permute-start | bytes 786440 | tf_op jit(solution)/shard_map/ppermute | solution.py:147
  20.3 23.2 %collective-permute-start.7 = (bf16[1024,128]{1,0:T(8,128)(2,1)}, bf16[1024,128]{1,0:T(8,128)(2,1)S(1)}, u32[]{:S(2)}, u32[]{:S(2)}) collective-permute-start(bf16[1024,128]{1,0:T(8,128)(2,1)} %get-tuple-element.37), channel_id=1, source_target_pairs={{0,4},{1,5},{2,6},{3,7},{4,0},{5,1},{6,2},{7,3},{8,12},{9,13},{10,... | collective-permute-start | bytes 786440 | tf_op jit(solution)/shard_map/ppermute | solution.py:147
  21.8 7.1 %copy-start.11 = (bf16[1152,128]{1,0:T(8,128)(2,1)}, bf16[1152,128]{1,0:T(8,128)(2,1)S(1)}, u32[]{:S(2)}) copy-start(bf16[1152,128]{1,0:T(8,128)(2,1)S(1)} %collective-permute-done.3.refs_2_) | copy-start | bytes 884740
  21.8 25.4 %collective-permute-start.8 = (bf16[1024,128]{1,0:T(8,128)(2,1)}, bf16[1024,128]{1,0:T(8,128)(2,1)S(1)}, u32[]{:S(2)}, u32[]{:S(2)}) collective-permute-start(bf16[1024,128]{1,0:T(8,128)(2,1)} %get-tuple-element.38), channel_id=1, source_target_pairs={{0,6},{1,7},{2,4},{3,5},{4,2},{5,3},{6,0},{7,1},{8,14},{9,15},{10,... | collective-permute-start | bytes 786440 | tf_op jit(solution)/shard_map/ppermute | solution.py:147
  28.7 0.7 copy-start.12
  36.1 53.4 %copy-start.1 = (f32[16,8,32,128]{3,2,1,0:T(8,128)}, f32[16,8,32,128]{3,2,1,0:T(8,128)S(1)}, u32[]{:S(2)}) copy-start(f32[16,8,32,128]{3,2,1,0:T(8,128)S(1)} %get-tuple-element.49) | copy-start | bytes 6291460
  39.7 16.0 %copy-start.8 = (bf16[1024,128]{1,0:T(8,128)(2,1)}, bf16[1024,128]{1,0:T(8,128)(2,1)S(1)}, u32[]{:S(2)}) copy-start(bf16[1024,128]{1,0:T(8,128)(2,1)S(1)} %get-tuple-element.36.refs_0_.refs_1_) | copy-start | bytes 786436
  39.8 16.0 %collective-permute-start.14 = (bf16[1024,128]{1,0:T(8,128)(2,1)S(1)}, bf16[1024,128]{1,0:T(8,128)(2,1)S(1)}, u32[]{:S(2)}, u32[]{:S(2)}) collective-permute-start(bf16[1024,128]{1,0:T(8,128)(2,1)S(1)} %get-tuple-element.43), channel_id=1, source_target_pairs={{0,2},{1,3},{2,0},{3,1},{4,6},{5,7},{6,4},{7,5},{8,10},{9,11},{10,... | collective-permute-start | bytes 786440 | tf_op jit(solution)/shard_map/ppermute | solution.py:147
  41.3 14.4 %collective-permute-start.15 = (bf16[1024,128]{1,0:T(8,128)(2,1)S(1)}, bf16[1024,128]{1,0:T(8,128)(2,1)S(1)}, u32[]{:S(2)}, u32[]{:S(2)}) collective-permute-start(bf16[1024,128]{1,0:T(8,128)(2,1)S(1)} %get-tuple-element.44), channel_id=1, source_target_pairs={{0,4},{1,5},{2,6},{3,7},{4,0},{5,1},{6,2},{7,3},{8,12},{9,13},{10,... | collective-permute-start | bytes 786440 | tf_op jit(solution)/shard_map/ppermute | solution.py:147
  42.1 13.7 %collective-permute-start.16 = (bf16[1024,128]{1,0:T(8,128)(2,1)S(1)}, bf16[1024,128]{1,0:T(8,128)(2,1)S(1)}, u32[]{:S(2)}, u32[]{:S(2)}) collective-permute-start(bf16[1024,128]{1,0:T(8,128)(2,1)S(1)} %get-tuple-element.45), channel_id=1, source_target_pairs={{0,6},{1,7},{2,4},{3,5},{4,2},{5,3},{6,0},{7,1},{8,14},{9,15},{10,... | collective-permute-start | bytes 786440 | tf_op jit(solution)/shard_map/ppermute | solution.py:147
  43.5 3.7 %copy-start.18 = (bf16[1024,128]{1,0:T(8,128)(2,1)}, bf16[1024,128]{1,0:T(8,128)(2,1)S(1)}, u32[]{:S(2)}) copy-start(bf16[1024,128]{1,0:T(8,128)(2,1)S(1)} %collective-permute-done.7.refs_3_) | copy-start | bytes 786436
  43.5 25.0 %collective-permute-start.24 = (s16[1,1040,128]{2,1,0:T(8,128)(2,1)S(1)}, s16[1,1040,128]{2,1,0:T(8,128)(2,1)S(1)}, u32[]{:S(2)}, u32[]{:S(2)}) collective-permute-start(s16[1,1040,128]{2,1,0:T(8,128)(2,1)S(1)} %get-tuple-element.34.refs_2_), channel_id=1, source_target_pairs={{0,8},{24,16},{1,9},{25,17},{2,10},{26,18},{3,11},{27,19},{4,12},{... | collective-permute-start | bytes 798728 | tf_op jit(solution)/shard_map/ppermute | solution.py:308
  54.4 21.1 %copy-start.2 = (f32[16,8,32,128]{3,2,1,0:T(8,128)}, f32[16,8,32,128]{3,2,1,0:T(8,128)S(1)}, u32[]{:S(2)}) copy-start(f32[16,8,32,128]{3,2,1,0:T(8,128)S(1)} %get-tuple-element.40) | copy-start | bytes 6291460
  54.4 16.9 %collective-permute-start.11 = (s16[1,1040,128]{2,1,0:T(8,128)(2,1)S(1)}, s16[1,1040,128]{2,1,0:T(8,128)(2,1)S(1)}, u32[]{:S(2)}, u32[]{:S(2)}) collective-permute-start(s16[1,1040,128]{2,1,0:T(8,128)(2,1)S(1)} %get-tuple-element.42.refs_0_), channel_id=1, source_target_pairs={{0,8},{24,16},{1,9},{25,17},{2,10},{26,18},{3,11},{27,19},{4,12},{... | collective-permute-start | bytes 798728 | tf_op jit(solution)/shard_map/ppermute | solution.py:308
  55.8 0.8 copy-start.21
  64.2 11.9 %copy-start.5 = (f32[16,8,32,128]{3,2,1,0:T(8,128)}, f32[16,8,32,128]{3,2,1,0:T(8,128)S(1)}, u32[]{:S(2)}) copy-start(f32[16,8,32,128]{3,2,1,0:T(8,128)S(1)} %get-tuple-element.46) | copy-start | bytes 6291460
  64.3 11.2 %collective-permute-start.19 = (s16[1,1040,128]{2,1,0:T(8,128)(2,1)S(1)}, s16[1,1040,128]{2,1,0:T(8,128)(2,1)S(1)}, u32[]{:S(2)}, u32[]{:S(2)}) collective-permute-start(s16[1,1040,128]{2,1,0:T(8,128)(2,1)S(1)} %get-tuple-element.48), channel_id=1, source_target_pairs={{0,8},{24,16},{1,9},{25,17},{2,10},{26,18},{3,11},{27,19},{4,12},{... | collective-permute-start | bytes 798728 | tf_op jit(solution)/shard_map/ppermute | solution.py:308
  65.8 12.5 %collective-permute-start.22 = (s16[1,1040,128]{2,1,0:T(8,128)(2,1)S(1)}, s16[1,1040,128]{2,1,0:T(8,128)(2,1)S(1)}, u32[]{:S(2)}, u32[]{:S(2)}) collective-permute-start(s16[1,1040,128]{2,1,0:T(8,128)(2,1)S(1)} %get-tuple-element.50), channel_id=1, source_target_pairs={{0,8},{24,16},{1,9},{25,17},{2,10},{26,18},{3,11},{27,19},{4,12},{... | collective-permute-start | bytes 798728 | tf_op jit(solution)/shard_map/ppermute | solution.py:308
  67.1 16.5 %collective-permute-start.9 = (s16[1,1040,128]{2,1,0:T(8,128)(2,1)S(1)}, s16[1,1040,128]{2,1,0:T(8,128)(2,1)S(1)}, u32[]{:S(2)}, u32[]{:S(2)}) collective-permute-start(s16[1,1040,128]{2,1,0:T(8,128)(2,1)S(1)} %get-tuple-element.41), channel_id=1, source_target_pairs={{0,8},{24,16},{1,9},{25,17},{2,10},{26,18},{3,11},{27,19},{4,12},{... | collective-permute-start | bytes 798728 | tf_op jit(solution)/shard_map/ppermute | solution.py:308
  69.9 18.1 %collective-permute-start.25 = (s16[1,1040,128]{2,1,0:T(8,128)(2,1)}, s16[1,1040,128]{2,1,0:T(8,128)(2,1)}, u32[]{:S(2)}, u32[]{:S(2)}) collective-permute-start(s16[1,1040,128]{2,1,0:T(8,128)(2,1)} %hop.16), channel_id=1, source_target_pairs={{8,16},{16,8},{9,17},{17,9},{10,18},{18,10},{11,19},{19,11},{12,20... | collective-permute-start | bytes 798728 | tf_op jit(solution)/shard_map/ppermute | solution.py:308
  71.3 20.0 %collective-permute-start.17 = (s16[1,1040,128]{2,1,0:T(8,128)(2,1)}, s16[1,1040,128]{2,1,0:T(8,128)(2,1)S(1)}, u32[]{:S(2)}, u32[]{:S(2)}) collective-permute-start(s16[1,1040,128]{2,1,0:T(8,128)(2,1)} %get-tuple-element.47), channel_id=1, source_target_pairs={{0,8},{24,16},{1,9},{25,17},{2,10},{26,18},{3,11},{27,19},{4,12},{... | collective-permute-start | bytes 798728 | tf_op jit(solution)/shard_map/ppermute | solution.py:308
  75.5 22.3 %collective-permute-start.12 = (s16[1,1040,128]{2,1,0:T(8,128)(2,1)S(1)}, s16[1,1040,128]{2,1,0:T(8,128)(2,1)S(1)}, u32[]{:S(2)}, u32[]{:S(2)}) collective-permute-start(s16[1,1040,128]{2,1,0:T(8,128)(2,1)S(1)} %hop.10), channel_id=1, source_target_pairs={{8,16},{16,8},{9,17},{17,9},{10,18},{18,10},{11,19},{19,11},{12,20... | collective-permute-start | bytes 798728 | tf_op jit(solution)/shard_map/ppermute | solution.py:308
  78.3 20.9 %collective-permute-start.20 = (s16[1,1040,128]{2,1,0:T(8,128)(2,1)S(1)}, s16[1,1040,128]{2,1,0:T(8,128)(2,1)}, u32[]{:S(2)}, u32[]{:S(2)}) collective-permute-start(s16[1,1040,128]{2,1,0:T(8,128)(2,1)S(1)} %hop.13), channel_id=1, source_target_pairs={{8,16},{16,8},{9,17},{17,9},{10,18},{18,10},{11,19},{19,11},{12,20... | collective-permute-start | bytes 798728 | tf_op jit(solution)/shard_map/ppermute | solution.py:308
  83.6 20.3 %collective-permute-start.23 = (s16[1,1040,128]{2,1,0:T(8,128)(2,1)}, s16[1,1040,128]{2,1,0:T(8,128)(2,1)}, u32[]{:S(2)}, u32[]{:S(2)}) collective-permute-start(s16[1,1040,128]{2,1,0:T(8,128)(2,1)} %hop.15), channel_id=1, source_target_pairs={{8,16},{16,8},{9,17},{17,9},{10,18},{18,10},{11,19},{19,11},{12,20... | collective-permute-start | bytes 798728 | tf_op jit(solution)/shard_map/ppermute | solution.py:308
  85.0 1.6 %copy-start.3 = (f32[16,8,32,128]{3,2,1,0:T(8,128)S(1)}, f32[16,8,32,128]{3,2,1,0:T(8,128)}, u32[]{:S(2)}) copy-start(f32[16,8,32,128]{3,2,1,0:T(8,128)} %copy-done.2) | copy-start | bytes 6291460
  86.6 10.4 %copy-start.6 = (f32[16,8,32,128]{3,2,1,0:T(8,128)S(1)}, f32[16,8,32,128]{3,2,1,0:T(8,128)}, u32[]{:S(2)}) copy-start(f32[16,8,32,128]{3,2,1,0:T(8,128)} %copy-done.5) | copy-start | bytes 6291460
  88.1 10.4 %copy-start.4 = (f32[16,8,32,128]{3,2,1,0:T(8,128)S(1)}, f32[16,8,32,128]{3,2,1,0:T(8,128)}, u32[]{:S(2)}) copy-start(f32[16,8,32,128]{3,2,1,0:T(8,128)} %copy-done.2) | copy-start | bytes 6291460
  88.1 16.6 %collective-permute-start.10 = (s16[1,1040,128]{2,1,0:T(8,128)(2,1)}, s16[1,1040,128]{2,1,0:T(8,128)(2,1)}, u32[]{:S(2)}, u32[]{:S(2)}) collective-permute-start(s16[1,1040,128]{2,1,0:T(8,128)(2,1)} %hop.9), channel_id=1, source_target_pairs={{8,16},{16,8},{9,17},{17,9},{10,18},{18,10},{11,19},{19,11},{12,20... | collective-permute-start | bytes 798728 | tf_op jit(solution)/shard_map/ppermute | solution.py:308
  91.3 13.4 %collective-permute-start.26 = (s16[1,1040,128]{2,1,0:T(8,128)(2,1)S(1)}, s16[1,1040,128]{2,1,0:T(8,128)(2,1)S(1)}, u32[]{:S(2)}, u32[]{:S(2)}) collective-permute-start(s16[1,1040,128]{2,1,0:T(8,128)(2,1)S(1)} %hop.17), channel_id=1, source_target_pairs={{8,0},{0,8},{16,24},{24,16},{9,1},{1,9},{17,25},{25,17},{10,2},{2,... | collective-permute-start | bytes 798728 | tf_op jit(solution)/shard_map/ppermute | solution.py:308
  97.8 6.9 %collective-permute-start.18 = (s16[1,1040,128]{2,1,0:T(8,128)(2,1)S(1)}, s16[1,1040,128]{2,1,0:T(8,128)(2,1)S(1)}, u32[]{:S(2)}, u32[]{:S(2)}) collective-permute-start(s16[1,1040,128]{2,1,0:T(8,128)(2,1)S(1)} %hop.12), channel_id=1, source_target_pairs={{8,16},{16,8},{9,17},{17,9},{10,18},{18,10},{11,19},{19,11},{12,20... | collective-permute-start | bytes 798728 | tf_op jit(solution)/shard_map/ppermute | solution.py:308
  99.3 8.4 %collective-permute-start.13 = (s16[1,1040,128]{2,1,0:T(8,128)(2,1)S(1)}, s16[1,1040,128]{2,1,0:T(8,128)(2,1)S(1)}, u32[]{:S(2)}, u32[]{:S(2)}) collective-permute-start(s16[1,1040,128]{2,1,0:T(8,128)(2,1)S(1)} %hop.11), channel_id=1, source_target_pairs={{8,0},{0,8},{16,24},{24,16},{9,1},{1,9},{17,25},{25,17},{10,2},{2,... | collective-permute-start | bytes 798728 | tf_op jit(solution)/shard_map/ppermute | solution.py:308
  103.9 6.6 %collective-permute-start.21 = (s16[1,1040,128]{2,1,0:T(8,128)(2,1)S(1)}, s16[1,1040,128]{2,1,0:T(8,128)(2,1)S(1)}, u32[]{:S(2)}, u32[]{:S(2)}) collective-permute-start(s16[1,1040,128]{2,1,0:T(8,128)(2,1)S(1)} %hop.14), channel_id=1, source_target_pairs={{8,0},{0,8},{16,24},{24,16},{9,1},{1,9},{17,25},{25,17},{10,2},{2,... | collective-permute-start | bytes 798728 | tf_op jit(solution)/shard_map/ppermute | solution.py:308
  104.6 5.9 %copy-start.14 = (s16[1,1040,128]{2,1,0:T(8,128)(2,1)}, s16[1,1040,128]{2,1,0:T(8,128)(2,1)S(1)}, u32[]{:S(2)}) copy-start(s16[1,1040,128]{2,1,0:T(8,128)(2,1)S(1)} %collective-permute-done.26.refs_8_) | copy-start | bytes 798724
  104.7 5.8 %copy-start.15 = (s16[1,1040,128]{2,1,0:T(8,128)(2,1)}, s16[1,1040,128]{2,1,0:T(8,128)(2,1)S(1)}, u32[]{:S(2)}) copy-start(s16[1,1040,128]{2,1,0:T(8,128)(2,1)S(1)} %collective-permute-done.18.refs_4_) | copy-start | bytes 798724
  107.6 2.9 %copy-start.16 = (s16[1,1040,128]{2,1,0:T(8,128)(2,1)}, s16[1,1040,128]{2,1,0:T(8,128)(2,1)S(1)}, u32[]{:S(2)}) copy-start(s16[1,1040,128]{2,1,0:T(8,128)(2,1)S(1)} %collective-permute-done.13.refs_2_) | copy-start | bytes 798724
  (5 other events, 3.6 us)

commit v4 on v3

--- a/solution.py
+++ b/solution.py
@@ -275,70 +275,69 @@
     return ((x * jnp.abs(x)).reshape(groups, 8, width) * scale).reshape(rows, width)
 
 
-def hop_kernel(places, idx_ref, sums_ref, prev_ref, out_ref):
+def hop_kernel(places, idx_ref, sums_ref, prev_ref, *refs):
+    out_ref = refs[-1]
     rows = sums_ref.shape[1]
     for i, place in enumerate(places):
         x = sums_ref[idx_ref[i]] + decode(prev_ref[place, :rows, :], prev_ref[place, rows:, :])
         out_ref[i, :rows, :], out_ref[i, rows:, :] = encode(x)
 
 
-def hop(index, sums, prev, places):
+def hop(index, sums, prev, places, ties):
     _, rows, width = sums.shape
     count = len(places)
     return pl.pallas_call(
         functools.partial(hop_kernel, places),
         out_shape=jax.ShapeDtypeStruct((count, rows + ALIGN, width), jnp.int16),
-        in_specs=[SCALARS, WHOLE, WHOLE],
+        in_specs=[SCALARS, WHOLE, WHOLE] + [UNREAD] * len(ties),
         out_specs=WHOLE,
         compiler_params=params(width),
         cost_estimate=cost(2.0 + count),
         name="hop",
-    )(index, sums, prev)
+    )(index, sums, prev, *ties)
 
 
 def portions(z, groups, r):
     return jnp.where(z >= groups // 2, groups - 1 - r, r).astype(jnp.int32)
 
 
-def along_z(sums, messages, payloads, z, groups, split):
-    half = groups // 2
-    depth = jnp.minimum(z, groups - 1 - z)
-
-    def send(payload, pairs):
-        return lax.ppermute(payload, "grp", pairs + [(groups - 1 - a, groups - 1 - b) for a, b in pairs])
-
-    def cut(rs):
-        return [[r] for r in rs] if split else [list(rs)]
-
-    def add(rs, got):
-        return hop(portions(z, groups, np.array(rs)), sums, got[rs[0]][0], [got[r][1] for r in rs])
-
-    def step(rs, got, pairs):
-        new = {}
-        for part in cut(rs):
-            payload = send(add(part, got), pairs)
-            new.update({r: (payload, i) for i, r in enumerate(part)})
-        return new
-
-    got = {}
-    for part, payload in zip(messages, payloads):
-        payload = send(payload, [(0, 1)])
-        got.update({r: (payload, i) for i, r in enumerate(part)})
-    inward = [None, got]
-    for k in range(2, half):
-        got = step(range(groups - 1, k, -1), got, [(k - 1, k)])
-        inward.append(got)
-    got = step(range(groups - 1, half - 1, -1), got, [(half - 1, half)])
-    got = {groups - 1 - r: x for r, x in got.items()}
-    ends = [got[half - 1]]
-    for j in range(half - 1, 1, -1):
-        ends.append((send(add([j], inward[j - 1]), [(j - 1, j)]), 0))
-        got = step(range(j), got, [(j, j - 1)])
-        ends.append(got[j - 1])
-    last = jnp.where(depth == 0, 1, 0).reshape(1)
-    payload = hop(portions(z, groups, last), sums, got[0][0], [got[0][1]])
-    ends.append((send(payload, [(1, 0), (0, 1)]), 0))
-    return ends
+class AlongZ:
+    def __init__(self, sums, first, payloads, z, groups):
+        self.sums, self.z, self.groups, self.ends = sums, z, groups, []
+        half = groups // 2
+        got = [{r: self.send(x, [(0, 1)]) for r, x in zip(first, payloads)}]
+        hops = []
+        for k in range(2, half):
+            got.append({})
+            for r in range(groups - 1, k, -1):
+                hops.append(functools.partial(self.move, got[k - 2], r, got[k - 1], r, [(k - 1, k)]))
+        across = {}
+        for r in range(groups - 1, half - 1, -1):
+            hops.append(functools.partial(self.move, got[half - 2], r, across, groups - 1 - r, [(half - 1, half)]))
+        outward = across
+        for j in range(half - 1, 1, -1):
+            kept, new = {}, {}
+            hops.append(functools.partial(self.move, got[j - 2], j, kept, j, [(j - 1, j)], True))
+            for r in range(j):
+                hops.append(functools.partial(self.move, outward, r, new, r, [(j, j - 1)], r == j - 1))
+            outward = new
+        hops.append(functools.partial(self.move, outward, 0, {}, 0, [(1, 0), (0, 1)], True, True))
+        self.hops, self.keep = hops, half - 1
+
+    def send(self, payload, pairs):
+        last = self.groups - 1
+        return lax.ppermute(payload, "grp", pairs + [(last - a, last - b) for a, b in pairs])
+
+    def move(self, source, r, target, place, pairs, final=False, both=False, ties=()):
+        last = self.groups - 1
+        wanted = jnp.full((1,), r, jnp.int32)
+        if both:
+            wanted = jnp.where(jnp.minimum(self.z, last - self.z) == 0, 1, 0).astype(jnp.int32).reshape(1)
+        payload = hop(portions(self.z, self.groups, wanted), self.sums, source[r], [0], ties)
+        target[place] = self.send(payload, pairs)
+        if final or (len(pairs) == 1 and pairs[0] == (self.keep, self.keep + 1) and place == self.keep):
+            self.ends.append((target[place], 0))
+        return payload
 
 
 def image_kernel(parts, zs, own_ref, *refs):
@@ -418,19 +417,26 @@
     first = list(range(groups - 1, 1, -1))
     index = portions(z, groups, np.array(first))
 
-    def volume(piece, meta, ties, split):
-        messages = [[r] for r in first] if split else [first]
-        sums, payloads, meta = volume_sums(window, index, [len(x) for x in messages], groups, piece, meta, ties)
-        return (sums, messages, payloads, z, groups, split), payloads[0], meta
+    def volume(piece, meta, ties):
+        sums, payloads, meta = volume_sums(window, index, [1] * len(first), groups, piece, meta, ties)
+        return AlongZ(sums, first, payloads, z, groups), payloads[0], meta
 
     real = sort_columns(slabs, me, order, spectra, 0, ())
     ctf, real_there = exchange(ctf), exchange(real)
-    ctf_part, ctf_code, meta = volume(ctf, None, (real[0],), True)
-    imag = sort_columns(slabs, me, order, spectra, 1, (ctf_code, real_there[1]))
+    ctf_part, coded, meta = volume(ctf, None, (real[0],))
+    imag = sort_columns(slabs, me, order, spectra, 1, (real[0],))
     imag_there = exchange(imag)
-    real_part, real_code, _ = volume(real_there, meta, (imag[0],), True)
-    imag_part, imag_code, _ = volume(imag_there, meta, (real_code,), True)
-    fields = [(part[0], along_z(*part)) for part in (ctf_part, real_part, imag_part)]
+    real_part, coded, _ = volume(real_there, meta, (imag[0],))
+    tie = coded
+    early = len(ctf_part.hops) - 1
+    for step in ctf_part.hops[:early]:
+        tie = step(ties=(tie,))
+    imag_part, coded, _ = volume(imag_there, meta, (tie,))
+    steps = real_part.hops[:-1] + ctf_part.hops[early:] + imag_part.hops[:1] + real_part.hops[-1:] + imag_part.hops[1:]
+    tie = coded
+    for step in steps:
+        tie = step(ties=(tie,))
+    fields = [(part.sums, part.ends) for part in (ctf_part, real_part, imag_part)]
     tau_here = lax.dynamic_slice_in_dim(tau, slab * width, width, 0)
     own = z.astype(jnp.int32).reshape(1)
     return image_of(own, [fields[1], fields[2], fields[0]], tau_here, KZ_DEV * slabs)

time: 117 us -> 115 us (0.983)
  waiting for transfers between devices: 18.6 us -> 14.3 us
  local copies, waits for them, and re-layouts: 6.85 us -> 9.47 us
  starting transfers between devices: 42.7 us -> 45.3 us
  Pallas kernels: 46.6 us -> 44.5 us
    ppermute x15, waiting for transfers between devices: 9.64 us -> 5.88 us  [send(): lax.ppermute(payload, 'grp', pairs + [(last - a, last - b) for a, b in pa...]
    unnamed x52 -> x50, local copies, waits for them, and re-layouts: 6.21 us -> 8.84 us
    ppermute x15, starting transfers between devices: 28.1 us -> 30.7 us  [send(): lax.ppermute(payload, 'grp', pairs + [(last - a, last - b) for a, b in pa...]
    pallas_call x9, Pallas kernels: 11 us -> 9.16 us  [hop(): pl.pallas_call(functools.partial(hop_kernel, places), out_shape=jax.Shape...]
  transfers between devices with their start and end apart: 27 -> 27, of which waited for: 8 -> 6; matrix products, arithmetic and copies ran while one was open for 1% -> 1% of each run, Pallas kernels for 36% -> 35%
where the time goes in v4:
time: 115 us
  starting transfers between devices  45.3 us (39%)
  Pallas kernels  44.5 us (39%)
  waiting for transfers between devices  14.3 us (12%)
  local copies, waits for them, and re-layouts  9.47 us (8%)
    ppermute x15, starting transfers between devices, send(): lax.ppermute(payload, 'grp', pairs + [(last - a, last - b) for a, b in pa...  30.7 us
    pallas_call x3, Pallas kernels, volume_sums(): pl.pallas_call(functools.partial(volume_kernel, slabs, window, messages,...  20.5 us
    ppermute x12, starting transfers between devices, swap(): return lax.ppermute(x, 'slab', [(i, i ^ offset) for i in range(slabs)])  14.5 us
    pallas_call x9, Pallas kernels, hop(): pl.pallas_call(functools.partial(hop_kernel, places), out_shape=jax.Shape...  9.16 us
    unnamed x50, local copies, waits for them, and re-layouts  8.84 us
    ppermute x12, waiting for transfers between devices, swap(): return lax.ppermute(x, 'slab', [(i, i ^ offset) for i in range(slabs)])  8.39 us
    pallas_call x2, Pallas kernels, sort_columns(): pl.pallas_call(functools.partial(sort_kernel, slabs, width, part, len(tie...  6.37 us
    ppermute x15, waiting for transfers between devices, send(): lax.ppermute(payload, 'grp', pairs + [(last - a, last - b) for a, b in pa...  5.88 us
  transfers between devices with their start and end apart: 27, of which 6 were waited for; matrix products, arithmetic and copies ran while one was open for 1% of the time, Pallas kernels for 35%

profile of v4, /device:TPU:0, one launch (start us, length us, event | category | flops | bytes accessed | tf_op | source)
XLA Modules:
  0.0 114.7 jit_solution(6138130927652530642)
XLA Ops:
  0.5 0.7 pad_add_fusion.refs_0_
  1.8 3.2 %collective-permute-done.refs_1_ = s32[3,512]{1,0:T(4,128)S(1)} collective-permute-done((s32[3,512]{1,0:T(4,128)S(1)}, s32[3,512]{1,0:T(4,128)S(1)}, u32[]{:S(2)}, u32[]{:S(2)}) %collective-permute-start) | collective-permute-done | bytes 6176 | tf_op jit(solution)/shard_map/ppermute | solution.py:147
  5.0 0.9 collective-permute-done.1.refs_4_
  5.9 1.0 copy-done.11
  6.9 3.7 %plan_rows.1 = (bf16[2,512,512]{2,1,0:T(8,128)(2,1)S(1)}, bf16[1152,128]{1,0:T(8,128)(2,1)S(1)}, bf16[1152,128]{1,0:T(8,128)(2,1)S(1)}, bf16[1152,128]{1,0:T(8,128)(2,1)S(1)}, bf16[1152,128]{1,0:T(8,128)(2,1)S(1)}) custom-call(s32[1]{0:T(128)} %bitcast.1.me_ref, s32[3,512]{1,0:T(4,128)} %copy-done.22, s32[3,512]{1,0:T(4,128)} %copy-done.23, ...), custom_call_target="tpu_custom_call" | custom-call | bytes 18000000 | tf_op jit(solution)/shard_map/plan_rows/pallas_call | solution.py:101
  10.6 2.7 %collective-permute-start.6 = (bf16[1152,128]{1,0:T(8,128)(2,1)S(1)}, bf16[1152,128]{1,0:T(8,128)(2,1)S(1)}, u32[]{:S(2)}, u32[]{:S(2)}) collective-permute-start(bf16[1152,128]{1,0:T(8,128)(2,1)S(1)} %get-tuple-element.35), channel_id=1, source_target_pairs={{0,2},{1,3},{2,0},{3,1},{4,6},{5,7},{6,4},{7,5},{8,10},{9,11},{10,... | collective-permute-start | bytes 884744 | tf_op jit(solution)/shard_map/ppermute | solution.py:147
  13.2 1.5 %collective-permute-start.7 = (bf16[1152,128]{1,0:T(8,128)(2,1)S(1)}, bf16[1152,128]{1,0:T(8,128)(2,1)}, u32[]{:S(2)}, u32[]{:S(2)}) collective-permute-start(bf16[1152,128]{1,0:T(8,128)(2,1)S(1)} %get-tuple-element.36), channel_id=1, source_target_pairs={{0,4},{1,5},{2,6},{3,7},{4,0},{5,1},{6,2},{7,3},{8,12},{9,13},{10,... | collective-permute-start | bytes 884744 | tf_op jit(solution)/shard_map/ppermute | solution.py:147
  14.8 3.5 %sort_columns.2 = (bf16[1024,128]{1,0:T(8,128)(2,1)S(1)}, bf16[1024,128]{1,0:T(8,128)(2,1)}, bf16[1024,128]{1,0:T(8,128)(2,1)}, bf16[1024,128]{1,0:T(8,128)(2,1)}) custom-call(s32[1]{0:T(128)} %bitcast.1.me_ref, bf16[2,512,512]{2,1,0:T(8,128)(2,1)S(1)} %get-tuple-element.28.order_ref, bf16[512,2048]{1,0:T(8,128)(2,1)} %refs_0_.3, ...), custom_call_target="tpu_custom_call" | custom-call | bytes 9000000 | tf_op jit(solution)/shard_map/sort_columns/pallas_call | solution.py:131
  18.3 1.9 %collective-permute-start.3 = (bf16[1024,128]{1,0:T(8,128)(2,1)}, bf16[1024,128]{1,0:T(8,128)(2,1)}, u32[]{:S(2)}, u32[]{:S(2)}) collective-permute-start(bf16[1024,128]{1,0:T(8,128)(2,1)} %get-tuple-element.31), channel_id=1, source_target_pairs={{0,2},{1,3},{2,0},{3,1},{4,6},{5,7},{6,4},{7,5},{8,10},{9,11},{10,... | collective-permute-start | bytes 786440 | tf_op jit(solution)/shard_map/ppermute | solution.py:147
  20.2 1.5 %collective-permute-start.4 = (bf16[1024,128]{1,0:T(8,128)(2,1)}, bf16[1024,128]{1,0:T(8,128)(2,1)}, u32[]{:S(2)}, u32[]{:S(2)}) collective-permute-start(bf16[1024,128]{1,0:T(8,128)(2,1)} %get-tuple-element.32), channel_id=1, source_target_pairs={{0,4},{1,5},{2,6},{3,7},{4,0},{5,1},{6,2},{7,3},{8,12},{9,13},{10,... | collective-permute-start | bytes 786440 | tf_op jit(solution)/shard_map/ppermute | solution.py:147
  21.8 0.7 copy-done.12
  22.5 2.2 %collective-permute-start.5 = (bf16[1024,128]{1,0:T(8,128)(2,1)}, bf16[1024,128]{1,0:T(8,128)(2,1)}, u32[]{:S(2)}, u32[]{:S(2)}) collective-permute-start(bf16[1024,128]{1,0:T(8,128)(2,1)} %get-tuple-element.33), channel_id=1, source_target_pairs={{0,6},{1,7},{2,4},{3,5},{4,2},{5,3},{6,0},{7,1},{8,14},{9,15},{10,... | collective-permute-start | bytes 786440 | tf_op jit(solution)/shard_map/ppermute | solution.py:147
  24.7 4.1 %collective-permute-done.7.refs_3_ = bf16[1152,128]{1,0:T(8,128)(2,1)} collective-permute-done((bf16[1152,128]{1,0:T(8,128)(2,1)S(1)}, bf16[1152,128]{1,0:T(8,128)(2,1)}, u32[]{:S(2)}, u32[]{:S(2)}) %collective-permute-start.7) | collective-permute-done | bytes 294944 | tf_op jit(solution)/shard_map/ppermute | solution.py:147
  29.0 6.6 %volume_sums.3 = (f32[16,8,32,128]{3,2,1,0:T(8,128)S(1)}, bf16[8,16,512]{2,1,0:T(8,128)(2,1)S(1)}, s16[1,1040,128]{2,1,0:T(8,128)(2,1)S(1)}, s16[1,1040,128]{2,1,0:T(8,128)(2,1)S(1)}) custom-call(s32[2]{0:T(128)S(1)} %broadcast_select_fusion.idx_ref, bf16[1024,128]{1,0:T(8,128)(2,1)S(1)} %get-tuple-element.29.refs_2_.refs_0_.refs_1_, ...), custom_call_target="tpu_custom_call" | custom-call | bytes 21000000 | tf_op jit(solution)/shard_map/volume_sums/pallas_call | solution.py:224
  35.5 3.5 %collective-permute-start.12 = (s16[1,1040,128]{2,1,0:T(8,128)(2,1)S(1)}, s16[1,1040,128]{2,1,0:T(8,128)(2,1)S(1)}, u32[]{:S(2)}, u32[]{:S(2)}) collective-permute-start(s16[1,1040,128]{2,1,0:T(8,128)(2,1)S(1)} %get-tuple-element.44), channel_id=1, source_target_pairs={{0,8},{24,16},{1,9},{25,17},{2,10},{26,18},{3,11},{27,19},{4,12},{... | collective-permute-start | bytes 798728 | tf_op jit(solution)/shard_map/ppermute | solution.py:329
  39.1 1.5 %collective-permute-start.11 = (s16[1,1040,128]{2,1,0:T(8,128)(2,1)S(1)}, s16[1,1040,128]{2,1,0:T(8,128)(2,1)S(1)}, u32[]{:S(2)}, u32[]{:S(2)}) collective-permute-start(s16[1,1040,128]{2,1,0:T(8,128)(2,1)S(1)} %get-tuple-element.43), channel_id=1, source_target_pairs={{0,8},{24,16},{1,9},{25,17},{2,10},{26,18},{3,11},{27,19},{4,12},{... | collective-permute-start | bytes 798728 | tf_op jit(solution)/shard_map/ppermute | solution.py:329
  40.5 2.8 %sort_columns.3 = (bf16[1024,128]{1,0:T(8,128)(2,1)S(1)}, bf16[1024,128]{1,0:T(8,128)(2,1)S(1)}, bf16[1024,128]{1,0:T(8,128)(2,1)S(1)}, bf16[1024,128]{1,0:T(8,128)(2,1)S(1)}) custom-call(s32[1]{0:T(128)} %bitcast.1.me_ref, bf16[2,512,512]{2,1,0:T(8,128)(2,1)S(1)} %get-tuple-element.28.order_ref, bf16[512,2048]{1,0:T(8,128)(2,1)} %refs_0_.3, ...), custom_call_target="tpu_custom_call" | custom-call | bytes 9000000 | tf_op jit(solution)/shard_map/sort_columns/pallas_call | solution.py:131
  43.4 1.5 %collective-permute-start.13 = (bf16[1024,128]{1,0:T(8,128)(2,1)S(1)}, bf16[1024,128]{1,0:T(8,128)(2,1)S(1)}, u32[]{:S(2)}, u32[]{:S(2)}) collective-permute-start(bf16[1024,128]{1,0:T(8,128)(2,1)S(1)} %get-tuple-element.45), channel_id=1, source_target_pairs={{0,2},{1,3},{2,0},{3,1},{4,6},{5,7},{6,4},{7,5},{8,10},{9,11},{10,... | collective-permute-start | bytes 786440 | tf_op jit(solution)/shard_map/ppermute | solution.py:147
  45.6 1.4 %collective-permute-start.15 = (bf16[1024,128]{1,0:T(8,128)(2,1)S(1)}, bf16[1024,128]{1,0:T(8,128)(2,1)S(1)}, u32[]{:S(2)}, u32[]{:S(2)}) collective-permute-start(bf16[1024,128]{1,0:T(8,128)(2,1)S(1)} %get-tuple-element.47), channel_id=1, source_target_pairs={{0,6},{1,7},{2,4},{3,5},{4,2},{5,3},{6,0},{7,1},{8,14},{9,15},{10,... | collective-permute-start | bytes 786440 | tf_op jit(solution)/shard_map/ppermute | solution.py:147
  47.1 7.0 %volume_sums.4 = (f32[16,8,32,128]{3,2,1,0:T(8,128)S(1)}, s16[1,1040,128]{2,1,0:T(8,128)(2,1)S(1)}, s16[1,1040,128]{2,1,0:T(8,128)(2,1)}) custom-call(s32[2]{0:T(128)S(1)} %broadcast_select_fusion.idx_ref, bf16[1024,128]{1,0:T(8,128)(2,1)S(1)} %get-tuple-element.30.refs_0_.refs_1_, bf16[1024,128]{1,0:T(8,128)(2,1)} %copy-done.7, ...), custom_call_target="tpu_custom_call" | custom-call | bytes 21000000 | tf_op jit(solution)/shard_map/volume_sums/pallas_call | solution.py:224
  54.1 1.4 %copy-done.2 = f32[16,8,32,128]{3,2,1,0:T(8,128)} copy-done((f32[16,8,32,128]{3,2,1,0:T(8,128)}, f32[16,8,32,128]{3,2,1,0:T(8,128)S(1)}, u32[]{:S(2)}) %copy-start.2) | copy-done | bytes 2097176
  55.4 1.3 %collective-permute-start.10 = (s16[1,1040,128]{2,1,0:T(8,128)(2,1)S(1)}, s16[1,1040,128]{2,1,0:T(8,128)(2,1)S(1)}, u32[]{:S(2)}, u32[]{:S(2)}) collective-permute-start(s16[1,1040,128]{2,1,0:T(8,128)(2,1)S(1)} %get-tuple-element.41.refs_0_), channel_id=1, source_target_pairs={{0,8},{24,16},{1,9},{25,17},{2,10},{26,18},{3,11},{27,19},{4,12},{... | collective-permute-start | bytes 798728 | tf_op jit(solution)/shard_map/ppermute | solution.py:329
  56.7 0.8 hop.9.refs_0_
  57.5 1.3 %collective-permute-start.9 = (s16[1,1040,128]{2,1,0:T(8,128)(2,1)}, s16[1,1040,128]{2,1,0:T(8,128)(2,1)S(1)}, u32[]{:S(2)}, u32[]{:S(2)}) collective-permute-start(s16[1,1040,128]{2,1,0:T(8,128)(2,1)} %get-tuple-element.40), channel_id=1, source_target_pairs={{0,8},{24,16},{1,9},{25,17},{2,10},{26,18},{3,11},{27,19},{4,12},{... | collective-permute-start | bytes 798728 | tf_op jit(solution)/shard_map/ppermute | solution.py:329
  58.8 0.8 hop.10.refs_0_
  59.6 1.4 %collective-permute-start.19 = (s16[1,1040,128]{2,1,0:T(8,128)(2,1)S(1)}, s16[1,1040,128]{2,1,0:T(8,128)(2,1)}, u32[]{:S(2)}, u32[]{:S(2)}) collective-permute-start(s16[1,1040,128]{2,1,0:T(8,128)(2,1)S(1)} %hop.9.refs_0_), channel_id=1, source_target_pairs={{8,16},{16,8},{9,17},{17,9},{10,18},{18,10},{11,19},{19,11},{12,20... | collective-permute-start | bytes 798728 | tf_op jit(solution)/shard_map/ppermute | solution.py:329
  61.0 0.7 copy-done.20
  61.8 0.7 copy-done.21
  62.5 7.0 %volume_sums.5 = (f32[16,8,32,128]{3,2,1,0:T(8,128)S(1)}, s16[1,1040,128]{2,1,0:T(8,128)(2,1)}, s16[1,1040,128]{2,1,0:T(8,128)(2,1)S(1)}) custom-call(s32[2]{0:T(128)S(1)} %broadcast_select_fusion.idx_ref, s16[1,1040,128]{2,1,0:T(8,128)(2,1)S(1)} %hop.10.refs_0_, bf16[1024,128]{1,0:T(8,128)(2,1)} %copy-done.8, bf16[1024,128]{1,0:T(8,128)(2,1)} %copy-done.19, ...), custom_call_target="tpu_custom_call" | custom-call | bytes 21000000 | tf_op jit(solution)/shard_map/volume_sums/pallas_call | solution.py:224
  69.4 1.3 %copy-done.5 = f32[16,8,32,128]{3,2,1,0:T(8,128)} copy-done((f32[16,8,32,128]{3,2,1,0:T(8,128)}, f32[16,8,32,128]{3,2,1,0:T(8,128)S(1)}, u32[]{:S(2)}) %copy-start.5) | copy-done | bytes 2097176
  70.8 0.7 copy-done.10
  71.5 4.1 %collective-permute-start.18 = (s16[1,1040,128]{2,1,0:T(8,128)(2,1)}, s16[1,1040,128]{2,1,0:T(8,128)(2,1)}, u32[]{:S(2)}, u32[]{:S(2)}) collective-permute-start(s16[1,1040,128]{2,1,0:T(8,128)(2,1)} %get-tuple-element.48.refs_0_), channel_id=1, source_target_pairs={{0,8},{24,16},{1,9},{25,17},{2,10},{26,18},{3,11},{27,19},{4,12},{... | collective-permute-start | bytes 798728 | tf_op jit(solution)/shard_map/ppermute | solution.py:329
  75.6 1.5 %collective-permute-start.21 = (s16[1,1040,128]{2,1,0:T(8,128)(2,1)}, s16[1,1040,128]{2,1,0:T(8,128)(2,1)S(1)}, u32[]{:S(2)}, u32[]{:S(2)}) collective-permute-start(s16[1,1040,128]{2,1,0:T(8,128)(2,1)} %copy-done.10), channel_id=1, source_target_pairs={{0,8},{24,16},{1,9},{25,17},{2,10},{26,18},{3,11},{27,19},{4,12},{... | collective-permute-start | bytes 798728 | tf_op jit(solution)/shard_map/ppermute | solution.py:329
  77.1 1.6 %copy-done.3 = f32[16,8,32,128]{3,2,1,0:T(8,128)S(1)} copy-done((f32[16,8,32,128]{3,2,1,0:T(8,128)S(1)}, f32[16,8,32,128]{3,2,1,0:T(8,128)}, u32[]{:S(2)}) %copy-start.3) | copy-done | bytes 2097176
  78.7 0.8 hop.11.refs_0_
  79.5 0.7 collective-permute-start.17
  80.2 0.8 hop.12.refs_0_
  81.0 1.9 %hop.13.refs_0_ = s16[1,1040,128]{2,1,0:T(8,128)(2,1)S(1)} custom-call(s32[1]{0:T(128)S(6)} %select_n.51.idx_ref, f32[4,1024,128]{2,1,0:T(8,128)S(1)} %bitcast.15, s16[1,1040,128]{2,1,0:T(8,128)(2,1)} %collective-permute-done.19.prev_ref, s16[1,1040,128]{2,1,0:T(8,128)(2,1)S(1)} %hop.12.refs_0_), custom_call_target="tpu_custom_call" | custom-call | bytes 9000000 | tf_op jit(solution)/shard_map/hop/pallas_call | solution.py:289
  82.9 1.9 %hop.14.refs_0_ = s16[1,1040,128]{2,1,0:T(8,128)(2,1)S(1)} custom-call(s32[1]{0:T(128)S(6)} %select_n.49.idx_ref, f32[4,1024,128]{2,1,0:T(8,128)S(1)} %bitcast.22, s16[1,1040,128]{2,1,0:T(8,128)(2,1)} %collective-permute-done.18.prev_ref, s16[1,1040,128]{2,1,0:T(8,128)(2,1)S(1)} %hop.13.refs_0_), custom_call_target="tpu_custom_call" | custom-call | bytes 9000000 | tf_op jit(solution)/shard_map/hop/pallas_call | solution.py:289
  86.8 7.7 %collective-permute-start.26 = (s16[1,1040,128]{2,1,0:T(8,128)(2,1)S(1)}, s16[1,1040,128]{2,1,0:T(8,128)(2,1)S(1)}, u32[]{:S(2)}, u32[]{:S(2)}) collective-permute-start(s16[1,1040,128]{2,1,0:T(8,128)(2,1)S(1)} %hop.13.refs_0_), channel_id=1, source_target_pairs={{8,0},{0,8},{16,24},{24,16},{9,1},{1,9},{17,25},{25,17},{10,2},{2,... | collective-permute-start | bytes 798728 | tf_op jit(solution)/shard_map/ppermute | solution.py:329
  94.5 0.8 hop.15.refs_0_
  95.4 0.8 hop.16.refs_0_
  96.9 0.8 hop.17
  97.7 5.0 %collective-permute-start.24 = (s16[1,1040,128]{2,1,0:T(8,128)(2,1)S(1)}, s16[1,1040,128]{2,1,0:T(8,128)(2,1)S(1)}, u32[]{:S(2)}, u32[]{:S(2)}) collective-permute-start(s16[1,1040,128]{2,1,0:T(8,128)(2,1)S(1)} %hop.17), channel_id=1, source_target_pairs={{8,0},{0,8},{16,24},{24,16},{9,1},{1,9},{17,25},{25,17},{10,2},{2,... | collective-permute-start | bytes 798728 | tf_op jit(solution)/shard_map/ppermute | solution.py:329
  103.3 3.0 %collective-permute-done.20.refs_2_ = s16[1,1040,128]{2,1,0:T(8,128)(2,1)S(1)} collective-permute-done((s16[1,1040,128]{2,1,0:T(8,128)(2,1)S(1)}, s16[1,1040,128]{2,1,0:T(8,128)(2,1)S(1)}, u32[]{:S(2)}, u32[]{:S(2)}) %collective-permute-start.20) | collective-permute-done | bytes 266272 | tf_op jit(solution)/shard_map/ppermute | solution.py:329
  106.3 2.8 %collective-permute-done.24.refs_5_ = s16[1,1040,128]{2,1,0:T(8,128)(2,1)S(1)} collective-permute-done((s16[1,1040,128]{2,1,0:T(8,128)(2,1)S(1)}, s16[1,1040,128]{2,1,0:T(8,128)(2,1)S(1)}, u32[]{:S(2)}, u32[]{:S(2)}) %collective-permute-start.24) | collective-permute-done | bytes 266272 | tf_op jit(solution)/shard_map/ppermute | solution.py:329
  109.2 0.7 copy-done.18
  109.9 4.8 %image_of.1 = f32[2,4,256,128]{3,2,1,0:T(8,128)} custom-call(s32[1]{0:T(128)} %bitcast.own_ref, f32[4,1024,128]{2,1,0:T(8,128)} %bitcast.17, s16[1,1040,128]{2,1,0:T(8,128)(2,1)} %copy-done.14, s16[1,1040,128]{2,1,0:T(8,128)(2,1)} %copy-done.16, f32[4,1024,128]{2,1,0:T(8,128)} %bitcast.21, s16[1,1040,128]{2,1,0:T(8,128)(2,1)} %copy-done.17, ...), custom_call_target="tpu_custom_call" | custom-call | bytes 18000000 | tf_op jit(solution)/shard_map/image_of/pallas_call | solution.py:391
  (75 shorter events, 5.4 us)
Async XLA Ops:
  0.0 102.7 %copy-start = (f32[1024]{0:T(1024)S(1)}, f32[1024]{0:T(1024)}, u32[]{:S(2)}) copy-start(f32[1024]{0:T(1024)} %param.17) | copy-start | bytes 12292
  0.0 14.8 %collective-permute-start.2 = (bf16[512,2048]{1,0:T(8,128)(2,1)}, bf16[512,2048]{1,0:T(8,128)(2,1)}, u32[]{:S(2)}, u32[]{:S(2)}) collective-permute-start(bf16[512,2048]{1,0:T(8,128)(2,1)} %refs_0_.3), channel_id=1, source_target_pairs={{0,1},{1,0},{2,3},{3,2},{4,5},{5,4},{6,7},{7,6},{8,9},{9,8},{10,11... | collective-permute-start | bytes 6291464 | tf_op jit(solution)/shard_map/ppermute | solution.py:147
  0.5 5.4 %collective-permute-start.1 = (bf16[512,1024]{1,0:T(8,128)(2,1)}, bf16[512,1024]{1,0:T(8,128)(2,1)S(1)}, u32[]{:S(2)}, u32[]{:S(2)}) collective-permute-start(bf16[512,1024]{1,0:T(8,128)(2,1)} %refs_3_.1), channel_id=1, source_target_pairs={{0,1},{1,0},{2,3},{3,2},{4,5},{5,4},{6,7},{7,6},{8,9},{9,8},{10,11... | collective-permute-start | bytes 3145736 | tf_op jit(solution)/shard_map/ppermute | solution.py:147
  1.3 5.6 %copy-start.22 = (s32[3,512]{1,0:T(4,128)}, s32[3,512]{1,0:T(4,128)S(1)}, u32[]{:S(2)}) copy-start(s32[3,512]{1,0:T(4,128)S(1)} %pad_add_fusion.refs_0_) | copy-start | bytes 18436
  1.3 3.7 %collective-permute-start = (s32[3,512]{1,0:T(4,128)S(1)}, s32[3,512]{1,0:T(4,128)S(1)}, u32[]{:S(2)}, u32[]{:S(2)}) collective-permute-start(s32[3,512]{1,0:T(4,128)S(1)} %pad_add_fusion.refs_0_), channel_id=1, source_target_pairs={{0,1},{1,0},{2,3},{3,2},{4,5},{5,4},{6,7},{7,6},{8,9},{9,8},{10,11... | collective-permute-start | bytes 18440 | tf_op jit(solution)/shard_map/ppermute | solution.py:147
  5.0 1.9 %copy-start.23 = (s32[3,512]{1,0:T(4,128)}, s32[3,512]{1,0:T(4,128)S(1)}, u32[]{:S(2)}) copy-start(s32[3,512]{1,0:T(4,128)S(1)} %collective-permute-done.refs_1_) | copy-start | bytes 18436
  5.9 1.0 copy-start.11
  10.6 7.8 %copy-start.9 = (bf16[1152,128]{1,0:T(8,128)(2,1)}, bf16[1152,128]{1,0:T(8,128)(2,1)S(1)}, u32[]{:S(2)}) copy-start(bf16[1152,128]{1,0:T(8,128)(2,1)S(1)} %get-tuple-element.34.refs_1_) | copy-start | bytes 884740
  10.6 11.2 %collective-permute-start.6 = (bf16[1152,128]{1,0:T(8,128)(2,1)S(1)}, bf16[1152,128]{1,0:T(8,128)(2,1)S(1)}, u32[]{:S(2)}, u32[]{:S(2)}) collective-permute-start(bf16[1152,128]{1,0:T(8,128)(2,1)S(1)} %get-tuple-element.35), channel_id=1, source_target_pairs={{0,2},{1,3},{2,0},{3,1},{4,6},{5,7},{6,4},{7,5},{8,10},{9,11},{10,... | collective-permute-start | bytes 884744 | tf_op jit(solution)/shard_map/ppermute | solution.py:147
  13.2 15.6 %collective-permute-start.7 = (bf16[1152,128]{1,0:T(8,128)(2,1)S(1)}, bf16[1152,128]{1,0:T(8,128)(2,1)}, u32[]{:S(2)}, u32[]{:S(2)}) collective-permute-start(bf16[1152,128]{1,0:T(8,128)(2,1)S(1)} %get-tuple-element.36), channel_id=1, source_target_pairs={{0,4},{1,5},{2,6},{3,7},{4,0},{5,1},{6,2},{7,3},{8,12},{9,13},{10,... | collective-permute-start | bytes 884744 | tf_op jit(solution)/shard_map/ppermute | solution.py:147
  14.7 14.2 %collective-permute-start.8 = (bf16[1152,128]{1,0:T(8,128)(2,1)S(1)}, bf16[1152,128]{1,0:T(8,128)(2,1)}, u32[]{:S(2)}, u32[]{:S(2)}) collective-permute-start(bf16[1152,128]{1,0:T(8,128)(2,1)S(1)} %get-tuple-element.37), channel_id=1, source_target_pairs={{0,6},{1,7},{2,4},{3,5},{4,2},{5,3},{6,0},{7,1},{8,14},{9,15},{10,... | collective-permute-start | bytes 884744 | tf_op jit(solution)/shard_map/ppermute | solution.py:147
  14.8 10.0 %copy-start.24 = (s32[2]{0:T(128)S(1)}, s32[2]{0:T(128)}, u32[]{:S(2)}) copy-start(s32[2]{0:T(128)} %constant.36.clone) | copy-start | bytes 28
  18.3 25.1 %copy-start.7 = (bf16[1024,128]{1,0:T(8,128)(2,1)}, bf16[1024,128]{1,0:T(8,128)(2,1)S(1)}, u32[]{:S(2)}) copy-start(bf16[1024,128]{1,0:T(8,128)(2,1)S(1)} %get-tuple-element.29.refs_2_.refs_0_.refs_1_) | copy-start | bytes 786436
  18.3 25.1 %collective-permute-start.3 = (bf16[1024,128]{1,0:T(8,128)(2,1)}, bf16[1024,128]{1,0:T(8,128)(2,1)}, u32[]{:S(2)}, u32[]{:S(2)}) collective-permute-start(bf16[1024,128]{1,0:T(8,128)(2,1)} %get-tuple-element.31), channel_id=1, source_target_pairs={{0,2},{1,3},{2,0},{3,1},{4,6},{5,7},{6,4},{7,5},{8,10},{9,11},{10,... | collective-permute-start | bytes 786440 | tf_op jit(solution)/shard_map/ppermute | solution.py:147
  20.2 24.7 %collective-permute-start.4 = (bf16[1024,128]{1,0:T(8,128)(2,1)}, bf16[1024,128]{1,0:T(8,128)(2,1)}, u32[]{:S(2)}, u32[]{:S(2)}) collective-permute-start(bf16[1024,128]{1,0:T(8,128)(2,1)} %get-tuple-element.32), channel_id=1, source_target_pairs={{0,4},{1,5},{2,6},{3,7},{4,0},{5,1},{6,2},{7,3},{8,12},{9,13},{10,... | collective-permute-start | bytes 786440 | tf_op jit(solution)/shard_map/ppermute | solution.py:147
  22.5 23.1 %collective-permute-start.5 = (bf16[1024,128]{1,0:T(8,128)(2,1)}, bf16[1024,128]{1,0:T(8,128)(2,1)}, u32[]{:S(2)}, u32[]{:S(2)}) collective-permute-start(bf16[1024,128]{1,0:T(8,128)(2,1)} %get-tuple-element.33), channel_id=1, source_target_pairs={{0,6},{1,7},{2,4},{3,5},{4,2},{5,3},{6,0},{7,1},{8,14},{9,15},{10,... | collective-permute-start | bytes 786440 | tf_op jit(solution)/shard_map/ppermute | solution.py:147
  35.5 45.4 %copy-start.1 = (f32[16,8,32,128]{3,2,1,0:T(8,128)}, f32[16,8,32,128]{3,2,1,0:T(8,128)S(1)}, u32[]{:S(2)}) copy-start(f32[16,8,32,128]{3,2,1,0:T(8,128)S(1)} %get-tuple-element.42) | copy-start | bytes 6291460
  35.5 19.9 %collective-permute-start.12 = (s16[1,1040,128]{2,1,0:T(8,128)(2,1)S(1)}, s16[1,1040,128]{2,1,0:T(8,128)(2,1)S(1)}, u32[]{:S(2)}, u32[]{:S(2)}) collective-permute-start(s16[1,1040,128]{2,1,0:T(8,128)(2,1)S(1)} %get-tuple-element.44), channel_id=1, source_target_pairs={{0,8},{24,16},{1,9},{25,17},{2,10},{26,18},{3,11},{27,19},{4,12},{... | collective-permute-start | bytes 798728 | tf_op jit(solution)/shard_map/ppermute | solution.py:329
  39.1 18.5 %collective-permute-start.11 = (s16[1,1040,128]{2,1,0:T(8,128)(2,1)S(1)}, s16[1,1040,128]{2,1,0:T(8,128)(2,1)S(1)}, u32[]{:S(2)}, u32[]{:S(2)}) collective-permute-start(s16[1,1040,128]{2,1,0:T(8,128)(2,1)S(1)} %get-tuple-element.43), channel_id=1, source_target_pairs={{0,8},{24,16},{1,9},{25,17},{2,10},{26,18},{3,11},{27,19},{4,12},{... | collective-permute-start | bytes 798728 | tf_op jit(solution)/shard_map/ppermute | solution.py:329
  43.4 14.1 %copy-start.8 = (bf16[1024,128]{1,0:T(8,128)(2,1)}, bf16[1024,128]{1,0:T(8,128)(2,1)S(1)}, u32[]{:S(2)}) copy-start(bf16[1024,128]{1,0:T(8,128)(2,1)S(1)} %get-tuple-element.30.refs_0_.refs_1_) | copy-start | bytes 786436
  43.4 16.2 %collective-permute-start.13 = (bf16[1024,128]{1,0:T(8,128)(2,1)S(1)}, bf16[1024,128]{1,0:T(8,128)(2,1)S(1)}, u32[]{:S(2)}, u32[]{:S(2)}) collective-permute-start(bf16[1024,128]{1,0:T(8,128)(2,1)S(1)} %get-tuple-element.45), channel_id=1, source_target_pairs={{0,2},{1,3},{2,0},{3,1},{4,6},{5,7},{6,4},{7,5},{8,10},{9,11},{10,... | collective-permute-start | bytes 786440 | tf_op jit(solution)/shard_map/ppermute | solution.py:147
  45.0 16.1 %collective-permute-start.14 = (bf16[1024,128]{1,0:T(8,128)(2,1)S(1)}, bf16[1024,128]{1,0:T(8,128)(2,1)S(1)}, u32[]{:S(2)}, u32[]{:S(2)}) collective-permute-start(bf16[1024,128]{1,0:T(8,128)(2,1)S(1)} %get-tuple-element.46), channel_id=1, source_target_pairs={{0,4},{1,5},{2,6},{3,7},{4,0},{5,1},{6,2},{7,3},{8,12},{9,13},{10,... | collective-permute-start | bytes 786440 | tf_op jit(solution)/shard_map/ppermute | solution.py:147
  45.6 15.4 %collective-permute-start.15 = (bf16[1024,128]{1,0:T(8,128)(2,1)S(1)}, bf16[1024,128]{1,0:T(8,128)(2,1)S(1)}, u32[]{:S(2)}, u32[]{:S(2)}) collective-permute-start(bf16[1024,128]{1,0:T(8,128)(2,1)S(1)} %get-tuple-element.47), channel_id=1, source_target_pairs={{0,6},{1,7},{2,4},{3,5},{4,2},{5,3},{6,0},{7,1},{8,14},{9,15},{10,... | collective-permute-start | bytes 786440 | tf_op jit(solution)/shard_map/ppermute | solution.py:147
  54.1 1.4 %copy-start.2 = (f32[16,8,32,128]{3,2,1,0:T(8,128)}, f32[16,8,32,128]{3,2,1,0:T(8,128)S(1)}, u32[]{:S(2)}) copy-start(f32[16,8,32,128]{3,2,1,0:T(8,128)S(1)} %get-tuple-element.39) | copy-start | bytes 6291460
  55.4 21.7 %collective-permute-start.10 = (s16[1,1040,128]{2,1,0:T(8,128)(2,1)S(1)}, s16[1,1040,128]{2,1,0:T(8,128)(2,1)S(1)}, u32[]{:S(2)}, u32[]{:S(2)}) collective-permute-start(s16[1,1040,128]{2,1,0:T(8,128)(2,1)S(1)} %get-tuple-element.41.refs_0_), channel_id=1, source_target_pairs={{0,8},{24,16},{1,9},{25,17},{2,10},{26,18},{3,11},{27,19},{4,12},{... | collective-permute-start | bytes 798728 | tf_op jit(solution)/shard_map/ppermute | solution.py:329
  57.5 22.6 %collective-permute-start.9 = (s16[1,1040,128]{2,1,0:T(8,128)(2,1)}, s16[1,1040,128]{2,1,0:T(8,128)(2,1)S(1)}, u32[]{:S(2)}, u32[]{:S(2)}) collective-permute-start(s16[1,1040,128]{2,1,0:T(8,128)(2,1)} %get-tuple-element.40), channel_id=1, source_target_pairs={{0,8},{24,16},{1,9},{25,17},{2,10},{26,18},{3,11},{27,19},{4,12},{... | collective-permute-start | bytes 798728 | tf_op jit(solution)/shard_map/ppermute | solution.py:329
  59.6 1.4 %copy-start.19 = (bf16[1024,128]{1,0:T(8,128)(2,1)}, bf16[1024,128]{1,0:T(8,128)(2,1)S(1)}, u32[]{:S(2)}) copy-start(bf16[1024,128]{1,0:T(8,128)(2,1)S(1)} %collective-permute-done.13.refs_2_) | copy-start | bytes 786436
  59.6 21.3 %collective-permute-start.19 = (s16[1,1040,128]{2,1,0:T(8,128)(2,1)S(1)}, s16[1,1040,128]{2,1,0:T(8,128)(2,1)}, u32[]{:S(2)}, u32[]{:S(2)}) collective-permute-start(s16[1,1040,128]{2,1,0:T(8,128)(2,1)S(1)} %hop.9.refs_0_), channel_id=1, source_target_pairs={{8,16},{16,8},{9,17},{17,9},{10,18},{18,10},{11,19},{19,11},{12,20... | collective-permute-start | bytes 798728 | tf_op jit(solution)/shard_map/ppermute | solution.py:329
  61.0 0.7 copy-start.20
  69.4 1.4 %copy-start.5 = (f32[16,8,32,128]{3,2,1,0:T(8,128)}, f32[16,8,32,128]{3,2,1,0:T(8,128)S(1)}, u32[]{:S(2)}) copy-start(f32[16,8,32,128]{3,2,1,0:T(8,128)S(1)} %get-tuple-element.49) | copy-start | bytes 6291460
  71.5 11.4 %collective-permute-start.18 = (s16[1,1040,128]{2,1,0:T(8,128)(2,1)}, s16[1,1040,128]{2,1,0:T(8,128)(2,1)}, u32[]{:S(2)}, u32[]{:S(2)}) collective-permute-start(s16[1,1040,128]{2,1,0:T(8,128)(2,1)} %get-tuple-element.48.refs_0_), channel_id=1, source_target_pairs={{0,8},{24,16},{1,9},{25,17},{2,10},{26,18},{3,11},{27,19},{4,12},{... | collective-permute-start | bytes 798728 | tf_op jit(solution)/shard_map/ppermute | solution.py:329
  75.6 19.8 %collective-permute-start.21 = (s16[1,1040,128]{2,1,0:T(8,128)(2,1)}, s16[1,1040,128]{2,1,0:T(8,128)(2,1)S(1)}, u32[]{:S(2)}, u32[]{:S(2)}) collective-permute-start(s16[1,1040,128]{2,1,0:T(8,128)(2,1)} %copy-done.10), channel_id=1, source_target_pairs={{0,8},{24,16},{1,9},{25,17},{2,10},{26,18},{3,11},{27,19},{4,12},{... | collective-permute-start | bytes 798728 | tf_op jit(solution)/shard_map/ppermute | solution.py:329
  77.1 1.6 %copy-start.3 = (f32[16,8,32,128]{3,2,1,0:T(8,128)S(1)}, f32[16,8,32,128]{3,2,1,0:T(8,128)}, u32[]{:S(2)}) copy-start(f32[16,8,32,128]{3,2,1,0:T(8,128)} %copy-done.2) | copy-start | bytes 6291460
  79.5 7.3 %collective-permute-start.17 = (s16[1,1040,128]{2,1,0:T(8,128)(2,1)S(1)}, s16[1,1040,128]{2,1,0:T(8,128)(2,1)S(1)}, u32[]{:S(2)}, u32[]{:S(2)}) collective-permute-start(s16[1,1040,128]{2,1,0:T(8,128)(2,1)S(1)} %hop.11.refs_0_), channel_id=1, source_target_pairs={{8,16},{16,8},{9,17},{17,9},{10,18},{18,10},{11,19},{19,11},{12,20... | collective-permute-start | bytes 798728 | tf_op jit(solution)/shard_map/ppermute | solution.py:329
  80.9 1.9 %copy-start.6 = (f32[16,8,32,128]{3,2,1,0:T(8,128)S(1)}, f32[16,8,32,128]{3,2,1,0:T(8,128)}, u32[]{:S(2)}) copy-start(f32[16,8,32,128]{3,2,1,0:T(8,128)} %copy-done.5) | copy-start | bytes 6291460
  82.8 11.7 %copy-start.4 = (f32[16,8,32,128]{3,2,1,0:T(8,128)S(1)}, f32[16,8,32,128]{3,2,1,0:T(8,128)}, u32[]{:S(2)}) copy-start(f32[16,8,32,128]{3,2,1,0:T(8,128)} %copy-done.2) | copy-start | bytes 6291460
  84.7 11.4 %collective-permute-start.23 = (s16[1,1040,128]{2,1,0:T(8,128)(2,1)S(1)}, s16[1,1040,128]{2,1,0:T(8,128)(2,1)S(1)}, u32[]{:S(2)}, u32[]{:S(2)}) collective-permute-start(s16[1,1040,128]{2,1,0:T(8,128)(2,1)S(1)} %hop.14.refs_0_), channel_id=1, source_target_pairs={{8,16},{16,8},{9,17},{17,9},{10,18},{18,10},{11,19},{19,11},{12,20... | collective-permute-start | bytes 798728 | tf_op jit(solution)/shard_map/ppermute | solution.py:329
  85.4 12.2 %collective-permute-start.25 = (s16[1,1040,128]{2,1,0:T(8,128)(2,1)S(1)}, s16[1,1040,128]{2,1,0:T(8,128)(2,1)S(1)}, u32[]{:S(2)}, u32[]{:S(2)}) collective-permute-start(s16[1,1040,128]{2,1,0:T(8,128)(2,1)S(1)} %hop.10.refs_0_), channel_id=1, source_target_pairs={{8,16},{16,8},{9,17},{17,9},{10,18},{18,10},{11,19},{19,11},{12,20... | collective-permute-start | bytes 798728 | tf_op jit(solution)/shard_map/ppermute | solution.py:329
  86.1 17.2 %collective-permute-start.16 = (s16[1,1040,128]{2,1,0:T(8,128)(2,1)S(1)}, s16[1,1040,128]{2,1,0:T(8,128)(2,1)S(1)}, u32[]{:S(2)}, u32[]{:S(2)}) collective-permute-start(s16[1,1040,128]{2,1,0:T(8,128)(2,1)S(1)} %hop.12.refs_0_), channel_id=1, source_target_pairs={{8,16},{16,8},{9,17},{17,9},{10,18},{18,10},{11,19},{19,11},{12,20... | collective-permute-start | bytes 798728 | tf_op jit(solution)/shard_map/ppermute | solution.py:329
  86.8 16.5 %collective-permute-start.26 = (s16[1,1040,128]{2,1,0:T(8,128)(2,1)S(1)}, s16[1,1040,128]{2,1,0:T(8,128)(2,1)S(1)}, u32[]{:S(2)}, u32[]{:S(2)}) collective-permute-start(s16[1,1040,128]{2,1,0:T(8,128)(2,1)S(1)} %hop.13.refs_0_), channel_id=1, source_target_pairs={{8,0},{0,8},{16,24},{24,16},{9,1},{1,9},{17,25},{25,17},{10,2},{2,... | collective-permute-start | bytes 798728 | tf_op jit(solution)/shard_map/ppermute | solution.py:329
  95.3 11.0 %collective-permute-start.20 = (s16[1,1040,128]{2,1,0:T(8,128)(2,1)S(1)}, s16[1,1040,128]{2,1,0:T(8,128)(2,1)S(1)}, u32[]{:S(2)}, u32[]{:S(2)}) collective-permute-start(s16[1,1040,128]{2,1,0:T(8,128)(2,1)S(1)} %hop.15.refs_0_), channel_id=1, source_target_pairs={{8,0},{0,8},{16,24},{24,16},{9,1},{1,9},{17,25},{25,17},{10,2},{2,... | collective-permute-start | bytes 798728 | tf_op jit(solution)/shard_map/ppermute | solution.py:329
  96.2 10.1 %collective-permute-start.22 = (s16[1,1040,128]{2,1,0:T(8,128)(2,1)S(1)}, s16[1,1040,128]{2,1,0:T(8,128)(2,1)S(1)}, u32[]{:S(2)}, u32[]{:S(2)}) collective-permute-start(s16[1,1040,128]{2,1,0:T(8,128)(2,1)S(1)} %hop.16.refs_0_), channel_id=1, source_target_pairs={{8,16},{16,8},{9,17},{17,9},{10,18},{18,10},{11,19},{19,11},{12,20... | collective-permute-start | bytes 798728 | tf_op jit(solution)/shard_map/ppermute | solution.py:329
  97.7 11.5 %copy-start.13 = (s16[1,1040,128]{2,1,0:T(8,128)(2,1)}, s16[1,1040,128]{2,1,0:T(8,128)(2,1)S(1)}, u32[]{:S(2)}) copy-start(s16[1,1040,128]{2,1,0:T(8,128)(2,1)S(1)} %collective-permute-done.25.refs_7_) | copy-start | bytes 798724
  97.7 11.5 %collective-permute-start.24 = (s16[1,1040,128]{2,1,0:T(8,128)(2,1)S(1)}, s16[1,1040,128]{2,1,0:T(8,128)(2,1)S(1)}, u32[]{:S(2)}, u32[]{:S(2)}) collective-permute-start(s16[1,1040,128]{2,1,0:T(8,128)(2,1)S(1)} %hop.17), channel_id=1, source_target_pairs={{8,0},{0,8},{16,24},{24,16},{9,1},{1,9},{17,25},{25,17},{10,2},{2,... | collective-permute-start | bytes 798728 | tf_op jit(solution)/shard_map/ppermute | solution.py:329
  103.3 5.9 %copy-start.14 = (s16[1,1040,128]{2,1,0:T(8,128)(2,1)}, s16[1,1040,128]{2,1,0:T(8,128)(2,1)S(1)}, u32[]{:S(2)}) copy-start(s16[1,1040,128]{2,1,0:T(8,128)(2,1)S(1)} %collective-permute-done.16.refs_1_) | copy-start | bytes 798724
  103.3 5.9 %copy-start.15 = (s16[1,1040,128]{2,1,0:T(8,128)(2,1)}, s16[1,1040,128]{2,1,0:T(8,128)(2,1)S(1)}, u32[]{:S(2)}) copy-start(s16[1,1040,128]{2,1,0:T(8,128)(2,1)S(1)} %collective-permute-done.26.refs_8_) | copy-start | bytes 798724
  106.3 2.9 %copy-start.16 = (s16[1,1040,128]{2,1,0:T(8,128)(2,1)}, s16[1,1040,128]{2,1,0:T(8,128)(2,1)S(1)}, u32[]{:S(2)}) copy-start(s16[1,1040,128]{2,1,0:T(8,128)(2,1)S(1)} %collective-permute-done.20.refs_2_) | copy-start | bytes 798724
  106.3 2.9 %copy-start.17 = (s16[1,1040,128]{2,1,0:T(8,128)(2,1)}, s16[1,1040,128]{2,1,0:T(8,128)(2,1)S(1)}, u32[]{:S(2)}) copy-start(s16[1,1040,128]{2,1,0:T(8,128)(2,1)S(1)} %collective-permute-done.22.refs_4_) | copy-start | bytes 798724
  (4 other events, 2.8 us)

commit v5 on v4

--- a/solution.py
+++ b/solution.py
@@ -106,7 +106,7 @@
         compiler_params=params(width),
         cost_estimate=cost(6.0),
         name="plan_rows",
-    )(me, *[far(x) for x in ids], far(table.T), *[far(by_slab(x, slabs, width)) for x in xs])
+    )(me, far(ids[0]), ids[1], far(table.T), far(by_slab(xs[0], slabs, width)), by_slab(xs[1], slabs, width))
     return done[0], done[1:]
 
 
@@ -423,16 +423,16 @@
 
     real = sort_columns(slabs, me, order, spectra, 0, ())
     ctf, real_there = exchange(ctf), exchange(real)
-    ctf_part, coded, meta = volume(ctf, None, (real[0],))
     imag = sort_columns(slabs, me, order, spectra, 1, (real[0],))
+    ctf_part, coded, meta = volume(ctf, None, (imag[0],))
     imag_there = exchange(imag)
-    real_part, coded, _ = volume(real_there, meta, (imag[0],))
+    real_part, coded, _ = volume(real_there, meta, (coded,))
     tie = coded
     early = len(ctf_part.hops) - 1
     for step in ctf_part.hops[:early]:
         tie = step(ties=(tie,))
     imag_part, coded, _ = volume(imag_there, meta, (tie,))
-    steps = real_part.hops[:-1] + ctf_part.hops[early:] + imag_part.hops[:1] + real_part.hops[-1:] + imag_part.hops[1:]
+    steps = real_part.hops[:-1] + imag_part.hops[:1] + ctf_part.hops[early:] + real_part.hops[-1:] + imag_part.hops[1:]
     tie = coded
     for step in steps:
         tie = step(ties=(tie,))

time: 115 us -> 107 us (0.930)
  waiting for transfers between devices: 14.3 us -> 9.88 us
  local copies, waits for them, and re-layouts: 9.47 us -> 6.2 us
    unnamed x50 -> x40, local copies, waits for them, and re-layouts: 8.84 us -> 5.53 us
    ppermute x12, waiting for transfers between devices: 8.39 us -> 5.65 us  [swap(): return lax.ppermute(x, 'slab', [(i, i ^ offset) for i in range(slabs)])]
    ppermute x15, waiting for transfers between devices: 5.88 us -> 4.22 us  [send(): lax.ppermute(payload, 'grp', pairs + [(last - a, last - b) for a, b in pa...]
    pallas_call x9, Pallas kernels: 9.16 us -> 10.5 us  [hop(): pl.pallas_call(functools.partial(hop_kernel, places), out_shape=jax.Shape...]
  transfers between devices with their start and end apart: 27 -> 27, of which waited for: 6 -> 5; matrix products, arithmetic and copies ran while one was open for 1% -> 1% of each run, Pallas kernels for 35% -> 37%
where the time goes in v5:
time: 107 us; the launch traced here: 106 us
  Pallas kernels  44.7 us (42%)
  starting transfers between devices  44.6 us (42%)
  waiting for transfers between devices  9.88 us (9%)
  local copies, waits for them, and re-layouts  6.2 us (6%)
    ppermute x15, starting transfers between devices, send(): lax.ppermute(payload, 'grp', pairs + [(last - a, last - b) for a, b in pa...  29.8 us
    pallas_call x3, Pallas kernels, volume_sums(): pl.pallas_call(functools.partial(volume_kernel, slabs, window, messages,...  20 us
    ppermute x12, starting transfers between devices, swap(): return lax.ppermute(x, 'slab', [(i, i ^ offset) for i in range(slabs)])  14.8 us
    pallas_call x9, Pallas kernels, hop(): pl.pallas_call(functools.partial(hop_kernel, places), out_shape=jax.Shape...  10.5 us
    pallas_call x2, Pallas kernels, sort_columns(): pl.pallas_call(functools.partial(sort_kernel, slabs, width, part, len(tie...  6.01 us
    ppermute x12, waiting for transfers between devices, swap(): return lax.ppermute(x, 'slab', [(i, i ^ offset) for i in range(slabs)])  5.65 us
    unnamed x40, local copies, waits for them, and re-layouts  5.53 us
    pallas_call x1, Pallas kernels, image_of(): pl.pallas_call(functools.partial(image_kernel, parts, zs), out_shape=jax....  4.76 us
  transfers between devices with their start and end apart: 27, of which 5 were waited for; matrix products, arithmetic and copies ran while one was open for 1% of the time, Pallas kernels for 37%

profile of v5, /device:TPU:0, one launch (start us, length us, event | category | flops | bytes accessed | tf_op | source)
XLA Modules:
  0.0 106.5 jit_solution(10361375519283522328)
XLA Ops:
  0.5 0.7 pad_add_fusion.refs_0_
  1.8 3.2 %collective-permute-done.refs_1_ = s32[3,512]{1,0:T(4,128)S(1)} collective-permute-done((s32[3,512]{1,0:T(4,128)S(1)}, s32[3,512]{1,0:T(4,128)S(1)}, u32[]{:S(2)}, u32[]{:S(2)}) %collective-permute-start) | collective-permute-done | bytes 6176 | tf_op jit(solution)/shard_map/ppermute | solution.py:147
  5.0 0.9 collective-permute-done.1.refs_4_
  5.9 3.4 %plan_rows.1 = (bf16[2,512,512]{2,1,0:T(8,128)(2,1)S(1)}, bf16[1152,128]{1,0:T(8,128)(2,1)S(1)}, bf16[1152,128]{1,0:T(8,128)(2,1)S(1)}, bf16[1152,128]{1,0:T(8,128)(2,1)S(1)}, bf16[1152,128]{1,0:T(8,128)(2,1)S(1)}) custom-call(s32[1]{0:T(128)} %bitcast.1.me_ref, s32[3,512]{1,0:T(4,128)} %copy-done.18, s32[3,512]{1,0:T(4,128)S(1)} %collective-permute-done.refs_1_, ...), custom_call_target="tpu_custom_call" | custom-call | bytes 18000000 | tf_op jit(solution)/shard_map/plan_rows/pallas_call | solution.py:101
  9.3 2.6 %collective-permute-start.3 = (bf16[1152,128]{1,0:T(8,128)(2,1)S(1)}, bf16[1152,128]{1,0:T(8,128)(2,1)S(1)}, u32[]{:S(2)}, u32[]{:S(2)}) collective-permute-start(bf16[1152,128]{1,0:T(8,128)(2,1)S(1)} %get-tuple-element.32), channel_id=1, source_target_pairs={{0,2},{1,3},{2,0},{3,1},{4,6},{5,7},{6,4},{7,5},{8,10},{9,11},{10,... | collective-permute-start | bytes 884744 | tf_op jit(solution)/shard_map/ppermute | solution.py:147
  11.9 1.5 %collective-permute-start.4 = (bf16[1152,128]{1,0:T(8,128)(2,1)S(1)}, bf16[1152,128]{1,0:T(8,128)(2,1)S(1)}, u32[]{:S(2)}, u32[]{:S(2)}) collective-permute-start(bf16[1152,128]{1,0:T(8,128)(2,1)S(1)} %get-tuple-element.33), channel_id=1, source_target_pairs={{0,4},{1,5},{2,6},{3,7},{4,0},{5,1},{6,2},{7,3},{8,12},{9,13},{10,... | collective-permute-start | bytes 884744 | tf_op jit(solution)/shard_map/ppermute | solution.py:147
  13.5 3.2 %sort_columns.2 = (bf16[1024,128]{1,0:T(8,128)(2,1)S(1)}, bf16[1024,128]{1,0:T(8,128)(2,1)}, bf16[1024,128]{1,0:T(8,128)(2,1)S(1)}, bf16[1024,128]{1,0:T(8,128)(2,1)S(1)}) custom-call(s32[1]{0:T(128)} %bitcast.1.me_ref, bf16[2,512,512]{2,1,0:T(8,128)(2,1)S(1)} %get-tuple-element.28.order_ref, bf16[512,2048]{1,0:T(8,128)(2,1)} %refs_0_.3, ...), custom_call_target="tpu_custom_call" | custom-call | bytes 9000000 | tf_op jit(solution)/shard_map/sort_columns/pallas_call | solution.py:131
  16.7 2.0 %collective-permute-start.6 = (bf16[1024,128]{1,0:T(8,128)(2,1)}, bf16[1024,128]{1,0:T(8,128)(2,1)}, u32[]{:S(2)}, u32[]{:S(2)}) collective-permute-start(bf16[1024,128]{1,0:T(8,128)(2,1)} %get-tuple-element.36), channel_id=1, source_target_pairs={{0,2},{1,3},{2,0},{3,1},{4,6},{5,7},{6,4},{7,5},{8,10},{9,11},{10,... | collective-permute-start | bytes 786440 | tf_op jit(solution)/shard_map/ppermute | solution.py:147
  18.6 1.5 %collective-permute-start.7 = (bf16[1024,128]{1,0:T(8,128)(2,1)S(1)}, bf16[1024,128]{1,0:T(8,128)(2,1)}, u32[]{:S(2)}, u32[]{:S(2)}) collective-permute-start(bf16[1024,128]{1,0:T(8,128)(2,1)S(1)} %get-tuple-element.37), channel_id=1, source_target_pairs={{0,4},{1,5},{2,6},{3,7},{4,0},{5,1},{6,2},{7,3},{8,12},{9,13},{10,... | collective-permute-start | bytes 786440 | tf_op jit(solution)/shard_map/ppermute | solution.py:147
  20.1 0.7 copy-done.11
  20.9 2.6 %collective-permute-start.8 = (bf16[1024,128]{1,0:T(8,128)(2,1)S(1)}, bf16[1024,128]{1,0:T(8,128)(2,1)}, u32[]{:S(2)}, u32[]{:S(2)}) collective-permute-start(bf16[1024,128]{1,0:T(8,128)(2,1)S(1)} %get-tuple-element.38), channel_id=1, source_target_pairs={{0,6},{1,7},{2,4},{3,5},{4,2},{5,3},{6,0},{7,1},{8,14},{9,15},{10,... | collective-permute-start | bytes 786440 | tf_op jit(solution)/shard_map/ppermute | solution.py:147
  23.4 2.8 %sort_columns.3 = (bf16[1024,128]{1,0:T(8,128)(2,1)S(1)}, bf16[1024,128]{1,0:T(8,128)(2,1)S(1)}, bf16[1024,128]{1,0:T(8,128)(2,1)S(1)}, bf16[1024,128]{1,0:T(8,128)(2,1)S(1)}) custom-call(s32[1]{0:T(128)} %bitcast.1.me_ref, bf16[2,512,512]{2,1,0:T(8,128)(2,1)S(1)} %get-tuple-element.28.order_ref, bf16[512,2048]{1,0:T(8,128)(2,1)} %refs_0_.3, ...), custom_call_target="tpu_custom_call" | custom-call | bytes 9000000 | tf_op jit(solution)/shard_map/sort_columns/pallas_call | solution.py:131
  26.3 1.5 %collective-permute-done.4.refs_3_ = bf16[1152,128]{1,0:T(8,128)(2,1)S(1)} collective-permute-done((bf16[1152,128]{1,0:T(8,128)(2,1)S(1)}, bf16[1152,128]{1,0:T(8,128)(2,1)S(1)}, u32[]{:S(2)}, u32[]{:S(2)}) %collective-permute-start.4) | collective-permute-done | bytes 294944 | tf_op jit(solution)/shard_map/ppermute | solution.py:147
  28.6 6.6 %volume_sums.3 = (f32[16,8,32,128]{3,2,1,0:T(8,128)S(1)}, bf16[8,16,512]{2,1,0:T(8,128)(2,1)S(1)}, s16[1,1040,128]{2,1,0:T(8,128)(2,1)S(1)}, s16[1,1040,128]{2,1,0:T(8,128)(2,1)S(1)}) custom-call(s32[2]{0:T(128)S(1)} %broadcast_select_fusion.idx_ref, bf16[1024,128]{1,0:T(8,128)(2,1)S(1)} %get-tuple-element.30.refs_0_.refs_1_, bf16[1152,128]{1,0:T(8,128)(2,1)} %copy-done.8, ...), custom_call_target="tpu_custom_call" | custom-call | bytes 21000000 | tf_op jit(solution)/shard_map/volume_sums/pallas_call | solution.py:224
  35.2 3.5 %collective-permute-start.12 = (s16[1,1040,128]{2,1,0:T(8,128)(2,1)S(1)}, s16[1,1040,128]{2,1,0:T(8,128)(2,1)S(1)}, u32[]{:S(2)}, u32[]{:S(2)}) collective-permute-start(s16[1,1040,128]{2,1,0:T(8,128)(2,1)S(1)} %get-tuple-element.35.refs_0_), channel_id=1, source_target_pairs={{0,8},{24,16},{1,9},{25,17},{2,10},{26,18},{3,11},{27,19},{4,12},{... | collective-permute-start | bytes 798728 | tf_op jit(solution)/shard_map/ppermute | solution.py:329
  38.7 1.5 %collective-permute-start.11 = (s16[1,1040,128]{2,1,0:T(8,128)(2,1)S(1)}, s16[1,1040,128]{2,1,0:T(8,128)(2,1)S(1)}, u32[]{:S(2)}, u32[]{:S(2)}) collective-permute-start(s16[1,1040,128]{2,1,0:T(8,128)(2,1)S(1)} %get-tuple-element.44), channel_id=1, source_target_pairs={{0,8},{24,16},{1,9},{25,17},{2,10},{26,18},{3,11},{27,19},{4,12},{... | collective-permute-start | bytes 798728 | tf_op jit(solution)/shard_map/ppermute | solution.py:329
  40.2 1.2 %collective-permute-start.13 = (bf16[1024,128]{1,0:T(8,128)(2,1)S(1)}, bf16[1024,128]{1,0:T(8,128)(2,1)S(1)}, u32[]{:S(2)}, u32[]{:S(2)}) collective-permute-start(bf16[1024,128]{1,0:T(8,128)(2,1)S(1)} %get-tuple-element.45), channel_id=1, source_target_pairs={{0,2},{1,3},{2,0},{3,1},{4,6},{5,7},{6,4},{7,5},{8,10},{9,11},{10,... | collective-permute-start | bytes 786440 | tf_op jit(solution)/shard_map/ppermute | solution.py:147
  41.4 0.9 collective-permute-start.14
  42.4 1.4 %collective-permute-start.15 = (bf16[1024,128]{1,0:T(8,128)(2,1)S(1)}, bf16[1024,128]{1,0:T(8,128)(2,1)S(1)}, u32[]{:S(2)}, u32[]{:S(2)}) collective-permute-start(bf16[1024,128]{1,0:T(8,128)(2,1)S(1)} %get-tuple-element.47), channel_id=1, source_target_pairs={{0,6},{1,7},{2,4},{3,5},{4,2},{5,3},{6,0},{7,1},{8,14},{9,15},{10,... | collective-permute-start | bytes 786440 | tf_op jit(solution)/shard_map/ppermute | solution.py:147
  43.8 6.5 %volume_sums.4 = (f32[16,8,32,128]{3,2,1,0:T(8,128)S(1)}, s16[1,1040,128]{2,1,0:T(8,128)(2,1)S(1)}, s16[1,1040,128]{2,1,0:T(8,128)(2,1)S(1)}) custom-call(s32[2]{0:T(128)S(1)} %broadcast_select_fusion.idx_ref, s16[1,1040,128]{2,1,0:T(8,128)(2,1)S(1)} %get-tuple-element.35.refs_0_, bf16[1024,128]{1,0:T(8,128)(2,1)} %copy-done.6, ...), custom_call_target="tpu_custom_call" | custom-call | bytes 21000000 | tf_op jit(solution)/shard_map/volume_sums/pallas_call | solution.py:224
  50.3 1.3 %collective-permute-start.10 = (s16[1,1040,128]{2,1,0:T(8,128)(2,1)S(1)}, s16[1,1040,128]{2,1,0:T(8,128)(2,1)S(1)}, u32[]{:S(2)}, u32[]{:S(2)}) collective-permute-start(s16[1,1040,128]{2,1,0:T(8,128)(2,1)S(1)} %get-tuple-element.42.refs_0_), channel_id=1, source_target_pairs={{0,8},{24,16},{1,9},{25,17},{2,10},{26,18},{3,11},{27,19},{4,12},{... | collective-permute-start | bytes 798728 | tf_op jit(solution)/shard_map/ppermute | solution.py:329
  51.6 0.8 hop.9.refs_0_
  52.4 1.3 %collective-permute-start.9 = (s16[1,1040,128]{2,1,0:T(8,128)(2,1)S(1)}, s16[1,1040,128]{2,1,0:T(8,128)(2,1)S(1)}, u32[]{:S(2)}, u32[]{:S(2)}) collective-permute-start(s16[1,1040,128]{2,1,0:T(8,128)(2,1)S(1)} %get-tuple-element.41), channel_id=1, source_target_pairs={{0,8},{24,16},{1,9},{25,17},{2,10},{26,18},{3,11},{27,19},{4,12},{... | collective-permute-start | bytes 798728 | tf_op jit(solution)/shard_map/ppermute | solution.py:329
  53.7 1.5 %hop.10.refs_0_ = s16[1,1040,128]{2,1,0:T(8,128)(2,1)} custom-call(s32[1]{0:T(128)S(6)} %select_n.48.idx_ref, f32[4,1024,128]{2,1,0:T(8,128)S(1)} %bitcast.14, s16[1,1040,128]{2,1,0:T(8,128)(2,1)S(1)} %collective-permute-done.11.prev_ref, s16[1,1040,128]{2,1,0:T(8,128)(2,1)S(1)} %hop.9.refs_0_), custom_call_target="tpu_custom_call" | custom-call | bytes 9000000 | tf_op jit(solution)/shard_map/hop/pallas_call | solution.py:289
  56.7 7.0 %volume_sums.5 = (f32[16,8,32,128]{3,2,1,0:T(8,128)S(1)}, s16[1,1040,128]{2,1,0:T(8,128)(2,1)S(1)}, s16[1,1040,128]{2,1,0:T(8,128)(2,1)}) custom-call(s32[2]{0:T(128)S(1)} %broadcast_select_fusion.idx_ref, s16[1,1040,128]{2,1,0:T(8,128)(2,1)} %hop.10.refs_0_, bf16[1024,128]{1,0:T(8,128)(2,1)} %copy-done.7, bf16[1024,128]{1,0:T(8,128)(2,1)} %copy-done.15, ...), custom_call_target="tpu_custom_call" | custom-call | bytes 21000000 | tf_op jit(solution)/shard_map/volume_sums/pallas_call | solution.py:224
  63.7 1.3 %collective-permute-start.19 = (s16[1,1040,128]{2,1,0:T(8,128)(2,1)S(1)}, s16[1,1040,128]{2,1,0:T(8,128)(2,1)S(1)}, u32[]{:S(2)}, u32[]{:S(2)}) collective-permute-start(s16[1,1040,128]{2,1,0:T(8,128)(2,1)S(1)} %get-tuple-element.48.refs_0_), channel_id=1, source_target_pairs={{0,8},{24,16},{1,9},{25,17},{2,10},{26,18},{3,11},{27,19},{4,12},{... | collective-permute-start | bytes 798728 | tf_op jit(solution)/shard_map/ppermute | solution.py:329
  65.0 1.4 %collective-permute-start.18 = (s16[1,1040,128]{2,1,0:T(8,128)(2,1)S(1)}, s16[1,1040,128]{2,1,0:T(8,128)(2,1)}, u32[]{:S(2)}, u32[]{:S(2)}) collective-permute-start(s16[1,1040,128]{2,1,0:T(8,128)(2,1)S(1)} %hop.9.refs_0_), channel_id=1, source_target_pairs={{8,16},{16,8},{9,17},{17,9},{10,18},{18,10},{11,19},{19,11},{12,20... | collective-permute-start | bytes 798728 | tf_op jit(solution)/shard_map/ppermute | solution.py:329
  66.4 3.4 %collective-permute-start.21 = (s16[1,1040,128]{2,1,0:T(8,128)(2,1)}, s16[1,1040,128]{2,1,0:T(8,128)(2,1)S(1)}, u32[]{:S(2)}, u32[]{:S(2)}) collective-permute-start(s16[1,1040,128]{2,1,0:T(8,128)(2,1)} %get-tuple-element.50), channel_id=1, source_target_pairs={{0,8},{24,16},{1,9},{25,17},{2,10},{26,18},{3,11},{27,19},{4,12},{... | collective-permute-start | bytes 798728 | tf_op jit(solution)/shard_map/ppermute | solution.py:329
  69.8 0.8 hop.11.refs_0_
  70.6 1.4 %collective-permute-start.17 = (s16[1,1040,128]{2,1,0:T(8,128)(2,1)S(1)}, s16[1,1040,128]{2,1,0:T(8,128)(2,1)}, u32[]{:S(2)}, u32[]{:S(2)}) collective-permute-start(s16[1,1040,128]{2,1,0:T(8,128)(2,1)S(1)} %hop.11.refs_0_), channel_id=1, source_target_pairs={{8,16},{16,8},{9,17},{17,9},{10,18},{18,10},{11,19},{19,11},{12,20... | collective-permute-start | bytes 798728 | tf_op jit(solution)/shard_map/ppermute | solution.py:329
  72.0 0.8 hop.12.refs_0_
  72.8 0.8 hop.13.refs_0_
  73.6 1.4 %collective-permute-start.23 = (s16[1,1040,128]{2,1,0:T(8,128)(2,1)S(1)}, s16[1,1040,128]{2,1,0:T(8,128)(2,1)}, u32[]{:S(2)}, u32[]{:S(2)}) collective-permute-start(s16[1,1040,128]{2,1,0:T(8,128)(2,1)S(1)} %hop.13.refs_0_), channel_id=1, source_target_pairs={{8,16},{16,8},{9,17},{17,9},{10,18},{18,10},{11,19},{19,11},{12,20... | collective-permute-start | bytes 798728 | tf_op jit(solution)/shard_map/ppermute | solution.py:329
  75.0 1.4 %collective-permute-start.25 = (s16[1,1040,128]{2,1,0:T(8,128)(2,1)}, s16[1,1040,128]{2,1,0:T(8,128)(2,1)}, u32[]{:S(2)}, u32[]{:S(2)}) collective-permute-start(s16[1,1040,128]{2,1,0:T(8,128)(2,1)} %hop.10.refs_0_), channel_id=1, source_target_pairs={{8,16},{16,8},{9,17},{17,9},{10,18},{18,10},{11,19},{19,11},{12,20... | collective-permute-start | bytes 798728 | tf_op jit(solution)/shard_map/ppermute | solution.py:329
  76.4 1.5 %collective-permute-start.16 = (s16[1,1040,128]{2,1,0:T(8,128)(2,1)S(1)}, s16[1,1040,128]{2,1,0:T(8,128)(2,1)}, u32[]{:S(2)}, u32[]{:S(2)}) collective-permute-start(s16[1,1040,128]{2,1,0:T(8,128)(2,1)S(1)} %hop.12.refs_0_), channel_id=1, source_target_pairs={{8,16},{16,8},{9,17},{17,9},{10,18},{18,10},{11,19},{19,11},{12,20... | collective-permute-start | bytes 798728 | tf_op jit(solution)/shard_map/ppermute | solution.py:329
  77.9 1.7 %hop.14.refs_0_ = s16[1,1040,128]{2,1,0:T(8,128)(2,1)S(1)} custom-call(s32[1]{0:T(128)S(6)} %select_n.51.idx_ref, f32[4,1024,128]{2,1,0:T(8,128)S(1)} %bitcast.15, s16[1,1040,128]{2,1,0:T(8,128)(2,1)} %collective-permute-done.18.prev_ref, s16[1,1040,128]{2,1,0:T(8,128)(2,1)S(1)} %hop.13.refs_0_), custom_call_target="tpu_custom_call" | custom-call | bytes 9000000 | tf_op jit(solution)/shard_map/hop/pallas_call | solution.py:289
  79.6 6.5 %collective-permute-start.26 = (s16[1,1040,128]{2,1,0:T(8,128)(2,1)S(1)}, s16[1,1040,128]{2,1,0:T(8,128)(2,1)}, u32[]{:S(2)}, u32[]{:S(2)}) collective-permute-start(s16[1,1040,128]{2,1,0:T(8,128)(2,1)S(1)} %hop.14.refs_0_), channel_id=1, source_target_pairs={{8,0},{0,8},{16,24},{24,16},{9,1},{1,9},{17,25},{25,17},{10,2},{2,... | collective-permute-start | bytes 798728 | tf_op jit(solution)/shard_map/ppermute | solution.py:329
  86.1 1.7 %hop.15.refs_0_ = s16[1,1040,128]{2,1,0:T(8,128)(2,1)S(1)} custom-call(s32[1]{0:T(128)S(6)} %select_n.51.idx_ref, f32[4,1024,128]{2,1,0:T(8,128)S(1)} %bitcast.20, s16[1,1040,128]{2,1,0:T(8,128)(2,1)} %collective-permute-done.17.prev_ref, s16[1,1040,128]{2,1,0:T(8,128)(2,1)S(1)} %hop.14.refs_0_), custom_call_target="tpu_custom_call" | custom-call | bytes 9000000 | tf_op jit(solution)/shard_map/hop/pallas_call | solution.py:289
  87.8 0.7 copy-done.9
  88.7 0.9 copy-done.10
  89.7 0.8 hop.16.refs_0_
  90.5 1.4 %collective-permute-start.22 = (s16[1,1040,128]{2,1,0:T(8,128)(2,1)S(1)}, s16[1,1040,128]{2,1,0:T(8,128)(2,1)}, u32[]{:S(2)}, u32[]{:S(2)}) collective-permute-start(s16[1,1040,128]{2,1,0:T(8,128)(2,1)S(1)} %hop.16.refs_0_), channel_id=1, source_target_pairs={{8,16},{16,8},{9,17},{17,9},{10,18},{18,10},{11,19},{19,11},{12,20... | collective-permute-start | bytes 798728 | tf_op jit(solution)/shard_map/ppermute | solution.py:329
  91.9 1.7 %hop.17 = s16[1,1040,128]{2,1,0:T(8,128)(2,1)S(1)} custom-call(s32[1]{0:T(128)S(6)} %select_n.51.idx_ref, f32[4,1024,128]{2,1,0:T(8,128)S(1)} %bitcast.24, s16[1,1040,128]{2,1,0:T(8,128)(2,1)} %collective-permute-done.23.prev_ref, s16[1,1040,128]{2,1,0:T(8,128)(2,1)S(1)} %hop.16.refs_0_), custom_call_target="tpu_custom_call" | custom-call | bytes 9000000 | tf_op jit(solution)/shard_map/hop/pallas_call | solution.py:289
  93.6 2.5 %collective-permute-start.24 = (s16[1,1040,128]{2,1,0:T(8,128)(2,1)S(1)}, s16[1,1040,128]{2,1,0:T(8,128)(2,1)S(1)}, u32[]{:S(2)}, u32[]{:S(2)}) collective-permute-start(s16[1,1040,128]{2,1,0:T(8,128)(2,1)S(1)} %hop.17), channel_id=1, source_target_pairs={{8,0},{0,8},{16,24},{24,16},{9,1},{1,9},{17,25},{25,17},{10,2},{2,... | collective-permute-start | bytes 798728 | tf_op jit(solution)/shard_map/ppermute | solution.py:329
  96.7 1.4 %collective-permute-done.20.refs_2_ = s16[1,1040,128]{2,1,0:T(8,128)(2,1)} collective-permute-done((s16[1,1040,128]{2,1,0:T(8,128)(2,1)S(1)}, s16[1,1040,128]{2,1,0:T(8,128)(2,1)}, u32[]{:S(2)}, u32[]{:S(2)}) %collective-permute-start.20) | collective-permute-done | bytes 266272 | tf_op jit(solution)/shard_map/ppermute | solution.py:329
  98.2 2.8 %collective-permute-done.24.refs_5_ = s16[1,1040,128]{2,1,0:T(8,128)(2,1)S(1)} collective-permute-done((s16[1,1040,128]{2,1,0:T(8,128)(2,1)S(1)}, s16[1,1040,128]{2,1,0:T(8,128)(2,1)S(1)}, u32[]{:S(2)}, u32[]{:S(2)}) %collective-permute-start.24) | collective-permute-done | bytes 266272 | tf_op jit(solution)/shard_map/ppermute | solution.py:329
  100.9 0.8 copy-done.14
  101.7 4.8 %image_of.1 = f32[2,4,256,128]{3,2,1,0:T(8,128)} custom-call(s32[1]{0:T(128)} %bitcast.own_ref, f32[4,1024,128]{2,1,0:T(8,128)} %bitcast.19, s16[1,1040,128]{2,1,0:T(8,128)(2,1)} %collective-permute-done.16.refs_1_, s16[1,1040,128]{2,1,0:T(8,128)(2,1)} %collective-permute-done.20.refs_2_, f32[4,1024,128]{2,1,0:T(8,128)} %bitcast.22, ...), custom_call_target="tpu_custom_call" | custom-call | bytes 18000000 | tf_op jit(solution)/shard_map/image_of/pallas_call | solution.py:391
  (65 shorter events, 4.3 us)
Async XLA Ops:
  0.0 96.1 %copy-start = (f32[1024]{0:T(1024)S(1)}, f32[1024]{0:T(1024)}, u32[]{:S(2)}) copy-start(f32[1024]{0:T(1024)} %param.17) | copy-start | bytes 12292
  0.0 13.5 %collective-permute-start.2 = (bf16[512,2048]{1,0:T(8,128)(2,1)}, bf16[512,2048]{1,0:T(8,128)(2,1)}, u32[]{:S(2)}, u32[]{:S(2)}) collective-permute-start(bf16[512,2048]{1,0:T(8,128)(2,1)} %refs_0_.3), channel_id=1, source_target_pairs={{0,1},{1,0},{2,3},{3,2},{4,5},{5,4},{6,7},{7,6},{8,9},{9,8},{10,11... | collective-permute-start | bytes 6291464 | tf_op jit(solution)/shard_map/ppermute | solution.py:147
  0.5 5.4 %collective-permute-start.1 = (bf16[512,1024]{1,0:T(8,128)(2,1)}, bf16[512,1024]{1,0:T(8,128)(2,1)S(1)}, u32[]{:S(2)}, u32[]{:S(2)}) collective-permute-start(bf16[512,1024]{1,0:T(8,128)(2,1)} %refs_3_.1), channel_id=1, source_target_pairs={{0,1},{1,0},{2,3},{3,2},{4,5},{5,4},{6,7},{7,6},{8,9},{9,8},{10,11... | collective-permute-start | bytes 3145736 | tf_op jit(solution)/shard_map/ppermute | solution.py:147
  1.3 4.6 %copy-start.18 = (s32[3,512]{1,0:T(4,128)}, s32[3,512]{1,0:T(4,128)S(1)}, u32[]{:S(2)}) copy-start(s32[3,512]{1,0:T(4,128)S(1)} %pad_add_fusion.refs_0_) | copy-start | bytes 18436
  1.3 3.7 %collective-permute-start = (s32[3,512]{1,0:T(4,128)S(1)}, s32[3,512]{1,0:T(4,128)S(1)}, u32[]{:S(2)}, u32[]{:S(2)}) collective-permute-start(s32[3,512]{1,0:T(4,128)S(1)} %pad_add_fusion.refs_0_), channel_id=1, source_target_pairs={{0,1},{1,0},{2,3},{3,2},{4,5},{5,4},{6,7},{7,6},{8,9},{9,8},{10,11... | collective-permute-start | bytes 18440 | tf_op jit(solution)/shard_map/ppermute | solution.py:147
  9.3 7.4 %copy-start.8 = (bf16[1152,128]{1,0:T(8,128)(2,1)}, bf16[1152,128]{1,0:T(8,128)(2,1)S(1)}, u32[]{:S(2)}) copy-start(bf16[1152,128]{1,0:T(8,128)(2,1)S(1)} %get-tuple-element.31.refs_1_) | copy-start | bytes 884740
  9.3 10.9 %collective-permute-start.3 = (bf16[1152,128]{1,0:T(8,128)(2,1)S(1)}, bf16[1152,128]{1,0:T(8,128)(2,1)S(1)}, u32[]{:S(2)}, u32[]{:S(2)}) collective-permute-start(bf16[1152,128]{1,0:T(8,128)(2,1)S(1)} %get-tuple-element.32), channel_id=1, source_target_pairs={{0,2},{1,3},{2,0},{3,1},{4,6},{5,7},{6,4},{7,5},{8,10},{9,11},{10,... | collective-permute-start | bytes 884744 | tf_op jit(solution)/shard_map/ppermute | solution.py:147
  11.9 15.9 %collective-permute-start.4 = (bf16[1152,128]{1,0:T(8,128)(2,1)S(1)}, bf16[1152,128]{1,0:T(8,128)(2,1)S(1)}, u32[]{:S(2)}, u32[]{:S(2)}) collective-permute-start(bf16[1152,128]{1,0:T(8,128)(2,1)S(1)} %get-tuple-element.33), channel_id=1, source_target_pairs={{0,4},{1,5},{2,6},{3,7},{4,0},{5,1},{6,2},{7,3},{8,12},{9,13},{10,... | collective-permute-start | bytes 884744 | tf_op jit(solution)/shard_map/ppermute | solution.py:147
  13.4 14.4 %collective-permute-start.5 = (bf16[1152,128]{1,0:T(8,128)(2,1)S(1)}, bf16[1152,128]{1,0:T(8,128)(2,1)S(1)}, u32[]{:S(2)}, u32[]{:S(2)}) collective-permute-start(bf16[1152,128]{1,0:T(8,128)(2,1)S(1)} %get-tuple-element.34), channel_id=1, source_target_pairs={{0,6},{1,7},{2,4},{3,5},{4,2},{5,3},{6,0},{7,1},{8,14},{9,15},{10,... | collective-permute-start | bytes 884744 | tf_op jit(solution)/shard_map/ppermute | solution.py:147
  13.5 10.0 %copy-start.19 = (s32[2]{0:T(128)S(1)}, s32[2]{0:T(128)}, u32[]{:S(2)}) copy-start(s32[2]{0:T(128)} %constant.36.clone) | copy-start | bytes 28
  16.7 9.6 %copy-start.6 = (bf16[1024,128]{1,0:T(8,128)(2,1)}, bf16[1024,128]{1,0:T(8,128)(2,1)S(1)}, u32[]{:S(2)}) copy-start(bf16[1024,128]{1,0:T(8,128)(2,1)S(1)} %get-tuple-element.29.refs_2_.refs_1_) | copy-start | bytes 786436
  16.7 23.5 %collective-permute-start.6 = (bf16[1024,128]{1,0:T(8,128)(2,1)}, bf16[1024,128]{1,0:T(8,128)(2,1)}, u32[]{:S(2)}, u32[]{:S(2)}) collective-permute-start(bf16[1024,128]{1,0:T(8,128)(2,1)} %get-tuple-element.36), channel_id=1, source_target_pairs={{0,2},{1,3},{2,0},{3,1},{4,6},{5,7},{6,4},{7,5},{8,10},{9,11},{10,... | collective-permute-start | bytes 786440 | tf_op jit(solution)/shard_map/ppermute | solution.py:147
  18.6 22.8 %collective-permute-start.7 = (bf16[1024,128]{1,0:T(8,128)(2,1)S(1)}, bf16[1024,128]{1,0:T(8,128)(2,1)}, u32[]{:S(2)}, u32[]{:S(2)}) collective-permute-start(bf16[1024,128]{1,0:T(8,128)(2,1)S(1)} %get-tuple-element.37), channel_id=1, source_target_pairs={{0,4},{1,5},{2,6},{3,7},{4,0},{5,1},{6,2},{7,3},{8,12},{9,13},{10,... | collective-permute-start | bytes 786440 | tf_op jit(solution)/shard_map/ppermute | solution.py:147
  20.1 0.7 copy-start.11
  20.9 21.5 %collective-permute-start.8 = (bf16[1024,128]{1,0:T(8,128)(2,1)S(1)}, bf16[1024,128]{1,0:T(8,128)(2,1)}, u32[]{:S(2)}, u32[]{:S(2)}) collective-permute-start(bf16[1024,128]{1,0:T(8,128)(2,1)S(1)} %get-tuple-element.38), channel_id=1, source_target_pairs={{0,6},{1,7},{2,4},{3,5},{4,2},{5,3},{6,0},{7,1},{8,14},{9,15},{10,... | collective-permute-start | bytes 786440 | tf_op jit(solution)/shard_map/ppermute | solution.py:147
  26.3 26.1 %copy-start.7 = (bf16[1024,128]{1,0:T(8,128)(2,1)}, bf16[1024,128]{1,0:T(8,128)(2,1)S(1)}, u32[]{:S(2)}) copy-start(bf16[1024,128]{1,0:T(8,128)(2,1)S(1)} %get-tuple-element.30.refs_0_.refs_1_) | copy-start | bytes 786436
  27.8 0.7 copy-start.12
  27.8 0.8 copy-start.13
  35.2 42.7 %copy-start.1 = (f32[16,8,32,128]{3,2,1,0:T(8,128)}, f32[16,8,32,128]{3,2,1,0:T(8,128)S(1)}, u32[]{:S(2)}) copy-start(f32[16,8,32,128]{3,2,1,0:T(8,128)S(1)} %get-tuple-element.43) | copy-start | bytes 6291460
  35.2 15.1 %collective-permute-start.12 = (s16[1,1040,128]{2,1,0:T(8,128)(2,1)S(1)}, s16[1,1040,128]{2,1,0:T(8,128)(2,1)S(1)}, u32[]{:S(2)}, u32[]{:S(2)}) collective-permute-start(s16[1,1040,128]{2,1,0:T(8,128)(2,1)S(1)} %get-tuple-element.35.refs_0_), channel_id=1, source_target_pairs={{0,8},{24,16},{1,9},{25,17},{2,10},{26,18},{3,11},{27,19},{4,12},{... | collective-permute-start | bytes 798728 | tf_op jit(solution)/shard_map/ppermute | solution.py:329
  38.7 13.7 %collective-permute-start.11 = (s16[1,1040,128]{2,1,0:T(8,128)(2,1)S(1)}, s16[1,1040,128]{2,1,0:T(8,128)(2,1)S(1)}, u32[]{:S(2)}, u32[]{:S(2)}) collective-permute-start(s16[1,1040,128]{2,1,0:T(8,128)(2,1)S(1)} %get-tuple-element.44), channel_id=1, source_target_pairs={{0,8},{24,16},{1,9},{25,17},{2,10},{26,18},{3,11},{27,19},{4,12},{... | collective-permute-start | bytes 798728 | tf_op jit(solution)/shard_map/ppermute | solution.py:329
  40.2 15.0 %collective-permute-start.13 = (bf16[1024,128]{1,0:T(8,128)(2,1)S(1)}, bf16[1024,128]{1,0:T(8,128)(2,1)S(1)}, u32[]{:S(2)}, u32[]{:S(2)}) collective-permute-start(bf16[1024,128]{1,0:T(8,128)(2,1)S(1)} %get-tuple-element.45), channel_id=1, source_target_pairs={{0,2},{1,3},{2,0},{3,1},{4,6},{5,7},{6,4},{7,5},{8,10},{9,11},{10,... | collective-permute-start | bytes 786440 | tf_op jit(solution)/shard_map/ppermute | solution.py:147
  41.4 13.8 %collective-permute-start.14 = (bf16[1024,128]{1,0:T(8,128)(2,1)S(1)}, bf16[1024,128]{1,0:T(8,128)(2,1)S(1)}, u32[]{:S(2)}, u32[]{:S(2)}) collective-permute-start(bf16[1024,128]{1,0:T(8,128)(2,1)S(1)} %get-tuple-element.46), channel_id=1, source_target_pairs={{0,4},{1,5},{2,6},{3,7},{4,0},{5,1},{6,2},{7,3},{8,12},{9,13},{10,... | collective-permute-start | bytes 786440 | tf_op jit(solution)/shard_map/ppermute | solution.py:147
  42.4 12.9 %collective-permute-start.15 = (bf16[1024,128]{1,0:T(8,128)(2,1)S(1)}, bf16[1024,128]{1,0:T(8,128)(2,1)S(1)}, u32[]{:S(2)}, u32[]{:S(2)}) collective-permute-start(bf16[1024,128]{1,0:T(8,128)(2,1)S(1)} %get-tuple-element.47), channel_id=1, source_target_pairs={{0,6},{1,7},{2,4},{3,5},{4,2},{5,3},{6,0},{7,1},{8,14},{9,15},{10,... | collective-permute-start | bytes 786440 | tf_op jit(solution)/shard_map/ppermute | solution.py:147
  50.3 21.7 %copy-start.2 = (f32[16,8,32,128]{3,2,1,0:T(8,128)}, f32[16,8,32,128]{3,2,1,0:T(8,128)S(1)}, u32[]{:S(2)}) copy-start(f32[16,8,32,128]{3,2,1,0:T(8,128)S(1)} %get-tuple-element.40) | copy-start | bytes 6291460
  50.3 19.5 %collective-permute-start.10 = (s16[1,1040,128]{2,1,0:T(8,128)(2,1)S(1)}, s16[1,1040,128]{2,1,0:T(8,128)(2,1)S(1)}, u32[]{:S(2)}, u32[]{:S(2)}) collective-permute-start(s16[1,1040,128]{2,1,0:T(8,128)(2,1)S(1)} %get-tuple-element.42.refs_0_), channel_id=1, source_target_pairs={{0,8},{24,16},{1,9},{25,17},{2,10},{26,18},{3,11},{27,19},{4,12},{... | collective-permute-start | bytes 798728 | tf_op jit(solution)/shard_map/ppermute | solution.py:329
  52.4 19.6 %collective-permute-start.9 = (s16[1,1040,128]{2,1,0:T(8,128)(2,1)S(1)}, s16[1,1040,128]{2,1,0:T(8,128)(2,1)S(1)}, u32[]{:S(2)}, u32[]{:S(2)}) collective-permute-start(s16[1,1040,128]{2,1,0:T(8,128)(2,1)S(1)} %get-tuple-element.41), channel_id=1, source_target_pairs={{0,8},{24,16},{1,9},{25,17},{2,10},{26,18},{3,11},{27,19},{4,12},{... | collective-permute-start | bytes 798728 | tf_op jit(solution)/shard_map/ppermute | solution.py:329
  55.2 0.7 copy-start.15
  55.2 0.8 copy-start.16
  56.0 0.7 copy-start.17
  63.7 9.1 %copy-start.4 = (f32[16,8,32,128]{3,2,1,0:T(8,128)}, f32[16,8,32,128]{3,2,1,0:T(8,128)S(1)}, u32[]{:S(2)}) copy-start(f32[16,8,32,128]{3,2,1,0:T(8,128)S(1)} %get-tuple-element.49) | copy-start | bytes 6291460
  63.7 9.0 %collective-permute-start.19 = (s16[1,1040,128]{2,1,0:T(8,128)(2,1)S(1)}, s16[1,1040,128]{2,1,0:T(8,128)(2,1)S(1)}, u32[]{:S(2)}, u32[]{:S(2)}) collective-permute-start(s16[1,1040,128]{2,1,0:T(8,128)(2,1)S(1)} %get-tuple-element.48.refs_0_), channel_id=1, source_target_pairs={{0,8},{24,16},{1,9},{25,17},{2,10},{26,18},{3,11},{27,19},{4,12},{... | collective-permute-start | bytes 798728 | tf_op jit(solution)/shard_map/ppermute | solution.py:329
  65.0 11.3 %collective-permute-start.18 = (s16[1,1040,128]{2,1,0:T(8,128)(2,1)S(1)}, s16[1,1040,128]{2,1,0:T(8,128)(2,1)}, u32[]{:S(2)}, u32[]{:S(2)}) collective-permute-start(s16[1,1040,128]{2,1,0:T(8,128)(2,1)S(1)} %hop.9.refs_0_), channel_id=1, source_target_pairs={{8,16},{16,8},{9,17},{17,9},{10,18},{18,10},{11,19},{19,11},{12,20... | collective-permute-start | bytes 798728 | tf_op jit(solution)/shard_map/ppermute | solution.py:329
  66.4 21.4 %collective-permute-start.21 = (s16[1,1040,128]{2,1,0:T(8,128)(2,1)}, s16[1,1040,128]{2,1,0:T(8,128)(2,1)S(1)}, u32[]{:S(2)}, u32[]{:S(2)}) collective-permute-start(s16[1,1040,128]{2,1,0:T(8,128)(2,1)} %get-tuple-element.50), channel_id=1, source_target_pairs={{0,8},{24,16},{1,9},{25,17},{2,10},{26,18},{3,11},{27,19},{4,12},{... | collective-permute-start | bytes 798728 | tf_op jit(solution)/shard_map/ppermute | solution.py:329
  70.6 9.0 %collective-permute-start.17 = (s16[1,1040,128]{2,1,0:T(8,128)(2,1)S(1)}, s16[1,1040,128]{2,1,0:T(8,128)(2,1)}, u32[]{:S(2)}, u32[]{:S(2)}) collective-permute-start(s16[1,1040,128]{2,1,0:T(8,128)(2,1)S(1)} %hop.11.refs_0_), channel_id=1, source_target_pairs={{8,16},{16,8},{9,17},{17,9},{10,18},{18,10},{11,19},{19,11},{12,20... | collective-permute-start | bytes 798728 | tf_op jit(solution)/shard_map/ppermute | solution.py:329
  73.6 16.9 %collective-permute-start.23 = (s16[1,1040,128]{2,1,0:T(8,128)(2,1)S(1)}, s16[1,1040,128]{2,1,0:T(8,128)(2,1)}, u32[]{:S(2)}, u32[]{:S(2)}) collective-permute-start(s16[1,1040,128]{2,1,0:T(8,128)(2,1)S(1)} %hop.13.refs_0_), channel_id=1, source_target_pairs={{8,16},{16,8},{9,17},{17,9},{10,18},{18,10},{11,19},{19,11},{12,20... | collective-permute-start | bytes 798728 | tf_op jit(solution)/shard_map/ppermute | solution.py:329
  75.0 18.6 %collective-permute-start.25 = (s16[1,1040,128]{2,1,0:T(8,128)(2,1)}, s16[1,1040,128]{2,1,0:T(8,128)(2,1)}, u32[]{:S(2)}, u32[]{:S(2)}) collective-permute-start(s16[1,1040,128]{2,1,0:T(8,128)(2,1)} %hop.10.refs_0_), channel_id=1, source_target_pairs={{8,16},{16,8},{9,17},{17,9},{10,18},{18,10},{11,19},{19,11},{12,20... | collective-permute-start | bytes 798728 | tf_op jit(solution)/shard_map/ppermute | solution.py:329
  76.4 9.7 %copy-start.3 = (f32[16,8,32,128]{3,2,1,0:T(8,128)S(1)}, f32[16,8,32,128]{3,2,1,0:T(8,128)}, u32[]{:S(2)}) copy-start(f32[16,8,32,128]{3,2,1,0:T(8,128)} %copy-done.2) | copy-start | bytes 6291460
  76.4 20.4 %collective-permute-start.16 = (s16[1,1040,128]{2,1,0:T(8,128)(2,1)S(1)}, s16[1,1040,128]{2,1,0:T(8,128)(2,1)}, u32[]{:S(2)}, u32[]{:S(2)}) collective-permute-start(s16[1,1040,128]{2,1,0:T(8,128)(2,1)S(1)} %hop.12.refs_0_), channel_id=1, source_target_pairs={{8,16},{16,8},{9,17},{17,9},{10,18},{18,10},{11,19},{19,11},{12,20... | collective-permute-start | bytes 798728 | tf_op jit(solution)/shard_map/ppermute | solution.py:329
  79.6 9.1 %copy-start.5 = (f32[16,8,32,128]{3,2,1,0:T(8,128)S(1)}, f32[16,8,32,128]{3,2,1,0:T(8,128)}, u32[]{:S(2)}) copy-start(f32[16,8,32,128]{3,2,1,0:T(8,128)} %copy-done.4) | copy-start | bytes 6291460
  79.6 17.1 %collective-permute-start.26 = (s16[1,1040,128]{2,1,0:T(8,128)(2,1)S(1)}, s16[1,1040,128]{2,1,0:T(8,128)(2,1)}, u32[]{:S(2)}, u32[]{:S(2)}) collective-permute-start(s16[1,1040,128]{2,1,0:T(8,128)(2,1)S(1)} %hop.14.refs_0_), channel_id=1, source_target_pairs={{8,0},{0,8},{16,24},{24,16},{9,1},{1,9},{17,25},{25,17},{10,2},{2,... | collective-permute-start | bytes 798728 | tf_op jit(solution)/shard_map/ppermute | solution.py:329
  87.8 0.7 copy-start.9
  88.6 9.6 %collective-permute-start.20 = (s16[1,1040,128]{2,1,0:T(8,128)(2,1)S(1)}, s16[1,1040,128]{2,1,0:T(8,128)(2,1)}, u32[]{:S(2)}, u32[]{:S(2)}) collective-permute-start(s16[1,1040,128]{2,1,0:T(8,128)(2,1)S(1)} %hop.15.refs_0_), channel_id=1, source_target_pairs={{8,0},{0,8},{16,24},{24,16},{9,1},{1,9},{17,25},{25,17},{10,2},{2,... | collective-permute-start | bytes 798728 | tf_op jit(solution)/shard_map/ppermute | solution.py:329
  88.7 1.0 copy-start.10
  90.5 7.7 %collective-permute-start.22 = (s16[1,1040,128]{2,1,0:T(8,128)(2,1)S(1)}, s16[1,1040,128]{2,1,0:T(8,128)(2,1)}, u32[]{:S(2)}, u32[]{:S(2)}) collective-permute-start(s16[1,1040,128]{2,1,0:T(8,128)(2,1)S(1)} %hop.16.refs_0_), channel_id=1, source_target_pairs={{8,16},{16,8},{9,17},{17,9},{10,18},{18,10},{11,19},{19,11},{12,20... | collective-permute-start | bytes 798728 | tf_op jit(solution)/shard_map/ppermute | solution.py:329
  93.6 7.3 %collective-permute-start.24 = (s16[1,1040,128]{2,1,0:T(8,128)(2,1)S(1)}, s16[1,1040,128]{2,1,0:T(8,128)(2,1)S(1)}, u32[]{:S(2)}, u32[]{:S(2)}) collective-permute-start(s16[1,1040,128]{2,1,0:T(8,128)(2,1)S(1)} %hop.17), channel_id=1, source_target_pairs={{8,0},{0,8},{16,24},{24,16},{9,1},{1,9},{17,25},{25,17},{10,2},{2,... | collective-permute-start | bytes 798728 | tf_op jit(solution)/shard_map/ppermute | solution.py:329
  100.9 0.8 copy-start.14

commit v6 on v5

--- a/solution.py
+++ b/solution.py
@@ -432,7 +432,10 @@
     for step in ctf_part.hops[:early]:
         tie = step(ties=(tie,))
     imag_part, coded, _ = volume(imag_there, meta, (tie,))
-    steps = real_part.hops[:-1] + imag_part.hops[:1] + ctf_part.hops[early:] + real_part.hops[-1:] + imag_part.hops[1:]
+    left = imag_part.hops[1:]
+    if groups == 4:
+        left = left[::-1]
+    steps = real_part.hops[:-1] + imag_part.hops[:1] + ctf_part.hops[early:] + real_part.hops[-1:] + left
     tie = coded
     for step in steps:
         tie = step(ties=(tie,))

time: 107 us -> 106 us (level)
  starting transfers between devices: 44.6 us -> 42.7 us
  local copies, waits for them, and re-layouts: 6.2 us -> 4.32 us
  waiting for transfers between devices: 9.88 us -> 11.2 us
  Pallas kernels: 44.7 us -> 46 us
    ppermute x15, starting transfers between devices: 29.8 us -> 28 us  [send(): lax.ppermute(payload, 'grp', pairs + [(last - a, last - b) for a, b in pa...]
    unnamed x40 -> x36, local copies, waits for them, and re-layouts: 5.53 us -> 3.74 us
    ppermute x15, waiting for transfers between devices: 4.22 us -> 5.74 us  [send(): lax.ppermute(payload, 'grp', pairs + [(last - a, last - b) for a, b in pa...]
  transfers between devices with their start and end apart: 27 -> 27, of which waited for: 5 -> 6; matrix products, arithmetic and copies ran while one was open for 1% -> 1% of each run, Pallas kernels for 37% -> 39%
where the time goes in v6:
time: 106 us; the launch traced here: 105 us
  Pallas kernels  46 us (43%)
  starting transfers between devices  42.7 us (40%)
  waiting for transfers between devices  11.2 us (11%)
  local copies, waits for them, and re-layouts  4.32 us (4%)
    ppermute x15, starting transfers between devices, send(): lax.ppermute(payload, 'grp', pairs + [(last - a, last - b) for a, b in pa...  28 us
    pallas_call x3, Pallas kernels, volume_sums(): pl.pallas_call(functools.partial(volume_kernel, slabs, window, messages,...  20 us
    ppermute x12, starting transfers between devices, swap(): return lax.ppermute(x, 'slab', [(i, i ^ offset) for i in range(slabs)])  14.6 us
    pallas_call x9, Pallas kernels, hop(): pl.pallas_call(functools.partial(hop_kernel, places), out_shape=jax.Shape...  11.5 us
    pallas_call x2, Pallas kernels, sort_columns(): pl.pallas_call(functools.partial(sort_kernel, slabs, width, part, len(tie...  6.34 us
    ppermute x15, waiting for transfers between devices, send(): lax.ppermute(payload, 'grp', pairs + [(last - a, last - b) for a, b in pa...  5.74 us
    ppermute x12, waiting for transfers between devices, swap(): return lax.ppermute(x, 'slab', [(i, i ^ offset) for i in range(slabs)])  5.42 us
    pallas_call x1, Pallas kernels, image_of(): pl.pallas_call(functools.partial(image_kernel, parts, zs), out_shape=jax....  4.77 us
  transfers between devices with their start and end apart: 27, of which 6 were waited for; matrix products, arithmetic and copies ran while one was open for 1% of the time, Pallas kernels for 39%

profile of v6, /device:TPU:0, one launch (start us, length us, event | category | flops | bytes accessed | tf_op | source)
XLA Modules:
  0.0 105.2 jit_solution(2976058256373986368)
XLA Ops:
  0.5 0.7 pad_add_fusion.refs_0_
  1.8 3.2 %collective-permute-done.refs_1_ = s32[3,512]{1,0:T(4,128)S(1)} collective-permute-done((s32[3,512]{1,0:T(4,128)S(1)}, s32[3,512]{1,0:T(4,128)S(1)}, u32[]{:S(2)}, u32[]{:S(2)}) %collective-permute-start) | collective-permute-done | bytes 6176 | tf_op jit(solution)/shard_map/ppermute | solution.py:147
  5.0 0.9 collective-permute-done.1.refs_4_
  5.9 3.4 %plan_rows.1 = (bf16[2,512,512]{2,1,0:T(8,128)(2,1)S(1)}, bf16[1152,128]{1,0:T(8,128)(2,1)S(1)}, bf16[1152,128]{1,0:T(8,128)(2,1)S(1)}, bf16[1152,128]{1,0:T(8,128)(2,1)S(1)}, bf16[1152,128]{1,0:T(8,128)(2,1)S(1)}) custom-call(s32[1]{0:T(128)} %bitcast.1.me_ref, s32[3,512]{1,0:T(4,128)} %copy-done.16, s32[3,512]{1,0:T(4,128)S(1)} %collective-permute-done.refs_1_, ...), custom_call_target="tpu_custom_call" | custom-call | bytes 18000000 | tf_op jit(solution)/shard_map/plan_rows/pallas_call | solution.py:101
  9.3 2.6 %collective-permute-start.3 = (bf16[1152,128]{1,0:T(8,128)(2,1)S(1)}, bf16[1152,128]{1,0:T(8,128)(2,1)S(1)}, u32[]{:S(2)}, u32[]{:S(2)}) collective-permute-start(bf16[1152,128]{1,0:T(8,128)(2,1)S(1)} %get-tuple-element.32), channel_id=1, source_target_pairs={{0,2},{1,3},{2,0},{3,1},{4,6},{5,7},{6,4},{7,5},{8,10},{9,11},{10,... | collective-permute-start | bytes 884744 | tf_op jit(solution)/shard_map/ppermute | solution.py:147
  11.9 1.5 %collective-permute-start.4 = (bf16[1152,128]{1,0:T(8,128)(2,1)S(1)}, bf16[1152,128]{1,0:T(8,128)(2,1)S(1)}, u32[]{:S(2)}, u32[]{:S(2)}) collective-permute-start(bf16[1152,128]{1,0:T(8,128)(2,1)S(1)} %get-tuple-element.33), channel_id=1, source_target_pairs={{0,4},{1,5},{2,6},{3,7},{4,0},{5,1},{6,2},{7,3},{8,12},{9,13},{10,... | collective-permute-start | bytes 884744 | tf_op jit(solution)/shard_map/ppermute | solution.py:147
  13.5 3.5 %sort_columns.2 = (bf16[1024,128]{1,0:T(8,128)(2,1)S(1)}, bf16[1024,128]{1,0:T(8,128)(2,1)}, bf16[1024,128]{1,0:T(8,128)(2,1)}, bf16[1024,128]{1,0:T(8,128)(2,1)}) custom-call(s32[1]{0:T(128)} %bitcast.1.me_ref, bf16[2,512,512]{2,1,0:T(8,128)(2,1)S(1)} %get-tuple-element.28.order_ref, bf16[512,2048]{1,0:T(8,128)(2,1)} %refs_0_.3, ...), custom_call_target="tpu_custom_call" | custom-call | bytes 9000000 | tf_op jit(solution)/shard_map/sort_columns/pallas_call | solution.py:131
  17.0 2.0 %collective-permute-start.6 = (bf16[1024,128]{1,0:T(8,128)(2,1)}, bf16[1024,128]{1,0:T(8,128)(2,1)}, u32[]{:S(2)}, u32[]{:S(2)}) collective-permute-start(bf16[1024,128]{1,0:T(8,128)(2,1)} %get-tuple-element.36), channel_id=1, source_target_pairs={{0,2},{1,3},{2,0},{3,1},{4,6},{5,7},{6,4},{7,5},{8,10},{9,11},{10,... | collective-permute-start | bytes 786440 | tf_op jit(solution)/shard_map/ppermute | solution.py:147
  18.9 1.5 %collective-permute-start.7 = (bf16[1024,128]{1,0:T(8,128)(2,1)}, bf16[1024,128]{1,0:T(8,128)(2,1)}, u32[]{:S(2)}, u32[]{:S(2)}) collective-permute-start(bf16[1024,128]{1,0:T(8,128)(2,1)} %get-tuple-element.37), channel_id=1, source_target_pairs={{0,4},{1,5},{2,6},{3,7},{4,0},{5,1},{6,2},{7,3},{8,12},{9,13},{10,... | collective-permute-start | bytes 786440 | tf_op jit(solution)/shard_map/ppermute | solution.py:147
  20.5 0.7 copy-done.9
  21.2 2.2 %collective-permute-start.8 = (bf16[1024,128]{1,0:T(8,128)(2,1)}, bf16[1024,128]{1,0:T(8,128)(2,1)}, u32[]{:S(2)}, u32[]{:S(2)}) collective-permute-start(bf16[1024,128]{1,0:T(8,128)(2,1)} %get-tuple-element.38), channel_id=1, source_target_pairs={{0,6},{1,7},{2,4},{3,5},{4,2},{5,3},{6,0},{7,1},{8,14},{9,15},{10,... | collective-permute-start | bytes 786440 | tf_op jit(solution)/shard_map/ppermute | solution.py:147
  23.4 2.8 %sort_columns.3 = (bf16[1024,128]{1,0:T(8,128)(2,1)S(1)}, bf16[1024,128]{1,0:T(8,128)(2,1)S(1)}, bf16[1024,128]{1,0:T(8,128)(2,1)S(1)}, bf16[1024,128]{1,0:T(8,128)(2,1)S(1)}) custom-call(s32[1]{0:T(128)} %bitcast.1.me_ref, bf16[2,512,512]{2,1,0:T(8,128)(2,1)S(1)} %get-tuple-element.28.order_ref, bf16[512,2048]{1,0:T(8,128)(2,1)} %refs_0_.3, ...), custom_call_target="tpu_custom_call" | custom-call | bytes 9000000 | tf_op jit(solution)/shard_map/sort_columns/pallas_call | solution.py:131
  26.3 1.2 %collective-permute-done.4.refs_3_ = bf16[1152,128]{1,0:T(8,128)(2,1)S(1)} collective-permute-done((bf16[1152,128]{1,0:T(8,128)(2,1)S(1)}, bf16[1152,128]{1,0:T(8,128)(2,1)S(1)}, u32[]{:S(2)}, u32[]{:S(2)}) %collective-permute-start.4) | collective-permute-done | bytes 294944 | tf_op jit(solution)/shard_map/ppermute | solution.py:147
  28.3 6.6 %volume_sums.3 = (f32[16,8,32,128]{3,2,1,0:T(8,128)S(1)}, bf16[8,16,512]{2,1,0:T(8,128)(2,1)S(1)}, s16[1,1040,128]{2,1,0:T(8,128)(2,1)S(1)}, s16[1,1040,128]{2,1,0:T(8,128)(2,1)S(1)}) custom-call(s32[2]{0:T(128)S(1)} %broadcast_select_fusion.idx_ref, bf16[1024,128]{1,0:T(8,128)(2,1)S(1)} %get-tuple-element.30.refs_0_.refs_1_, bf16[1152,128]{1,0:T(8,128)(2,1)} %copy-done.8, ...), custom_call_target="tpu_custom_call" | custom-call | bytes 21000000 | tf_op jit(solution)/shard_map/volume_sums/pallas_call | solution.py:224
  34.9 3.5 %collective-permute-start.12 = (s16[1,1040,128]{2,1,0:T(8,128)(2,1)S(1)}, s16[1,1040,128]{2,1,0:T(8,128)(2,1)S(1)}, u32[]{:S(2)}, u32[]{:S(2)}) collective-permute-start(s16[1,1040,128]{2,1,0:T(8,128)(2,1)S(1)} %get-tuple-element.35.refs_0_), channel_id=1, source_target_pairs={{0,8},{24,16},{1,9},{25,17},{2,10},{26,18},{3,11},{27,19},{4,12},{... | collective-permute-start | bytes 798728 | tf_op jit(solution)/shard_map/ppermute | solution.py:329
  38.4 1.5 %collective-permute-start.11 = (s16[1,1040,128]{2,1,0:T(8,128)(2,1)S(1)}, s16[1,1040,128]{2,1,0:T(8,128)(2,1)S(1)}, u32[]{:S(2)}, u32[]{:S(2)}) collective-permute-start(s16[1,1040,128]{2,1,0:T(8,128)(2,1)S(1)} %get-tuple-element.44), channel_id=1, source_target_pairs={{0,8},{24,16},{1,9},{25,17},{2,10},{26,18},{3,11},{27,19},{4,12},{... | collective-permute-start | bytes 798728 | tf_op jit(solution)/shard_map/ppermute | solution.py:329
  39.9 1.5 %collective-permute-start.13 = (bf16[1024,128]{1,0:T(8,128)(2,1)S(1)}, bf16[1024,128]{1,0:T(8,128)(2,1)S(1)}, u32[]{:S(2)}, u32[]{:S(2)}) collective-permute-start(bf16[1024,128]{1,0:T(8,128)(2,1)S(1)} %get-tuple-element.45), channel_id=1, source_target_pairs={{0,2},{1,3},{2,0},{3,1},{4,6},{5,7},{6,4},{7,5},{8,10},{9,11},{10,... | collective-permute-start | bytes 786440 | tf_op jit(solution)/shard_map/ppermute | solution.py:147
  41.4 0.8 collective-permute-start.14
  42.2 1.4 %collective-permute-start.15 = (bf16[1024,128]{1,0:T(8,128)(2,1)S(1)}, bf16[1024,128]{1,0:T(8,128)(2,1)S(1)}, u32[]{:S(2)}, u32[]{:S(2)}) collective-permute-start(bf16[1024,128]{1,0:T(8,128)(2,1)S(1)} %get-tuple-element.47), channel_id=1, source_target_pairs={{0,6},{1,7},{2,4},{3,5},{4,2},{5,3},{6,0},{7,1},{8,14},{9,15},{10,... | collective-permute-start | bytes 786440 | tf_op jit(solution)/shard_map/ppermute | solution.py:147
  43.6 6.5 %volume_sums.4 = (f32[16,8,32,128]{3,2,1,0:T(8,128)S(1)}, s16[1,1040,128]{2,1,0:T(8,128)(2,1)S(1)}, s16[1,1040,128]{2,1,0:T(8,128)(2,1)S(1)}) custom-call(s32[2]{0:T(128)S(1)} %broadcast_select_fusion.idx_ref, s16[1,1040,128]{2,1,0:T(8,128)(2,1)S(1)} %get-tuple-element.35.refs_0_, bf16[1024,128]{1,0:T(8,128)(2,1)} %copy-done.6, ...), custom_call_target="tpu_custom_call" | custom-call | bytes 21000000 | tf_op jit(solution)/shard_map/volume_sums/pallas_call | solution.py:224
  50.2 1.3 %collective-permute-start.10 = (s16[1,1040,128]{2,1,0:T(8,128)(2,1)S(1)}, s16[1,1040,128]{2,1,0:T(8,128)(2,1)S(1)}, u32[]{:S(2)}, u32[]{:S(2)}) collective-permute-start(s16[1,1040,128]{2,1,0:T(8,128)(2,1)S(1)} %get-tuple-element.42.refs_0_), channel_id=1, source_target_pairs={{0,8},{24,16},{1,9},{25,17},{2,10},{26,18},{3,11},{27,19},{4,12},{... | collective-permute-start | bytes 798728 | tf_op jit(solution)/shard_map/ppermute | solution.py:329
  51.5 0.8 hop.9.refs_0_
  52.3 1.3 %collective-permute-start.9 = (s16[1,1040,128]{2,1,0:T(8,128)(2,1)S(1)}, s16[1,1040,128]{2,1,0:T(8,128)(2,1)S(1)}, u32[]{:S(2)}, u32[]{:S(2)}) collective-permute-start(s16[1,1040,128]{2,1,0:T(8,128)(2,1)S(1)} %get-tuple-element.41), channel_id=1, source_target_pairs={{0,8},{24,16},{1,9},{25,17},{2,10},{26,18},{3,11},{27,19},{4,12},{... | collective-permute-start | bytes 798728 | tf_op jit(solution)/shard_map/ppermute | solution.py:329
  53.6 0.8 hop.10.refs_0_
  54.4 0.7 copy-done.13
  55.2 0.7 copy-done.15
  55.9 7.0 %volume_sums.5 = (f32[16,8,32,128]{3,2,1,0:T(8,128)S(1)}, s16[1,1040,128]{2,1,0:T(8,128)(2,1)S(1)}, s16[1,1040,128]{2,1,0:T(8,128)(2,1)}) custom-call(s32[2]{0:T(128)S(1)} %broadcast_select_fusion.idx_ref, s16[1,1040,128]{2,1,0:T(8,128)(2,1)S(1)} %hop.10.refs_0_, bf16[1024,128]{1,0:T(8,128)(2,1)} %copy-done.7, bf16[1024,128]{1,0:T(8,128)(2,1)} %copy-done.13, ...), custom_call_target="tpu_custom_call" | custom-call | bytes 21000000 | tf_op jit(solution)/shard_map/volume_sums/pallas_call | solution.py:224
  62.9 1.3 %collective-permute-start.19 = (s16[1,1040,128]{2,1,0:T(8,128)(2,1)S(1)}, s16[1,1040,128]{2,1,0:T(8,128)(2,1)S(1)}, u32[]{:S(2)}, u32[]{:S(2)}) collective-permute-start(s16[1,1040,128]{2,1,0:T(8,128)(2,1)S(1)} %get-tuple-element.48.refs_0_), channel_id=1, source_target_pairs={{0,8},{24,16},{1,9},{25,17},{2,10},{26,18},{3,11},{27,19},{4,12},{... | collective-permute-start | bytes 798728 | tf_op jit(solution)/shard_map/ppermute | solution.py:329
  64.2 1.4 %collective-permute-start.18 = (s16[1,1040,128]{2,1,0:T(8,128)(2,1)S(1)}, s16[1,1040,128]{2,1,0:T(8,128)(2,1)}, u32[]{:S(2)}, u32[]{:S(2)}) collective-permute-start(s16[1,1040,128]{2,1,0:T(8,128)(2,1)S(1)} %hop.9.refs_0_), channel_id=1, source_target_pairs={{8,16},{16,8},{9,17},{17,9},{10,18},{18,10},{11,19},{19,11},{12,20... | collective-permute-start | bytes 798728 | tf_op jit(solution)/shard_map/ppermute | solution.py:329
  65.6 0.8 hop.11.refs_0_
  66.4 1.4 %collective-permute-start.17 = (s16[1,1040,128]{2,1,0:T(8,128)(2,1)S(1)}, s16[1,1040,128]{2,1,0:T(8,128)(2,1)}, u32[]{:S(2)}, u32[]{:S(2)}) collective-permute-start(s16[1,1040,128]{2,1,0:T(8,128)(2,1)S(1)} %hop.11.refs_0_), channel_id=1, source_target_pairs={{8,16},{16,8},{9,17},{17,9},{10,18},{18,10},{11,19},{19,11},{12,20... | collective-permute-start | bytes 798728 | tf_op jit(solution)/shard_map/ppermute | solution.py:329
  67.8 0.8 hop.12.refs_0_
  68.6 0.8 hop.13.refs_0_
  69.3 1.4 %collective-permute-start.21 = (s16[1,1040,128]{2,1,0:T(8,128)(2,1)S(1)}, s16[1,1040,128]{2,1,0:T(8,128)(2,1)}, u32[]{:S(2)}, u32[]{:S(2)}) collective-permute-start(s16[1,1040,128]{2,1,0:T(8,128)(2,1)S(1)} %hop.13.refs_0_), channel_id=1, source_target_pairs={{8,16},{16,8},{9,17},{17,9},{10,18},{18,10},{11,19},{19,11},{12,20... | collective-permute-start | bytes 798728 | tf_op jit(solution)/shard_map/ppermute | solution.py:329
  70.8 7.4 %collective-permute-start.23 = (s16[1,1040,128]{2,1,0:T(8,128)(2,1)}, s16[1,1040,128]{2,1,0:T(8,128)(2,1)}, u32[]{:S(2)}, u32[]{:S(2)}) collective-permute-start(s16[1,1040,128]{2,1,0:T(8,128)(2,1)} %get-tuple-element.50), channel_id=1, source_target_pairs={{0,8},{24,16},{1,9},{25,17},{2,10},{26,18},{3,11},{27,19},{4,12},{... | collective-permute-start | bytes 798728 | tf_op jit(solution)/shard_map/ppermute | solution.py:329
  78.1 1.4 %collective-permute-start.25 = (s16[1,1040,128]{2,1,0:T(8,128)(2,1)S(1)}, s16[1,1040,128]{2,1,0:T(8,128)(2,1)}, u32[]{:S(2)}, u32[]{:S(2)}) collective-permute-start(s16[1,1040,128]{2,1,0:T(8,128)(2,1)S(1)} %hop.10.refs_0_), channel_id=1, source_target_pairs={{8,16},{16,8},{9,17},{17,9},{10,18},{18,10},{11,19},{19,11},{12,20... | collective-permute-start | bytes 798728 | tf_op jit(solution)/shard_map/ppermute | solution.py:329
  79.5 1.5 %collective-permute-start.16 = (s16[1,1040,128]{2,1,0:T(8,128)(2,1)S(1)}, s16[1,1040,128]{2,1,0:T(8,128)(2,1)}, u32[]{:S(2)}, u32[]{:S(2)}) collective-permute-start(s16[1,1040,128]{2,1,0:T(8,128)(2,1)S(1)} %hop.12.refs_0_), channel_id=1, source_target_pairs={{8,16},{16,8},{9,17},{17,9},{10,18},{18,10},{11,19},{19,11},{12,20... | collective-permute-start | bytes 798728 | tf_op jit(solution)/shard_map/ppermute | solution.py:329
  81.0 1.7 %hop.14.refs_0_ = s16[1,1040,128]{2,1,0:T(8,128)(2,1)S(1)} custom-call(s32[1]{0:T(128)S(6)} %select_n.51.idx_ref, f32[4,1024,128]{2,1,0:T(8,128)S(1)} %bitcast.15, s16[1,1040,128]{2,1,0:T(8,128)(2,1)} %collective-permute-done.18.prev_ref, s16[1,1040,128]{2,1,0:T(8,128)(2,1)S(1)} %hop.13.refs_0_), custom_call_target="tpu_custom_call" | custom-call | bytes 9000000 | tf_op jit(solution)/shard_map/hop/pallas_call | solution.py:289
  82.8 1.9 %collective-permute-start.26 = (s16[1,1040,128]{2,1,0:T(8,128)(2,1)S(1)}, s16[1,1040,128]{2,1,0:T(8,128)(2,1)}, u32[]{:S(2)}, u32[]{:S(2)}) collective-permute-start(s16[1,1040,128]{2,1,0:T(8,128)(2,1)S(1)} %hop.14.refs_0_), channel_id=1, source_target_pairs={{8,0},{0,8},{16,24},{24,16},{9,1},{1,9},{17,25},{25,17},{10,2},{2,... | collective-permute-start | bytes 798728 | tf_op jit(solution)/shard_map/ppermute | solution.py:329
  84.7 1.7 %hop.15.refs_0_ = s16[1,1040,128]{2,1,0:T(8,128)(2,1)S(1)} custom-call(s32[1]{0:T(128)S(6)} %select_n.51.idx_ref, f32[4,1024,128]{2,1,0:T(8,128)S(1)} %bitcast.20, s16[1,1040,128]{2,1,0:T(8,128)(2,1)} %collective-permute-done.17.prev_ref, s16[1,1040,128]{2,1,0:T(8,128)(2,1)S(1)} %hop.14.refs_0_), custom_call_target="tpu_custom_call" | custom-call | bytes 9000000 | tf_op jit(solution)/shard_map/hop/pallas_call | solution.py:289
  86.8 1.7 %hop.16.refs_0_ = s16[1,1040,128]{2,1,0:T(8,128)(2,1)S(1)} custom-call(s32[1]{0:T(128)S(6)} %select_n.51.idx_ref, f32[4,1024,128]{2,1,0:T(8,128)S(1)} %bitcast.23, s16[1,1040,128]{2,1,0:T(8,128)(2,1)} %collective-permute-done.21.prev_ref, s16[1,1040,128]{2,1,0:T(8,128)(2,1)S(1)} %hop.15.refs_0_), custom_call_target="tpu_custom_call" | custom-call | bytes 9000000 | tf_op jit(solution)/shard_map/hop/pallas_call | solution.py:289
  88.5 1.8 %collective-permute-start.22 = (s16[1,1040,128]{2,1,0:T(8,128)(2,1)S(1)}, s16[1,1040,128]{2,1,0:T(8,128)(2,1)}, u32[]{:S(2)}, u32[]{:S(2)}) collective-permute-start(s16[1,1040,128]{2,1,0:T(8,128)(2,1)S(1)} %hop.16.refs_0_), channel_id=1, source_target_pairs={{8,0},{0,8},{16,24},{24,16},{9,1},{1,9},{17,25},{25,17},{10,2},{2,... | collective-permute-start | bytes 798728 | tf_op jit(solution)/shard_map/ppermute | solution.py:329
  90.3 2.4 %hop.17 = s16[1,1040,128]{2,1,0:T(8,128)(2,1)} custom-call(s32[1]{0:T(128)S(6)} %select_n.48.idx_ref, f32[4,1024,128]{2,1,0:T(8,128)S(1)} %bitcast.24, s16[1,1040,128]{2,1,0:T(8,128)(2,1)} %collective-permute-done.23.prev_ref, s16[1,1040,128]{2,1,0:T(8,128)(2,1)S(1)} %hop.16.refs_0_), custom_call_target="tpu_custom_call" | custom-call | bytes 9000000 | tf_op jit(solution)/shard_map/hop/pallas_call | solution.py:289
  92.7 0.7 collective-permute-start.24
  94.0 2.9 %collective-permute-done.20.refs_2_ = s16[1,1040,128]{2,1,0:T(8,128)(2,1)} collective-permute-done((s16[1,1040,128]{2,1,0:T(8,128)(2,1)S(1)}, s16[1,1040,128]{2,1,0:T(8,128)(2,1)}, u32[]{:S(2)}, u32[]{:S(2)}) %collective-permute-start.20) | collective-permute-done | bytes 266272 | tf_op jit(solution)/shard_map/ppermute | solution.py:329
  96.9 2.9 %collective-permute-done.22.refs_4_ = s16[1,1040,128]{2,1,0:T(8,128)(2,1)} collective-permute-done((s16[1,1040,128]{2,1,0:T(8,128)(2,1)S(1)}, s16[1,1040,128]{2,1,0:T(8,128)(2,1)}, u32[]{:S(2)}, u32[]{:S(2)}) %collective-permute-start.22) | collective-permute-done | bytes 266272 | tf_op jit(solution)/shard_map/ppermute | solution.py:329
  99.7 0.7 copy-done.12
  100.4 4.8 %image_of.1 = f32[2,4,256,128]{3,2,1,0:T(8,128)} custom-call(s32[1]{0:T(128)} %bitcast.own_ref, f32[4,1024,128]{2,1,0:T(8,128)} %bitcast.19, s16[1,1040,128]{2,1,0:T(8,128)(2,1)} %collective-permute-done.16.refs_1_, s16[1,1040,128]{2,1,0:T(8,128)(2,1)} %collective-permute-done.20.refs_2_, f32[4,1024,128]{2,1,0:T(8,128)} %bitcast.22, ...), custom_call_target="tpu_custom_call" | custom-call | bytes 18000000 | tf_op jit(solution)/shard_map/image_of/pallas_call | solution.py:391
  (61 shorter events, 3.1 us)
Async XLA Ops:
  0.0 93.4 %copy-start = (f32[1024]{0:T(1024)S(1)}, f32[1024]{0:T(1024)}, u32[]{:S(2)}) copy-start(f32[1024]{0:T(1024)} %param.17) | copy-start | bytes 12292
  0.0 13.5 %collective-permute-start.2 = (bf16[512,2048]{1,0:T(8,128)(2,1)}, bf16[512,2048]{1,0:T(8,128)(2,1)}, u32[]{:S(2)}, u32[]{:S(2)}) collective-permute-start(bf16[512,2048]{1,0:T(8,128)(2,1)} %refs_0_.3), channel_id=1, source_target_pairs={{0,1},{1,0},{2,3},{3,2},{4,5},{5,4},{6,7},{7,6},{8,9},{9,8},{10,11... | collective-permute-start | bytes 6291464 | tf_op jit(solution)/shard_map/ppermute | solution.py:147
  0.5 5.4 %collective-permute-start.1 = (bf16[512,1024]{1,0:T(8,128)(2,1)}, bf16[512,1024]{1,0:T(8,128)(2,1)S(1)}, u32[]{:S(2)}, u32[]{:S(2)}) collective-permute-start(bf16[512,1024]{1,0:T(8,128)(2,1)} %refs_3_.1), channel_id=1, source_target_pairs={{0,1},{1,0},{2,3},{3,2},{4,5},{5,4},{6,7},{7,6},{8,9},{9,8},{10,11... | collective-permute-start | bytes 3145736 | tf_op jit(solution)/shard_map/ppermute | solution.py:147
  1.3 4.6 %copy-start.16 = (s32[3,512]{1,0:T(4,128)}, s32[3,512]{1,0:T(4,128)S(1)}, u32[]{:S(2)}) copy-start(s32[3,512]{1,0:T(4,128)S(1)} %pad_add_fusion.refs_0_) | copy-start | bytes 18436
  1.3 3.7 %collective-permute-start = (s32[3,512]{1,0:T(4,128)S(1)}, s32[3,512]{1,0:T(4,128)S(1)}, u32[]{:S(2)}, u32[]{:S(2)}) collective-permute-start(s32[3,512]{1,0:T(4,128)S(1)} %pad_add_fusion.refs_0_), channel_id=1, source_target_pairs={{0,1},{1,0},{2,3},{3,2},{4,5},{5,4},{6,7},{7,6},{8,9},{9,8},{10,11... | collective-permute-start | bytes 18440 | tf_op jit(solution)/shard_map/ppermute | solution.py:147
  9.3 7.7 %copy-start.8 = (bf16[1152,128]{1,0:T(8,128)(2,1)}, bf16[1152,128]{1,0:T(8,128)(2,1)S(1)}, u32[]{:S(2)}) copy-start(bf16[1152,128]{1,0:T(8,128)(2,1)S(1)} %get-tuple-element.31.refs_1_) | copy-start | bytes 884740
  9.3 11.2 %collective-permute-start.3 = (bf16[1152,128]{1,0:T(8,128)(2,1)S(1)}, bf16[1152,128]{1,0:T(8,128)(2,1)S(1)}, u32[]{:S(2)}, u32[]{:S(2)}) collective-permute-start(bf16[1152,128]{1,0:T(8,128)(2,1)S(1)} %get-tuple-element.32), channel_id=1, source_target_pairs={{0,2},{1,3},{2,0},{3,1},{4,6},{5,7},{6,4},{7,5},{8,10},{9,11},{10,... | collective-permute-start | bytes 884744 | tf_op jit(solution)/shard_map/ppermute | solution.py:147
  11.9 15.5 %collective-permute-start.4 = (bf16[1152,128]{1,0:T(8,128)(2,1)S(1)}, bf16[1152,128]{1,0:T(8,128)(2,1)S(1)}, u32[]{:S(2)}, u32[]{:S(2)}) collective-permute-start(bf16[1152,128]{1,0:T(8,128)(2,1)S(1)} %get-tuple-element.33), channel_id=1, source_target_pairs={{0,4},{1,5},{2,6},{3,7},{4,0},{5,1},{6,2},{7,3},{8,12},{9,13},{10,... | collective-permute-start | bytes 884744 | tf_op jit(solution)/shard_map/ppermute | solution.py:147
  13.4 14.1 %collective-permute-start.5 = (bf16[1152,128]{1,0:T(8,128)(2,1)S(1)}, bf16[1152,128]{1,0:T(8,128)(2,1)S(1)}, u32[]{:S(2)}, u32[]{:S(2)}) collective-permute-start(bf16[1152,128]{1,0:T(8,128)(2,1)S(1)} %get-tuple-element.34), channel_id=1, source_target_pairs={{0,6},{1,7},{2,4},{3,5},{4,2},{5,3},{6,0},{7,1},{8,14},{9,15},{10,... | collective-permute-start | bytes 884744 | tf_op jit(solution)/shard_map/ppermute | solution.py:147
  13.5 10.0 %copy-start.17 = (s32[2]{0:T(128)S(1)}, s32[2]{0:T(128)}, u32[]{:S(2)}) copy-start(s32[2]{0:T(128)} %constant.36.clone) | copy-start | bytes 28
  17.0 9.3 %copy-start.6 = (bf16[1024,128]{1,0:T(8,128)(2,1)}, bf16[1024,128]{1,0:T(8,128)(2,1)S(1)}, u32[]{:S(2)}) copy-start(bf16[1024,128]{1,0:T(8,128)(2,1)S(1)} %get-tuple-element.29.refs_2_.refs_1_) | copy-start | bytes 786436
  17.0 22.9 %collective-permute-start.6 = (bf16[1024,128]{1,0:T(8,128)(2,1)}, bf16[1024,128]{1,0:T(8,128)(2,1)}, u32[]{:S(2)}, u32[]{:S(2)}) collective-permute-start(bf16[1024,128]{1,0:T(8,128)(2,1)} %get-tuple-element.36), channel_id=1, source_target_pairs={{0,2},{1,3},{2,0},{3,1},{4,6},{5,7},{6,4},{7,5},{8,10},{9,11},{10,... | collective-permute-start | bytes 786440 | tf_op jit(solution)/shard_map/ppermute | solution.py:147
  18.9 22.5 %collective-permute-start.7 = (bf16[1024,128]{1,0:T(8,128)(2,1)}, bf16[1024,128]{1,0:T(8,128)(2,1)}, u32[]{:S(2)}, u32[]{:S(2)}) collective-permute-start(bf16[1024,128]{1,0:T(8,128)(2,1)} %get-tuple-element.37), channel_id=1, source_target_pairs={{0,4},{1,5},{2,6},{3,7},{4,0},{5,1},{6,2},{7,3},{8,12},{9,13},{10,... | collective-permute-start | bytes 786440 | tf_op jit(solution)/shard_map/ppermute | solution.py:147
  20.5 0.7 copy-start.9
  21.2 21.0 %collective-permute-start.8 = (bf16[1024,128]{1,0:T(8,128)(2,1)}, bf16[1024,128]{1,0:T(8,128)(2,1)}, u32[]{:S(2)}, u32[]{:S(2)}) collective-permute-start(bf16[1024,128]{1,0:T(8,128)(2,1)} %get-tuple-element.38), channel_id=1, source_target_pairs={{0,6},{1,7},{2,4},{3,5},{4,2},{5,3},{6,0},{7,1},{8,14},{9,15},{10,... | collective-permute-start | bytes 786440 | tf_op jit(solution)/shard_map/ppermute | solution.py:147
  26.3 26.0 %copy-start.7 = (bf16[1024,128]{1,0:T(8,128)(2,1)}, bf16[1024,128]{1,0:T(8,128)(2,1)S(1)}, u32[]{:S(2)}) copy-start(bf16[1024,128]{1,0:T(8,128)(2,1)S(1)} %get-tuple-element.30.refs_0_.refs_1_) | copy-start | bytes 786436
  27.5 0.7 copy-start.10
  27.6 0.7 copy-start.11
  34.9 46.2 %copy-start.1 = (f32[16,8,32,128]{3,2,1,0:T(8,128)}, f32[16,8,32,128]{3,2,1,0:T(8,128)S(1)}, u32[]{:S(2)}) copy-start(f32[16,8,32,128]{3,2,1,0:T(8,128)S(1)} %get-tuple-element.43) | copy-start | bytes 6291460
  34.9 15.3 %collective-permute-start.12 = (s16[1,1040,128]{2,1,0:T(8,128)(2,1)S(1)}, s16[1,1040,128]{2,1,0:T(8,128)(2,1)S(1)}, u32[]{:S(2)}, u32[]{:S(2)}) collective-permute-start(s16[1,1040,128]{2,1,0:T(8,128)(2,1)S(1)} %get-tuple-element.35.refs_0_), channel_id=1, source_target_pairs={{0,8},{24,16},{1,9},{25,17},{2,10},{26,18},{3,11},{27,19},{4,12},{... | collective-permute-start | bytes 798728 | tf_op jit(solution)/shard_map/ppermute | solution.py:329
  38.4 13.9 %collective-permute-start.11 = (s16[1,1040,128]{2,1,0:T(8,128)(2,1)S(1)}, s16[1,1040,128]{2,1,0:T(8,128)(2,1)S(1)}, u32[]{:S(2)}, u32[]{:S(2)}) collective-permute-start(s16[1,1040,128]{2,1,0:T(8,128)(2,1)S(1)} %get-tuple-element.44), channel_id=1, source_target_pairs={{0,8},{24,16},{1,9},{25,17},{2,10},{26,18},{3,11},{27,19},{4,12},{... | collective-permute-start | bytes 798728 | tf_op jit(solution)/shard_map/ppermute | solution.py:329
  39.9 14.5 %collective-permute-start.13 = (bf16[1024,128]{1,0:T(8,128)(2,1)S(1)}, bf16[1024,128]{1,0:T(8,128)(2,1)S(1)}, u32[]{:S(2)}, u32[]{:S(2)}) collective-permute-start(bf16[1024,128]{1,0:T(8,128)(2,1)S(1)} %get-tuple-element.45), channel_id=1, source_target_pairs={{0,2},{1,3},{2,0},{3,1},{4,6},{5,7},{6,4},{7,5},{8,10},{9,11},{10,... | collective-permute-start | bytes 786440 | tf_op jit(solution)/shard_map/ppermute | solution.py:147
  41.4 13.0 %collective-permute-start.14 = (bf16[1024,128]{1,0:T(8,128)(2,1)S(1)}, bf16[1024,128]{1,0:T(8,128)(2,1)S(1)}, u32[]{:S(2)}, u32[]{:S(2)}) collective-permute-start(bf16[1024,128]{1,0:T(8,128)(2,1)S(1)} %get-tuple-element.46), channel_id=1, source_target_pairs={{0,4},{1,5},{2,6},{3,7},{4,0},{5,1},{6,2},{7,3},{8,12},{9,13},{10,... | collective-permute-start | bytes 786440 | tf_op jit(solution)/shard_map/ppermute | solution.py:147
  42.2 12.2 %collective-permute-start.15 = (bf16[1024,128]{1,0:T(8,128)(2,1)S(1)}, bf16[1024,128]{1,0:T(8,128)(2,1)S(1)}, u32[]{:S(2)}, u32[]{:S(2)}) collective-permute-start(bf16[1024,128]{1,0:T(8,128)(2,1)S(1)} %get-tuple-element.47), channel_id=1, source_target_pairs={{0,6},{1,7},{2,4},{3,5},{4,2},{5,3},{6,0},{7,1},{8,14},{9,15},{10,... | collective-permute-start | bytes 786440 | tf_op jit(solution)/shard_map/ppermute | solution.py:147
  50.1 17.6 %copy-start.2 = (f32[16,8,32,128]{3,2,1,0:T(8,128)}, f32[16,8,32,128]{3,2,1,0:T(8,128)S(1)}, u32[]{:S(2)}) copy-start(f32[16,8,32,128]{3,2,1,0:T(8,128)S(1)} %get-tuple-element.40) | copy-start | bytes 6291460
  50.2 15.4 %collective-permute-start.10 = (s16[1,1040,128]{2,1,0:T(8,128)(2,1)S(1)}, s16[1,1040,128]{2,1,0:T(8,128)(2,1)S(1)}, u32[]{:S(2)}, u32[]{:S(2)}) collective-permute-start(s16[1,1040,128]{2,1,0:T(8,128)(2,1)S(1)} %get-tuple-element.42.refs_0_), channel_id=1, source_target_pairs={{0,8},{24,16},{1,9},{25,17},{2,10},{26,18},{3,11},{27,19},{4,12},{... | collective-permute-start | bytes 798728 | tf_op jit(solution)/shard_map/ppermute | solution.py:329
  52.3 15.5 %collective-permute-start.9 = (s16[1,1040,128]{2,1,0:T(8,128)(2,1)S(1)}, s16[1,1040,128]{2,1,0:T(8,128)(2,1)S(1)}, u32[]{:S(2)}, u32[]{:S(2)}) collective-permute-start(s16[1,1040,128]{2,1,0:T(8,128)(2,1)S(1)} %get-tuple-element.41), channel_id=1, source_target_pairs={{0,8},{24,16},{1,9},{25,17},{2,10},{26,18},{3,11},{27,19},{4,12},{... | collective-permute-start | bytes 798728 | tf_op jit(solution)/shard_map/ppermute | solution.py:329
  54.4 0.7 copy-start.13
  54.4 0.8 copy-start.14
  55.2 0.7 copy-start.15
  62.9 5.6 %copy-start.4 = (f32[16,8,32,128]{3,2,1,0:T(8,128)}, f32[16,8,32,128]{3,2,1,0:T(8,128)S(1)}, u32[]{:S(2)}) copy-start(f32[16,8,32,128]{3,2,1,0:T(8,128)S(1)} %get-tuple-element.49) | copy-start | bytes 6291460
  62.9 5.6 %collective-permute-start.19 = (s16[1,1040,128]{2,1,0:T(8,128)(2,1)S(1)}, s16[1,1040,128]{2,1,0:T(8,128)(2,1)S(1)}, u32[]{:S(2)}, u32[]{:S(2)}) collective-permute-start(s16[1,1040,128]{2,1,0:T(8,128)(2,1)S(1)} %get-tuple-element.48.refs_0_), channel_id=1, source_target_pairs={{0,8},{24,16},{1,9},{25,17},{2,10},{26,18},{3,11},{27,19},{4,12},{... | collective-permute-start | bytes 798728 | tf_op jit(solution)/shard_map/ppermute | solution.py:329
  64.2 15.3 %collective-permute-start.18 = (s16[1,1040,128]{2,1,0:T(8,128)(2,1)S(1)}, s16[1,1040,128]{2,1,0:T(8,128)(2,1)}, u32[]{:S(2)}, u32[]{:S(2)}) collective-permute-start(s16[1,1040,128]{2,1,0:T(8,128)(2,1)S(1)} %hop.9.refs_0_), channel_id=1, source_target_pairs={{8,16},{16,8},{9,17},{17,9},{10,18},{18,10},{11,19},{19,11},{12,20... | collective-permute-start | bytes 798728 | tf_op jit(solution)/shard_map/ppermute | solution.py:329
  66.4 16.4 %collective-permute-start.17 = (s16[1,1040,128]{2,1,0:T(8,128)(2,1)S(1)}, s16[1,1040,128]{2,1,0:T(8,128)(2,1)}, u32[]{:S(2)}, u32[]{:S(2)}) collective-permute-start(s16[1,1040,128]{2,1,0:T(8,128)(2,1)S(1)} %hop.11.refs_0_), channel_id=1, source_target_pairs={{8,16},{16,8},{9,17},{17,9},{10,18},{18,10},{11,19},{19,11},{12,20... | collective-permute-start | bytes 798728 | tf_op jit(solution)/shard_map/ppermute | solution.py:329
  69.3 17.1 %collective-permute-start.21 = (s16[1,1040,128]{2,1,0:T(8,128)(2,1)S(1)}, s16[1,1040,128]{2,1,0:T(8,128)(2,1)}, u32[]{:S(2)}, u32[]{:S(2)}) collective-permute-start(s16[1,1040,128]{2,1,0:T(8,128)(2,1)S(1)} %hop.13.refs_0_), channel_id=1, source_target_pairs={{8,16},{16,8},{9,17},{17,9},{10,18},{18,10},{11,19},{19,11},{12,20... | collective-permute-start | bytes 798728 | tf_op jit(solution)/shard_map/ppermute | solution.py:329
  70.8 17.8 %collective-permute-start.23 = (s16[1,1040,128]{2,1,0:T(8,128)(2,1)}, s16[1,1040,128]{2,1,0:T(8,128)(2,1)}, u32[]{:S(2)}, u32[]{:S(2)}) collective-permute-start(s16[1,1040,128]{2,1,0:T(8,128)(2,1)} %get-tuple-element.50), channel_id=1, source_target_pairs={{0,8},{24,16},{1,9},{25,17},{2,10},{26,18},{3,11},{27,19},{4,12},{... | collective-permute-start | bytes 798728 | tf_op jit(solution)/shard_map/ppermute | solution.py:329
  78.1 14.6 %collective-permute-start.25 = (s16[1,1040,128]{2,1,0:T(8,128)(2,1)S(1)}, s16[1,1040,128]{2,1,0:T(8,128)(2,1)}, u32[]{:S(2)}, u32[]{:S(2)}) collective-permute-start(s16[1,1040,128]{2,1,0:T(8,128)(2,1)S(1)} %hop.10.refs_0_), channel_id=1, source_target_pairs={{8,16},{16,8},{9,17},{17,9},{10,18},{18,10},{11,19},{19,11},{12,20... | collective-permute-start | bytes 798728 | tf_op jit(solution)/shard_map/ppermute | solution.py:329
  79.5 5.1 %copy-start.3 = (f32[16,8,32,128]{3,2,1,0:T(8,128)S(1)}, f32[16,8,32,128]{3,2,1,0:T(8,128)}, u32[]{:S(2)}) copy-start(f32[16,8,32,128]{3,2,1,0:T(8,128)} %copy-done.2) | copy-start | bytes 6291460
  79.5 14.5 %collective-permute-start.16 = (s16[1,1040,128]{2,1,0:T(8,128)(2,1)S(1)}, s16[1,1040,128]{2,1,0:T(8,128)(2,1)}, u32[]{:S(2)}, u32[]{:S(2)}) collective-permute-start(s16[1,1040,128]{2,1,0:T(8,128)(2,1)S(1)} %hop.12.refs_0_), channel_id=1, source_target_pairs={{8,16},{16,8},{9,17},{17,9},{10,18},{18,10},{11,19},{19,11},{12,20... | collective-permute-start | bytes 798728 | tf_op jit(solution)/shard_map/ppermute | solution.py:329
  82.7 4.1 %copy-start.5 = (f32[16,8,32,128]{3,2,1,0:T(8,128)S(1)}, f32[16,8,32,128]{3,2,1,0:T(8,128)}, u32[]{:S(2)}) copy-start(f32[16,8,32,128]{3,2,1,0:T(8,128)} %copy-done.4) | copy-start | bytes 6291460
  82.8 11.2 %collective-permute-start.26 = (s16[1,1040,128]{2,1,0:T(8,128)(2,1)S(1)}, s16[1,1040,128]{2,1,0:T(8,128)(2,1)}, u32[]{:S(2)}, u32[]{:S(2)}) collective-permute-start(s16[1,1040,128]{2,1,0:T(8,128)(2,1)S(1)} %hop.14.refs_0_), channel_id=1, source_target_pairs={{8,0},{0,8},{16,24},{24,16},{9,1},{1,9},{17,25},{25,17},{10,2},{2,... | collective-permute-start | bytes 798728 | tf_op jit(solution)/shard_map/ppermute | solution.py:329
  86.4 10.5 %collective-permute-start.20 = (s16[1,1040,128]{2,1,0:T(8,128)(2,1)S(1)}, s16[1,1040,128]{2,1,0:T(8,128)(2,1)}, u32[]{:S(2)}, u32[]{:S(2)}) collective-permute-start(s16[1,1040,128]{2,1,0:T(8,128)(2,1)S(1)} %hop.15.refs_0_), channel_id=1, source_target_pairs={{8,0},{0,8},{16,24},{24,16},{9,1},{1,9},{17,25},{25,17},{10,2},{2,... | collective-permute-start | bytes 798728 | tf_op jit(solution)/shard_map/ppermute | solution.py:329
  88.5 11.2 %collective-permute-start.22 = (s16[1,1040,128]{2,1,0:T(8,128)(2,1)S(1)}, s16[1,1040,128]{2,1,0:T(8,128)(2,1)}, u32[]{:S(2)}, u32[]{:S(2)}) collective-permute-start(s16[1,1040,128]{2,1,0:T(8,128)(2,1)S(1)} %hop.16.refs_0_), channel_id=1, source_target_pairs={{8,0},{0,8},{16,24},{24,16},{9,1},{1,9},{17,25},{25,17},{10,2},{2,... | collective-permute-start | bytes 798728 | tf_op jit(solution)/shard_map/ppermute | solution.py:329
  92.7 7.0 %collective-permute-start.24 = (s16[1,1040,128]{2,1,0:T(8,128)(2,1)}, s16[1,1040,128]{2,1,0:T(8,128)(2,1)S(1)}, u32[]{:S(2)}, u32[]{:S(2)}) collective-permute-start(s16[1,1040,128]{2,1,0:T(8,128)(2,1)} %hop.17), channel_id=1, source_target_pairs={{8,16},{16,8},{9,17},{17,9},{10,18},{18,10},{11,19},{19,11},{12,20... | collective-permute-start | bytes 798728 | tf_op jit(solution)/shard_map/ppermute | solution.py:329
  99.7 0.7 copy-start.12

commit v7 on v6

--- a/solution.py
+++ b/solution.py
@@ -246,7 +246,7 @@
     tiles = x.reshape(groups, 8, width)
     size = jnp.abs(tiles)
     most = jnp.max(jnp.max(size, axis=1), axis=1, keepdims=True)
-    level = jnp.ceil(jnp.log2(jnp.maximum(most, 1e-30)) * STEPS) + 1.0
+    level = jnp.ceil(jnp.log2(jnp.maximum(most, 1e-36)) * STEPS) + 1.0
     inverse = jnp.broadcast_to(jnp.exp2(level * (-1.0 / STEPS)), (groups, width)).reshape(groups, 1, width)
     share = jnp.maximum(size * inverse, 1e-12)
     root = jnp.minimum(share * lax.rsqrt(share) * TOP + 0.5, TOP)
@@ -270,9 +270,10 @@
         [jnp.sum(jnp.where(eye, lines[i : i + 1], 0.0), axis=1, keepdims=True) for i in range(groups // width)],
         axis=0,
     )
-    scale = jnp.exp2(level * (1.0 / STEPS)) * (1.0 / (TOP * TOP))
+    scale = jnp.exp2(level * (1.0 / STEPS))
     scale = jnp.broadcast_to(scale, (groups, width)).reshape(groups, 1, width)
-    return ((x * jnp.abs(x)).reshape(groups, 8, width) * scale).reshape(rows, width)
+    share = x * jnp.abs(x) * (1.0 / (TOP * TOP))
+    return (share.reshape(groups, 8, width) * scale).reshape(rows, width)
 
 
 def hop_kernel(places, idx_ref, sums_ref, prev_ref, *refs):

time: 106 us -> 106 us (level)
  no operation moved by 1% of the time
where the time goes in v7:
time: 106 us; the launch traced here: 105 us
  Pallas kernels  46.1 us (43%)
  starting transfers between devices  42.7 us (40%)
  waiting for transfers between devices  11.1 us (10%)
  local copies, waits for them, and re-layouts  4.32 us (4%)
    ppermute x15, starting transfers between devices, send(): lax.ppermute(payload, 'grp', pairs + [(last - a, last - b) for a, b in pa...  28 us
    pallas_call x3, Pallas kernels, volume_sums(): pl.pallas_call(functools.partial(volume_kernel, slabs, window, messages,...  20 us
    ppermute x12, starting transfers between devices, swap(): return lax.ppermute(x, 'slab', [(i, i ^ offset) for i in range(slabs)])  14.6 us
    pallas_call x9, Pallas kernels, hop(): pl.pallas_call(functools.partial(hop_kernel, places), out_shape=jax.Shape...  11.6 us
    pallas_call x2, Pallas kernels, sort_columns(): pl.pallas_call(functools.partial(sort_kernel, slabs, width, part, len(tie...  6.34 us
    ppermute x15, waiting for transfers between devices, send(): lax.ppermute(payload, 'grp', pairs + [(last - a, last - b) for a, b in pa...  5.71 us
    ppermute x12, waiting for transfers between devices, swap(): return lax.ppermute(x, 'slab', [(i, i ^ offset) for i in range(slabs)])  5.42 us
    pallas_call x1, Pallas kernels, image_of(): pl.pallas_call(functools.partial(image_kernel, parts, zs), out_shape=jax....  4.78 us
  transfers between devices with their start and end apart: 27, of which 6 were waited for; matrix products, arithmetic and copies ran while one was open for 1% of the time, Pallas kernels for 39%

profile of v7, /device:TPU:0, one launch (start us, length us, event | category | flops | bytes accessed | tf_op | source)
XLA Modules:
  0.0 105.3 jit_solution(1867278413951792703)
XLA Ops:
  0.5 0.7 pad_add_fusion.refs_0_
  1.8 3.2 %collective-permute-done.refs_1_ = s32[3,512]{1,0:T(4,128)S(1)} collective-permute-done((s32[3,512]{1,0:T(4,128)S(1)}, s32[3,512]{1,0:T(4,128)S(1)}, u32[]{:S(2)}, u32[]{:S(2)}) %collective-permute-start) | collective-permute-done | bytes 6176 | tf_op jit(solution)/shard_map/ppermute | solution.py:147
  5.0 0.9 collective-permute-done.1.refs_4_
  5.9 3.4 %plan_rows.1 = (bf16[2,512,512]{2,1,0:T(8,128)(2,1)S(1)}, bf16[1152,128]{1,0:T(8,128)(2,1)S(1)}, bf16[1152,128]{1,0:T(8,128)(2,1)S(1)}, bf16[1152,128]{1,0:T(8,128)(2,1)S(1)}, bf16[1152,128]{1,0:T(8,128)(2,1)S(1)}) custom-call(s32[1]{0:T(128)} %bitcast.1.me_ref, s32[3,512]{1,0:T(4,128)} %copy-done.16, s32[3,512]{1,0:T(4,128)S(1)} %collective-permute-done.refs_1_, ...), custom_call_target="tpu_custom_call" | custom-call | bytes 18000000 | tf_op jit(solution)/shard_map/plan_rows/pallas_call | solution.py:101
  9.3 2.6 %collective-permute-start.3 = (bf16[1152,128]{1,0:T(8,128)(2,1)S(1)}, bf16[1152,128]{1,0:T(8,128)(2,1)S(1)}, u32[]{:S(2)}, u32[]{:S(2)}) collective-permute-start(bf16[1152,128]{1,0:T(8,128)(2,1)S(1)} %get-tuple-element.32), channel_id=1, source_target_pairs={{0,2},{1,3},{2,0},{3,1},{4,6},{5,7},{6,4},{7,5},{8,10},{9,11},{10,... | collective-permute-start | bytes 884744 | tf_op jit(solution)/shard_map/ppermute | solution.py:147
  11.9 1.5 %collective-permute-start.4 = (bf16[1152,128]{1,0:T(8,128)(2,1)S(1)}, bf16[1152,128]{1,0:T(8,128)(2,1)S(1)}, u32[]{:S(2)}, u32[]{:S(2)}) collective-permute-start(bf16[1152,128]{1,0:T(8,128)(2,1)S(1)} %get-tuple-element.33), channel_id=1, source_target_pairs={{0,4},{1,5},{2,6},{3,7},{4,0},{5,1},{6,2},{7,3},{8,12},{9,13},{10,... | collective-permute-start | bytes 884744 | tf_op jit(solution)/shard_map/ppermute | solution.py:147
  13.5 3.5 %sort_columns.2 = (bf16[1024,128]{1,0:T(8,128)(2,1)S(1)}, bf16[1024,128]{1,0:T(8,128)(2,1)}, bf16[1024,128]{1,0:T(8,128)(2,1)}, bf16[1024,128]{1,0:T(8,128)(2,1)}) custom-call(s32[1]{0:T(128)} %bitcast.1.me_ref, bf16[2,512,512]{2,1,0:T(8,128)(2,1)S(1)} %get-tuple-element.28.order_ref, bf16[512,2048]{1,0:T(8,128)(2,1)} %refs_0_.3, ...), custom_call_target="tpu_custom_call" | custom-call | bytes 9000000 | tf_op jit(solution)/shard_map/sort_columns/pallas_call | solution.py:131
  17.0 2.0 %collective-permute-start.6 = (bf16[1024,128]{1,0:T(8,128)(2,1)}, bf16[1024,128]{1,0:T(8,128)(2,1)}, u32[]{:S(2)}, u32[]{:S(2)}) collective-permute-start(bf16[1024,128]{1,0:T(8,128)(2,1)} %get-tuple-element.36), channel_id=1, source_target_pairs={{0,2},{1,3},{2,0},{3,1},{4,6},{5,7},{6,4},{7,5},{8,10},{9,11},{10,... | collective-permute-start | bytes 786440 | tf_op jit(solution)/shard_map/ppermute | solution.py:147
  18.9 1.5 %collective-permute-start.7 = (bf16[1024,128]{1,0:T(8,128)(2,1)}, bf16[1024,128]{1,0:T(8,128)(2,1)}, u32[]{:S(2)}, u32[]{:S(2)}) collective-permute-start(bf16[1024,128]{1,0:T(8,128)(2,1)} %get-tuple-element.37), channel_id=1, source_target_pairs={{0,4},{1,5},{2,6},{3,7},{4,0},{5,1},{6,2},{7,3},{8,12},{9,13},{10,... | collective-permute-start | bytes 786440 | tf_op jit(solution)/shard_map/ppermute | solution.py:147
  20.5 0.7 copy-done.9
  21.2 2.2 %collective-permute-start.8 = (bf16[1024,128]{1,0:T(8,128)(2,1)}, bf16[1024,128]{1,0:T(8,128)(2,1)}, u32[]{:S(2)}, u32[]{:S(2)}) collective-permute-start(bf16[1024,128]{1,0:T(8,128)(2,1)} %get-tuple-element.38), channel_id=1, source_target_pairs={{0,6},{1,7},{2,4},{3,5},{4,2},{5,3},{6,0},{7,1},{8,14},{9,15},{10,... | collective-permute-start | bytes 786440 | tf_op jit(solution)/shard_map/ppermute | solution.py:147
  23.4 2.8 %sort_columns.3 = (bf16[1024,128]{1,0:T(8,128)(2,1)S(1)}, bf16[1024,128]{1,0:T(8,128)(2,1)S(1)}, bf16[1024,128]{1,0:T(8,128)(2,1)S(1)}, bf16[1024,128]{1,0:T(8,128)(2,1)S(1)}) custom-call(s32[1]{0:T(128)} %bitcast.1.me_ref, bf16[2,512,512]{2,1,0:T(8,128)(2,1)S(1)} %get-tuple-element.28.order_ref, bf16[512,2048]{1,0:T(8,128)(2,1)} %refs_0_.3, ...), custom_call_target="tpu_custom_call" | custom-call | bytes 9000000 | tf_op jit(solution)/shard_map/sort_columns/pallas_call | solution.py:131
  26.3 1.2 %collective-permute-done.4.refs_3_ = bf16[1152,128]{1,0:T(8,128)(2,1)S(1)} collective-permute-done((bf16[1152,128]{1,0:T(8,128)(2,1)S(1)}, bf16[1152,128]{1,0:T(8,128)(2,1)S(1)}, u32[]{:S(2)}, u32[]{:S(2)}) %collective-permute-start.4) | collective-permute-done | bytes 294944 | tf_op jit(solution)/shard_map/ppermute | solution.py:147
  28.3 6.6 %volume_sums.3 = (f32[16,8,32,128]{3,2,1,0:T(8,128)S(1)}, bf16[8,16,512]{2,1,0:T(8,128)(2,1)S(1)}, s16[1,1040,128]{2,1,0:T(8,128)(2,1)S(1)}, s16[1,1040,128]{2,1,0:T(8,128)(2,1)S(1)}) custom-call(s32[2]{0:T(128)S(1)} %broadcast_select_fusion.idx_ref, bf16[1024,128]{1,0:T(8,128)(2,1)S(1)} %get-tuple-element.30.refs_0_.refs_1_, bf16[1152,128]{1,0:T(8,128)(2,1)} %copy-done.8, ...), custom_call_target="tpu_custom_call" | custom-call | bytes 21000000 | tf_op jit(solution)/shard_map/volume_sums/pallas_call | solution.py:224
  34.9 3.5 %collective-permute-start.12 = (s16[1,1040,128]{2,1,0:T(8,128)(2,1)S(1)}, s16[1,1040,128]{2,1,0:T(8,128)(2,1)S(1)}, u32[]{:S(2)}, u32[]{:S(2)}) collective-permute-start(s16[1,1040,128]{2,1,0:T(8,128)(2,1)S(1)} %get-tuple-element.35.refs_0_), channel_id=1, source_target_pairs={{0,8},{24,16},{1,9},{25,17},{2,10},{26,18},{3,11},{27,19},{4,12},{... | collective-permute-start | bytes 798728 | tf_op jit(solution)/shard_map/ppermute | solution.py:330
  38.4 1.5 %collective-permute-start.11 = (s16[1,1040,128]{2,1,0:T(8,128)(2,1)S(1)}, s16[1,1040,128]{2,1,0:T(8,128)(2,1)S(1)}, u32[]{:S(2)}, u32[]{:S(2)}) collective-permute-start(s16[1,1040,128]{2,1,0:T(8,128)(2,1)S(1)} %get-tuple-element.44), channel_id=1, source_target_pairs={{0,8},{24,16},{1,9},{25,17},{2,10},{26,18},{3,11},{27,19},{4,12},{... | collective-permute-start | bytes 798728 | tf_op jit(solution)/shard_map/ppermute | solution.py:330
  39.9 1.5 %collective-permute-start.13 = (bf16[1024,128]{1,0:T(8,128)(2,1)S(1)}, bf16[1024,128]{1,0:T(8,128)(2,1)S(1)}, u32[]{:S(2)}, u32[]{:S(2)}) collective-permute-start(bf16[1024,128]{1,0:T(8,128)(2,1)S(1)} %get-tuple-element.45), channel_id=1, source_target_pairs={{0,2},{1,3},{2,0},{3,1},{4,6},{5,7},{6,4},{7,5},{8,10},{9,11},{10,... | collective-permute-start | bytes 786440 | tf_op jit(solution)/shard_map/ppermute | solution.py:147
  41.4 0.8 collective-permute-start.14
  42.2 1.4 %collective-permute-start.15 = (bf16[1024,128]{1,0:T(8,128)(2,1)S(1)}, bf16[1024,128]{1,0:T(8,128)(2,1)S(1)}, u32[]{:S(2)}, u32[]{:S(2)}) collective-permute-start(bf16[1024,128]{1,0:T(8,128)(2,1)S(1)} %get-tuple-element.47), channel_id=1, source_target_pairs={{0,6},{1,7},{2,4},{3,5},{4,2},{5,3},{6,0},{7,1},{8,14},{9,15},{10,... | collective-permute-start | bytes 786440 | tf_op jit(solution)/shard_map/ppermute | solution.py:147
  43.6 6.5 %volume_sums.4 = (f32[16,8,32,128]{3,2,1,0:T(8,128)S(1)}, s16[1,1040,128]{2,1,0:T(8,128)(2,1)S(1)}, s16[1,1040,128]{2,1,0:T(8,128)(2,1)S(1)}) custom-call(s32[2]{0:T(128)S(1)} %broadcast_select_fusion.idx_ref, s16[1,1040,128]{2,1,0:T(8,128)(2,1)S(1)} %get-tuple-element.35.refs_0_, bf16[1024,128]{1,0:T(8,128)(2,1)} %copy-done.6, ...), custom_call_target="tpu_custom_call" | custom-call | bytes 21000000 | tf_op jit(solution)/shard_map/volume_sums/pallas_call | solution.py:224
  50.2 1.3 %collective-permute-start.10 = (s16[1,1040,128]{2,1,0:T(8,128)(2,1)S(1)}, s16[1,1040,128]{2,1,0:T(8,128)(2,1)S(1)}, u32[]{:S(2)}, u32[]{:S(2)}) collective-permute-start(s16[1,1040,128]{2,1,0:T(8,128)(2,1)S(1)} %get-tuple-element.42.refs_0_), channel_id=1, source_target_pairs={{0,8},{24,16},{1,9},{25,17},{2,10},{26,18},{3,11},{27,19},{4,12},{... | collective-permute-start | bytes 798728 | tf_op jit(solution)/shard_map/ppermute | solution.py:330
  51.5 0.8 hop.9.refs_0_
  52.3 1.3 %collective-permute-start.9 = (s16[1,1040,128]{2,1,0:T(8,128)(2,1)S(1)}, s16[1,1040,128]{2,1,0:T(8,128)(2,1)S(1)}, u32[]{:S(2)}, u32[]{:S(2)}) collective-permute-start(s16[1,1040,128]{2,1,0:T(8,128)(2,1)S(1)} %get-tuple-element.41), channel_id=1, source_target_pairs={{0,8},{24,16},{1,9},{25,17},{2,10},{26,18},{3,11},{27,19},{4,12},{... | collective-permute-start | bytes 798728 | tf_op jit(solution)/shard_map/ppermute | solution.py:330
  53.6 0.8 hop.10.refs_0_
  54.4 0.7 copy-done.13
  55.2 0.7 copy-done.15
  55.9 7.0 %volume_sums.5 = (f32[16,8,32,128]{3,2,1,0:T(8,128)S(1)}, s16[1,1040,128]{2,1,0:T(8,128)(2,1)S(1)}, s16[1,1040,128]{2,1,0:T(8,128)(2,1)}) custom-call(s32[2]{0:T(128)S(1)} %broadcast_select_fusion.idx_ref, s16[1,1040,128]{2,1,0:T(8,128)(2,1)S(1)} %hop.10.refs_0_, bf16[1024,128]{1,0:T(8,128)(2,1)} %copy-done.7, bf16[1024,128]{1,0:T(8,128)(2,1)} %copy-done.13, ...), custom_call_target="tpu_custom_call" | custom-call | bytes 21000000 | tf_op jit(solution)/shard_map/volume_sums/pallas_call | solution.py:224
  62.9 1.3 %collective-permute-start.19 = (s16[1,1040,128]{2,1,0:T(8,128)(2,1)S(1)}, s16[1,1040,128]{2,1,0:T(8,128)(2,1)S(1)}, u32[]{:S(2)}, u32[]{:S(2)}) collective-permute-start(s16[1,1040,128]{2,1,0:T(8,128)(2,1)S(1)} %get-tuple-element.48.refs_0_), channel_id=1, source_target_pairs={{0,8},{24,16},{1,9},{25,17},{2,10},{26,18},{3,11},{27,19},{4,12},{... | collective-permute-start | bytes 798728 | tf_op jit(solution)/shard_map/ppermute | solution.py:330
  64.3 1.4 %collective-permute-start.18 = (s16[1,1040,128]{2,1,0:T(8,128)(2,1)S(1)}, s16[1,1040,128]{2,1,0:T(8,128)(2,1)}, u32[]{:S(2)}, u32[]{:S(2)}) collective-permute-start(s16[1,1040,128]{2,1,0:T(8,128)(2,1)S(1)} %hop.9.refs_0_), channel_id=1, source_target_pairs={{8,16},{16,8},{9,17},{17,9},{10,18},{18,10},{11,19},{19,11},{12,20... | collective-permute-start | bytes 798728 | tf_op jit(solution)/shard_map/ppermute | solution.py:330
  65.6 0.8 hop.11.refs_0_
  66.4 1.4 %collective-permute-start.17 = (s16[1,1040,128]{2,1,0:T(8,128)(2,1)S(1)}, s16[1,1040,128]{2,1,0:T(8,128)(2,1)}, u32[]{:S(2)}, u32[]{:S(2)}) collective-permute-start(s16[1,1040,128]{2,1,0:T(8,128)(2,1)S(1)} %hop.11.refs_0_), channel_id=1, source_target_pairs={{8,16},{16,8},{9,17},{17,9},{10,18},{18,10},{11,19},{19,11},{12,20... | collective-permute-start | bytes 798728 | tf_op jit(solution)/shard_map/ppermute | solution.py:330
  67.8 0.8 hop.12.refs_0_
  68.6 0.8 hop.13.refs_0_
  69.4 1.4 %collective-permute-start.21 = (s16[1,1040,128]{2,1,0:T(8,128)(2,1)S(1)}, s16[1,1040,128]{2,1,0:T(8,128)(2,1)}, u32[]{:S(2)}, u32[]{:S(2)}) collective-permute-start(s16[1,1040,128]{2,1,0:T(8,128)(2,1)S(1)} %hop.13.refs_0_), channel_id=1, source_target_pairs={{8,16},{16,8},{9,17},{17,9},{10,18},{18,10},{11,19},{19,11},{12,20... | collective-permute-start | bytes 798728 | tf_op jit(solution)/shard_map/ppermute | solution.py:330
  70.8 7.4 %collective-permute-start.23 = (s16[1,1040,128]{2,1,0:T(8,128)(2,1)}, s16[1,1040,128]{2,1,0:T(8,128)(2,1)}, u32[]{:S(2)}, u32[]{:S(2)}) collective-permute-start(s16[1,1040,128]{2,1,0:T(8,128)(2,1)} %get-tuple-element.50), channel_id=1, source_target_pairs={{0,8},{24,16},{1,9},{25,17},{2,10},{26,18},{3,11},{27,19},{4,12},{... | collective-permute-start | bytes 798728 | tf_op jit(solution)/shard_map/ppermute | solution.py:330
  78.2 1.4 %collective-permute-start.25 = (s16[1,1040,128]{2,1,0:T(8,128)(2,1)S(1)}, s16[1,1040,128]{2,1,0:T(8,128)(2,1)}, u32[]{:S(2)}, u32[]{:S(2)}) collective-permute-start(s16[1,1040,128]{2,1,0:T(8,128)(2,1)S(1)} %hop.10.refs_0_), channel_id=1, source_target_pairs={{8,16},{16,8},{9,17},{17,9},{10,18},{18,10},{11,19},{19,11},{12,20... | collective-permute-start | bytes 798728 | tf_op jit(solution)/shard_map/ppermute | solution.py:330
  79.6 1.5 %collective-permute-start.16 = (s16[1,1040,128]{2,1,0:T(8,128)(2,1)S(1)}, s16[1,1040,128]{2,1,0:T(8,128)(2,1)}, u32[]{:S(2)}, u32[]{:S(2)}) collective-permute-start(s16[1,1040,128]{2,1,0:T(8,128)(2,1)S(1)} %hop.12.refs_0_), channel_id=1, source_target_pairs={{8,16},{16,8},{9,17},{17,9},{10,18},{18,10},{11,19},{19,11},{12,20... | collective-permute-start | bytes 798728 | tf_op jit(solution)/shard_map/ppermute | solution.py:330
  81.1 1.7 %hop.14.refs_0_ = s16[1,1040,128]{2,1,0:T(8,128)(2,1)S(1)} custom-call(s32[1]{0:T(128)S(6)} %select_n.51.idx_ref, f32[4,1024,128]{2,1,0:T(8,128)S(1)} %bitcast.15, s16[1,1040,128]{2,1,0:T(8,128)(2,1)} %collective-permute-done.18.prev_ref, s16[1,1040,128]{2,1,0:T(8,128)(2,1)S(1)} %hop.13.refs_0_), custom_call_target="tpu_custom_call" | custom-call | bytes 9000000 | tf_op jit(solution)/shard_map/hop/pallas_call | solution.py:290
  82.9 1.9 %collective-permute-start.26 = (s16[1,1040,128]{2,1,0:T(8,128)(2,1)S(1)}, s16[1,1040,128]{2,1,0:T(8,128)(2,1)}, u32[]{:S(2)}, u32[]{:S(2)}) collective-permute-start(s16[1,1040,128]{2,1,0:T(8,128)(2,1)S(1)} %hop.14.refs_0_), channel_id=1, source_target_pairs={{8,0},{0,8},{16,24},{24,16},{9,1},{1,9},{17,25},{25,17},{10,2},{2,... | collective-permute-start | bytes 798728 | tf_op jit(solution)/shard_map/ppermute | solution.py:330
  84.8 1.7 %hop.15.refs_0_ = s16[1,1040,128]{2,1,0:T(8,128)(2,1)S(1)} custom-call(s32[1]{0:T(128)S(6)} %select_n.51.idx_ref, f32[4,1024,128]{2,1,0:T(8,128)S(1)} %bitcast.20, s16[1,1040,128]{2,1,0:T(8,128)(2,1)} %collective-permute-done.17.prev_ref, s16[1,1040,128]{2,1,0:T(8,128)(2,1)S(1)} %hop.14.refs_0_), custom_call_target="tpu_custom_call" | custom-call | bytes 9000000 | tf_op jit(solution)/shard_map/hop/pallas_call | solution.py:290
  86.9 1.7 %hop.16.refs_0_ = s16[1,1040,128]{2,1,0:T(8,128)(2,1)S(1)} custom-call(s32[1]{0:T(128)S(6)} %select_n.51.idx_ref, f32[4,1024,128]{2,1,0:T(8,128)S(1)} %bitcast.23, s16[1,1040,128]{2,1,0:T(8,128)(2,1)} %collective-permute-done.21.prev_ref, s16[1,1040,128]{2,1,0:T(8,128)(2,1)S(1)} %hop.15.refs_0_), custom_call_target="tpu_custom_call" | custom-call | bytes 9000000 | tf_op jit(solution)/shard_map/hop/pallas_call | solution.py:290
  88.7 1.8 %collective-permute-start.22 = (s16[1,1040,128]{2,1,0:T(8,128)(2,1)S(1)}, s16[1,1040,128]{2,1,0:T(8,128)(2,1)}, u32[]{:S(2)}, u32[]{:S(2)}) collective-permute-start(s16[1,1040,128]{2,1,0:T(8,128)(2,1)S(1)} %hop.16.refs_0_), channel_id=1, source_target_pairs={{8,0},{0,8},{16,24},{24,16},{9,1},{1,9},{17,25},{25,17},{10,2},{2,... | collective-permute-start | bytes 798728 | tf_op jit(solution)/shard_map/ppermute | solution.py:330
  90.4 2.4 %hop.17 = s16[1,1040,128]{2,1,0:T(8,128)(2,1)} custom-call(s32[1]{0:T(128)S(6)} %select_n.48.idx_ref, f32[4,1024,128]{2,1,0:T(8,128)S(1)} %bitcast.24, s16[1,1040,128]{2,1,0:T(8,128)(2,1)} %collective-permute-done.23.prev_ref, s16[1,1040,128]{2,1,0:T(8,128)(2,1)S(1)} %hop.16.refs_0_), custom_call_target="tpu_custom_call" | custom-call | bytes 9000000 | tf_op jit(solution)/shard_map/hop/pallas_call | solution.py:290
  92.9 0.7 collective-permute-start.24
  94.1 2.8 %collective-permute-done.20.refs_2_ = s16[1,1040,128]{2,1,0:T(8,128)(2,1)} collective-permute-done((s16[1,1040,128]{2,1,0:T(8,128)(2,1)S(1)}, s16[1,1040,128]{2,1,0:T(8,128)(2,1)}, u32[]{:S(2)}, u32[]{:S(2)}) %collective-permute-start.20) | collective-permute-done | bytes 266272 | tf_op jit(solution)/shard_map/ppermute | solution.py:330
  97.0 2.9 %collective-permute-done.22.refs_4_ = s16[1,1040,128]{2,1,0:T(8,128)(2,1)} collective-permute-done((s16[1,1040,128]{2,1,0:T(8,128)(2,1)S(1)}, s16[1,1040,128]{2,1,0:T(8,128)(2,1)}, u32[]{:S(2)}, u32[]{:S(2)}) %collective-permute-start.22) | collective-permute-done | bytes 266272 | tf_op jit(solution)/shard_map/ppermute | solution.py:330
  99.8 0.7 copy-done.12
  100.5 4.8 %image_of.1 = f32[2,4,256,128]{3,2,1,0:T(8,128)} custom-call(s32[1]{0:T(128)} %bitcast.own_ref, f32[4,1024,128]{2,1,0:T(8,128)} %bitcast.19, s16[1,1040,128]{2,1,0:T(8,128)(2,1)} %collective-permute-done.16.refs_1_, s16[1,1040,128]{2,1,0:T(8,128)(2,1)} %collective-permute-done.20.refs_2_, f32[4,1024,128]{2,1,0:T(8,128)} %bitcast.22, ...), custom_call_target="tpu_custom_call" | custom-call | bytes 18000000 | tf_op jit(solution)/shard_map/image_of/pallas_call | solution.py:392
  (61 shorter events, 3.1 us)
Async XLA Ops:
  0.0 93.5 %copy-start = (f32[1024]{0:T(1024)S(1)}, f32[1024]{0:T(1024)}, u32[]{:S(2)}) copy-start(f32[1024]{0:T(1024)} %param.17) | copy-start | bytes 12292
  0.0 13.5 %collective-permute-start.2 = (bf16[512,2048]{1,0:T(8,128)(2,1)}, bf16[512,2048]{1,0:T(8,128)(2,1)}, u32[]{:S(2)}, u32[]{:S(2)}) collective-permute-start(bf16[512,2048]{1,0:T(8,128)(2,1)} %refs_0_.3), channel_id=1, source_target_pairs={{0,1},{1,0},{2,3},{3,2},{4,5},{5,4},{6,7},{7,6},{8,9},{9,8},{10,11... | collective-permute-start | bytes 6291464 | tf_op jit(solution)/shard_map/ppermute | solution.py:147
  0.5 5.4 %collective-permute-start.1 = (bf16[512,1024]{1,0:T(8,128)(2,1)}, bf16[512,1024]{1,0:T(8,128)(2,1)S(1)}, u32[]{:S(2)}, u32[]{:S(2)}) collective-permute-start(bf16[512,1024]{1,0:T(8,128)(2,1)} %refs_3_.1), channel_id=1, source_target_pairs={{0,1},{1,0},{2,3},{3,2},{4,5},{5,4},{6,7},{7,6},{8,9},{9,8},{10,11... | collective-permute-start | bytes 3145736 | tf_op jit(solution)/shard_map/ppermute | solution.py:147
  1.3 4.6 %copy-start.16 = (s32[3,512]{1,0:T(4,128)}, s32[3,512]{1,0:T(4,128)S(1)}, u32[]{:S(2)}) copy-start(s32[3,512]{1,0:T(4,128)S(1)} %pad_add_fusion.refs_0_) | copy-start | bytes 18436
  1.3 3.7 %collective-permute-start = (s32[3,512]{1,0:T(4,128)S(1)}, s32[3,512]{1,0:T(4,128)S(1)}, u32[]{:S(2)}, u32[]{:S(2)}) collective-permute-start(s32[3,512]{1,0:T(4,128)S(1)} %pad_add_fusion.refs_0_), channel_id=1, source_target_pairs={{0,1},{1,0},{2,3},{3,2},{4,5},{5,4},{6,7},{7,6},{8,9},{9,8},{10,11... | collective-permute-start | bytes 18440 | tf_op jit(solution)/shard_map/ppermute | solution.py:147
  9.3 7.7 %copy-start.8 = (bf16[1152,128]{1,0:T(8,128)(2,1)}, bf16[1152,128]{1,0:T(8,128)(2,1)S(1)}, u32[]{:S(2)}) copy-start(bf16[1152,128]{1,0:T(8,128)(2,1)S(1)} %get-tuple-element.31.refs_1_) | copy-start | bytes 884740
  9.3 11.2 %collective-permute-start.3 = (bf16[1152,128]{1,0:T(8,128)(2,1)S(1)}, bf16[1152,128]{1,0:T(8,128)(2,1)S(1)}, u32[]{:S(2)}, u32[]{:S(2)}) collective-permute-start(bf16[1152,128]{1,0:T(8,128)(2,1)S(1)} %get-tuple-element.32), channel_id=1, source_target_pairs={{0,2},{1,3},{2,0},{3,1},{4,6},{5,7},{6,4},{7,5},{8,10},{9,11},{10,... | collective-permute-start | bytes 884744 | tf_op jit(solution)/shard_map/ppermute | solution.py:147
  11.9 15.5 %collective-permute-start.4 = (bf16[1152,128]{1,0:T(8,128)(2,1)S(1)}, bf16[1152,128]{1,0:T(8,128)(2,1)S(1)}, u32[]{:S(2)}, u32[]{:S(2)}) collective-permute-start(bf16[1152,128]{1,0:T(8,128)(2,1)S(1)} %get-tuple-element.33), channel_id=1, source_target_pairs={{0,4},{1,5},{2,6},{3,7},{4,0},{5,1},{6,2},{7,3},{8,12},{9,13},{10,... | collective-permute-start | bytes 884744 | tf_op jit(solution)/shard_map/ppermute | solution.py:147
  13.4 14.1 %collective-permute-start.5 = (bf16[1152,128]{1,0:T(8,128)(2,1)S(1)}, bf16[1152,128]{1,0:T(8,128)(2,1)S(1)}, u32[]{:S(2)}, u32[]{:S(2)}) collective-permute-start(bf16[1152,128]{1,0:T(8,128)(2,1)S(1)} %get-tuple-element.34), channel_id=1, source_target_pairs={{0,6},{1,7},{2,4},{3,5},{4,2},{5,3},{6,0},{7,1},{8,14},{9,15},{10,... | collective-permute-start | bytes 884744 | tf_op jit(solution)/shard_map/ppermute | solution.py:147
  13.5 10.0 %copy-start.17 = (s32[2]{0:T(128)S(1)}, s32[2]{0:T(128)}, u32[]{:S(2)}) copy-start(s32[2]{0:T(128)} %constant.36.clone) | copy-start | bytes 28
  17.0 9.3 %copy-start.6 = (bf16[1024,128]{1,0:T(8,128)(2,1)}, bf16[1024,128]{1,0:T(8,128)(2,1)S(1)}, u32[]{:S(2)}) copy-start(bf16[1024,128]{1,0:T(8,128)(2,1)S(1)} %get-tuple-element.29.refs_2_.refs_1_) | copy-start | bytes 786436
  17.0 22.9 %collective-permute-start.6 = (bf16[1024,128]{1,0:T(8,128)(2,1)}, bf16[1024,128]{1,0:T(8,128)(2,1)}, u32[]{:S(2)}, u32[]{:S(2)}) collective-permute-start(bf16[1024,128]{1,0:T(8,128)(2,1)} %get-tuple-element.36), channel_id=1, source_target_pairs={{0,2},{1,3},{2,0},{3,1},{4,6},{5,7},{6,4},{7,5},{8,10},{9,11},{10,... | collective-permute-start | bytes 786440 | tf_op jit(solution)/shard_map/ppermute | solution.py:147
  18.9 22.5 %collective-permute-start.7 = (bf16[1024,128]{1,0:T(8,128)(2,1)}, bf16[1024,128]{1,0:T(8,128)(2,1)}, u32[]{:S(2)}, u32[]{:S(2)}) collective-permute-start(bf16[1024,128]{1,0:T(8,128)(2,1)} %get-tuple-element.37), channel_id=1, source_target_pairs={{0,4},{1,5},{2,6},{3,7},{4,0},{5,1},{6,2},{7,3},{8,12},{9,13},{10,... | collective-permute-start | bytes 786440 | tf_op jit(solution)/shard_map/ppermute | solution.py:147
  20.5 0.7 copy-start.9
  21.2 21.0 %collective-permute-start.8 = (bf16[1024,128]{1,0:T(8,128)(2,1)}, bf16[1024,128]{1,0:T(8,128)(2,1)}, u32[]{:S(2)}, u32[]{:S(2)}) collective-permute-start(bf16[1024,128]{1,0:T(8,128)(2,1)} %get-tuple-element.38), channel_id=1, source_target_pairs={{0,6},{1,7},{2,4},{3,5},{4,2},{5,3},{6,0},{7,1},{8,14},{9,15},{10,... | collective-permute-start | bytes 786440 | tf_op jit(solution)/shard_map/ppermute | solution.py:147
  26.3 26.0 %copy-start.7 = (bf16[1024,128]{1,0:T(8,128)(2,1)}, bf16[1024,128]{1,0:T(8,128)(2,1)S(1)}, u32[]{:S(2)}) copy-start(bf16[1024,128]{1,0:T(8,128)(2,1)S(1)} %get-tuple-element.30.refs_0_.refs_1_) | copy-start | bytes 786436
  27.5 0.7 copy-start.10
  27.6 0.7 copy-start.11
  34.9 46.2 %copy-start.1 = (f32[16,8,32,128]{3,2,1,0:T(8,128)}, f32[16,8,32,128]{3,2,1,0:T(8,128)S(1)}, u32[]{:S(2)}) copy-start(f32[16,8,32,128]{3,2,1,0:T(8,128)S(1)} %get-tuple-element.43) | copy-start | bytes 6291460
  34.9 15.3 %collective-permute-start.12 = (s16[1,1040,128]{2,1,0:T(8,128)(2,1)S(1)}, s16[1,1040,128]{2,1,0:T(8,128)(2,1)S(1)}, u32[]{:S(2)}, u32[]{:S(2)}) collective-permute-start(s16[1,1040,128]{2,1,0:T(8,128)(2,1)S(1)} %get-tuple-element.35.refs_0_), channel_id=1, source_target_pairs={{0,8},{24,16},{1,9},{25,17},{2,10},{26,18},{3,11},{27,19},{4,12},{... | collective-permute-start | bytes 798728 | tf_op jit(solution)/shard_map/ppermute | solution.py:330
  38.4 13.9 %collective-permute-start.11 = (s16[1,1040,128]{2,1,0:T(8,128)(2,1)S(1)}, s16[1,1040,128]{2,1,0:T(8,128)(2,1)S(1)}, u32[]{:S(2)}, u32[]{:S(2)}) collective-permute-start(s16[1,1040,128]{2,1,0:T(8,128)(2,1)S(1)} %get-tuple-element.44), channel_id=1, source_target_pairs={{0,8},{24,16},{1,9},{25,17},{2,10},{26,18},{3,11},{27,19},{4,12},{... | collective-permute-start | bytes 798728 | tf_op jit(solution)/shard_map/ppermute | solution.py:330
  39.9 14.5 %collective-permute-start.13 = (bf16[1024,128]{1,0:T(8,128)(2,1)S(1)}, bf16[1024,128]{1,0:T(8,128)(2,1)S(1)}, u32[]{:S(2)}, u32[]{:S(2)}) collective-permute-start(bf16[1024,128]{1,0:T(8,128)(2,1)S(1)} %get-tuple-element.45), channel_id=1, source_target_pairs={{0,2},{1,3},{2,0},{3,1},{4,6},{5,7},{6,4},{7,5},{8,10},{9,11},{10,... | collective-permute-start | bytes 786440 | tf_op jit(solution)/shard_map/ppermute | solution.py:147
  41.4 13.0 %collective-permute-start.14 = (bf16[1024,128]{1,0:T(8,128)(2,1)S(1)}, bf16[1024,128]{1,0:T(8,128)(2,1)S(1)}, u32[]{:S(2)}, u32[]{:S(2)}) collective-permute-start(bf16[1024,128]{1,0:T(8,128)(2,1)S(1)} %get-tuple-element.46), channel_id=1, source_target_pairs={{0,4},{1,5},{2,6},{3,7},{4,0},{5,1},{6,2},{7,3},{8,12},{9,13},{10,... | collective-permute-start | bytes 786440 | tf_op jit(solution)/shard_map/ppermute | solution.py:147
  42.2 12.3 %collective-permute-start.15 = (bf16[1024,128]{1,0:T(8,128)(2,1)S(1)}, bf16[1024,128]{1,0:T(8,128)(2,1)S(1)}, u32[]{:S(2)}, u32[]{:S(2)}) collective-permute-start(bf16[1024,128]{1,0:T(8,128)(2,1)S(1)} %get-tuple-element.47), channel_id=1, source_target_pairs={{0,6},{1,7},{2,4},{3,5},{4,2},{5,3},{6,0},{7,1},{8,14},{9,15},{10,... | collective-permute-start | bytes 786440 | tf_op jit(solution)/shard_map/ppermute | solution.py:147
  50.1 17.7 %copy-start.2 = (f32[16,8,32,128]{3,2,1,0:T(8,128)}, f32[16,8,32,128]{3,2,1,0:T(8,128)S(1)}, u32[]{:S(2)}) copy-start(f32[16,8,32,128]{3,2,1,0:T(8,128)S(1)} %get-tuple-element.40) | copy-start | bytes 6291460
  50.2 15.5 %collective-permute-start.10 = (s16[1,1040,128]{2,1,0:T(8,128)(2,1)S(1)}, s16[1,1040,128]{2,1,0:T(8,128)(2,1)S(1)}, u32[]{:S(2)}, u32[]{:S(2)}) collective-permute-start(s16[1,1040,128]{2,1,0:T(8,128)(2,1)S(1)} %get-tuple-element.42.refs_0_), channel_id=1, source_target_pairs={{0,8},{24,16},{1,9},{25,17},{2,10},{26,18},{3,11},{27,19},{4,12},{... | collective-permute-start | bytes 798728 | tf_op jit(solution)/shard_map/ppermute | solution.py:330
  52.3 15.5 %collective-permute-start.9 = (s16[1,1040,128]{2,1,0:T(8,128)(2,1)S(1)}, s16[1,1040,128]{2,1,0:T(8,128)(2,1)S(1)}, u32[]{:S(2)}, u32[]{:S(2)}) collective-permute-start(s16[1,1040,128]{2,1,0:T(8,128)(2,1)S(1)} %get-tuple-element.41), channel_id=1, source_target_pairs={{0,8},{24,16},{1,9},{25,17},{2,10},{26,18},{3,11},{27,19},{4,12},{... | collective-permute-start | bytes 798728 | tf_op jit(solution)/shard_map/ppermute | solution.py:330
  54.4 0.7 copy-start.13
  54.4 0.8 copy-start.14
  55.2 0.7 copy-start.15
  62.9 5.7 %copy-start.4 = (f32[16,8,32,128]{3,2,1,0:T(8,128)}, f32[16,8,32,128]{3,2,1,0:T(8,128)S(1)}, u32[]{:S(2)}) copy-start(f32[16,8,32,128]{3,2,1,0:T(8,128)S(1)} %get-tuple-element.49) | copy-start | bytes 6291460
  62.9 5.7 %collective-permute-start.19 = (s16[1,1040,128]{2,1,0:T(8,128)(2,1)S(1)}, s16[1,1040,128]{2,1,0:T(8,128)(2,1)S(1)}, u32[]{:S(2)}, u32[]{:S(2)}) collective-permute-start(s16[1,1040,128]{2,1,0:T(8,128)(2,1)S(1)} %get-tuple-element.48.refs_0_), channel_id=1, source_target_pairs={{0,8},{24,16},{1,9},{25,17},{2,10},{26,18},{3,11},{27,19},{4,12},{... | collective-permute-start | bytes 798728 | tf_op jit(solution)/shard_map/ppermute | solution.py:330
  64.3 15.4 %collective-permute-start.18 = (s16[1,1040,128]{2,1,0:T(8,128)(2,1)S(1)}, s16[1,1040,128]{2,1,0:T(8,128)(2,1)}, u32[]{:S(2)}, u32[]{:S(2)}) collective-permute-start(s16[1,1040,128]{2,1,0:T(8,128)(2,1)S(1)} %hop.9.refs_0_), channel_id=1, source_target_pairs={{8,16},{16,8},{9,17},{17,9},{10,18},{18,10},{11,19},{19,11},{12,20... | collective-permute-start | bytes 798728 | tf_op jit(solution)/shard_map/ppermute | solution.py:330
  66.4 16.4 %collective-permute-start.17 = (s16[1,1040,128]{2,1,0:T(8,128)(2,1)S(1)}, s16[1,1040,128]{2,1,0:T(8,128)(2,1)}, u32[]{:S(2)}, u32[]{:S(2)}) collective-permute-start(s16[1,1040,128]{2,1,0:T(8,128)(2,1)S(1)} %hop.11.refs_0_), channel_id=1, source_target_pairs={{8,16},{16,8},{9,17},{17,9},{10,18},{18,10},{11,19},{19,11},{12,20... | collective-permute-start | bytes 798728 | tf_op jit(solution)/shard_map/ppermute | solution.py:330
  69.4 17.1 %collective-permute-start.21 = (s16[1,1040,128]{2,1,0:T(8,128)(2,1)S(1)}, s16[1,1040,128]{2,1,0:T(8,128)(2,1)}, u32[]{:S(2)}, u32[]{:S(2)}) collective-permute-start(s16[1,1040,128]{2,1,0:T(8,128)(2,1)S(1)} %hop.13.refs_0_), channel_id=1, source_target_pairs={{8,16},{16,8},{9,17},{17,9},{10,18},{18,10},{11,19},{19,11},{12,20... | collective-permute-start | bytes 798728 | tf_op jit(solution)/shard_map/ppermute | solution.py:330
  70.8 17.8 %collective-permute-start.23 = (s16[1,1040,128]{2,1,0:T(8,128)(2,1)}, s16[1,1040,128]{2,1,0:T(8,128)(2,1)}, u32[]{:S(2)}, u32[]{:S(2)}) collective-permute-start(s16[1,1040,128]{2,1,0:T(8,128)(2,1)} %get-tuple-element.50), channel_id=1, source_target_pairs={{0,8},{24,16},{1,9},{25,17},{2,10},{26,18},{3,11},{27,19},{4,12},{... | collective-permute-start | bytes 798728 | tf_op jit(solution)/shard_map/ppermute | solution.py:330
  78.2 14.6 %collective-permute-start.25 = (s16[1,1040,128]{2,1,0:T(8,128)(2,1)S(1)}, s16[1,1040,128]{2,1,0:T(8,128)(2,1)}, u32[]{:S(2)}, u32[]{:S(2)}) collective-permute-start(s16[1,1040,128]{2,1,0:T(8,128)(2,1)S(1)} %hop.10.refs_0_), channel_id=1, source_target_pairs={{8,16},{16,8},{9,17},{17,9},{10,18},{18,10},{11,19},{19,11},{12,20... | collective-permute-start | bytes 798728 | tf_op jit(solution)/shard_map/ppermute | solution.py:330
  79.6 5.2 %copy-start.3 = (f32[16,8,32,128]{3,2,1,0:T(8,128)S(1)}, f32[16,8,32,128]{3,2,1,0:T(8,128)}, u32[]{:S(2)}) copy-start(f32[16,8,32,128]{3,2,1,0:T(8,128)} %copy-done.2) | copy-start | bytes 6291460
  79.6 14.5 %collective-permute-start.16 = (s16[1,1040,128]{2,1,0:T(8,128)(2,1)S(1)}, s16[1,1040,128]{2,1,0:T(8,128)(2,1)}, u32[]{:S(2)}, u32[]{:S(2)}) collective-permute-start(s16[1,1040,128]{2,1,0:T(8,128)(2,1)S(1)} %hop.12.refs_0_), channel_id=1, source_target_pairs={{8,16},{16,8},{9,17},{17,9},{10,18},{18,10},{11,19},{19,11},{12,20... | collective-permute-start | bytes 798728 | tf_op jit(solution)/shard_map/ppermute | solution.py:330
  82.8 4.1 %copy-start.5 = (f32[16,8,32,128]{3,2,1,0:T(8,128)S(1)}, f32[16,8,32,128]{3,2,1,0:T(8,128)}, u32[]{:S(2)}) copy-start(f32[16,8,32,128]{3,2,1,0:T(8,128)} %copy-done.4) | copy-start | bytes 6291460
  82.9 11.3 %collective-permute-start.26 = (s16[1,1040,128]{2,1,0:T(8,128)(2,1)S(1)}, s16[1,1040,128]{2,1,0:T(8,128)(2,1)}, u32[]{:S(2)}, u32[]{:S(2)}) collective-permute-start(s16[1,1040,128]{2,1,0:T(8,128)(2,1)S(1)} %hop.14.refs_0_), channel_id=1, source_target_pairs={{8,0},{0,8},{16,24},{24,16},{9,1},{1,9},{17,25},{25,17},{10,2},{2,... | collective-permute-start | bytes 798728 | tf_op jit(solution)/shard_map/ppermute | solution.py:330
  86.5 10.5 %collective-permute-start.20 = (s16[1,1040,128]{2,1,0:T(8,128)(2,1)S(1)}, s16[1,1040,128]{2,1,0:T(8,128)(2,1)}, u32[]{:S(2)}, u32[]{:S(2)}) collective-permute-start(s16[1,1040,128]{2,1,0:T(8,128)(2,1)S(1)} %hop.15.refs_0_), channel_id=1, source_target_pairs={{8,0},{0,8},{16,24},{24,16},{9,1},{1,9},{17,25},{25,17},{10,2},{2,... | collective-permute-start | bytes 798728 | tf_op jit(solution)/shard_map/ppermute | solution.py:330
  88.7 11.1 %collective-permute-start.22 = (s16[1,1040,128]{2,1,0:T(8,128)(2,1)S(1)}, s16[1,1040,128]{2,1,0:T(8,128)(2,1)}, u32[]{:S(2)}, u32[]{:S(2)}) collective-permute-start(s16[1,1040,128]{2,1,0:T(8,128)(2,1)S(1)} %hop.16.refs_0_), channel_id=1, source_target_pairs={{8,0},{0,8},{16,24},{24,16},{9,1},{1,9},{17,25},{25,17},{10,2},{2,... | collective-permute-start | bytes 798728 | tf_op jit(solution)/shard_map/ppermute | solution.py:330
  92.9 7.0 %collective-permute-start.24 = (s16[1,1040,128]{2,1,0:T(8,128)(2,1)}, s16[1,1040,128]{2,1,0:T(8,128)(2,1)S(1)}, u32[]{:S(2)}, u32[]{:S(2)}) collective-permute-start(s16[1,1040,128]{2,1,0:T(8,128)(2,1)} %hop.17), channel_id=1, source_target_pairs={{8,16},{16,8},{9,17},{17,9},{10,18},{18,10},{11,19},{19,11},{12,20... | collective-permute-start | bytes 798728 | tf_op jit(solution)/shard_map/ppermute | solution.py:330
  99.8 0.7 copy-start.12

commit v8 on v7

--- a/solution.py
+++ b/solution.py
@@ -235,7 +235,7 @@
         compiler_params=params(width),
         cost_estimate=cost(7.0),
         name="volume_sums",
-    )(index, *ties, *[far(x) for x in pieces], *([] if first else [meta]))
+    )(index, *ties, *([far(x) for x in pieces] if meta is None else pieces), *([] if first else [meta]))
     sums = done[0].reshape(groups, portion, width)
     return (sums, done[2:], done[1]) if first else (sums, done[1:], meta)
 
@@ -381,6 +381,7 @@
         for payload, place in ends:
             operands.append(payload)
             specs.append(pl.BlockSpec((1, rows + ALIGN, width), functools.partial(lambda place, i, s: (place, 0, 0), place)))
+    late = [payload for payload, _ in fields[1][1]]
     steps = np.arange(zs)
     angles = (steps[:, None] * steps[None, :] % zs) * (2.0 * math.pi / zs)
     table = (np.concatenate([np.cos(angles), np.sin(angles)], axis=0) / math.sqrt(zs)).astype(np.float32)
@@ -401,7 +402,7 @@
         compiler_params=params(width),
         cost_estimate=cost(6.0),
         name="image_of",
-    )(own, *[far(x) for x in operands])
+    )(own, *[x if any(x is y for y in late) else far(x) for x in operands])
 
 
 def on_device(spectra, ctf_sq, dest, block, pattern, pattern_table, tau):

time: 106 us -> 105 us (level)
    pallas_call x3, Pallas kernels: 20 us -> 18.7 us  [volume_sums(): pl.pallas_call(functools.partial(volume_kernel, slabs, window, messages,...]
    unnamed x36 -> x28, local copies, waits for them, and re-layouts: 3.74 us -> 3.21 us
  transfers between devices with their start and end apart: 27 -> 27, of which waited for: 6 -> 5; matrix products, arithmetic and copies ran while one was open for 1% -> 1% of each run, Pallas kernels for 39% -> 39%
where the time goes in v8:
time: 105 us; the launch traced here: 104 us
  Pallas kernels  45.6 us (43%)
  starting transfers between devices  42.4 us (40%)
  waiting for transfers between devices  11.4 us (11%)
  local copies, waits for them, and re-layouts  3.77 us (4%)
    ppermute x15, starting transfers between devices, send(): lax.ppermute(payload, 'grp', pairs + [(last - a, last - b) for a, b in pa...  28 us
    pallas_call x3, Pallas kernels, volume_sums(): pl.pallas_call(functools.partial(volume_kernel, slabs, window, messages,...  18.7 us
    ppermute x12, starting transfers between devices, swap(): return lax.ppermute(x, 'slab', [(i, i ^ offset) for i in range(slabs)])  14.4 us
    pallas_call x9, Pallas kernels, hop(): pl.pallas_call(functools.partial(hop_kernel, places), out_shape=jax.Shape...  11.6 us
    pallas_call x2, Pallas kernels, sort_columns(): pl.pallas_call(functools.partial(sort_kernel, slabs, width, part, len(tie...  6.34 us
    ppermute x12, waiting for transfers between devices, swap(): return lax.ppermute(x, 'slab', [(i, i ^ offset) for i in range(slabs)])  5.84 us
    ppermute x15, waiting for transfers between devices, send(): lax.ppermute(payload, 'grp', pairs + [(last - a, last - b) for a, b in pa...  5.6 us
    pallas_call x1, Pallas kernels, image_of(): pl.pallas_call(functools.partial(image_kernel, parts, zs), out_shape=jax....  4.71 us
  transfers between devices with their start and end apart: 27, of which 5 were waited for; matrix products, arithmetic and copies ran while one was open for 1% of the time, Pallas kernels for 39%

profile of v8, /device:TPU:0, one launch (start us, length us, event | category | flops | bytes accessed | tf_op | source)
XLA Modules:
  0.0 104.2 jit_solution(9911024176862196739)
XLA Ops:
  0.5 0.7 pad_add_fusion.refs_0_
  1.8 3.2 %collective-permute-done.refs_1_ = s32[3,512]{1,0:T(4,128)S(1)} collective-permute-done((s32[3,512]{1,0:T(4,128)S(1)}, s32[3,512]{1,0:T(4,128)S(1)}, u32[]{:S(2)}, u32[]{:S(2)}) %collective-permute-start) | collective-permute-done | bytes 6176 | tf_op jit(solution)/shard_map/ppermute | solution.py:147
  5.0 0.9 collective-permute-done.1.refs_4_
  5.9 4.2 %plan_rows.1 = (bf16[2,512,512]{2,1,0:T(8,128)(2,1)S(1)}, bf16[1152,128]{1,0:T(8,128)(2,1)S(1)}, bf16[1152,128]{1,0:T(8,128)(2,1)S(1)}, bf16[1152,128]{1,0:T(8,128)(2,1)}, bf16[1152,128]{1,0:T(8,128)(2,1)}) custom-call(s32[1]{0:T(128)} %bitcast.1.me_ref, s32[3,512]{1,0:T(4,128)} %copy-done.12, s32[3,512]{1,0:T(4,128)S(1)} %collective-permute-done.refs_1_, ...), custom_call_target="tpu_custom_call" | custom-call | bytes 18000000 | tf_op jit(solution)/shard_map/plan_rows/pallas_call | solution.py:101
  10.1 2.6 %collective-permute-start.3 = (bf16[1152,128]{1,0:T(8,128)(2,1)S(1)}, bf16[1152,128]{1,0:T(8,128)(2,1)S(1)}, u32[]{:S(2)}, u32[]{:S(2)}) collective-permute-start(bf16[1152,128]{1,0:T(8,128)(2,1)S(1)} %get-tuple-element.32), channel_id=1, source_target_pairs={{0,2},{1,3},{2,0},{3,1},{4,6},{5,7},{6,4},{7,5},{8,10},{9,11},{10,... | collective-permute-start | bytes 884744 | tf_op jit(solution)/shard_map/ppermute | solution.py:147
  12.7 1.5 %collective-permute-start.4 = (bf16[1152,128]{1,0:T(8,128)(2,1)}, bf16[1152,128]{1,0:T(8,128)(2,1)S(1)}, u32[]{:S(2)}, u32[]{:S(2)}) collective-permute-start(bf16[1152,128]{1,0:T(8,128)(2,1)} %get-tuple-element.33), channel_id=1, source_target_pairs={{0,4},{1,5},{2,6},{3,7},{4,0},{5,1},{6,2},{7,3},{8,12},{9,13},{10,... | collective-permute-start | bytes 884744 | tf_op jit(solution)/shard_map/ppermute | solution.py:147
  14.2 3.5 %sort_columns.2 = (bf16[1024,128]{1,0:T(8,128)(2,1)S(1)}, bf16[1024,128]{1,0:T(8,128)(2,1)}, bf16[1024,128]{1,0:T(8,128)(2,1)}, bf16[1024,128]{1,0:T(8,128)(2,1)}) custom-call(s32[1]{0:T(128)} %bitcast.1.me_ref, bf16[2,512,512]{2,1,0:T(8,128)(2,1)S(1)} %get-tuple-element.28.order_ref, bf16[512,2048]{1,0:T(8,128)(2,1)} %refs_0_.3, ...), custom_call_target="tpu_custom_call" | custom-call | bytes 9000000 | tf_op jit(solution)/shard_map/sort_columns/pallas_call | solution.py:131
  17.7 2.0 %collective-permute-start.6 = (bf16[1024,128]{1,0:T(8,128)(2,1)}, bf16[1024,128]{1,0:T(8,128)(2,1)S(1)}, u32[]{:S(2)}, u32[]{:S(2)}) collective-permute-start(bf16[1024,128]{1,0:T(8,128)(2,1)} %get-tuple-element.36), channel_id=1, source_target_pairs={{0,2},{1,3},{2,0},{3,1},{4,6},{5,7},{6,4},{7,5},{8,10},{9,11},{10,... | collective-permute-start | bytes 786440 | tf_op jit(solution)/shard_map/ppermute | solution.py:147
  19.7 1.5 %collective-permute-start.7 = (bf16[1024,128]{1,0:T(8,128)(2,1)}, bf16[1024,128]{1,0:T(8,128)(2,1)S(1)}, u32[]{:S(2)}, u32[]{:S(2)}) collective-permute-start(bf16[1024,128]{1,0:T(8,128)(2,1)} %get-tuple-element.37), channel_id=1, source_target_pairs={{0,4},{1,5},{2,6},{3,7},{4,0},{5,1},{6,2},{7,3},{8,12},{9,13},{10,... | collective-permute-start | bytes 786440 | tf_op jit(solution)/shard_map/ppermute | solution.py:147
  21.2 0.7 copy-done.9
  21.9 2.2 %collective-permute-start.8 = (bf16[1024,128]{1,0:T(8,128)(2,1)}, bf16[1024,128]{1,0:T(8,128)(2,1)S(1)}, u32[]{:S(2)}, u32[]{:S(2)}) collective-permute-start(bf16[1024,128]{1,0:T(8,128)(2,1)} %get-tuple-element.38), channel_id=1, source_target_pairs={{0,6},{1,7},{2,4},{3,5},{4,2},{5,3},{6,0},{7,1},{8,14},{9,15},{10,... | collective-permute-start | bytes 786440 | tf_op jit(solution)/shard_map/ppermute | solution.py:147
  24.2 2.8 %sort_columns.3 = (bf16[1024,128]{1,0:T(8,128)(2,1)S(1)}, bf16[1024,128]{1,0:T(8,128)(2,1)S(1)}, bf16[1024,128]{1,0:T(8,128)(2,1)S(1)}, bf16[1024,128]{1,0:T(8,128)(2,1)S(1)}) custom-call(s32[1]{0:T(128)} %bitcast.1.me_ref, bf16[2,512,512]{2,1,0:T(8,128)(2,1)S(1)} %get-tuple-element.28.order_ref, bf16[512,2048]{1,0:T(8,128)(2,1)} %refs_0_.3, ...), custom_call_target="tpu_custom_call" | custom-call | bytes 9000000 | tf_op jit(solution)/shard_map/sort_columns/pallas_call | solution.py:131
  27.0 1.7 %collective-permute-done.4.refs_3_ = bf16[1152,128]{1,0:T(8,128)(2,1)S(1)} collective-permute-done((bf16[1152,128]{1,0:T(8,128)(2,1)}, bf16[1152,128]{1,0:T(8,128)(2,1)S(1)}, u32[]{:S(2)}, u32[]{:S(2)}) %collective-permute-start.4) | collective-permute-done | bytes 294944 | tf_op jit(solution)/shard_map/ppermute | solution.py:147
  28.7 0.7 copy-done.10
  29.5 6.6 %volume_sums.3 = (f32[16,8,32,128]{3,2,1,0:T(8,128)S(1)}, bf16[8,16,512]{2,1,0:T(8,128)(2,1)S(1)}, s16[1,1040,128]{2,1,0:T(8,128)(2,1)S(1)}, s16[1,1040,128]{2,1,0:T(8,128)(2,1)S(1)}) custom-call(s32[2]{0:T(128)S(1)} %broadcast_select_fusion.idx_ref, bf16[1024,128]{1,0:T(8,128)(2,1)S(1)} %get-tuple-element.30.refs_0_.refs_1_, bf16[1152,128]{1,0:T(8,128)(2,1)} %copy-done.6, ...), custom_call_target="tpu_custom_call" | custom-call | bytes 21000000 | tf_op jit(solution)/shard_map/volume_sums/pallas_call | solution.py:224
  36.1 3.5 %collective-permute-start.12 = (s16[1,1040,128]{2,1,0:T(8,128)(2,1)S(1)}, s16[1,1040,128]{2,1,0:T(8,128)(2,1)S(1)}, u32[]{:S(2)}, u32[]{:S(2)}) collective-permute-start(s16[1,1040,128]{2,1,0:T(8,128)(2,1)S(1)} %get-tuple-element.35.refs_0_), channel_id=1, source_target_pairs={{0,8},{24,16},{1,9},{25,17},{2,10},{26,18},{3,11},{27,19},{4,12},{... | collective-permute-start | bytes 798728 | tf_op jit(solution)/shard_map/ppermute | solution.py:330
  39.6 1.5 %collective-permute-start.11 = (s16[1,1040,128]{2,1,0:T(8,128)(2,1)S(1)}, s16[1,1040,128]{2,1,0:T(8,128)(2,1)S(1)}, u32[]{:S(2)}, u32[]{:S(2)}) collective-permute-start(s16[1,1040,128]{2,1,0:T(8,128)(2,1)S(1)} %get-tuple-element.44), channel_id=1, source_target_pairs={{0,8},{24,16},{1,9},{25,17},{2,10},{26,18},{3,11},{27,19},{4,12},{... | collective-permute-start | bytes 798728 | tf_op jit(solution)/shard_map/ppermute | solution.py:330
  41.1 1.1 %collective-permute-start.13 = (bf16[1024,128]{1,0:T(8,128)(2,1)S(1)}, bf16[1024,128]{1,0:T(8,128)(2,1)S(1)}, u32[]{:S(2)}, u32[]{:S(2)}) collective-permute-start(bf16[1024,128]{1,0:T(8,128)(2,1)S(1)} %get-tuple-element.45), channel_id=1, source_target_pairs={{0,2},{1,3},{2,0},{3,1},{4,6},{5,7},{6,4},{7,5},{8,10},{9,11},{10,... | collective-permute-start | bytes 786440 | tf_op jit(solution)/shard_map/ppermute | solution.py:147
  42.2 1.1 %collective-permute-start.14 = (bf16[1024,128]{1,0:T(8,128)(2,1)S(1)}, bf16[1024,128]{1,0:T(8,128)(2,1)S(1)}, u32[]{:S(2)}, u32[]{:S(2)}) collective-permute-start(bf16[1024,128]{1,0:T(8,128)(2,1)S(1)} %get-tuple-element.46), channel_id=1, source_target_pairs={{0,4},{1,5},{2,6},{3,7},{4,0},{5,1},{6,2},{7,3},{8,12},{9,13},{10,... | collective-permute-start | bytes 786440 | tf_op jit(solution)/shard_map/ppermute | solution.py:147
  43.2 0.7 copy-done.7
  43.9 1.4 %collective-permute-start.15 = (bf16[1024,128]{1,0:T(8,128)(2,1)S(1)}, bf16[1024,128]{1,0:T(8,128)(2,1)S(1)}, u32[]{:S(2)}, u32[]{:S(2)}) collective-permute-start(bf16[1024,128]{1,0:T(8,128)(2,1)S(1)} %get-tuple-element.47), channel_id=1, source_target_pairs={{0,6},{1,7},{2,4},{3,5},{4,2},{5,3},{6,0},{7,1},{8,14},{9,15},{10,... | collective-permute-start | bytes 786440 | tf_op jit(solution)/shard_map/ppermute | solution.py:147
  45.4 0.9 copy-done.8
  46.3 5.8 %volume_sums.4 = (f32[16,8,32,128]{3,2,1,0:T(8,128)S(1)}, s16[1,1040,128]{2,1,0:T(8,128)(2,1)S(1)}, s16[1,1040,128]{2,1,0:T(8,128)(2,1)S(1)}) custom-call(s32[2]{0:T(128)S(1)} %broadcast_select_fusion.idx_ref, s16[1,1040,128]{2,1,0:T(8,128)(2,1)S(1)} %get-tuple-element.35.refs_0_, bf16[1024,128]{1,0:T(8,128)(2,1)S(1)} %get-tuple-element.29.refs_2_.refs_1_, ...), custom_call_target="tpu_custom_call" | custom-call | bytes 21000000 | tf_op jit(solution)/shard_map/volume_sums/pallas_call | solution.py:224
  52.2 1.3 %collective-permute-start.10 = (s16[1,1040,128]{2,1,0:T(8,128)(2,1)S(1)}, s16[1,1040,128]{2,1,0:T(8,128)(2,1)S(1)}, u32[]{:S(2)}, u32[]{:S(2)}) collective-permute-start(s16[1,1040,128]{2,1,0:T(8,128)(2,1)S(1)} %get-tuple-element.42.refs_0_), channel_id=1, source_target_pairs={{0,8},{24,16},{1,9},{25,17},{2,10},{26,18},{3,11},{27,19},{4,12},{... | collective-permute-start | bytes 798728 | tf_op jit(solution)/shard_map/ppermute | solution.py:330
  53.5 0.8 hop.9.refs_0_
  54.3 1.3 %collective-permute-start.9 = (s16[1,1040,128]{2,1,0:T(8,128)(2,1)S(1)}, s16[1,1040,128]{2,1,0:T(8,128)(2,1)S(1)}, u32[]{:S(2)}, u32[]{:S(2)}) collective-permute-start(s16[1,1040,128]{2,1,0:T(8,128)(2,1)S(1)} %get-tuple-element.41), channel_id=1, source_target_pairs={{0,8},{24,16},{1,9},{25,17},{2,10},{26,18},{3,11},{27,19},{4,12},{... | collective-permute-start | bytes 798728 | tf_op jit(solution)/shard_map/ppermute | solution.py:330
  55.6 0.8 hop.10.refs_0_
  56.4 6.3 %volume_sums.5 = (f32[16,8,32,128]{3,2,1,0:T(8,128)S(1)}, s16[1,1040,128]{2,1,0:T(8,128)(2,1)S(1)}, s16[1,1040,128]{2,1,0:T(8,128)(2,1)}) custom-call(s32[2]{0:T(128)S(1)} %broadcast_select_fusion.idx_ref, s16[1,1040,128]{2,1,0:T(8,128)(2,1)S(1)} %hop.10.refs_0_, bf16[1024,128]{1,0:T(8,128)(2,1)S(1)} %get-tuple-element.30.refs_0_.refs_1_, ...), custom_call_target="tpu_custom_call" | custom-call | bytes 21000000 | tf_op jit(solution)/shard_map/volume_sums/pallas_call | solution.py:224
  62.8 1.3 %collective-permute-start.19 = (s16[1,1040,128]{2,1,0:T(8,128)(2,1)S(1)}, s16[1,1040,128]{2,1,0:T(8,128)(2,1)S(1)}, u32[]{:S(2)}, u32[]{:S(2)}) collective-permute-start(s16[1,1040,128]{2,1,0:T(8,128)(2,1)S(1)} %get-tuple-element.48.refs_0_), channel_id=1, source_target_pairs={{0,8},{24,16},{1,9},{25,17},{2,10},{26,18},{3,11},{27,19},{4,12},{... | collective-permute-start | bytes 798728 | tf_op jit(solution)/shard_map/ppermute | solution.py:330
  64.1 1.4 %collective-permute-start.18 = (s16[1,1040,128]{2,1,0:T(8,128)(2,1)S(1)}, s16[1,1040,128]{2,1,0:T(8,128)(2,1)}, u32[]{:S(2)}, u32[]{:S(2)}) collective-permute-start(s16[1,1040,128]{2,1,0:T(8,128)(2,1)S(1)} %hop.9.refs_0_), channel_id=1, source_target_pairs={{8,16},{16,8},{9,17},{17,9},{10,18},{18,10},{11,19},{19,11},{12,20... | collective-permute-start | bytes 798728 | tf_op jit(solution)/shard_map/ppermute | solution.py:330
  65.5 0.8 hop.11.refs_0_
  66.3 1.4 %collective-permute-start.17 = (s16[1,1040,128]{2,1,0:T(8,128)(2,1)S(1)}, s16[1,1040,128]{2,1,0:T(8,128)(2,1)}, u32[]{:S(2)}, u32[]{:S(2)}) collective-permute-start(s16[1,1040,128]{2,1,0:T(8,128)(2,1)S(1)} %hop.11.refs_0_), channel_id=1, source_target_pairs={{8,16},{16,8},{9,17},{17,9},{10,18},{18,10},{11,19},{19,11},{12,20... | collective-permute-start | bytes 798728 | tf_op jit(solution)/shard_map/ppermute | solution.py:330
  67.6 0.8 hop.12.refs_0_
  68.4 0.8 hop.13.refs_0_
  69.2 1.4 %collective-permute-start.21 = (s16[1,1040,128]{2,1,0:T(8,128)(2,1)S(1)}, s16[1,1040,128]{2,1,0:T(8,128)(2,1)}, u32[]{:S(2)}, u32[]{:S(2)}) collective-permute-start(s16[1,1040,128]{2,1,0:T(8,128)(2,1)S(1)} %hop.13.refs_0_), channel_id=1, source_target_pairs={{8,16},{16,8},{9,17},{17,9},{10,18},{18,10},{11,19},{19,11},{12,20... | collective-permute-start | bytes 798728 | tf_op jit(solution)/shard_map/ppermute | solution.py:330
  70.6 7.4 %collective-permute-start.23 = (s16[1,1040,128]{2,1,0:T(8,128)(2,1)}, s16[1,1040,128]{2,1,0:T(8,128)(2,1)}, u32[]{:S(2)}, u32[]{:S(2)}) collective-permute-start(s16[1,1040,128]{2,1,0:T(8,128)(2,1)} %get-tuple-element.50), channel_id=1, source_target_pairs={{0,8},{24,16},{1,9},{25,17},{2,10},{26,18},{3,11},{27,19},{4,12},{... | collective-permute-start | bytes 798728 | tf_op jit(solution)/shard_map/ppermute | solution.py:330
  78.1 1.4 %collective-permute-start.25 = (s16[1,1040,128]{2,1,0:T(8,128)(2,1)S(1)}, s16[1,1040,128]{2,1,0:T(8,128)(2,1)}, u32[]{:S(2)}, u32[]{:S(2)}) collective-permute-start(s16[1,1040,128]{2,1,0:T(8,128)(2,1)S(1)} %hop.10.refs_0_), channel_id=1, source_target_pairs={{8,16},{16,8},{9,17},{17,9},{10,18},{18,10},{11,19},{19,11},{12,20... | collective-permute-start | bytes 798728 | tf_op jit(solution)/shard_map/ppermute | solution.py:330
  79.5 1.5 %collective-permute-start.16 = (s16[1,1040,128]{2,1,0:T(8,128)(2,1)S(1)}, s16[1,1040,128]{2,1,0:T(8,128)(2,1)}, u32[]{:S(2)}, u32[]{:S(2)}) collective-permute-start(s16[1,1040,128]{2,1,0:T(8,128)(2,1)S(1)} %hop.12.refs_0_), channel_id=1, source_target_pairs={{8,16},{16,8},{9,17},{17,9},{10,18},{18,10},{11,19},{19,11},{12,20... | collective-permute-start | bytes 798728 | tf_op jit(solution)/shard_map/ppermute | solution.py:330
  81.0 1.7 %hop.14.refs_0_ = s16[1,1040,128]{2,1,0:T(8,128)(2,1)S(1)} custom-call(s32[1]{0:T(128)S(6)} %select_n.51.idx_ref, f32[4,1024,128]{2,1,0:T(8,128)S(1)} %bitcast.15, s16[1,1040,128]{2,1,0:T(8,128)(2,1)} %collective-permute-done.18.prev_ref, s16[1,1040,128]{2,1,0:T(8,128)(2,1)S(1)} %hop.13.refs_0_), custom_call_target="tpu_custom_call" | custom-call | bytes 9000000 | tf_op jit(solution)/shard_map/hop/pallas_call | solution.py:290
  82.7 1.9 %collective-permute-start.26 = (s16[1,1040,128]{2,1,0:T(8,128)(2,1)S(1)}, s16[1,1040,128]{2,1,0:T(8,128)(2,1)}, u32[]{:S(2)}, u32[]{:S(2)}) collective-permute-start(s16[1,1040,128]{2,1,0:T(8,128)(2,1)S(1)} %hop.14.refs_0_), channel_id=1, source_target_pairs={{8,0},{0,8},{16,24},{24,16},{9,1},{1,9},{17,25},{25,17},{10,2},{2,... | collective-permute-start | bytes 798728 | tf_op jit(solution)/shard_map/ppermute | solution.py:330
  84.6 1.7 %hop.15.refs_0_ = s16[1,1040,128]{2,1,0:T(8,128)(2,1)S(1)} custom-call(s32[1]{0:T(128)S(6)} %select_n.51.idx_ref, f32[4,1024,128]{2,1,0:T(8,128)S(1)} %bitcast.20, s16[1,1040,128]{2,1,0:T(8,128)(2,1)} %collective-permute-done.17.prev_ref, s16[1,1040,128]{2,1,0:T(8,128)(2,1)S(1)} %hop.14.refs_0_), custom_call_target="tpu_custom_call" | custom-call | bytes 9000000 | tf_op jit(solution)/shard_map/hop/pallas_call | solution.py:290
  86.8 1.7 %hop.16.refs_0_ = s16[1,1040,128]{2,1,0:T(8,128)(2,1)S(1)} custom-call(s32[1]{0:T(128)S(6)} %select_n.51.idx_ref, f32[4,1024,128]{2,1,0:T(8,128)S(1)} %bitcast.23, s16[1,1040,128]{2,1,0:T(8,128)(2,1)} %collective-permute-done.21.prev_ref, s16[1,1040,128]{2,1,0:T(8,128)(2,1)S(1)} %hop.15.refs_0_), custom_call_target="tpu_custom_call" | custom-call | bytes 9000000 | tf_op jit(solution)/shard_map/hop/pallas_call | solution.py:290
  88.5 1.7 %collective-permute-start.22 = (s16[1,1040,128]{2,1,0:T(8,128)(2,1)S(1)}, s16[1,1040,128]{2,1,0:T(8,128)(2,1)}, u32[]{:S(2)}, u32[]{:S(2)}) collective-permute-start(s16[1,1040,128]{2,1,0:T(8,128)(2,1)S(1)} %hop.16.refs_0_), channel_id=1, source_target_pairs={{8,0},{0,8},{16,24},{24,16},{9,1},{1,9},{17,25},{25,17},{10,2},{2,... | collective-permute-start | bytes 798728 | tf_op jit(solution)/shard_map/ppermute | solution.py:330
  90.3 2.4 %hop.17 = s16[1,1040,128]{2,1,0:T(8,128)(2,1)} custom-call(s32[1]{0:T(128)S(6)} %select_n.48.idx_ref, f32[4,1024,128]{2,1,0:T(8,128)S(1)} %bitcast.24, s16[1,1040,128]{2,1,0:T(8,128)(2,1)} %collective-permute-done.23.prev_ref, s16[1,1040,128]{2,1,0:T(8,128)(2,1)S(1)} %hop.16.refs_0_), custom_call_target="tpu_custom_call" | custom-call | bytes 9000000 | tf_op jit(solution)/shard_map/hop/pallas_call | solution.py:290
  92.7 0.7 collective-permute-start.24
  94.0 2.7 %collective-permute-done.20.refs_2_ = s16[1,1040,128]{2,1,0:T(8,128)(2,1)} collective-permute-done((s16[1,1040,128]{2,1,0:T(8,128)(2,1)S(1)}, s16[1,1040,128]{2,1,0:T(8,128)(2,1)}, u32[]{:S(2)}, u32[]{:S(2)}) %collective-permute-start.20) | collective-permute-done | bytes 266272 | tf_op jit(solution)/shard_map/ppermute | solution.py:330
  96.7 2.9 %collective-permute-done.22.refs_4_ = s16[1,1040,128]{2,1,0:T(8,128)(2,1)} collective-permute-done((s16[1,1040,128]{2,1,0:T(8,128)(2,1)S(1)}, s16[1,1040,128]{2,1,0:T(8,128)(2,1)}, u32[]{:S(2)}, u32[]{:S(2)}) %collective-permute-start.22) | collective-permute-done | bytes 266272 | tf_op jit(solution)/shard_map/ppermute | solution.py:330
  99.5 4.7 %image_of.1 = f32[2,4,256,128]{3,2,1,0:T(8,128)} custom-call(s32[1]{0:T(128)} %bitcast.own_ref, f32[4,1024,128]{2,1,0:T(8,128)} %bitcast.19, s16[1,1040,128]{2,1,0:T(8,128)(2,1)} %collective-permute-done.16.refs_1_, s16[1,1040,128]{2,1,0:T(8,128)(2,1)} %collective-permute-done.20.refs_2_, f32[4,1024,128]{2,1,0:T(8,128)} %bitcast.22, ...), custom_call_target="tpu_custom_call" | custom-call | bytes 18000000 | tf_op jit(solution)/shard_map/image_of/pallas_call | solution.py:393
  (53 shorter events, 2.2 us)
Async XLA Ops:
  0.0 93.4 %copy-start = (f32[1024]{0:T(1024)S(1)}, f32[1024]{0:T(1024)}, u32[]{:S(2)}) copy-start(f32[1024]{0:T(1024)} %param.17) | copy-start | bytes 12292
  0.0 14.2 %collective-permute-start.2 = (bf16[512,2048]{1,0:T(8,128)(2,1)}, bf16[512,2048]{1,0:T(8,128)(2,1)}, u32[]{:S(2)}, u32[]{:S(2)}) collective-permute-start(bf16[512,2048]{1,0:T(8,128)(2,1)} %refs_0_.3), channel_id=1, source_target_pairs={{0,1},{1,0},{2,3},{3,2},{4,5},{5,4},{6,7},{7,6},{8,9},{9,8},{10,11... | collective-permute-start | bytes 6291464 | tf_op jit(solution)/shard_map/ppermute | solution.py:147
  0.5 5.4 %collective-permute-start.1 = (bf16[512,1024]{1,0:T(8,128)(2,1)}, bf16[512,1024]{1,0:T(8,128)(2,1)S(1)}, u32[]{:S(2)}, u32[]{:S(2)}) collective-permute-start(bf16[512,1024]{1,0:T(8,128)(2,1)} %refs_3_.1), channel_id=1, source_target_pairs={{0,1},{1,0},{2,3},{3,2},{4,5},{5,4},{6,7},{7,6},{8,9},{9,8},{10,11... | collective-permute-start | bytes 3145736 | tf_op jit(solution)/shard_map/ppermute | solution.py:147
  1.3 4.6 %copy-start.12 = (s32[3,512]{1,0:T(4,128)}, s32[3,512]{1,0:T(4,128)S(1)}, u32[]{:S(2)}) copy-start(s32[3,512]{1,0:T(4,128)S(1)} %pad_add_fusion.refs_0_) | copy-start | bytes 18436
  1.3 3.7 %collective-permute-start = (s32[3,512]{1,0:T(4,128)S(1)}, s32[3,512]{1,0:T(4,128)S(1)}, u32[]{:S(2)}, u32[]{:S(2)}) collective-permute-start(s32[3,512]{1,0:T(4,128)S(1)} %pad_add_fusion.refs_0_), channel_id=1, source_target_pairs={{0,1},{1,0},{2,3},{3,2},{4,5},{5,4},{6,7},{7,6},{8,9},{9,8},{10,11... | collective-permute-start | bytes 18440 | tf_op jit(solution)/shard_map/ppermute | solution.py:147
  10.1 7.6 %copy-start.6 = (bf16[1152,128]{1,0:T(8,128)(2,1)}, bf16[1152,128]{1,0:T(8,128)(2,1)S(1)}, u32[]{:S(2)}) copy-start(bf16[1152,128]{1,0:T(8,128)(2,1)S(1)} %get-tuple-element.31.refs_1_) | copy-start | bytes 884740
  10.1 11.1 %collective-permute-start.3 = (bf16[1152,128]{1,0:T(8,128)(2,1)S(1)}, bf16[1152,128]{1,0:T(8,128)(2,1)S(1)}, u32[]{:S(2)}, u32[]{:S(2)}) collective-permute-start(bf16[1152,128]{1,0:T(8,128)(2,1)S(1)} %get-tuple-element.32), channel_id=1, source_target_pairs={{0,2},{1,3},{2,0},{3,1},{4,6},{5,7},{6,4},{7,5},{8,10},{9,11},{10,... | collective-permute-start | bytes 884744 | tf_op jit(solution)/shard_map/ppermute | solution.py:147
  12.7 16.0 %collective-permute-start.4 = (bf16[1152,128]{1,0:T(8,128)(2,1)}, bf16[1152,128]{1,0:T(8,128)(2,1)S(1)}, u32[]{:S(2)}, u32[]{:S(2)}) collective-permute-start(bf16[1152,128]{1,0:T(8,128)(2,1)} %get-tuple-element.33), channel_id=1, source_target_pairs={{0,4},{1,5},{2,6},{3,7},{4,0},{5,1},{6,2},{7,3},{8,12},{9,13},{10,... | collective-permute-start | bytes 884744 | tf_op jit(solution)/shard_map/ppermute | solution.py:147
  14.2 14.5 %collective-permute-start.5 = (bf16[1152,128]{1,0:T(8,128)(2,1)}, bf16[1152,128]{1,0:T(8,128)(2,1)S(1)}, u32[]{:S(2)}, u32[]{:S(2)}) collective-permute-start(bf16[1152,128]{1,0:T(8,128)(2,1)} %get-tuple-element.34), channel_id=1, source_target_pairs={{0,6},{1,7},{2,4},{3,5},{4,2},{5,3},{6,0},{7,1},{8,14},{9,15},{10,... | collective-permute-start | bytes 884744 | tf_op jit(solution)/shard_map/ppermute | solution.py:147
  14.2 10.0 %copy-start.13 = (s32[2]{0:T(128)S(1)}, s32[2]{0:T(128)}, u32[]{:S(2)}) copy-start(s32[2]{0:T(128)} %constant.36.clone) | copy-start | bytes 28
  17.7 23.4 %collective-permute-start.6 = (bf16[1024,128]{1,0:T(8,128)(2,1)}, bf16[1024,128]{1,0:T(8,128)(2,1)S(1)}, u32[]{:S(2)}, u32[]{:S(2)}) collective-permute-start(bf16[1024,128]{1,0:T(8,128)(2,1)} %get-tuple-element.36), channel_id=1, source_target_pairs={{0,2},{1,3},{2,0},{3,1},{4,6},{5,7},{6,4},{7,5},{8,10},{9,11},{10,... | collective-permute-start | bytes 786440 | tf_op jit(solution)/shard_map/ppermute | solution.py:147
  19.7 22.5 %collective-permute-start.7 = (bf16[1024,128]{1,0:T(8,128)(2,1)}, bf16[1024,128]{1,0:T(8,128)(2,1)S(1)}, u32[]{:S(2)}, u32[]{:S(2)}) collective-permute-start(bf16[1024,128]{1,0:T(8,128)(2,1)} %get-tuple-element.37), channel_id=1, source_target_pairs={{0,4},{1,5},{2,6},{3,7},{4,0},{5,1},{6,2},{7,3},{8,12},{9,13},{10,... | collective-permute-start | bytes 786440 | tf_op jit(solution)/shard_map/ppermute | solution.py:147
  21.2 0.7 copy-start.9
  21.9 21.3 %collective-permute-start.8 = (bf16[1024,128]{1,0:T(8,128)(2,1)}, bf16[1024,128]{1,0:T(8,128)(2,1)S(1)}, u32[]{:S(2)}, u32[]{:S(2)}) collective-permute-start(bf16[1024,128]{1,0:T(8,128)(2,1)} %get-tuple-element.38), channel_id=1, source_target_pairs={{0,6},{1,7},{2,4},{3,5},{4,2},{5,3},{6,0},{7,1},{8,14},{9,15},{10,... | collective-permute-start | bytes 786440 | tf_op jit(solution)/shard_map/ppermute | solution.py:147
  28.7 0.7 copy-start.10
  28.7 0.8 copy-start.11
  36.1 44.9 %copy-start.1 = (f32[16,8,32,128]{3,2,1,0:T(8,128)}, f32[16,8,32,128]{3,2,1,0:T(8,128)S(1)}, u32[]{:S(2)}) copy-start(f32[16,8,32,128]{3,2,1,0:T(8,128)S(1)} %get-tuple-element.43) | copy-start | bytes 6291460
  36.1 16.1 %collective-permute-start.12 = (s16[1,1040,128]{2,1,0:T(8,128)(2,1)S(1)}, s16[1,1040,128]{2,1,0:T(8,128)(2,1)S(1)}, u32[]{:S(2)}, u32[]{:S(2)}) collective-permute-start(s16[1,1040,128]{2,1,0:T(8,128)(2,1)S(1)} %get-tuple-element.35.refs_0_), channel_id=1, source_target_pairs={{0,8},{24,16},{1,9},{25,17},{2,10},{26,18},{3,11},{27,19},{4,12},{... | collective-permute-start | bytes 798728 | tf_op jit(solution)/shard_map/ppermute | solution.py:330
  39.6 14.7 %collective-permute-start.11 = (s16[1,1040,128]{2,1,0:T(8,128)(2,1)S(1)}, s16[1,1040,128]{2,1,0:T(8,128)(2,1)S(1)}, u32[]{:S(2)}, u32[]{:S(2)}) collective-permute-start(s16[1,1040,128]{2,1,0:T(8,128)(2,1)S(1)} %get-tuple-element.44), channel_id=1, source_target_pairs={{0,8},{24,16},{1,9},{25,17},{2,10},{26,18},{3,11},{27,19},{4,12},{... | collective-permute-start | bytes 798728 | tf_op jit(solution)/shard_map/ppermute | solution.py:330
  41.1 15.3 %collective-permute-start.13 = (bf16[1024,128]{1,0:T(8,128)(2,1)S(1)}, bf16[1024,128]{1,0:T(8,128)(2,1)S(1)}, u32[]{:S(2)}, u32[]{:S(2)}) collective-permute-start(bf16[1024,128]{1,0:T(8,128)(2,1)S(1)} %get-tuple-element.45), channel_id=1, source_target_pairs={{0,2},{1,3},{2,0},{3,1},{4,6},{5,7},{6,4},{7,5},{8,10},{9,11},{10,... | collective-permute-start | bytes 786440 | tf_op jit(solution)/shard_map/ppermute | solution.py:147
  42.2 14.2 %collective-permute-start.14 = (bf16[1024,128]{1,0:T(8,128)(2,1)S(1)}, bf16[1024,128]{1,0:T(8,128)(2,1)S(1)}, u32[]{:S(2)}, u32[]{:S(2)}) collective-permute-start(bf16[1024,128]{1,0:T(8,128)(2,1)S(1)} %get-tuple-element.46), channel_id=1, source_target_pairs={{0,4},{1,5},{2,6},{3,7},{4,0},{5,1},{6,2},{7,3},{8,12},{9,13},{10,... | collective-permute-start | bytes 786440 | tf_op jit(solution)/shard_map/ppermute | solution.py:147
  43.2 0.7 copy-start.7
  43.9 12.5 %collective-permute-start.15 = (bf16[1024,128]{1,0:T(8,128)(2,1)S(1)}, bf16[1024,128]{1,0:T(8,128)(2,1)S(1)}, u32[]{:S(2)}, u32[]{:S(2)}) collective-permute-start(bf16[1024,128]{1,0:T(8,128)(2,1)S(1)} %get-tuple-element.47), channel_id=1, source_target_pairs={{0,6},{1,7},{2,4},{3,5},{4,2},{5,3},{6,0},{7,1},{8,14},{9,15},{10,... | collective-permute-start | bytes 786440 | tf_op jit(solution)/shard_map/ppermute | solution.py:147
  45.4 0.9 copy-start.8
  52.2 15.5 %copy-start.2 = (f32[16,8,32,128]{3,2,1,0:T(8,128)}, f32[16,8,32,128]{3,2,1,0:T(8,128)S(1)}, u32[]{:S(2)}) copy-start(f32[16,8,32,128]{3,2,1,0:T(8,128)S(1)} %get-tuple-element.40) | copy-start | bytes 6291460
  52.2 13.3 %collective-permute-start.10 = (s16[1,1040,128]{2,1,0:T(8,128)(2,1)S(1)}, s16[1,1040,128]{2,1,0:T(8,128)(2,1)S(1)}, u32[]{:S(2)}, u32[]{:S(2)}) collective-permute-start(s16[1,1040,128]{2,1,0:T(8,128)(2,1)S(1)} %get-tuple-element.42.refs_0_), channel_id=1, source_target_pairs={{0,8},{24,16},{1,9},{25,17},{2,10},{26,18},{3,11},{27,19},{4,12},{... | collective-permute-start | bytes 798728 | tf_op jit(solution)/shard_map/ppermute | solution.py:330
  54.3 13.3 %collective-permute-start.9 = (s16[1,1040,128]{2,1,0:T(8,128)(2,1)S(1)}, s16[1,1040,128]{2,1,0:T(8,128)(2,1)S(1)}, u32[]{:S(2)}, u32[]{:S(2)}) collective-permute-start(s16[1,1040,128]{2,1,0:T(8,128)(2,1)S(1)} %get-tuple-element.41), channel_id=1, source_target_pairs={{0,8},{24,16},{1,9},{25,17},{2,10},{26,18},{3,11},{27,19},{4,12},{... | collective-permute-start | bytes 798728 | tf_op jit(solution)/shard_map/ppermute | solution.py:330
  62.8 5.7 %copy-start.4 = (f32[16,8,32,128]{3,2,1,0:T(8,128)}, f32[16,8,32,128]{3,2,1,0:T(8,128)S(1)}, u32[]{:S(2)}) copy-start(f32[16,8,32,128]{3,2,1,0:T(8,128)S(1)} %get-tuple-element.49) | copy-start | bytes 6291460
  62.8 5.6 %collective-permute-start.19 = (s16[1,1040,128]{2,1,0:T(8,128)(2,1)S(1)}, s16[1,1040,128]{2,1,0:T(8,128)(2,1)S(1)}, u32[]{:S(2)}, u32[]{:S(2)}) collective-permute-start(s16[1,1040,128]{2,1,0:T(8,128)(2,1)S(1)} %get-tuple-element.48.refs_0_), channel_id=1, source_target_pairs={{0,8},{24,16},{1,9},{25,17},{2,10},{26,18},{3,11},{27,19},{4,12},{... | collective-permute-start | bytes 798728 | tf_op jit(solution)/shard_map/ppermute | solution.py:330
  64.1 15.4 %collective-permute-start.18 = (s16[1,1040,128]{2,1,0:T(8,128)(2,1)S(1)}, s16[1,1040,128]{2,1,0:T(8,128)(2,1)}, u32[]{:S(2)}, u32[]{:S(2)}) collective-permute-start(s16[1,1040,128]{2,1,0:T(8,128)(2,1)S(1)} %hop.9.refs_0_), channel_id=1, source_target_pairs={{8,16},{16,8},{9,17},{17,9},{10,18},{18,10},{11,19},{19,11},{12,20... | collective-permute-start | bytes 798728 | tf_op jit(solution)/shard_map/ppermute | solution.py:330
  66.3 16.5 %collective-permute-start.17 = (s16[1,1040,128]{2,1,0:T(8,128)(2,1)S(1)}, s16[1,1040,128]{2,1,0:T(8,128)(2,1)}, u32[]{:S(2)}, u32[]{:S(2)}) collective-permute-start(s16[1,1040,128]{2,1,0:T(8,128)(2,1)S(1)} %hop.11.refs_0_), channel_id=1, source_target_pairs={{8,16},{16,8},{9,17},{17,9},{10,18},{18,10},{11,19},{19,11},{12,20... | collective-permute-start | bytes 798728 | tf_op jit(solution)/shard_map/ppermute | solution.py:330
  69.2 17.1 %collective-permute-start.21 = (s16[1,1040,128]{2,1,0:T(8,128)(2,1)S(1)}, s16[1,1040,128]{2,1,0:T(8,128)(2,1)}, u32[]{:S(2)}, u32[]{:S(2)}) collective-permute-start(s16[1,1040,128]{2,1,0:T(8,128)(2,1)S(1)} %hop.13.refs_0_), channel_id=1, source_target_pairs={{8,16},{16,8},{9,17},{17,9},{10,18},{18,10},{11,19},{19,11},{12,20... | collective-permute-start | bytes 798728 | tf_op jit(solution)/shard_map/ppermute | solution.py:330
  70.6 17.9 %collective-permute-start.23 = (s16[1,1040,128]{2,1,0:T(8,128)(2,1)}, s16[1,1040,128]{2,1,0:T(8,128)(2,1)}, u32[]{:S(2)}, u32[]{:S(2)}) collective-permute-start(s16[1,1040,128]{2,1,0:T(8,128)(2,1)} %get-tuple-element.50), channel_id=1, source_target_pairs={{0,8},{24,16},{1,9},{25,17},{2,10},{26,18},{3,11},{27,19},{4,12},{... | collective-permute-start | bytes 798728 | tf_op jit(solution)/shard_map/ppermute | solution.py:330
  78.1 14.6 %collective-permute-start.25 = (s16[1,1040,128]{2,1,0:T(8,128)(2,1)S(1)}, s16[1,1040,128]{2,1,0:T(8,128)(2,1)}, u32[]{:S(2)}, u32[]{:S(2)}) collective-permute-start(s16[1,1040,128]{2,1,0:T(8,128)(2,1)S(1)} %hop.10.refs_0_), channel_id=1, source_target_pairs={{8,16},{16,8},{9,17},{17,9},{10,18},{18,10},{11,19},{19,11},{12,20... | collective-permute-start | bytes 798728 | tf_op jit(solution)/shard_map/ppermute | solution.py:330
  79.5 5.2 %copy-start.3 = (f32[16,8,32,128]{3,2,1,0:T(8,128)S(1)}, f32[16,8,32,128]{3,2,1,0:T(8,128)}, u32[]{:S(2)}) copy-start(f32[16,8,32,128]{3,2,1,0:T(8,128)} %copy-done.2) | copy-start | bytes 6291460
  79.5 14.5 %collective-permute-start.16 = (s16[1,1040,128]{2,1,0:T(8,128)(2,1)S(1)}, s16[1,1040,128]{2,1,0:T(8,128)(2,1)}, u32[]{:S(2)}, u32[]{:S(2)}) collective-permute-start(s16[1,1040,128]{2,1,0:T(8,128)(2,1)S(1)} %hop.12.refs_0_), channel_id=1, source_target_pairs={{8,16},{16,8},{9,17},{17,9},{10,18},{18,10},{11,19},{19,11},{12,20... | collective-permute-start | bytes 798728 | tf_op jit(solution)/shard_map/ppermute | solution.py:330
  82.7 4.1 %copy-start.5 = (f32[16,8,32,128]{3,2,1,0:T(8,128)S(1)}, f32[16,8,32,128]{3,2,1,0:T(8,128)}, u32[]{:S(2)}) copy-start(f32[16,8,32,128]{3,2,1,0:T(8,128)} %copy-done.4) | copy-start | bytes 6291460
  82.7 11.2 %collective-permute-start.26 = (s16[1,1040,128]{2,1,0:T(8,128)(2,1)S(1)}, s16[1,1040,128]{2,1,0:T(8,128)(2,1)}, u32[]{:S(2)}, u32[]{:S(2)}) collective-permute-start(s16[1,1040,128]{2,1,0:T(8,128)(2,1)S(1)} %hop.14.refs_0_), channel_id=1, source_target_pairs={{8,0},{0,8},{16,24},{24,16},{9,1},{1,9},{17,25},{25,17},{10,2},{2,... | collective-permute-start | bytes 798728 | tf_op jit(solution)/shard_map/ppermute | solution.py:330
  86.4 10.3 %collective-permute-start.20 = (s16[1,1040,128]{2,1,0:T(8,128)(2,1)S(1)}, s16[1,1040,128]{2,1,0:T(8,128)(2,1)}, u32[]{:S(2)}, u32[]{:S(2)}) collective-permute-start(s16[1,1040,128]{2,1,0:T(8,128)(2,1)S(1)} %hop.15.refs_0_), channel_id=1, source_target_pairs={{8,0},{0,8},{16,24},{24,16},{9,1},{1,9},{17,25},{25,17},{10,2},{2,... | collective-permute-start | bytes 798728 | tf_op jit(solution)/shard_map/ppermute | solution.py:330
  88.5 11.0 %collective-permute-start.22 = (s16[1,1040,128]{2,1,0:T(8,128)(2,1)S(1)}, s16[1,1040,128]{2,1,0:T(8,128)(2,1)}, u32[]{:S(2)}, u32[]{:S(2)}) collective-permute-start(s16[1,1040,128]{2,1,0:T(8,128)(2,1)S(1)} %hop.16.refs_0_), channel_id=1, source_target_pairs={{8,0},{0,8},{16,24},{24,16},{9,1},{1,9},{17,25},{25,17},{10,2},{2,... | collective-permute-start | bytes 798728 | tf_op jit(solution)/shard_map/ppermute | solution.py:330
  92.7 6.8 %collective-permute-start.24 = (s16[1,1040,128]{2,1,0:T(8,128)(2,1)}, s16[1,1040,128]{2,1,0:T(8,128)(2,1)S(1)}, u32[]{:S(2)}, u32[]{:S(2)}) collective-permute-start(s16[1,1040,128]{2,1,0:T(8,128)(2,1)} %hop.17), channel_id=1, source_target_pairs={{8,16},{16,8},{9,17},{17,9},{10,18},{18,10},{11,19},{19,11},{12,20... | collective-permute-start | bytes 798728 | tf_op jit(solution)/shard_map/ppermute | solution.py:330
